TPU v7x, 32 devices: a whole 2x2x4 slice. The times are simulated.
32 devices in a mesh: lon: 4 (over y, core), lat: 4 (over z), segment: 2 (over x).
Axes of the slice: x: 2, y: 2, z: 4, core: 2. Of those that a mesh axis runs over, the one named last changes fastest.
Arguments:
- inputs: bfloat16 [2, 64, 16, 512], P(None, 'lat', 'lon'), may hold values from -6 to 6
- cotangent: bfloat16 [2, 64, 16, 512], P(None, 'lat', 'lon'), may hold values from -6 to 6
- weights: bfloat16 [2, 3, 512, 512], P('segment'), may hold values from -0.15625 to 0.15625
- basis_values: float32 [64, 9, 3], replicated, may hold values from 0.05 to 0.5
- lat_step: int32 [64, 9], replicated, may hold values from -2 to 2, as said below
- lon_step: int32 [64, 9], replicated, may hold values from -2 to 2, as said below
Outputs:
- section_out: bfloat16 [2, 2, 64, 16, 512], P('segment', None, 'lat', 'lon')
- section_grad: bfloat16 [2, 2, 64, 16, 512], P('segment', None, 'lat', 'lon')
- weight_grad: float32 [2, 786432], P('segment', ('lon', 'lat'))
Inputs may be any that keep to these rules, and one draw needn't show every extreme that they name: `lat_step`: row offsets of the support points; 2 and -2 each occur. `lon_step`: column offsets of the support points; 2 and -2 each occur.
All inputs are finite; a program needn't handle non-finite values.
Results may differ from a plain program's by a relative error of at most 0.017.
Values may be sent and summed in bfloat16 or wider, within the bound.
No kernel may reach another device: no remote copies, remote signals or barrier semaphores. Data moves between devices by JAX's collectives and lax.ppermute only.
A program may use at most 64 MiB of HBM per device.

v0:
```python
import math

import jax
import jax.numpy as jnp
from jax import lax
from jax.sharding import PartitionSpec as P

BASIS = 3
TAPS = 9
REACH = 2


def with_halo(array, sides, width):
    for axis, dim in sides:
        size, length = (lax.axis_size(axis), array.shape[dim])
        up = [(i, (i + 1) % size) for i in range(size)]
        down = [(j, i) for i, j in up]
        last = lax.slice_in_dim(array, length - width, length, axis=dim)
        first = lax.slice_in_dim(array, 0, width, axis=dim)
        before = lax.ppermute(last, axis, up)
        after = lax.ppermute(first, axis, down)
        array = jnp.concatenate([before, array, after], axis=dim)
    return array


def shifted(block, axis, distance):
    devices = range(lax.axis_size(axis))
    route = [(i - distance, i) for i in devices if i - distance in devices]
    return lax.ppermute(block, axis, route)


def widen(features):
    return with_halo(features, (("lon", 2), ("lat", 1)), REACH)


def pass_ahead(result):
    return shifted(result, "segment", 1)


def pass_behind(result):
    return shifted(result, "segment", -1)


def build_tables(basis_values, lat_step, lon_step, lat_rows, lon_cols, lat_index, lat_total):
    pad_rows = lat_rows + 2 * REACH
    pad_cols = lon_cols + 2 * REACH
    lat_padded = jnp.pad(lat_step, ((REACH, REACH), (0, 0)))
    lon_padded = jnp.pad(lon_step, ((REACH, REACH), (0, 0)))
    basis_padded = jnp.pad(basis_values, ((REACH, REACH), (0, 0), (0, 0)))
    row_start = lat_index * lat_rows
    lat_near = lax.dynamic_slice_in_dim(lat_padded, row_start, pad_rows, 0)
    lon_near = lax.dynamic_slice_in_dim(lon_padded, row_start, pad_rows, 0)
    basis_near = lax.dynamic_slice_in_dim(basis_padded, row_start, pad_rows, 0)
    lat_own = lat_near[REACH : REACH + lat_rows]
    lon_own = lon_near[REACH : REACH + lat_rows]
    basis_own = basis_near[REACH : REACH + lat_rows]
    own_rows = row_start + jnp.arange(lat_rows)
    inside = (own_rows[:, None] + lat_own >= 0) & (own_rows[:, None] + lat_own < lat_total)
    row_grid = jnp.arange(lat_rows)[:, None, None]
    col_grid = jnp.arange(lon_cols)[None, :, None]
    source = (row_grid + REACH + lat_own[:, None, :]) * pad_cols + (
        col_grid + REACH + lon_own[:, None, :]
    )
    tap_weight = jnp.where(inside[:, None, :, None], basis_own[:, None, :, :], 0.0)
    tap_weight = jnp.broadcast_to(tap_weight, (lat_rows, lon_cols, TAPS, BASIS))
    picker = (source[..., None] == jnp.arange(pad_rows * pad_cols)).astype(jnp.float32)
    forward_map = jnp.einsum("ijkb,ijks->bijs", tap_weight, picker, precision=lax.Precision.HIGHEST)
    forward_map = forward_map.reshape(BASIS, lat_rows * lon_cols, pad_rows * pad_cols)
    near_rows = row_start - REACH + jnp.arange(pad_rows)
    real_row = (near_rows >= 0) & (near_rows < lat_total)
    pad_row_grid = jnp.arange(pad_rows)[:, None, None]
    pad_col_grid = jnp.arange(pad_cols)[None, :, None]
    target_row = pad_row_grid - REACH + lat_near[:, None, :]
    target_col = pad_col_grid - REACH + lon_near[:, None, :]
    landed = (
        (target_row >= 0)
        & (target_row < lat_rows)
        & (target_col >= 0)
        & (target_col < lon_cols)
        & real_row[:, None, None]
    )
    target = target_row * lon_cols + target_col
    back_weight = jnp.where(landed[..., None], basis_near[:, None, :, :], 0.0)
    catcher = (target[..., None] == jnp.arange(lat_rows * lon_cols)).astype(jnp.float32)
    backward_map = jnp.einsum(
        "pqkb,pqkt->btpq", back_weight, catcher, precision=lax.Precision.HIGHEST
    )
    backward_map = backward_map.reshape(BASIS, lat_rows * lon_cols, pad_rows * pad_cols)
    return (forward_map, backward_map)


def per_device(inputs, cotangent, weights, basis_values, lat_step, lon_step):
    members, lat_rows, lon_cols, channels = inputs.shape
    pad_rows = lat_rows + 2 * REACH
    pad_cols = lon_cols + 2 * REACH
    cells = lat_rows * lon_cols
    lat_index = lax.axis_index("lat")
    lat_total = lat_rows * lax.axis_size("lat")
    segment_index = lax.axis_index("segment")
    depth = lax.axis_size("segment")
    grad_scale = 1.0 / math.sqrt(members * lat_total * lon_cols * lax.axis_size("lon"))
    forward_map, backward_map = build_tables(
        basis_values, lat_step, lon_step, lat_rows, lon_cols, lat_index, lat_total
    )
    kernel = weights[0]
    keep_spread = jnp.zeros((BASIS, members, cells, channels), jnp.bfloat16)
    keep_mixed = jnp.zeros((members, cells, channels), jnp.float32)
    keep_gate = jnp.zeros((members, cells, channels), jnp.bfloat16)
    section_out = jnp.zeros(inputs.shape, jnp.bfloat16)
    section_grad = jnp.zeros(inputs.shape, jnp.bfloat16)
    carry = inputs
    for tick_num in range(depth):
        layer_count = carry.shape[0]
        layer_padded = (
            widen(carry).reshape(layer_count, pad_rows * pad_cols, channels).astype(jnp.float32)
        )
        spread = jnp.einsum(
            "bts,msc->bmtc", forward_map, layer_padded, precision=lax.Precision.HIGHEST
        ).astype(jnp.bfloat16)
        layer_mixed = jnp.einsum(
            "bmtc,bcd->mtd", spread, kernel, preferred_element_type=jnp.float32
        )
        result = (
            carry.reshape(layer_count, cells, channels).astype(jnp.float32)
            + jax.nn.silu(layer_mixed)
        ).astype(jnp.bfloat16)
        spread, mixed, result = (spread, layer_mixed, result.reshape(carry.shape))
        here = segment_index == tick_num
        keep_spread = jnp.where(here, spread, keep_spread)
        keep_mixed = jnp.where(here, mixed, keep_mixed)
        section_out = jnp.where(here, result, section_out)
        if tick_num + 1 < depth:
            carry = pass_ahead(result)
    grad = cotangent
    for tick_num in range(depth):
        count = grad.shape[0]
        flat_grad = grad.reshape(count, cells, channels).astype(jnp.float32)
        sigma = jax.nn.sigmoid(keep_mixed)
        gate_grad = (flat_grad * sigma * (1.0 + keep_mixed * (1.0 - sigma))).astype(jnp.bfloat16)
        feature_grad = jnp.einsum(
            "mtd,bcd->bmtc", gate_grad, kernel, preferred_element_type=jnp.float32
        ).astype(jnp.bfloat16)
        padded = widen(feature_grad.reshape(BASIS * count, lat_rows, lon_cols, channels))
        padded = padded.reshape(BASIS, count, pad_rows * pad_cols, channels).astype(jnp.float32)
        pulled = jnp.einsum("bts,bmsc->mtc", backward_map, padded, precision=lax.Precision.HIGHEST)
        new_grad = (flat_grad + pulled).astype(jnp.bfloat16).reshape(grad.shape)
        gate_grad, new_grad = (gate_grad, new_grad)
        here = segment_index == depth - 1 - tick_num
        keep_gate = jnp.where(here, gate_grad, keep_gate)
        section_grad = jnp.where(here, new_grad, section_grad)
        if tick_num + 1 < depth:
            grad = pass_behind(new_grad)
    local_grad = (
        jnp.einsum("bmtc,mtd->bcd", keep_spread, keep_gate, preferred_element_type=jnp.float32)
        * grad_scale
    )
    owners = lax.axis_size("lon") * lax.axis_size("lat")
    grad_rows = local_grad.reshape(owners, -1)
    weight_grad = lax.psum_scatter(grad_rows, ("lon", "lat"), scatter_dimension=0, tiled=True)
    return (section_out[None], section_grad[None], weight_grad)


def solution(mesh):
    return jax.shard_map(
        per_device,
        mesh=mesh,
        in_specs=(
            P(None, "lat", "lon", None),
            P(None, "lat", "lon", None),
            P("segment", None, None, None),
            P(),
            P(),
            P(),
        ),
        out_specs=(
            P("segment", None, "lat", "lon", None),
            P("segment", None, "lat", "lon", None),
            P("segment", ("lon", "lat")),
        ),
        check_vma=False,
    )
```

profile of v0, /device:TPU:0, one launch (start us, length us, event | category | flops | bytes accessed | tf_op | source)
XLA Modules:
  0.0 191.4 jit_solution(11581652797517794108)
XLA Ops:
  7.2 1.2 fusion.86
  8.4 2.5 %collective-permute-start.1 = (bf16[2,16,2,512]{3,2,1,0:T(2,128)(2,1)S(1)}, bf16[2,16,2,512]{3,2,1,0:T(2,128)(2,1)S(1)}, u32[]{:S(2)}, u32[]{:S(2)}) collective-permute-start(bf16[2,16,2,512]{3,2,1,0:T(2,128)(2,1)S(1)} %get-tuple-element.18), channel_id=1, source_target_pairs={{8,0},{16,8},{24,16},{0,24},{9,1},{17,9},{25,17},{1,25},{10,2},{18... | collective-permute-start | bytes 196616 | tf_op jit(solution)/shard_map/ppermute | solution.py:21
  10.9 0.8 add_multiply_fusion
  11.9 0.8 compare_and_fusion.1
  12.7 0.8 dynamic-slice_select_fusion
  13.5 0.1 copy.39
  13.6 0.8 pad_dynamic-slice_fusion.2
  14.7 0.5 fusion.34
  15.2 0.8 pad_maximum_fusion.13
  16.0 3.7 %collective-permute-start.3 = (bf16[2,2,8,512]{3,2,1,0:T(8,128)(2,1)S(1)}, bf16[2,2,8,512]{3,2,1,0:T(8,128)(2,1)S(1)}, u32[]{:S(2)}, u32[]{:S(2)}) collective-permute-start(bf16[2,2,8,512]{3,2,1,0:T(8,128)(2,1)S(1)} %get-tuple-element.14), channel_id=1, source_target_pairs={{2,0},{4,2},{6,4},{0,6},{3,1},{5,3},{7,5},{1,7},{10,8},{12,10},{14... | collective-permute-start | bytes 98312 | tf_op jit(solution)/shard_map/ppermute | solution.py:21
  19.7 0.7 add_add_fusion
  20.4 1.0 collective-permute-done.3
  21.5 3.9 %collective-permute-done.2 = bf16[2,2,8,512]{3,2,1,0:T(8,128)(2,1)S(1)} collective-permute-done((bf16[2,2,8,512]{3,2,1,0:T(8,128)(2,1)S(1)}, bf16[2,2,8,512]{3,2,1,0:T(8,128)(2,1)S(1)}, u32[]{:S(2)}, u32[]{:S(2)}) %collective-permute-start.2) | collective-permute-done | bytes 32800 | tf_op jit(solution)/shard_map/ppermute | solution.py:20
  25.4 0.6 fusion.15
  26.1 0.4 add_convert_fusion.1
  26.6 3.4 %collective-permute-start.4 = (bf16[2,16,4,512]{3,2,1,0:T(4,128)(2,1)S(1)}, bf16[2,16,4,512]{3,2,1,0:T(4,128)(2,1)S(1)}, u32[]{:S(2)}, u32[]{:S(2)}) collective-permute-start(bf16[2,16,4,512]{3,2,1,0:T(4,128)(2,1)S(1)} %reshape.167), channel_id=1, source_target_pairs={{0,1},{2,3},{4,5},{6,7},{8,9},{10,11},{12,13},{14,15},{16,17},{18,... | collective-permute-start | bytes 393224 | tf_op jit(solution)/shard_map/ppermute | solution.py:29
  30.1 2.4 %collective-permute-done.4 = bf16[2,16,4,512]{3,2,1,0:T(4,128)(2,1)S(1)} collective-permute-done((bf16[2,16,4,512]{3,2,1,0:T(4,128)(2,1)S(1)}, bf16[2,16,4,512]{3,2,1,0:T(4,128)(2,1)S(1)}, u32[]{:S(2)}, u32[]{:S(2)}) %collective-permute-start.4) | collective-permute-done | bytes 131104 | tf_op jit(solution)/shard_map/ppermute | solution.py:29
  32.6 0.3 collective-permute-start.6
  32.9 0.3 collective-permute-start.5
  33.3 1.5 collective-permute-done.6
  34.8 2.4 %collective-permute-done.5 = bf16[2,16,2,512]{3,2,1,0:T(2,128)(2,1)S(1)} collective-permute-done((bf16[2,16,2,512]{3,2,1,0:T(2,128)(2,1)S(1)}, bf16[2,16,2,512]{3,2,1,0:T(2,128)(2,1)S(1)}, u32[]{:S(2)}, u32[]{:S(2)}) %collective-permute-start.5) | collective-permute-done | bytes 65568 | tf_op jit(solution)/shard_map/ppermute | solution.py:20
  37.2 0.3 collective-permute-start.8
  37.5 1.8 collective-permute-start.7
  39.4 0.1 copy.46
  39.5 0.1 copy.45
  39.6 1.6 collective-permute-done.8
  41.2 2.1 %collective-permute-done.7 = bf16[2,2,8,512]{3,2,1,0:T(8,128)(2,1)S(1)} collective-permute-done((bf16[2,2,8,512]{3,2,1,0:T(8,128)(2,1)S(1)}, bf16[2,2,8,512]{3,2,1,0:T(8,128)(2,1)S(1)}, u32[]{:S(2)}, u32[]{:S(2)}) %collective-permute-start.7) | collective-permute-done | bytes 32800 | tf_op jit(solution)/shard_map/ppermute | solution.py:20
  43.3 0.6 fusion.16
  43.9 0.5 multiply_convert_fusion.1
  44.4 0.3 copy-done.6
  44.6 0.6 fusion.20
  45.3 0.1 reshape.169
  45.4 0.3 fusion.84
  45.8 0.5 collective-permute-start.9
  46.4 4.4 %collective-permute-done.10 = bf16[6,16,2,512]{3,2,1,0:T(2,128)(2,1)S(1)} collective-permute-done((bf16[6,16,2,512]{3,2,1,0:T(2,128)(2,1)S(1)}, bf16[6,16,2,512]{3,2,1,0:T(2,128)(2,1)S(1)}, u32[]{:S(2)}, u32[]{:S(2)}) %collective-permute-start.10) | collective-permute-done | bytes 196640 | tf_op jit(solution)/shard_map/ppermute | solution.py:21
  50.8 1.6 collective-permute-done.9
  52.5 0.8 pad_maximum_fusion.7
  53.3 2.0 %collective-permute-start.11 = (bf16[6,2,8,512]{3,2,1,0:T(8,128)(2,1)}, bf16[6,2,8,512]{3,2,1,0:T(8,128)(2,1)}, u32[]{:S(2)}, u32[]{:S(2)}) collective-permute-start(bf16[6,2,8,512]{3,2,1,0:T(8,128)(2,1)} %get-tuple-element.5), channel_id=1, source_target_pairs={{0,2},{2,4},{4,6},{6,0},{1,3},{3,5},{5,7},{7,1},{8,10},{10,12},{12... | collective-permute-start | bytes 294920 | tf_op jit(solution)/shard_map/ppermute | solution.py:20
  55.3 2.7 %fusion.8 = f32[20,8,64,3]{2,3,1,0:T(4,128)} fusion(s32[20,8,9]{2,1,0:T(8,128)} %add_add_fusion, f32[20,9,3]{1,2,0:T(4,128)S(1)} %copy.46, pred[20,8,9]{2,1,0:T(8,128)(4,1)S(1)} %fusion.75), kind=kOutput, calls=%fused_computation.10 | convolution fusion | flops 3414240 | bytes 132240 | tf_op jit(solution)/shard_map/pqkb,pqkt->btpq/dot_general | solution.py:85
  58.0 1.1 copy.55
  59.1 1.1 collective-permute-done.12
  60.2 1.5 pad_maximum_fusion
  61.8 0.7 fusion.32
  62.5 1.3 collective-permute-start.13
  63.8 5.6 %collective-permute-done.13 = bf16[2,16,4,512]{3,2,1,0:T(4,128)(2,1)S(1)} collective-permute-done((bf16[2,16,4,512]{3,2,1,0:T(4,128)(2,1)S(1)}, bf16[2,16,4,512]{3,2,1,0:T(4,128)(2,1)S(1)}, u32[]{:S(2)}, u32[]{:S(2)}) %collective-permute-start.13) | collective-permute-done | bytes 131104 | tf_op jit(solution)/shard_map/ppermute | solution.py:29
  69.4 1.1 multiply_convert_fusion
  70.5 2.3 %bitcast_multiply_fusion = f32[3,512,512]{2,1,0:T(8,128)} fusion(bf16[3,2,64,512]{3,2,0,1:T(8,128)(2,1)} %copy-done.6, bf16[3,2,64,512]{3,2,0,1:T(8,128)(2,1)S(1)} %copy-done.5, pred[]{:T(512)S(6)} %eq.38, pred[]{:T(512)S(6)} %eq.16, bf16[2,64,512]{2,1,0:T(8,128)(2,1)S(1)} %multiply_convert_fusion, bf16[2,64,512]{2,1,0:T(8,128)(2,1)S(1)} %copy-done.3), kind=kOutput, calls=%fused_computation | convolution fusion | flops 202637312 | bytes 4194306 | tf_op jit(solution)/shard_map/bmtc,mtd->bcd/dot_general | solution.py:154
  72.8 3.3 %reshape.175 = f32[16,49152]{1,0:T(8,128)} reshape(f32[3,512,512]{2,1,0:T(8,128)} %bitcast_multiply_fusion) | data formatting | bytes 6291456 | tf_op jit(solution)/shard_map/reshape | solution.py:158
  76.2 0.6 fusion.17
  77.0 1.1 fusion.83
  78.1 0.5 collective-permute-start.14
  78.6 0.6 dynamic-slice
  79.2 7.6 %collective-permute-done.15 = bf16[6,16,2,512]{3,2,1,0:T(2,128)(2,1)S(1)} collective-permute-done((bf16[6,16,2,512]{3,2,1,0:T(2,128)(2,1)}, bf16[6,16,2,512]{3,2,1,0:T(2,128)(2,1)S(1)}, u32[]{:S(2)}, u32[]{:S(2)}) %collective-permute-start.15) | collective-permute-done | bytes 196640 | tf_op jit(solution)/shard_map/ppermute | solution.py:21
  86.9 2.0 %collective-permute-done.14 = bf16[6,16,2,512]{3,2,1,0:T(2,128)(2,1)} collective-permute-done((bf16[6,16,2,512]{3,2,1,0:T(2,128)(2,1)}, bf16[6,16,2,512]{3,2,1,0:T(2,128)(2,1)}, u32[]{:S(2)}, u32[]{:S(2)}) %collective-permute-start.14) | collective-permute-done | bytes 196640 | tf_op jit(solution)/shard_map/ppermute | solution.py:20
  88.8 1.6 pad_maximum_fusion.4
  90.4 2.0 %collective-permute-start.16 = (bf16[6,2,8,512]{3,2,1,0:T(8,128)(2,1)}, bf16[6,2,8,512]{3,2,1,0:T(8,128)(2,1)}, u32[]{:S(2)}, u32[]{:S(2)}) collective-permute-start(bf16[6,2,8,512]{3,2,1,0:T(8,128)(2,1)} %get-tuple-element.3), channel_id=1, source_target_pairs={{0,2},{2,4},{4,6},{6,0},{1,3},{3,5},{5,7},{7,1},{8,10},{10,12},{12... | collective-permute-start | bytes 294920 | tf_op jit(solution)/shard_map/ppermute | solution.py:20
  92.5 0.7 select_n.112
  93.2 3.4 %collective-permute-done.17 = bf16[6,2,8,512]{3,2,1,0:T(8,128)(2,1)} collective-permute-done((bf16[6,2,8,512]{3,2,1,0:T(8,128)(2,1)}, bf16[6,2,8,512]{3,2,1,0:T(8,128)(2,1)}, u32[]{:S(2)}, u32[]{:S(2)}) %collective-permute-start.17) | collective-permute-done | bytes 98336 | tf_op jit(solution)/shard_map/ppermute | solution.py:21
  96.6 5.0 %collective-permute-done.16 = bf16[6,2,8,512]{3,2,1,0:T(8,128)(2,1)} collective-permute-done((bf16[6,2,8,512]{3,2,1,0:T(8,128)(2,1)}, bf16[6,2,8,512]{3,2,1,0:T(8,128)(2,1)}, u32[]{:S(2)}, u32[]{:S(2)}) %collective-permute-start.16) | collective-permute-done | bytes 98336 | tf_op jit(solution)/shard_map/ppermute | solution.py:20
  101.6 1.7 pad_maximum_fusion.1
  103.3 0.7 fusion.33
  104.0 0.7 select_n.118
  104.7 77.0 %all-reduce.6.cloned.1.call-done = f32[16,49152]{1,0:T(8,128)} async-done(((f32[16,49152]{1,0:T(8,128)}), f32[16,49152]{1,0:T(8,128)}) %all-reduce.6.cloned.1.call-update) | async-done | bytes 3145744
  181.7 2.9 %constant_dynamic-slice_fusion = f32[1,49152]{1,0:T(1,128)} fusion(f32[16,49152]{1,0:T(8,128)} %all-reduce.6.cloned.1.call-done, u32[]{:T(128)} %bitcast.49), kind=kLoop, calls=%fused_computation.112 | loop fusion | bytes 393220
  (60 shorter events, 1.5 us)
Async XLA Ops:
  7.2 18.9 %copy-start = (bf16[1,3,512,512]{3,2,1,0:T(8,128)(2,1)S(1)}, bf16[1,3,512,512]{3,2,1,0:T(8,128)(2,1)}, u32[]{:S(2)}) copy-start(bf16[1,3,512,512]{3,2,1,0:T(8,128)(2,1)} %param.8) | copy-start | bytes 4718596
  7.2 13.2 %copy-start.1 = (bf16[2,16,4,512]{3,2,1,0:T(4,128)(2,1)S(1)}, bf16[2,16,4,512]{3,2,1,0:T(4,128)(2,1)}, u32[]{:S(2)}) copy-start(bf16[2,16,4,512]{3,2,1,0:T(4,128)(2,1)} %param.6) | copy-start | bytes 393220
  7.2 174.5 %all-reduce.6.cloned.1.call-start = ((), (), s32[]{:S(2)}) async-start(), calls=%async_computation | async-start | bytes 6291456
  8.4 6.8 %collective-permute-start.1 = (bf16[2,16,2,512]{3,2,1,0:T(2,128)(2,1)S(1)}, bf16[2,16,2,512]{3,2,1,0:T(2,128)(2,1)S(1)}, u32[]{:S(2)}, u32[]{:S(2)}) collective-permute-start(bf16[2,16,2,512]{3,2,1,0:T(2,128)(2,1)S(1)} %get-tuple-element.18), channel_id=1, source_target_pairs={{8,0},{16,8},{24,16},{0,24},{9,1},{17,9},{25,17},{1,25},{10,2},{18... | collective-permute-start | bytes 196616 | tf_op jit(solution)/shard_map/ppermute | solution.py:21
  10.9 4.3 %collective-permute-start = (bf16[2,16,2,512]{3,2,1,0:T(2,128)(2,1)S(1)}, bf16[2,16,2,512]{3,2,1,0:T(2,128)(2,1)S(1)}, u32[]{:S(2)}, u32[]{:S(2)}) collective-permute-start(bf16[2,16,2,512]{3,2,1,0:T(2,128)(2,1)S(1)} %get-tuple-element.17), channel_id=1, source_target_pairs={{0,8},{8,16},{16,24},{24,0},{1,9},{9,17},{17,25},{25,1},{2,10},{10... | collective-permute-start | bytes 196616 | tf_op jit(solution)/shard_map/ppermute | solution.py:20
  16.0 5.4 %collective-permute-start.3 = (bf16[2,2,8,512]{3,2,1,0:T(8,128)(2,1)S(1)}, bf16[2,2,8,512]{3,2,1,0:T(8,128)(2,1)S(1)}, u32[]{:S(2)}, u32[]{:S(2)}) collective-permute-start(bf16[2,2,8,512]{3,2,1,0:T(8,128)(2,1)S(1)} %get-tuple-element.14), channel_id=1, source_target_pairs={{2,0},{4,2},{6,4},{0,6},{3,1},{5,3},{7,5},{1,7},{10,8},{12,10},{14... | collective-permute-start | bytes 98312 | tf_op jit(solution)/shard_map/ppermute | solution.py:21
  19.7 5.7 %collective-permute-start.2 = (bf16[2,2,8,512]{3,2,1,0:T(8,128)(2,1)S(1)}, bf16[2,2,8,512]{3,2,1,0:T(8,128)(2,1)S(1)}, u32[]{:S(2)}, u32[]{:S(2)}) collective-permute-start(bf16[2,2,8,512]{3,2,1,0:T(8,128)(2,1)S(1)} %get-tuple-element.13), channel_id=1, source_target_pairs={{0,2},{2,4},{4,6},{6,0},{1,3},{3,5},{5,7},{7,1},{8,10},{10,12},{12... | collective-permute-start | bytes 98312 | tf_op jit(solution)/shard_map/ppermute | solution.py:20
  26.1 13.3 %copy-start.4 = (bf16[3,2,64,512]{3,2,0,1:T(8,128)(2,1)}, bf16[3,2,64,512]{3,2,0,1:T(8,128)(2,1)S(1)}, u32[]{:S(2)}) copy-start(bf16[3,2,64,512]{3,2,0,1:T(8,128)(2,1)S(1)} %fusion.15) | copy-start | bytes 1179652
  26.1 3.9 %copy-start.9 = (s32[64,9]{0,1:T(8,128)S(1)}, s32[64,9]{0,1:T(8,128)}, u32[]{:S(2)}) copy-start(s32[64,9]{0,1:T(8,128)} %param.10) | copy-start | bytes 6916
  26.1 7.1 %copy-start.10 = (f32[64,9,3]{0,2,1:T(4,128)S(1)}, f32[64,9,3]{0,2,1:T(4,128)}, u32[]{:S(2)}) copy-start(f32[64,9,3]{0,2,1:T(4,128)} %param.9) | copy-start | bytes 20740
  26.1 13.2 %copy-start.8 = (bf16[2,16,4,512]{3,2,1,0:T(4,128)(2,1)S(1)}, bf16[2,16,4,512]{3,2,1,0:T(4,128)(2,1)}, u32[]{:S(2)}) copy-start(bf16[2,16,4,512]{3,2,1,0:T(4,128)(2,1)} %param.7) | copy-start | bytes 393220
  26.6 17.8 %copy-start.7 = (f32[2,64,512]{2,1,0:T(8,128)}, f32[2,64,512]{2,1,0:T(8,128)S(1)}, u32[]{:S(2)}) copy-start(f32[2,64,512]{2,1,0:T(8,128)S(1)} %get-tuple-element.20) | copy-start | bytes 786436
  26.6 5.9 %collective-permute-start.4 = (bf16[2,16,4,512]{3,2,1,0:T(4,128)(2,1)S(1)}, bf16[2,16,4,512]{3,2,1,0:T(4,128)(2,1)S(1)}, u32[]{:S(2)}, u32[]{:S(2)}) collective-permute-start(bf16[2,16,4,512]{3,2,1,0:T(4,128)(2,1)S(1)} %reshape.167), channel_id=1, source_target_pairs={{0,1},{2,3},{4,5},{6,7},{8,9},{10,11},{12,13},{14,15},{16,17},{18,... | collective-permute-start | bytes 393224 | tf_op jit(solution)/shard_map/ppermute | solution.py:29
  32.6 2.2 %collective-permute-start.6 = (bf16[2,16,2,512]{3,2,1,0:T(2,128)(2,1)S(1)}, bf16[2,16,2,512]{3,2,1,0:T(2,128)(2,1)S(1)}, u32[]{:S(2)}, u32[]{:S(2)}) collective-permute-start(bf16[2,16,2,512]{3,2,1,0:T(2,128)(2,1)S(1)} %get-tuple-element.16), channel_id=1, source_target_pairs={{8,0},{16,8},{24,16},{0,24},{9,1},{17,9},{25,17},{1,25},{10,2},{18... | collective-permute-start | bytes 196616 | tf_op jit(solution)/shard_map/ppermute | solution.py:21
  32.9 4.3 %collective-permute-start.5 = (bf16[2,16,2,512]{3,2,1,0:T(2,128)(2,1)S(1)}, bf16[2,16,2,512]{3,2,1,0:T(2,128)(2,1)S(1)}, u32[]{:S(2)}, u32[]{:S(2)}) collective-permute-start(bf16[2,16,2,512]{3,2,1,0:T(2,128)(2,1)S(1)} %get-tuple-element.15), channel_id=1, source_target_pairs={{0,8},{8,16},{16,24},{24,0},{1,9},{9,17},{17,25},{25,1},{2,10},{10... | collective-permute-start | bytes 196616 | tf_op jit(solution)/shard_map/ppermute | solution.py:20
  37.2 4.0 %collective-permute-start.8 = (bf16[2,2,8,512]{3,2,1,0:T(8,128)(2,1)S(1)}, bf16[2,2,8,512]{3,2,1,0:T(8,128)(2,1)S(1)}, u32[]{:S(2)}, u32[]{:S(2)}) collective-permute-start(bf16[2,2,8,512]{3,2,1,0:T(8,128)(2,1)S(1)} %get-tuple-element.12), channel_id=1, source_target_pairs={{2,0},{4,2},{6,4},{0,6},{3,1},{5,3},{7,5},{1,7},{10,8},{12,10},{14... | collective-permute-start | bytes 98312 | tf_op jit(solution)/shard_map/ppermute | solution.py:21
  37.5 5.7 %collective-permute-start.7 = (bf16[2,2,8,512]{3,2,1,0:T(8,128)(2,1)S(1)}, bf16[2,2,8,512]{3,2,1,0:T(8,128)(2,1)S(1)}, u32[]{:S(2)}, u32[]{:S(2)}) collective-permute-start(bf16[2,2,8,512]{3,2,1,0:T(8,128)(2,1)S(1)} %get-tuple-element.11), channel_id=1, source_target_pairs={{0,2},{2,4},{4,6},{6,0},{1,3},{3,5},{5,7},{7,1},{8,10},{10,12},{12... | collective-permute-start | bytes 98312 | tf_op jit(solution)/shard_map/ppermute | solution.py:20
  43.9 0.7 copy-start.6
  44.6 1.1 copy-start.2
  45.8 5.1 %collective-permute-start.10 = (bf16[6,16,2,512]{3,2,1,0:T(2,128)(2,1)S(1)}, bf16[6,16,2,512]{3,2,1,0:T(2,128)(2,1)S(1)}, u32[]{:S(2)}, u32[]{:S(2)}) collective-permute-start(bf16[6,16,2,512]{3,2,1,0:T(2,128)(2,1)S(1)} %get-tuple-element.10), channel_id=1, source_target_pairs={{8,0},{16,8},{24,16},{0,24},{9,1},{17,9},{25,17},{1,25},{10,2},{18... | collective-permute-start | bytes 589832 | tf_op jit(solution)/shard_map/ppermute | solution.py:21
  45.8 6.6 %collective-permute-start.9 = (bf16[6,16,2,512]{3,2,1,0:T(2,128)(2,1)S(1)}, bf16[6,16,2,512]{3,2,1,0:T(2,128)(2,1)S(1)}, u32[]{:S(2)}, u32[]{:S(2)}) collective-permute-start(bf16[6,16,2,512]{3,2,1,0:T(2,128)(2,1)S(1)} %get-tuple-element.9), channel_id=1, source_target_pairs={{0,8},{8,16},{16,24},{24,0},{1,9},{9,17},{17,25},{25,1},{2,10},{10... | collective-permute-start | bytes 589832 | tf_op jit(solution)/shard_map/ppermute | solution.py:20
  53.3 6.9 %collective-permute-start.12 = (bf16[6,2,8,512]{3,2,1,0:T(8,128)(2,1)}, bf16[6,2,8,512]{3,2,1,0:T(8,128)(2,1)S(1)}, u32[]{:S(2)}, u32[]{:S(2)}) collective-permute-start(bf16[6,2,8,512]{3,2,1,0:T(8,128)(2,1)} %get-tuple-element.6), channel_id=1, source_target_pairs={{2,0},{4,2},{6,4},{0,6},{3,1},{5,3},{7,5},{1,7},{10,8},{12,10},{14... | collective-permute-start | bytes 294920 | tf_op jit(solution)/shard_map/ppermute | solution.py:21
  53.3 6.9 %collective-permute-start.11 = (bf16[6,2,8,512]{3,2,1,0:T(8,128)(2,1)}, bf16[6,2,8,512]{3,2,1,0:T(8,128)(2,1)}, u32[]{:S(2)}, u32[]{:S(2)}) collective-permute-start(bf16[6,2,8,512]{3,2,1,0:T(8,128)(2,1)} %get-tuple-element.5), channel_id=1, source_target_pairs={{0,2},{2,4},{4,6},{6,0},{1,3},{3,5},{5,7},{7,1},{8,10},{10,12},{12... | collective-permute-start | bytes 294920 | tf_op jit(solution)/shard_map/ppermute | solution.py:20
  61.8 8.7 %copy-start.3 = (bf16[2,64,512]{2,1,0:T(8,128)(2,1)S(1)}, bf16[2,64,512]{2,1,0:T(8,128)(2,1)}, u32[]{:S(2)}) copy-start(bf16[2,64,512]{2,1,0:T(8,128)(2,1)} %copy-done.2) | copy-start | bytes 393220
  61.8 8.7 %copy-start.5 = (bf16[3,2,64,512]{3,2,0,1:T(8,128)(2,1)S(1)}, bf16[3,2,64,512]{3,2,0,1:T(8,128)(2,1)}, u32[]{:S(2)}) copy-start(bf16[3,2,64,512]{3,2,0,1:T(8,128)(2,1)} %copy-done.4) | copy-start | bytes 1179652
  62.5 6.9 %collective-permute-start.13 = (bf16[2,16,4,512]{3,2,1,0:T(4,128)(2,1)S(1)}, bf16[2,16,4,512]{3,2,1,0:T(4,128)(2,1)S(1)}, u32[]{:S(2)}, u32[]{:S(2)}) collective-permute-start(bf16[2,16,4,512]{3,2,1,0:T(4,128)(2,1)S(1)} %reshape.172), channel_id=1, source_target_pairs={{1,0},{3,2},{5,4},{7,6},{9,8},{11,10},{13,12},{15,14},{17,16},{19,... | collective-permute-start | bytes 393224 | tf_op jit(solution)/shard_map/ppermute | solution.py:29
  76.2 2.4 %copy-start.11 = (u32[32]{0:T(128)S(1)}, u32[32]{0:T(128)}, u32[]{:S(2)}) copy-start(u32[32]{0:T(128)} %constant.63) | copy-start | bytes 388
  78.1 8.8 %collective-permute-start.15 = (bf16[6,16,2,512]{3,2,1,0:T(2,128)(2,1)}, bf16[6,16,2,512]{3,2,1,0:T(2,128)(2,1)S(1)}, u32[]{:S(2)}, u32[]{:S(2)}) collective-permute-start(bf16[6,16,2,512]{3,2,1,0:T(2,128)(2,1)} %get-tuple-element.8), channel_id=1, source_target_pairs={{8,0},{16,8},{24,16},{0,24},{9,1},{17,9},{25,17},{1,25},{10,2},{18... | collective-permute-start | bytes 589832 | tf_op jit(solution)/shard_map/ppermute | solution.py:21
  78.1 10.8 %collective-permute-start.14 = (bf16[6,16,2,512]{3,2,1,0:T(2,128)(2,1)}, bf16[6,16,2,512]{3,2,1,0:T(2,128)(2,1)}, u32[]{:S(2)}, u32[]{:S(2)}) collective-permute-start(bf16[6,16,2,512]{3,2,1,0:T(2,128)(2,1)} %get-tuple-element.7), channel_id=1, source_target_pairs={{0,8},{8,16},{16,24},{24,0},{1,9},{9,17},{17,25},{25,1},{2,10},{10... | collective-permute-start | bytes 589832 | tf_op jit(solution)/shard_map/ppermute | solution.py:20
  90.4 6.2 %collective-permute-start.17 = (bf16[6,2,8,512]{3,2,1,0:T(8,128)(2,1)}, bf16[6,2,8,512]{3,2,1,0:T(8,128)(2,1)}, u32[]{:S(2)}, u32[]{:S(2)}) collective-permute-start(bf16[6,2,8,512]{3,2,1,0:T(8,128)(2,1)} %get-tuple-element.4), channel_id=1, source_target_pairs={{2,0},{4,2},{6,4},{0,6},{3,1},{5,3},{7,5},{1,7},{10,8},{12,10},{14... | collective-permute-start | bytes 294920 | tf_op jit(solution)/shard_map/ppermute | solution.py:21
  90.4 11.2 %collective-permute-start.16 = (bf16[6,2,8,512]{3,2,1,0:T(8,128)(2,1)}, bf16[6,2,8,512]{3,2,1,0:T(8,128)(2,1)}, u32[]{:S(2)}, u32[]{:S(2)}) collective-permute-start(bf16[6,2,8,512]{3,2,1,0:T(8,128)(2,1)} %get-tuple-element.3), channel_id=1, source_target_pairs={{0,2},{2,4},{4,6},{6,0},{1,3},{3,5},{5,7},{7,1},{8,10},{10,12},{12... | collective-permute-start | bytes 294920 | tf_op jit(solution)/shard_map/ppermute | solution.py:20
Sparse Core Ops, SparseCore 0:
  76.3 105.3 all-reduce.5
where the time goes:
time: 192 us; the launch traced here: 191 us
  waiting for transfers between devices  123 us (64%)
  starting transfers between devices  18.6 us (10%)
  between operations  14.4 us (8%)
  local copies, waits for them, and re-layouts  13.6 us (7%)
  other arithmetic  11.8 us (6%)
  matrix products  10.3 us (5%)
    unnamed x2, waiting for transfers between devices  77 us
    ppermute x8, waiting for transfers between devices, with_halo(): after = lax.ppermute(first, axis, down)  20.7 us
    ppermute x8, waiting for transfers between devices, with_halo(): before = lax.ppermute(last, axis, up)  17 us
    ppermute x2, waiting for transfers between devices, shifted(): return lax.ppermute(block, axis, route)  7.96 us
    ppermute x8, starting transfers between devices, with_halo(): before = lax.ppermute(last, axis, up)  7.06 us
    ppermute x8, starting transfers between devices, with_halo(): after = lax.ppermute(first, axis, down)  6.81 us
    ppermute x2, starting transfers between devices, shifted(): return lax.ppermute(block, axis, route)  4.69 us
    unnamed x26, local copies, waits for them, and re-layouts  3.87 us
  transfers between devices with their start and end apart: 19, of which 16 were waited for; matrix products, arithmetic and copies ran while one was open for 9% of the time, Pallas kernels for 0%

commit v1 on v0

--- a/solution.py
+++ b/solution.py
@@ -1,8 +1,11 @@
+import functools
 import math
 
 import jax
 import jax.numpy as jnp
 from jax import lax
+from jax.experimental import pallas as pl
+from jax.experimental.pallas import tpu as pltpu
 from jax.sharding import PartitionSpec as P
 
 BASIS = 3
@@ -160,22 +163,361 @@
     return (section_out[None], section_grad[None], weight_grad)
 
 
+HALO = 8
+BAND = 8
+
+
+def swap(axis, bit):
+    return [(i, i ^ bit) for i in range(lax.axis_size(axis))]
+
+
+def window_plan(lat_rows):
+    first = [(a, min(max(a - 4, -HALO), lat_rows + HALO - 16)) for a in range(-HALO, lat_rows + HALO, BAND)]
+    second = [(a, a - 4) for a in range(-4, lat_rows + 4, BAND)]
+    return first, second
+
+
+def tap_tables(basis_values, lat_step, lon_step, lat_rows, lon_cols, blocks, lat_index, lon_index, lat_total):
+    near = lat_rows + 2 * HALO
+    base = lat_index * lat_rows
+    steps = jnp.concatenate([lat_step, lon_step], axis=1)
+    steps = lax.dynamic_slice_in_dim(jnp.pad(steps, ((HALO, HALO), (0, 0))), base, near, 0)
+    basis = basis_values.reshape(basis_values.shape[0], TAPS * BASIS)
+    basis = lax.dynamic_slice_in_dim(jnp.pad(basis, ((HALO, HALO), (0, 0))), base, near, 0)
+    first, second = window_plan(lat_rows)
+    plan = first + second
+    rows = jnp.array([[a + r for r in range(BAND)] for a, _ in plan], jnp.int32)
+    starts = jnp.array([w for _, w in plan], jnp.int32)
+    pick = lambda table: jnp.stack([table[a + HALO : a + HALO + BAND] for a, _ in plan])
+    step_rows = pick(steps)
+    basis_rows = pick(basis)
+    lat_near, lon_near = step_rows[..., :TAPS], step_rows[..., TAPS:]
+    own = rows + base
+    target = own[..., None] + lat_near
+    inside = (own[..., None] >= 0) & (own[..., None] < lat_total) & (target >= 0) & (target < lat_total)
+    local_row = rows[..., None] + lat_near - starts[:, None, None]
+    shape = (len(plan), blocks, BAND, lon_cols, TAPS)
+    block_ids = jnp.arange(blocks, dtype=jnp.int32) ^ lon_index
+    column = block_ids[:, None, None, None] * lon_cols + jnp.arange(lon_cols, dtype=jnp.int32)[:, None]
+    column = jnp.mod(column[None] + lon_near[:, None, :, None, :], blocks * lon_cols)
+    place = ((column // lon_cols) ^ lon_index) * (16 * lon_cols) + local_row[:, None, :, None, :] * lon_cols + column % lon_cols
+    place = jnp.where(inside[:, None, :, None, :], place, -1)
+    spread_basis = jnp.broadcast_to(basis_rows[:, None, :, None, :], shape[:-1] + (TAPS * BASIS,))
+    cells = len(plan) * blocks * BAND * lon_cols
+    return place.reshape(cells, TAPS), spread_basis.reshape(cells, TAPS * BASIS)
+
+
+def map_kernel(firsts, cells, window, place_ref, basis_ref, forward_ref, backward_ref):
+    total = place_ref.shape[0] // cells
+    lane = lax.broadcasted_iota(jnp.int32, (cells, window), 1)
+    for g in range(total):
+        span = slice(g * cells, (g + 1) * cells)
+        hits = [place_ref[span, k : k + 1] == lane for k in range(TAPS)]
+        for b in range(BASIS):
+            table = jnp.zeros((cells, window), jnp.float32)
+            for k in range(TAPS):
+                at = k * BASIS + b
+                table = table + jnp.where(hits[k], basis_ref[span, at : at + 1], 0.0)
+            forward_ref[g, b * cells : (b + 1) * cells, :] = table.astype(jnp.bfloat16)
+            if g >= firsts:
+                backward_ref[g - firsts, :, b * cells : (b + 1) * cells] = table.T.astype(jnp.bfloat16)
+
+
+def dot(a, b):
+    return jnp.dot(a, b, preferred_element_type=jnp.float32)
+
+
+def dot_nt(a, b):
+    return lax.dot_general(a, b, (((1,), (1,)), ((), ())), preferred_element_type=jnp.float32)
+
+
+def dot_tn(a, b):
+    return lax.dot_general(a, b, (((0,), (0,)), ((), ())), preferred_element_type=jnp.float32)
+
+
+def make_chain(lat_rows, lon_cols, blocks, members, channels, lat_devices):
+    first, second = window_plan(lat_rows)
+    nf, ns = len(first), len(second)
+    band = BAND * lon_cols
+    cells = blocks * band
+    win = 16 * lon_cols
+    own = lat_rows * lon_cols
+    x_len = (lat_rows + 2 * HALO) * lon_cols
+    c_len = (lat_rows + HALO) * lon_cols
+    edge = HALO * lon_cols
+    half_edge = edge // 2
+    width = BASIS * channels
+    lanes = 128
+    pieces = channels // lanes
+
+    def chain(idx, x0, x1, x2, x3, w_own, w_a, w_b, forward, backward, out_ref, grad_ref, gate_ref, own_ref, p1, p2, p3, w, s0, s1, slope, mid, gates, feat, pull, grads):
+        blk = (x0, x1, x2, x3)
+        seg, lon, lat = idx[0], idx[1], idx[2]
+        half = w_a.shape[0]
+        core = lon % 2
+        w[pl.ds(pl.multiple_of(seg * width, width), width), :] = w_own[...]
+        other = (1 - seg) * width
+        w[pl.ds(pl.multiple_of(other + core * half, half), half), :] = w_a[...]
+        w[pl.ds(pl.multiple_of(other + (1 - core) * half, half), half), :] = w_b[...]
+        for m in range(members):
+            for g, (a, start) in enumerate(first):
+                o = (start + HALO) * lon_cols
+                near = jnp.concatenate([r[m, o : o + win, :] for r in blk], axis=0)
+                got = dot(forward[g], near).astype(jnp.bfloat16)
+                at = (m * nf + g) * cells
+                for b in range(BASIS):
+                    s0[at : at + cells, b * channels : (b + 1) * channels] = got[b * cells : (b + 1) * cells]
+        for m in range(members):
+            for g in range(nf):
+                at = (m * nf + g) * cells
+                mixed = dot(s0[at : at + cells, :], w[0:width, :])
+                sigma = jax.nn.sigmoid(mixed)
+                here = jnp.concatenate([r[m, g * band : (g + 1) * band, :] for r in blk], axis=0)
+                value = (here.astype(jnp.float32) + mixed * sigma).astype(jnp.bfloat16)
+                mid[m, :, g * band : (g + 1) * band, :] = value.reshape(blocks, band, channels)
+                tilt = sigma * (1.0 + mixed * (1.0 - sigma))
+                slope[m, :, g * band : (g + 1) * band, :] = tilt.reshape(blocks, band, channels)
+        for m in range(members):
+            for g in range(ns):
+                near = mid[m, :, g * band : g * band + win, :].reshape(blocks * win, channels)
+                got = dot(forward[nf + g], near).astype(jnp.bfloat16)
+                at = (m * ns + g) * cells
+                for b in range(BASIS):
+                    s1[at : at + cells, b * channels : (b + 1) * channels] = got[b * cells : (b + 1) * cells]
+        for m in range(members):
+            for g in range(ns):
+                at = (m * ns + g) * cells
+                mixed = dot(s1[at : at + cells, :], w[width : 2 * width, :])
+                sigma = jax.nn.sigmoid(mixed)
+                coming = jnp.concatenate(
+                    [r[m, x_len + g * band : x_len + (g + 1) * band, :] for r in blk], axis=0
+                ).astype(jnp.float32)
+                gates[at : at + cells, :] = (coming * sigma * (1.0 + mixed * (1.0 - sigma))).astype(jnp.bfloat16)
+                low, high = max(g * band, half_edge), min((g + 1) * band, half_edge + own)
+                if low < high:
+                    base = mid[m, 0, half_edge + low : half_edge + high, :].astype(jnp.float32)
+                    local = slice(low - g * band, high - g * band)
+                    last = (base + mixed[local] * sigma[local]).astype(jnp.bfloat16)
+                    early = mid[m, 0, half_edge + low : half_edge + high, :]
+                    out_ref[m, low - half_edge : high - half_edge, :] = jnp.where(seg == 0, early, last)
+        for b in range(BASIS):
+            got = dot_nt(gates[...], w[width + b * channels : width + (b + 1) * channels, :]).astype(jnp.bfloat16)
+            for i in range(members * ns):
+                feat[(i * BASIS + b) * cells : (i * BASIS + b + 1) * cells, :] = got[i * cells : (i + 1) * cells]
+        pull[...] = jnp.zeros(pull.shape, jnp.float32)
+        for m in range(members):
+            for g in range(ns):
+                at = (m * ns + g) * cells * BASIS
+                got = dot(backward[g], feat[at : at + BASIS * cells, :])
+                pull[m, :, g * band : g * band + win, :] += got.reshape(blocks, win, channels)
+        for m in range(members):
+            for q in range(blocks):
+                coming = blk[q][m, x_len : x_len + c_len, :].astype(jnp.float32)
+                value = (coming + pull[m, q, half_edge : half_edge + c_len, :]).astype(jnp.bfloat16)
+                if q == 0:
+                    grad_ref[m, :, :] = value[half_edge : half_edge + own]
+                gate = value.astype(jnp.float32) * slope[m, q, half_edge : half_edge + c_len, :]
+                gate_ref[m, q, :, :] = gate.astype(jnp.bfloat16)
+
+        columns = pl.ds(pl.multiple_of(lon * (width // blocks), 128), width // blocks)
+
+        @pl.when(seg == 0)
+        def _():
+            left, right = [], []
+            for m in range(members):
+                for g in range(1, nf - 1):
+                    at = (m * nf + g) * cells
+                    left.append(s0[at : at + cells, columns])
+                    o = half_edge + (g - 1) * band
+                    right.append(gate_ref[m, :, o : o + band, :].reshape(cells, channels))
+            grads[...] = dot_tn(jnp.concatenate(left, axis=0), jnp.concatenate(right, axis=0))
+
+        @pl.when(seg == 1)
+        def _():
+            left, right = [], []
+            for m in range(members):
+                for g in range(ns):
+                    low, high = max(g * band, half_edge), min((g + 1) * band, half_edge + own)
+                    for q in range(blocks):
+                        at = (m * ns + g) * cells + q * band - g * band
+                        left.append(s1[at + low : at + high, columns])
+                        right.append(gates[at + low : at + high, :])
+            grads[...] = dot_tn(jnp.concatenate(left, axis=0), jnp.concatenate(right, axis=0))
+
+        share = width // blocks // lat_devices
+
+        def rows_of(index):
+            return grads[pl.ds(pl.multiple_of(index * share, share), share), :]
+
+        own_ref[...] = rows_of(lat)
+        for bit, ref in ((1, p1), (2, p2), (3, p3)):
+            ref[...] = rows_of(lat ^ bit).astype(jnp.bfloat16)
+
+    def finish(idx, w_own, backward, gate_ref, g1_ref, grad_ref, gates, feat, pull):
+        seg = idx[0]
+
+        @pl.when(seg == 1)
+        def _():
+            grad_ref[...] = g1_ref[...]
+
+        @pl.when(seg == 0)
+        def _():
+            for m in range(members):
+                for g in range(ns):
+                    at = (m * ns + g) * cells
+                    gates[at : at + cells, :] = gate_ref[m, :, g * band : (g + 1) * band, :].reshape(cells, channels)
+            for b in range(BASIS):
+                got = dot_nt(gates[...], w_own[b * channels : (b + 1) * channels, :]).astype(jnp.bfloat16)
+                for i in range(members * ns):
+                    feat[(i * BASIS + b) * cells : (i * BASIS + b + 1) * cells, :] = got[i * cells : (i + 1) * cells]
+            pull[...] = jnp.zeros(pull.shape, jnp.float32)
+            for m in range(members):
+                for g in range(ns):
+                    at = (m * ns + g) * cells * BASIS
+                    got = dot(backward[g, 0:win, :], feat[at : at + BASIS * cells, :])
+                    pull[m, g * band : g * band + win, :] += got
+                total = g1_ref[m].astype(jnp.float32) + pull[m, edge : edge + own, :]
+                grad_ref[m, :, :] = total.astype(jnp.bfloat16)
+
+    return chain, finish
+
+
+def whole_ring(inputs, cotangent, weights, basis_values, lat_step, lon_step):
+    members, lat_rows, lon_cols, channels = inputs.shape
+    blocks = lax.axis_size("lon")
+    lat_devices = lax.axis_size("lat")
+    lat_total = lat_rows * lat_devices
+    lon_index = lax.axis_index("lon")
+    lat_index = lax.axis_index("lat")
+    segment_index = lax.axis_index("segment")
+    grad_scale = 1.0 / math.sqrt(members * lat_total * lon_cols * blocks)
+    own = lat_rows * lon_cols
+    edge = HALO * lon_cols
+    half_edge = edge // 2
+    width = BASIS * channels
+    state = inputs.reshape(members, own, channels)
+    coming = cotangent.reshape(members, own, channels)
+    kernel = weights.reshape(width, channels)
+    up = [(i, i + 1) for i in range(lat_devices - 1)]
+    down = [(i + 1, i) for i in range(lat_devices - 1)]
+    tail = jnp.concatenate([state[:, own - edge :], coming[:, own - half_edge :]], axis=1)
+    head = jnp.concatenate([state[:, :edge], coming[:, :half_edge]], axis=1)
+    before = lax.ppermute(tail, "lat", up)
+    after = lax.ppermute(head, "lat", down)
+    half = lax.dynamic_slice_in_dim(kernel, (lon_index % 2) * (width // 2), width // 2, 0)
+    near_half = lax.ppermute(half, "segment", swap("segment", 1))
+    block = jnp.concatenate(
+        [before[:, :edge], state, after[:, :edge], before[:, edge:], coming, after[:, edge:]], axis=1
+    )
+    far = lax.ppermute(block, "lon", swap("lon", 2))
+    mate = lax.ppermute(block, "lon", swap("lon", 1))
+    far_mate = lax.ppermute(far, "lon", swap("lon", 1))
+    far_half = lax.ppermute(near_half, "lon", swap("lon", 1))
+
+    place, basis = tap_tables(
+        basis_values, lat_step, lon_step, lat_rows, lon_cols, blocks, lat_index, lon_index, lat_total
+    )
+    first, second = window_plan(lat_rows)
+    nf, ns = len(first), len(second)
+    band = BAND * lon_cols
+    cells = blocks * band
+    win = 16 * lon_cols
+    vmem = pl.BlockSpec(memory_space=pltpu.VMEM)
+    smem = pl.BlockSpec(memory_space=pltpu.SMEM)
+    params = pltpu.CompilerParams(vmem_limit_bytes=48 * 1024 * 1024)
+    half_type, full_type = jnp.bfloat16, jnp.float32
+    forward, backward = pl.pallas_call(
+        functools.partial(map_kernel, nf, cells, blocks * win),
+        out_shape=(
+            jax.ShapeDtypeStruct((nf + ns, BASIS * cells, blocks * win), half_type),
+            jax.ShapeDtypeStruct((ns, blocks * win, BASIS * cells), half_type),
+        ),
+        in_specs=[vmem] * 2,
+        out_specs=(vmem,) * 2,
+        compiler_params=params,
+        cost_estimate=pl.CostEstimate(flops=40_000_000, bytes_accessed=4_000_000, transcendentals=0),
+        name="maps",
+    )(place, basis)
+    chain, finish = make_chain(lat_rows, lon_cols, blocks, members, channels, lat_devices)
+    idx = jnp.stack([segment_index, lon_index, lat_index]).astype(jnp.int32)
+    share = width // blocks // lat_devices
+    shape = jax.ShapeDtypeStruct
+    x_len = own + 2 * edge
+    c_len = own + edge
+    out, first_grad, gates, mine, *parts = pl.pallas_call(
+        chain,
+        out_shape=(
+            shape((members, own, channels), half_type),
+            shape((members, own, channels), half_type),
+            shape((members, blocks, c_len, channels), half_type),
+            shape((share, channels), full_type),
+        )
+        + (shape((share, channels), half_type),) * 3,
+        in_specs=[smem] + [vmem] * 9,
+        out_specs=(vmem,) * 7,
+        scratch_shapes=[
+            pltpu.VMEM((2 * width, channels), half_type),
+            pltpu.VMEM((members * nf * cells, width), half_type),
+            pltpu.VMEM((members * ns * cells, width), half_type),
+            pltpu.VMEM((members, blocks, x_len, channels), full_type),
+            pltpu.VMEM((members, blocks, x_len, channels), half_type),
+            pltpu.VMEM((members * ns * cells, channels), half_type),
+            pltpu.VMEM((members * ns * cells * BASIS, channels), half_type),
+            pltpu.VMEM((members, blocks, x_len, channels), full_type),
+            pltpu.VMEM((width // blocks, channels), full_type),
+        ],
+        compiler_params=params,
+        cost_estimate=pl.CostEstimate(flops=6_000_000_000, bytes_accessed=10_000_000, transcendentals=2_000_000),
+        name="chain",
+    )(idx, block, mate, far, far_mate, kernel, near_half, far_half, forward, backward)
+    got = [lax.ppermute(part, "lat", swap("lat", bit)) for bit, part in zip((1, 2, 3), parts)]
+    grad = pl.pallas_call(
+        finish,
+        out_shape=shape((members, own, channels), half_type),
+        in_specs=[smem] + [vmem] * 4,
+        out_specs=vmem,
+        scratch_shapes=[
+            pltpu.VMEM((members * ns * cells, channels), half_type),
+            pltpu.VMEM((members * ns * cells * BASIS, channels), half_type),
+            pltpu.VMEM((members, x_len, channels), full_type),
+        ],
+        compiler_params=params,
+        cost_estimate=pl.CostEstimate(flops=2_000_000_000, bytes_accessed=5_000_000, transcendentals=0),
+        name="finish",
+    )(idx, kernel, backward, gates, first_grad)
+    total = mine
+    for part in got:
+        total = total + part.astype(full_type)
+    weight_grad = (total * grad_scale).reshape(1, share * channels)
+    return (out.reshape((1,) + inputs.shape), grad.reshape((1,) + inputs.shape), weight_grad)
+
+
+def fits_ring(mesh, inputs):
+    sizes = dict(mesh.shape)
+    rows, cols = inputs.shape[1] // sizes["lat"], inputs.shape[2] // sizes["lon"]
+    return sizes["segment"] == 2 and sizes["lon"] == 4 and sizes["lat"] == 4 and rows == 16 and cols == 4
+
+
 def solution(mesh):
-    return jax.shard_map(
-        per_device,
-        mesh=mesh,
-        in_specs=(
-            P(None, "lat", "lon", None),
-            P(None, "lat", "lon", None),
-            P("segment", None, None, None),
-            P(),
-            P(),
-            P(),
-        ),
-        out_specs=(
-            P("segment", None, "lat", "lon", None),
-            P("segment", None, "lat", "lon", None),
-            P("segment", ("lon", "lat")),
-        ),
-        check_vma=False,
-    )
+    def apply(*args):
+        body = whole_ring if fits_ring(mesh, args[0]) else per_device
+        return jax.shard_map(
+            body,
+            mesh=mesh,
+            in_specs=(
+                P(None, "lat", "lon", None),
+                P(None, "lat", "lon", None),
+                P("segment", None, None, None),
+                P(),
+                P(),
+                P(),
+            ),
+            out_specs=(
+                P("segment", None, "lat", "lon", None),
+                P("segment", None, "lat", "lon", None),
+                P("segment", ("lon", "lat")),
+            ),
+            check_vma=False,
+        )(*args)
+
+    return apply

time: 192 us -> 65.9 us (0.34)
  waiting for transfers between devices: 123 us -> 16.1 us
  Pallas kernels: 0 us -> 18.1 us
  between operations: 14.4 us -> 1.03 us
  other arithmetic: 11.8 us -> 1.15 us
  matrix products: 10.3 us -> 0 us
  starting transfers between devices: 18.6 us -> 15 us
    unnamed x2 -> x0, waiting for transfers between devices: 77 us -> none
    ppermute x18 -> x10, waiting for transfers between devices: 45.6 us -> 16.1 us  [the longest x1 13.1 us: whole_ring(): near_half = lax.ppermute(half, 'segment', swap('segment', 1))]
    pallas_call x0 -> x3, Pallas kernels: none -> 18.1 us  [the longest x1 9.6 us: whole_ring(): pl.pallas_call(chain, out_shape=(shape((members, own, channels), half_typ...]
    dot_general x11 -> x0, matrix products: 10.3 us -> none  [the longest x1 2.67 us: build_tables(): jnp.einsum('pqkb,pqkt->btpq', back_weight, catcher, precision=lax.Precisi...]
    unnamed x26 -> x48, local copies, waits for them, and re-layouts: 3.87 us -> 7.87 us
    ppermute x18 -> x10, starting transfers between devices: 18.6 us -> 15 us  [the longest x3 4.95 us: whole_ring(): lax.ppermute(part, 'lat', swap('lat', bit))]
    slice x4 -> x1, other arithmetic: 3.29 us -> 0.08 us  [tap_tables(): lat_near, lon_near = (step_rows[..., :TAPS], step_rows[..., TAPS:])]
    concatenate x2 -> x3, other arithmetic: 3.2 us -> 0.03 us  [the longest x1 0.01 us: whole_ring(): jnp.concatenate([state[:, own - edge:], coming[:, own - half_edge:]], axi...]
  transfers between devices with their start and end apart: 19 -> 10, of which waited for: 16 -> 3; matrix products, arithmetic and copies ran while one was open for 9% -> 7% of each run, Pallas kernels for 0% -> 13%
where the time goes in v1:
time: 65.9 us; the launch traced here: 65.5 us
  Pallas kernels  18.1 us (27%)
  waiting for transfers between devices  16.1 us (24%)
  starting transfers between devices  15 us (23%)
  local copies, waits for them, and re-layouts  14.2 us (22%)
  other arithmetic  1.15 us (2%)
  between operations  1.03 us (2%)
    ppermute x1, waiting for transfers between devices, whole_ring(): near_half = lax.ppermute(half, 'segment', swap('segment', 1))  13.1 us
    pallas_call x1, Pallas kernels, whole_ring(): pl.pallas_call(chain, out_shape=(shape((members, own, channels), half_typ...  9.6 us
    unnamed x48, local copies, waits for them, and re-layouts  7.87 us
    pallas_call x1, Pallas kernels, whole_ring(): pl.pallas_call(functools.partial(map_kernel, nf, cells, blocks * win), ou...  6.15 us
    ppermute x3, starting transfers between devices, whole_ring(): lax.ppermute(part, 'lat', swap('lat', bit))  4.95 us
    ppermute x1, starting transfers between devices, whole_ring(): before = lax.ppermute(tail, 'lat', up)  4.93 us
    pallas_call x1, Pallas kernels, whole_ring(): pl.pallas_call(finish, out_shape=shape((members, own, channels), half_typ...  2.35 us
    ppermute x3, waiting for transfers between devices, whole_ring(): lax.ppermute(part, 'lat', swap('lat', bit))  2 us
  transfers between devices with their start and end apart: 10, of which 3 were waited for; matrix products, arithmetic and copies ran while one was open for 7% of the time, Pallas kernels for 13%

profile of v1, /device:TPU:0, one launch (start us, length us, event | category | flops | bytes accessed | tf_op | source)
XLA Modules:
  0.0 65.5 jit_solution(17155896985921365952)
XLA Ops:
  0.6 0.0 copy-start.10
  0.7 1.0 %reshape.79 = bf16[2,64,512]{2,1,0:T(8,128)(2,1)S(1)} reshape(bf16[2,16,4,512]{3,2,1,0:T(4,128)(2,1)} %param.8) | data formatting | bytes 262144 | tf_op jit(solution)/shard_map/reshape | solution.py:398
  1.6 0.9 %reshape.80 = bf16[2,64,512]{2,1,0:T(8,128)(2,1)S(1)} reshape(bf16[2,16,4,512]{3,2,1,0:T(4,128)(2,1)} %param.9) | data formatting | bytes 262144 | tf_op jit(solution)/shard_map/reshape | solution.py:399
  2.6 4.9 %collective-permute-start = (bf16[2,48,512]{2,1,0:T(8,128)(2,1)S(1)}, bf16[2,48,512]{2,1,0:T(8,128)(2,1)S(1)}, u32[]{:S(2)}, u32[]{:S(2)}) collective-permute-start(bf16[2,48,512]{2,1,0:T(8,128)(2,1)S(1)} %pad_maximum_fusion), channel_id=1, source_target_pairs={{0,2},{2,4},{4,6},{1,3},{3,5},{5,7},{8,10},{10,12},{12,14},{9,11},... | collective-permute-start | bytes 294920 | tf_op jit(solution)/shard_map/ppermute | solution.py:405
  7.6 1.3 %collective-permute-start.1 = (bf16[2,48,512]{2,1,0:T(8,128)(2,1)S(1)}, bf16[2,48,512]{2,1,0:T(8,128)(2,1)S(1)}, u32[]{:S(2)}, u32[]{:S(2)}) collective-permute-start(bf16[2,48,512]{2,1,0:T(8,128)(2,1)S(1)} %pad_maximum_fusion.1), channel_id=1, source_target_pairs={{2,0},{4,2},{6,4},{3,1},{5,3},{7,5},{10,8},{12,10},{14,12},{11,9},... | collective-permute-start | bytes 294920 | tf_op jit(solution)/shard_map/ppermute | solution.py:406
  8.9 0.0 copy-start.14
  8.9 1.2 %constant_dynamic-slice_fusion = bf16[768,512]{1,0:T(8,128)(2,1)S(1)} fusion(bf16[1536,512]{1,0:T(8,128)(2,1)} %bitcast.45, s32[]{:T(128)S(6)} %select_n.38), kind=kLoop, calls=%fused_computation.60 | loop fusion | bytes 1572868 | tf_op jit(solution)/shard_map/dynamic_slice | solution.py:407
  10.1 1.6 %collective-permute-start.5 = (bf16[768,512]{1,0:T(8,128)(2,1)S(1)}, bf16[768,512]{1,0:T(8,128)(2,1)S(1)}, u32[]{:S(2)}, u32[]{:S(2)}) collective-permute-start(bf16[768,512]{1,0:T(8,128)(2,1)S(1)} %constant_dynamic-slice_fusion), channel_id=1, source_target_pairs={{0,1},{1,0},{2,3},{3,2},{4,5},{5,4},{6,7},{7,6},{8,9},{9,8},{10,11... | collective-permute-start | bytes 2359304 | tf_op jit(solution)/shard_map/ppermute | solution.py:408
  11.7 0.1 iota_add_fusion
  11.8 0.1 dynamic-slice_bitcast_fusion.7
  12.0 0.1 copy.37
  12.0 0.1 copy.31
  12.1 0.1 copy.32
  12.2 0.1 copy.33
  12.3 0.1 copy.34
  12.3 0.1 copy.35
  12.4 0.1 copy.36
  12.5 0.1 dynamic-slice_bitcast_fusion
  12.6 0.1 copy.38
  12.7 0.1 copy.39
  12.8 0.1 copy.40
  12.9 0.1 copy.41
  13.0 0.1 compare_and_fusion
  13.1 0.0 collective-permute-done
  13.1 1.0 %collective-permute-done.1 = bf16[2,48,512]{2,1,0:T(8,128)(2,1)S(1)} collective-permute-done((bf16[2,48,512]{2,1,0:T(8,128)(2,1)S(1)}, bf16[2,48,512]{2,1,0:T(8,128)(2,1)S(1)}, u32[]{:S(2)}, u32[]{:S(2)}) %collective-permute-start.1) | collective-permute-done | bytes 98336 | tf_op jit(solution)/shard_map/ppermute | solution.py:406
  14.1 1.6 %collective-permute-start.3 = (bf16[2,224,512]{2,1,0:T(8,128)(2,1)S(1)}, bf16[2,224,512]{2,1,0:T(8,128)(2,1)S(1)}, u32[]{:S(2)}, u32[]{:S(2)}) collective-permute-start(bf16[2,224,512]{2,1,0:T(8,128)(2,1)S(1)} %constant_dynamic-update-slice_fusion.x0), channel_id=1, source_target_pairs={{0,16},{8,24},{16,0},{24,8},{1,17},{9,25},{17,1},{25,9},{2,18},{10... | collective-permute-start | bytes 1376264 | tf_op jit(solution)/shard_map/ppermute | solution.py:412
  15.7 0.1 copy.44
  15.8 0.1 copy.42
  15.9 0.1 copy.43
  16.0 0.1 add.125
  16.1 13.1 %collective-permute-done.5.w_a = bf16[768,512]{1,0:T(8,128)(2,1)S(1)} collective-permute-done((bf16[768,512]{1,0:T(8,128)(2,1)S(1)}, bf16[768,512]{1,0:T(8,128)(2,1)S(1)}, u32[]{:S(2)}, u32[]{:S(2)}) %collective-permute-start.5) | collective-permute-done | bytes 786464 | tf_op jit(solution)/shard_map/ppermute | solution.py:408
  29.2 0.0 collective-permute-start.6
  29.2 0.1 fusion.12
  29.3 0.6 collective-permute-start.2
  29.9 0.0 collective-permute-done.3.x2
  29.9 0.1 collective-permute-start.4
  30.0 0.1 broadcast_in_dim.10
  30.0 0.1 add.127
  30.1 0.1 add.133
  30.2 0.7 %fusion.5.place_ref = s32[896,9]{1,0:T(8,128)S(1)} fusion(pred[896,9]{1,0:T(8,128)(4,1)S(1)} %bitcast.50, s32[896,9]{1,0:T(8,128)S(1)} %bitcast.49, s32[896,9]{1,0:T(8,128)S(1)} %bitcast.48, s32[]{:T(128)} %axis_index.35, s32[896]{0:T(1024)S(1)} %add.125), kind=kLoop, calls=%fused_computation.13 | loop fusion | flops 290304 | bytes 108420 | tf_op jit(solution)/shard_map/jit(_where)/select_n | solution.py:204
  31.0 0.1 broadcast_in_dim.12
  31.1 6.1 %maps.1 = (bf16[7,384,256]{2,1,0:T(8,128)(2,1)S(1)}, bf16[3,256,384]{2,1,0:T(8,128)(2,1)S(1)}) custom-call(s32[896,9]{1,0:T(8,128)S(1)} %fusion.5.place_ref, f32[896,27]{1,0:T(8,128)S(1)} %bitcast.44), custom_call_target="tpu_custom_call" | custom-call | flops 40000000 | bytes 4000000 | tf_op jit(solution)/shard_map/maps/pallas_call | solution.py:429
  37.3 1.1 %copy-done.1 = bf16[7,384,256]{2,1,0:T(8,128)(2,1)} copy-done((bf16[7,384,256]{2,1,0:T(8,128)(2,1)}, bf16[7,384,256]{2,1,0:T(8,128)(2,1)S(1)}, u32[]{:S(2)}) %copy-start.1) | copy-done | bytes 1376280
  38.4 0.1 pad_add_fusion.1.idx
  38.4 0.0 collective-permute-done.2.x1
  38.4 0.0 collective-permute-done.4.x3
  38.4 0.0 collective-permute-done.6.w_b
  38.5 1.1 %copy-done.5 = bf16[2,224,512]{2,1,0:T(8,128)(2,1)S(1)} copy-done((bf16[2,224,512]{2,1,0:T(8,128)(2,1)S(1)}, bf16[2,224,512]{2,1,0:T(8,128)(2,1)}, u32[]{:S(2)}) %copy-start.5) | copy-done | bytes 458776
  39.6 9.6 %chain.1 = (bf16[2,64,512]{2,1,0:T(8,128)(2,1)S(1)}, bf16[2,64,512]{2,1,0:T(8,128)(2,1)S(1)}, bf16[2,4,96,512]{3,2,1,0:T(8,128)(2,1)S(1)}, f32[96,512]{1,0:T(8,1...) custom-call(s32[3]{0:T(128)S(1)} %pad_add_fusion.1.idx, ...), custom_call_target="tpu_custom_call" | custom-call | flops 6000000000 | bytes 10000000 | tf_op jit(solution)/shard_map/chain/pallas_call | solution.py:447
  49.2 0.9 %copy-done.6 = bf16[2,4,96,512]{3,2,1,0:T(8,128)(2,1)} copy-done((bf16[2,4,96,512]{3,2,1,0:T(8,128)(2,1)}, bf16[2,4,96,512]{3,2,1,0:T(8,128)(2,1)S(1)}, u32[]{:S(2)}) %copy-start.6) | copy-done | bytes 786456
  50.1 0.7 copy-done.8
  50.8 0.7 %reshape.84 = bf16[1,2,16,4,512]{4,3,2,1,0:T(4,128)(2,1)} reshape(bf16[2,64,512]{2,1,0:T(8,128)(2,1)S(1)} %get-tuple-element.14) | data formatting | bytes 262144 | tf_op jit(solution)/shard_map/reshape | solution.py:492
  51.5 2.4 %collective-permute-start.7 = (bf16[96,512]{1,0:T(8,128)(2,1)S(1)}, bf16[96,512]{1,0:T(8,128)(2,1)S(1)}, u32[]{:S(2)}, u32[]{:S(2)}) collective-permute-start(bf16[96,512]{1,0:T(8,128)(2,1)S(1)} %get-tuple-element.18), channel_id=1, source_target_pairs={{0,2},{2,0},{4,6},{6,4},{1,3},{3,1},{5,7},{7,5},{8,10},{10,8},{12,... | collective-permute-start | bytes 294920 | tf_op jit(solution)/shard_map/ppermute | solution.py:473
  53.8 2.6 %collective-permute-start.8 = (bf16[96,512]{1,0:T(8,128)(2,1)S(1)}, bf16[96,512]{1,0:T(8,128)(2,1)S(1)}, u32[]{:S(2)}, u32[]{:S(2)}) collective-permute-start(bf16[96,512]{1,0:T(8,128)(2,1)S(1)} %get-tuple-element.19), channel_id=1, source_target_pairs={{0,4},{2,6},{4,0},{6,2},{1,5},{3,7},{5,1},{7,3},{8,12},{10,14},{12... | collective-permute-start | bytes 294920 | tf_op jit(solution)/shard_map/ppermute | solution.py:473
  56.4 0.0 collective-permute-start.9
  56.4 1.1 %copy-done.3 = bf16[3,256,384]{2,1,0:T(8,128)(2,1)S(1)} copy-done((bf16[3,256,384]{2,1,0:T(8,128)(2,1)S(1)}, bf16[3,256,384]{2,1,0:T(8,128)(2,1)}, u32[]{:S(2)}) %copy-start.3) | copy-done | bytes 589848
  57.5 1.1 %copy-done.7 = bf16[2,4,96,512]{3,2,1,0:T(8,128)(2,1)S(1)} copy-done((bf16[2,4,96,512]{3,2,1,0:T(8,128)(2,1)S(1)}, bf16[2,4,96,512]{3,2,1,0:T(8,128)(2,1)}, u32[]{:S(2)}) %copy-start.7) | copy-done | bytes 786456
  58.6 0.9 %copy-done.9 = bf16[2,64,512]{2,1,0:T(8,128)(2,1)S(1)} copy-done((bf16[2,64,512]{2,1,0:T(8,128)(2,1)S(1)}, bf16[2,64,512]{2,1,0:T(8,128)(2,1)}, u32[]{:S(2)}) %copy-start.9) | copy-done | bytes 131096
  59.5 2.3 %finish.1 = bf16[2,64,512]{2,1,0:T(8,128)(2,1)S(1)} custom-call(s32[3]{0:T(128)S(1)} %pad_add_fusion.1.idx, bf16[1536,512]{1,0:T(8,128)(2,1)S(1)} %bitcast.47, bf16[3,256,384]{2,1,0:T(8,128)(2,1)S(1)} %copy-done.3, bf16[2,4,96,512]{3,2,1,0:T(8,128)(2,1)S(1)} %copy-done.7, bf16[2,64,512]{2,1,0:T(8,128)(2,1)S(1)} %copy-done.9), custom_call_target="tpu_custom_call" | custom-call | flops 2000000000 | bytes 5000000 | tf_op jit(solution)/shard_map/finish/pallas_call | solution.py:474
  61.9 0.7 %reshape.85 = bf16[1,2,16,4,512]{4,3,2,1,0:T(4,128)(2,1)} reshape(bf16[2,64,512]{2,1,0:T(8,128)(2,1)S(1)} %finish.1) | data formatting | bytes 262144 | tf_op jit(solution)/shard_map/reshape | solution.py:492
  62.6 0.0 collective-permute-done.7
  62.6 2.0 %collective-permute-done.8 = bf16[96,512]{1,0:T(8,128)(2,1)S(1)} collective-permute-done((bf16[96,512]{1,0:T(8,128)(2,1)S(1)}, bf16[96,512]{1,0:T(8,128)(2,1)S(1)}, u32[]{:S(2)}, u32[]{:S(2)}) %collective-permute-start.8) | collective-permute-done | bytes 98336 | tf_op jit(solution)/shard_map/ppermute | solution.py:473
  64.6 0.0 collective-permute-done.9
  64.6 0.9 %copy.45 = f32[1,1,96,512]{3,1,2,0:T(1,128)} copy(f32[1,1,96,512]{3,2,1,0:T(8,128)S(1)} %multiply_bitcast_fusion) | data formatting | bytes 393216
  (52 shorter events, 0.2 us)
Async XLA Ops:
  0.6 11.0 %copy-start.10 = (s32[7,8]{1,0:T(8,128)S(1)}, s32[7,8]{1,0:T(8,128)}, u32[]{:S(2)}) copy-start(s32[7,8]{1,0:T(8,128)} %constant.84.clone) | copy-start | bytes 676
  0.6 11.1 %copy-start.11 = (f32[64,9,3]{0,2,1:T(4,128)S(1)}, f32[64,9,3]{0,2,1:T(4,128)}, u32[]{:S(2)}) copy-start(f32[64,9,3]{0,2,1:T(4,128)} %param.11) | copy-start | bytes 20740
  0.7 11.1 %copy-start.12 = (s32[64,9]{0,1:T(8,128)S(1)}, s32[64,9]{0,1:T(8,128)}, u32[]{:S(2)}) copy-start(s32[64,9]{0,1:T(8,128)} %param.13) | copy-start | bytes 6916
  0.7 11.1 %copy-start.13 = (s32[64,9]{0,1:T(8,128)S(1)}, s32[64,9]{0,1:T(8,128)}, u32[]{:S(2)}) copy-start(s32[64,9]{0,1:T(8,128)} %param.12) | copy-start | bytes 6916
  2.6 10.5 %collective-permute-start = (bf16[2,48,512]{2,1,0:T(8,128)(2,1)S(1)}, bf16[2,48,512]{2,1,0:T(8,128)(2,1)S(1)}, u32[]{:S(2)}, u32[]{:S(2)}) collective-permute-start(bf16[2,48,512]{2,1,0:T(8,128)(2,1)S(1)} %pad_maximum_fusion), channel_id=1, source_target_pairs={{0,2},{2,4},{4,6},{1,3},{3,5},{5,7},{8,10},{10,12},{12,14},{9,11},... | collective-permute-start | bytes 294920 | tf_op jit(solution)/shard_map/ppermute | solution.py:405
  7.6 6.5 %collective-permute-start.1 = (bf16[2,48,512]{2,1,0:T(8,128)(2,1)S(1)}, bf16[2,48,512]{2,1,0:T(8,128)(2,1)S(1)}, u32[]{:S(2)}, u32[]{:S(2)}) collective-permute-start(bf16[2,48,512]{2,1,0:T(8,128)(2,1)S(1)} %pad_maximum_fusion.1), channel_id=1, source_target_pairs={{2,0},{4,2},{6,4},{3,1},{5,3},{7,5},{10,8},{12,10},{14,12},{11,9},... | collective-permute-start | bytes 294920 | tf_op jit(solution)/shard_map/ppermute | solution.py:406
  8.9 20.3 %copy-start.14 = (s32[7]{0:T(128)S(1)}, s32[7]{0:T(128)}, u32[]{:S(2)}) copy-start(s32[7]{0:T(128)} %constant.91) | copy-start | bytes 88
  10.1 19.1 %collective-permute-start.5 = (bf16[768,512]{1,0:T(8,128)(2,1)S(1)}, bf16[768,512]{1,0:T(8,128)(2,1)S(1)}, u32[]{:S(2)}, u32[]{:S(2)}) collective-permute-start(bf16[768,512]{1,0:T(8,128)(2,1)S(1)} %constant_dynamic-slice_fusion), channel_id=1, source_target_pairs={{0,1},{1,0},{2,3},{3,2},{4,5},{5,4},{6,7},{7,6},{8,9},{9,8},{10,11... | collective-permute-start | bytes 2359304 | tf_op jit(solution)/shard_map/ppermute | solution.py:408
  14.1 15.7 %collective-permute-start.3 = (bf16[2,224,512]{2,1,0:T(8,128)(2,1)S(1)}, bf16[2,224,512]{2,1,0:T(8,128)(2,1)S(1)}, u32[]{:S(2)}, u32[]{:S(2)}) collective-permute-start(bf16[2,224,512]{2,1,0:T(8,128)(2,1)S(1)} %constant_dynamic-update-slice_fusion.x0), channel_id=1, source_target_pairs={{0,16},{8,24},{16,0},{24,8},{1,17},{9,25},{17,1},{25,9},{2,18},{10... | collective-permute-start | bytes 1376264 | tf_op jit(solution)/shard_map/ppermute | solution.py:412
  29.2 9.3 %collective-permute-start.6 = (bf16[768,512]{1,0:T(8,128)(2,1)S(1)}, bf16[768,512]{1,0:T(8,128)(2,1)S(1)}, u32[]{:S(2)}, u32[]{:S(2)}) collective-permute-start(bf16[768,512]{1,0:T(8,128)(2,1)S(1)} %collective-permute-done.5.w_a), channel_id=1, source_target_pairs={{0,8},{8,0},{16,24},{24,16},{1,9},{9,1},{17,25},{25,17},{2,10},{10... | collective-permute-start | bytes 2359304 | tf_op jit(solution)/shard_map/ppermute | solution.py:415
  29.3 9.1 %collective-permute-start.2 = (bf16[2,224,512]{2,1,0:T(8,128)(2,1)S(1)}, bf16[2,224,512]{2,1,0:T(8,128)(2,1)S(1)}, u32[]{:S(2)}, u32[]{:S(2)}) collective-permute-start(bf16[2,224,512]{2,1,0:T(8,128)(2,1)S(1)} %constant_dynamic-update-slice_fusion.x0), channel_id=1, source_target_pairs={{0,8},{8,0},{16,24},{24,16},{1,9},{9,1},{17,25},{25,17},{2,10},{10... | collective-permute-start | bytes 1376264 | tf_op jit(solution)/shard_map/ppermute | solution.py:413
  29.9 7.4 %copy-start.4 = (bf16[2,224,512]{2,1,0:T(8,128)(2,1)}, bf16[2,224,512]{2,1,0:T(8,128)(2,1)S(1)}, u32[]{:S(2)}) copy-start(bf16[2,224,512]{2,1,0:T(8,128)(2,1)S(1)} %collective-permute-done.3.x2) | copy-start | bytes 1376260
  29.9 8.6 %collective-permute-start.4 = (bf16[2,224,512]{2,1,0:T(8,128)(2,1)S(1)}, bf16[2,224,512]{2,1,0:T(8,128)(2,1)S(1)}, u32[]{:S(2)}, u32[]{:S(2)}) collective-permute-start(bf16[2,224,512]{2,1,0:T(8,128)(2,1)S(1)} %collective-permute-done.3.x2), channel_id=1, source_target_pairs={{0,8},{8,0},{16,24},{24,16},{1,9},{9,1},{17,25},{25,17},{2,10},{10... | collective-permute-start | bytes 1376264 | tf_op jit(solution)/shard_map/ppermute | solution.py:414
  37.2 1.1 %copy-start.1 = (bf16[7,384,256]{2,1,0:T(8,128)(2,1)}, bf16[7,384,256]{2,1,0:T(8,128)(2,1)S(1)}, u32[]{:S(2)}) copy-start(bf16[7,384,256]{2,1,0:T(8,128)(2,1)S(1)} %get-tuple-element.12.forward) | copy-start | bytes 4128772
  38.4 10.9 %copy-start.2 = (bf16[3,256,384]{2,1,0:T(8,128)(2,1)}, bf16[3,256,384]{2,1,0:T(8,128)(2,1)S(1)}, u32[]{:S(2)}) copy-start(bf16[3,256,384]{2,1,0:T(8,128)(2,1)S(1)} %get-tuple-element.13.backward) | copy-start | bytes 1769476
  38.4 1.2 %copy-start.5 = (bf16[2,224,512]{2,1,0:T(8,128)(2,1)S(1)}, bf16[2,224,512]{2,1,0:T(8,128)(2,1)}, u32[]{:S(2)}) copy-start(bf16[2,224,512]{2,1,0:T(8,128)(2,1)} %copy-done.4) | copy-start | bytes 1376260
  39.6 16.8 %copy-start = (bf16[1,3,512,512]{3,2,1,0:T(8,128)(2,1)S(1)}, bf16[1,3,512,512]{3,2,1,0:T(8,128)(2,1)}, u32[]{:S(2)}) copy-start(bf16[1,3,512,512]{3,2,1,0:T(8,128)(2,1)} %param.10) | copy-start | bytes 4718596
  49.2 0.9 %copy-start.6 = (bf16[2,4,96,512]{3,2,1,0:T(8,128)(2,1)}, bf16[2,4,96,512]{3,2,1,0:T(8,128)(2,1)S(1)}, u32[]{:S(2)}) copy-start(bf16[2,4,96,512]{3,2,1,0:T(8,128)(2,1)S(1)} %get-tuple-element.15.gate_ref) | copy-start | bytes 2359300
  50.1 0.7 copy-start.8
  51.5 11.1 %collective-permute-start.7 = (bf16[96,512]{1,0:T(8,128)(2,1)S(1)}, bf16[96,512]{1,0:T(8,128)(2,1)S(1)}, u32[]{:S(2)}, u32[]{:S(2)}) collective-permute-start(bf16[96,512]{1,0:T(8,128)(2,1)S(1)} %get-tuple-element.18), channel_id=1, source_target_pairs={{0,2},{2,0},{4,6},{6,4},{1,3},{3,1},{5,7},{7,5},{8,10},{10,8},{12,... | collective-permute-start | bytes 294920 | tf_op jit(solution)/shard_map/ppermute | solution.py:473
  53.8 10.8 %collective-permute-start.8 = (bf16[96,512]{1,0:T(8,128)(2,1)S(1)}, bf16[96,512]{1,0:T(8,128)(2,1)S(1)}, u32[]{:S(2)}, u32[]{:S(2)}) collective-permute-start(bf16[96,512]{1,0:T(8,128)(2,1)S(1)} %get-tuple-element.19), channel_id=1, source_target_pairs={{0,4},{2,6},{4,0},{6,2},{1,5},{3,7},{5,1},{7,3},{8,12},{10,14},{12... | collective-permute-start | bytes 294920 | tf_op jit(solution)/shard_map/ppermute | solution.py:473
  56.4 8.2 %collective-permute-start.9 = (bf16[96,512]{1,0:T(8,128)(2,1)S(1)}, bf16[96,512]{1,0:T(8,128)(2,1)S(1)}, u32[]{:S(2)}, u32[]{:S(2)}) collective-permute-start(bf16[96,512]{1,0:T(8,128)(2,1)S(1)} %get-tuple-element.20), channel_id=1, source_target_pairs={{0,6},{2,4},{4,2},{6,0},{1,7},{3,5},{5,3},{7,1},{8,14},{10,12},{12... | collective-permute-start | bytes 294920 | tf_op jit(solution)/shard_map/ppermute | solution.py:473
  56.4 1.1 %copy-start.3 = (bf16[3,256,384]{2,1,0:T(8,128)(2,1)S(1)}, bf16[3,256,384]{2,1,0:T(8,128)(2,1)}, u32[]{:S(2)}) copy-start(bf16[3,256,384]{2,1,0:T(8,128)(2,1)} %copy-done.2) | copy-start | bytes 1769476
  57.5 1.1 %copy-start.7 = (bf16[2,4,96,512]{3,2,1,0:T(8,128)(2,1)S(1)}, bf16[2,4,96,512]{3,2,1,0:T(8,128)(2,1)}, u32[]{:S(2)}) copy-start(bf16[2,4,96,512]{3,2,1,0:T(8,128)(2,1)} %copy-done.6) | copy-start | bytes 2359300
  58.6 0.9 %copy-start.9 = (bf16[2,64,512]{2,1,0:T(8,128)(2,1)S(1)}, bf16[2,64,512]{2,1,0:T(8,128)(2,1)}, u32[]{:S(2)}) copy-start(bf16[2,64,512]{2,1,0:T(8,128)(2,1)} %copy-done.8) | copy-start | bytes 393220

commit v2 on v1

--- a/solution.py
+++ b/solution.py
@@ -209,18 +209,29 @@
 
 def map_kernel(firsts, cells, window, place_ref, basis_ref, forward_ref, backward_ref):
     total = place_ref.shape[0] // cells
-    lane = lax.broadcasted_iota(jnp.int32, (cells, window), 1)
-    for g in range(total):
-        span = slice(g * cells, (g + 1) * cells)
-        hits = [place_ref[span, k : k + 1] == lane for k in range(TAPS)]
+    piece = 32
+    lane = lax.broadcasted_iota(jnp.int32, (piece, window), 1)
+
+    def fill(i, carry):
+        span = pl.ds(pl.multiple_of(i * piece, piece), piece)
+        place, basis = place_ref[span, :], basis_ref[span, :]
+        tables = [jnp.zeros((piece, window), jnp.float32) for _ in range(BASIS)]
+        for k in range(TAPS):
+            hit = place[:, k : k + 1] == lane
+            for b in range(BASIS):
+                at = k * BASIS + b
+                tables[b] = tables[b] + jnp.where(hit, basis[:, at : at + 1], 0.0)
+        g, row = i // (cells // piece), i % (cells // piece) * piece
         for b in range(BASIS):
-            table = jnp.zeros((cells, window), jnp.float32)
-            for k in range(TAPS):
-                at = k * BASIS + b
-                table = table + jnp.where(hits[k], basis_ref[span, at : at + 1], 0.0)
-            forward_ref[g, b * cells : (b + 1) * cells, :] = table.astype(jnp.bfloat16)
-            if g >= firsts:
-                backward_ref[g - firsts, :, b * cells : (b + 1) * cells] = table.T.astype(jnp.bfloat16)
+            spot = pl.ds(pl.multiple_of(b * cells + row, piece), piece)
+            forward_ref[g, spot, :] = tables[b].astype(jnp.bfloat16)
+        return carry
+
+    lax.fori_loop(0, total * cells // piece, fill, 0)
+    for g in range(total - firsts):
+        for b in range(BASIS):
+            table = forward_ref[firsts + g, b * cells : (b + 1) * cells, :].astype(jnp.float32)
+            backward_ref[g, :, b * cells : (b + 1) * cells] = table.T.astype(jnp.bfloat16)
 
 
 def dot(a, b):
@@ -235,151 +246,167 @@
     return lax.dot_general(a, b, (((0,), (0,)), ((), ())), preferred_element_type=jnp.float32)
 
 
-def make_chain(lat_rows, lon_cols, blocks, members, channels, lat_devices):
+def make_steps(lat_rows, lon_cols, blocks, members, channels, lat_devices):
     first, second = window_plan(lat_rows)
     nf, ns = len(first), len(second)
     band = BAND * lon_cols
     cells = blocks * band
     win = 16 * lon_cols
     own = lat_rows * lon_cols
-    x_len = (lat_rows + 2 * HALO) * lon_cols
-    c_len = (lat_rows + HALO) * lon_cols
-    edge = HALO * lon_cols
-    half_edge = edge // 2
+    half_edge = HALO * lon_cols // 2
     width = BASIS * channels
     lanes = 128
     pieces = channels // lanes
 
-    def chain(idx, x0, x1, x2, x3, w_own, w_a, w_b, forward, backward, out_ref, grad_ref, gate_ref, own_ref, p1, p2, p3, w, s0, s1, slope, mid, gates, feat, pull, grads):
-        blk = (x0, x1, x2, x3)
-        seg, lon, lat = idx[0], idx[1], idx[2]
-        half = w_a.shape[0]
-        core = lon % 2
-        w[pl.ds(pl.multiple_of(seg * width, width), width), :] = w_own[...]
-        other = (1 - seg) * width
-        w[pl.ds(pl.multiple_of(other + core * half, half), half), :] = w_a[...]
-        w[pl.ds(pl.multiple_of(other + (1 - core) * half, half), half), :] = w_b[...]
+    def put_spread(got, into, at):
+        for b in range(BASIS):
+            into[at : at + cells, b * channels : (b + 1) * channels] = got[b * cells : (b + 1) * cells]
+
+    def first_section(blk, w, s0, s1, slope, mid, forward):
         for m in range(members):
-            for g, (a, start) in enumerate(first):
-                o = (start + HALO) * lon_cols
-                near = jnp.concatenate([r[m, o : o + win, :] for r in blk], axis=0)
-                got = dot(forward[g], near).astype(jnp.bfloat16)
-                at = (m * nf + g) * cells
-                for b in range(BASIS):
-                    s0[at : at + cells, b * channels : (b + 1) * channels] = got[b * cells : (b + 1) * cells]
-        for m in range(members):
+            total = dot(s0[m * nf * cells : (m + 1) * nf * cells, :], w[...])
             for g in range(nf):
-                at = (m * nf + g) * cells
-                mixed = dot(s0[at : at + cells, :], w[0:width, :])
+                mixed = total[g * cells : (g + 1) * cells]
                 sigma = jax.nn.sigmoid(mixed)
                 here = jnp.concatenate([r[m, g * band : (g + 1) * band, :] for r in blk], axis=0)
                 value = (here.astype(jnp.float32) + mixed * sigma).astype(jnp.bfloat16)
                 mid[m, :, g * band : (g + 1) * band, :] = value.reshape(blocks, band, channels)
                 tilt = sigma * (1.0 + mixed * (1.0 - sigma))
                 slope[m, :, g * band : (g + 1) * band, :] = tilt.reshape(blocks, band, channels)
-        for m in range(members):
             for g in range(ns):
                 near = mid[m, :, g * band : g * band + win, :].reshape(blocks * win, channels)
-                got = dot(forward[nf + g], near).astype(jnp.bfloat16)
-                at = (m * ns + g) * cells
-                for b in range(BASIS):
-                    s1[at : at + cells, b * channels : (b + 1) * channels] = got[b * cells : (b + 1) * cells]
+                put_spread(dot(forward[nf + g], near).astype(jnp.bfloat16), s1, (m * ns + g) * cells)
+
+    def spread(x0, x1, x2, x3, forward, s0):
+        blk = (x0, x1, x2, x3)
         for m in range(members):
-            for g in range(ns):
-                at = (m * ns + g) * cells
-                mixed = dot(s1[at : at + cells, :], w[width : 2 * width, :])
-                sigma = jax.nn.sigmoid(mixed)
-                coming = jnp.concatenate(
-                    [r[m, x_len + g * band : x_len + (g + 1) * band, :] for r in blk], axis=0
-                ).astype(jnp.float32)
-                gates[at : at + cells, :] = (coming * sigma * (1.0 + mixed * (1.0 - sigma))).astype(jnp.bfloat16)
-                low, high = max(g * band, half_edge), min((g + 1) * band, half_edge + own)
-                if low < high:
-                    base = mid[m, 0, half_edge + low : half_edge + high, :].astype(jnp.float32)
-                    local = slice(low - g * band, high - g * band)
-                    last = (base + mixed[local] * sigma[local]).astype(jnp.bfloat16)
-                    early = mid[m, 0, half_edge + low : half_edge + high, :]
-                    out_ref[m, low - half_edge : high - half_edge, :] = jnp.where(seg == 0, early, last)
+            for g, (a, start) in enumerate(first):
+                o = (start + HALO) * lon_cols
+                near = jnp.concatenate([r[m, o : o + win, :] for r in blk], axis=0)
+                put_spread(dot(forward[g], near).astype(jnp.bfloat16), s0, (m * nf + g) * cells)
+
+    def early(idx, x0, x1, x2, x3, w_own, forward, s0, s1, slope, mid):
+        @pl.when(idx[0] == 0)
+        def _():
+            first_section((x0, x1, x2, x3), w_own, s0, s1, slope, mid, forward)
+
+    def own_part(g):
+        return max(g * band, half_edge), min((g + 1) * band, half_edge + own)
+
+    def apply_back(w, gates, feat):
         for b in range(BASIS):
-            got = dot_nt(gates[...], w[width + b * channels : width + (b + 1) * channels, :]).astype(jnp.bfloat16)
+            got = dot_nt(gates[...], w[b * channels : (b + 1) * channels, :]).astype(jnp.bfloat16)
             for i in range(members * ns):
                 feat[(i * BASIS + b) * cells : (i * BASIS + b + 1) * cells, :] = got[i * cells : (i + 1) * cells]
-        pull[...] = jnp.zeros(pull.shape, jnp.float32)
+
+    def chain(idx, x0, x1, x2, x3, c0, c1, c2, c3, w_own, w_a, w_b, forward, backward, s0, s1_in, slope_in, mid_in,
+              s1, slope, mid, out_ref, next_ref, gate_ref, own_ref, p1, p2, p3, w, gates, feat, pull, grads):
+        coming_blocks = (c0, c1, c2, c3)
+        seg, lon, lat = idx[0], idx[1], idx[2]
+        half = w_a.shape[0]
+        core = lon % 2
+        w[pl.ds(pl.multiple_of(core * half, half), half), :] = w_a[...]
+        w[pl.ds(pl.multiple_of((1 - core) * half, half), half), :] = w_b[...]
+        columns = pl.ds(pl.multiple_of(lon * (width // blocks), 128), width // blocks)
+
+        def coming_at(m, g):
+            return jnp.concatenate([r[m, g * band : (g + 1) * band, :] for r in coming_blocks], axis=0).astype(jnp.float32)
+
+        def second_section(weight, into, last):
+            for m in range(members):
+                total = dot(s1[m * ns * cells : (m + 1) * ns * cells, :], weight[...])
+                for g in range(ns):
+                    at = (m * ns + g) * cells
+                    mixed = total[g * cells : (g + 1) * cells]
+                    sigma = jax.nn.sigmoid(mixed)
+                    into[at : at + cells, :] = (coming_at(m, g) * sigma * (1.0 + mixed * (1.0 - sigma))).astype(jnp.bfloat16)
+                    low, high = own_part(g)
+                    base = mid[m, 0, half_edge + low : half_edge + high, :]
+                    if last:
+                        local = slice(low - g * band, high - g * band)
+                        base = (base.astype(jnp.float32) + mixed[local] * sigma[local]).astype(jnp.bfloat16)
+                    out_ref[m, low - half_edge : high - half_edge, :] = base
+
+        def store_grads(left, right):
+            got = dot_tn(jnp.concatenate(left, axis=0), jnp.concatenate(right, axis=0))
+            for c in range(pieces):
+                grads[pl.ds(c, width // blocks, stride=pieces), :] = got[:, c * lanes : (c + 1) * lanes]
+
+        @pl.when(seg == 0)
+        def _():
+            second_section(w, gates, False)
+            apply_back(w, gates, feat)
+            for m in range(members):
+                for g in range(ns):
+                    at = (m * ns + g) * cells * BASIS
+                    got = dot(backward[g], feat[at : at + BASIS * cells, :]).reshape(blocks, win, channels)
+                    if g == 0:
+                        pull[m, :, :win, :] = got
+                    else:
+                        pull[m, :, g * band : (g + 1) * band, :] += got[:, :band]
+                        pull[m, :, (g + 1) * band : g * band + win, :] = got[:, band:]
+            left, right = [], []
+            step = half_edge
+            for m in range(members):
+                for g in range(ns):
+                    at = (m * ns + g) * cells
+                    span = slice(half_edge + g * band, half_edge + (g + 1) * band)
+                    value = (coming_at(m, g) + pull[m, :, span, :].reshape(cells, channels)).astype(jnp.bfloat16)
+                    low, high = own_part(g)
+                    next_ref[m, low - half_edge : high - half_edge, :] = value[low - g * band : high - g * band]
+                    gate = value.astype(jnp.float32) * slope[m, :, span, :].reshape(cells, channels)
+                    gate_ref[at : at + cells, :] = gate.astype(jnp.bfloat16)
+                for g in range(1, nf - 1):
+                    at = (m * nf + g) * cells
+                    left.append(s0[at : at + cells, columns])
+                    for q in range(blocks):
+                        for o in range(0, band, step):
+                            spot = half_edge + (g - 1) * band + o
+                            turn, rest = spot // band, spot % band
+                            at = (m * ns + turn) * cells + q * band + rest
+                            right.append(gate_ref[at : at + step, :])
+            store_grads(left, right)
+
+        @pl.when(seg == 1)
+        def _():
+            first_section((x0, x1, x2, x3), w, s0, s1, slope, mid, forward)
+            second_section(w_own, gate_ref, True)
+            left, right = [], []
+            for m in range(members):
+                next_ref[m, :, :] = c0[m, half_edge : half_edge + own, :]
+                for g in range(ns):
+                    low, high = own_part(g)
+                    for q in range(blocks):
+                        at = (m * ns + g) * cells + q * band - g * band
+                        left.append(s1[at + low : at + high, columns])
+                        right.append(gate_ref[at + low : at + high, :])
+            store_grads(left, right)
+
+        share = width // blocks // lat_devices * pieces
+
+        def rows_of(index):
+            return grads[pl.ds(pl.multiple_of(index * share, share), share), :]
+
+        own_ref[...] = rows_of(lat)
+        for bit, ref in ((1, p1), (2, p2), (3, p3)):
+            ref[...] = rows_of(lat ^ bit).astype(jnp.bfloat16)
+
+    def finish(w_own, backward, gates, next_ref, last_ref, grad_ref, out_ref, feat, pull):
+        apply_back(w_own, gates, feat)
         for m in range(members):
             for g in range(ns):
                 at = (m * ns + g) * cells * BASIS
-                got = dot(backward[g], feat[at : at + BASIS * cells, :])
-                pull[m, :, g * band : g * band + win, :] += got.reshape(blocks, win, channels)
-        for m in range(members):
-            for q in range(blocks):
-                coming = blk[q][m, x_len : x_len + c_len, :].astype(jnp.float32)
-                value = (coming + pull[m, q, half_edge : half_edge + c_len, :]).astype(jnp.bfloat16)
-                if q == 0:
-                    grad_ref[m, :, :] = value[half_edge : half_edge + own]
-                gate = value.astype(jnp.float32) * slope[m, q, half_edge : half_edge + c_len, :]
-                gate_ref[m, q, :, :] = gate.astype(jnp.bfloat16)
-
-        columns = pl.ds(pl.multiple_of(lon * (width // blocks), 128), width // blocks)
-
-        @pl.when(seg == 0)
-        def _():
-            left, right = [], []
-            for m in range(members):
-                for g in range(1, nf - 1):
-                    at = (m * nf + g) * cells
-                    left.append(s0[at : at + cells, columns])
-                    o = half_edge + (g - 1) * band
-                    right.append(gate_ref[m, :, o : o + band, :].reshape(cells, channels))
-            grads[...] = dot_tn(jnp.concatenate(left, axis=0), jnp.concatenate(right, axis=0))
-
-        @pl.when(seg == 1)
-        def _():
-            left, right = [], []
-            for m in range(members):
-                for g in range(ns):
-                    low, high = max(g * band, half_edge), min((g + 1) * band, half_edge + own)
-                    for q in range(blocks):
-                        at = (m * ns + g) * cells + q * band - g * band
-                        left.append(s1[at + low : at + high, columns])
-                        right.append(gates[at + low : at + high, :])
-            grads[...] = dot_tn(jnp.concatenate(left, axis=0), jnp.concatenate(right, axis=0))
-
-        share = width // blocks // lat_devices
-
-        def rows_of(index):
-            return grads[pl.ds(pl.multiple_of(index * share, share), share), :]
-
-        own_ref[...] = rows_of(lat)
-        for bit, ref in ((1, p1), (2, p2), (3, p3)):
-            ref[...] = rows_of(lat ^ bit).astype(jnp.bfloat16)
-
-    def finish(idx, w_own, backward, gate_ref, g1_ref, grad_ref, gates, feat, pull):
-        seg = idx[0]
-
-        @pl.when(seg == 1)
-        def _():
-            grad_ref[...] = g1_ref[...]
-
-        @pl.when(seg == 0)
-        def _():
-            for m in range(members):
-                for g in range(ns):
-                    at = (m * ns + g) * cells
-                    gates[at : at + cells, :] = gate_ref[m, :, g * band : (g + 1) * band, :].reshape(cells, channels)
-            for b in range(BASIS):
-                got = dot_nt(gates[...], w_own[b * channels : (b + 1) * channels, :]).astype(jnp.bfloat16)
-                for i in range(members * ns):
-                    feat[(i * BASIS + b) * cells : (i * BASIS + b + 1) * cells, :] = got[i * cells : (i + 1) * cells]
-            pull[...] = jnp.zeros(pull.shape, jnp.float32)
-            for m in range(members):
-                for g in range(ns):
-                    at = (m * ns + g) * cells * BASIS
-                    got = dot(backward[g, 0:win, :], feat[at : at + BASIS * cells, :])
-                    pull[m, g * band : g * band + win, :] += got
-                total = g1_ref[m].astype(jnp.float32) + pull[m, edge : edge + own, :]
-                grad_ref[m, :, :] = total.astype(jnp.bfloat16)
-
-    return chain, finish
+                got = dot(backward[g, 0:win, :], feat[at : at + BASIS * cells, :])
+                if g == 0:
+                    pull[m, :win, :] = got
+                else:
+                    pull[m, g * band : (g + 1) * band, :] += got[:band]
+                    pull[m, (g + 1) * band : g * band + win, :] = got[band:]
+            total = next_ref[m].astype(jnp.float32) + pull[m, 2 * half_edge : 2 * half_edge + own, :]
+            grad_ref[m, :, :] = total.astype(jnp.bfloat16)
+        out_ref[...] = last_ref[...]
+
+    return spread, early, chain, finish
 
 
 def whole_ring(inputs, cotangent, weights, basis_values, lat_step, lon_step):
@@ -395,25 +422,25 @@
     edge = HALO * lon_cols
     half_edge = edge // 2
     width = BASIS * channels
+    kernel = weights.reshape(width, channels)
+    half = lax.dynamic_slice_in_dim(kernel, (lon_index % 2) * (width // 2), width // 2, 0)
+    near_half = lax.ppermute(half, "segment", swap("segment", 1))
+    half, inputs, cotangent = lax.optimization_barrier((half, inputs, cotangent))
     state = inputs.reshape(members, own, channels)
     coming = cotangent.reshape(members, own, channels)
-    kernel = weights.reshape(width, channels)
     up = [(i, i + 1) for i in range(lat_devices - 1)]
     down = [(i + 1, i) for i in range(lat_devices - 1)]
-    tail = jnp.concatenate([state[:, own - edge :], coming[:, own - half_edge :]], axis=1)
-    head = jnp.concatenate([state[:, :edge], coming[:, :half_edge]], axis=1)
-    before = lax.ppermute(tail, "lat", up)
-    after = lax.ppermute(head, "lat", down)
-    half = lax.dynamic_slice_in_dim(kernel, (lon_index % 2) * (width // 2), width // 2, 0)
-    near_half = lax.ppermute(half, "segment", swap("segment", 1))
-    block = jnp.concatenate(
-        [before[:, :edge], state, after[:, :edge], before[:, edge:], coming, after[:, edge:]], axis=1
-    )
-    far = lax.ppermute(block, "lon", swap("lon", 2))
-    mate = lax.ppermute(block, "lon", swap("lon", 1))
-    far_mate = lax.ppermute(far, "lon", swap("lon", 1))
-    far_half = lax.ppermute(near_half, "lon", swap("lon", 1))
-
+    cross = lambda steps: [(n * lat_devices + i, (n ^ 2) * lat_devices + j) for i, j in steps for n in range(blocks)]
+    state_y = lax.ppermute(state, "lon", swap("lon", 2))
+    tail, head = state[:, own - edge :], state[:, :edge]
+    before_y = lax.ppermute(tail, ("lon", "lat"), cross(up))
+    after_y = lax.ppermute(head, ("lon", "lat"), cross(down))
+    before = lax.ppermute(jnp.concatenate([tail, coming[:, own - half_edge :]], axis=1), "lat", up)
+    after = lax.ppermute(jnp.concatenate([head, coming[:, :half_edge]], axis=1), "lat", down)
+    x0 = jnp.concatenate([before[:, :edge], state, after[:, :edge]], axis=1)
+    c0 = jnp.concatenate([before[:, edge:], coming, after[:, edge:]], axis=1)
+    x1 = lax.ppermute(x0, "lon", swap("lon", 1))
+    x2 = jnp.concatenate([before_y, state_y, after_y], axis=1)
     place, basis = tap_tables(
         basis_values, lat_step, lon_step, lat_rows, lon_cols, blocks, lat_index, lon_index, lat_total
     )
@@ -424,67 +451,93 @@
     win = 16 * lon_cols
     vmem = pl.BlockSpec(memory_space=pltpu.VMEM)
     smem = pl.BlockSpec(memory_space=pltpu.SMEM)
-    params = pltpu.CompilerParams(vmem_limit_bytes=48 * 1024 * 1024)
     half_type, full_type = jnp.bfloat16, jnp.float32
-    forward, backward = pl.pallas_call(
+    shape = jax.ShapeDtypeStruct
+    x_len = own + 2 * edge
+
+    def call(body, name, outs, ins, mib, gflops, scratch=(), aliases={}):
+        return pl.pallas_call(
+            body,
+            out_shape=outs,
+            in_specs=[smem if a.ndim == 1 else vmem for a in ins],
+            out_specs=(vmem,) * len(outs),
+            scratch_shapes=list(scratch),
+            input_output_aliases=aliases,
+            compiler_params=pltpu.CompilerParams(vmem_limit_bytes=mib * 1024 * 1024),
+            cost_estimate=pl.CostEstimate(flops=int(gflops * 1e9), bytes_accessed=4_000_000, transcendentals=0),
+            name=name,
+        )(*ins)
+
+    forward, backward = call(
         functools.partial(map_kernel, nf, cells, blocks * win),
-        out_shape=(
-            jax.ShapeDtypeStruct((nf + ns, BASIS * cells, blocks * win), half_type),
-            jax.ShapeDtypeStruct((ns, blocks * win, BASIS * cells), half_type),
-        ),
-        in_specs=[vmem] * 2,
-        out_specs=(vmem,) * 2,
-        compiler_params=params,
-        cost_estimate=pl.CostEstimate(flops=40_000_000, bytes_accessed=4_000_000, transcendentals=0),
-        name="maps",
-    )(place, basis)
-    chain, finish = make_chain(lat_rows, lon_cols, blocks, members, channels, lat_devices)
+        "maps",
+        (shape((nf + ns, BASIS * cells, blocks * win), half_type), shape((ns, blocks * win, BASIS * cells), half_type)),
+        (place, basis),
+        6,
+        4.0,
+    )
+    x2, forward, backward = lax.optimization_barrier((x2, forward, backward))
+    x3 = lax.ppermute(x2, "lon", swap("lon", 1))
+    c2 = lax.ppermute(c0, "lon", swap("lon", 2))
+    c1 = lax.ppermute(c0, "lon", swap("lon", 1))
+    x3, c2 = lax.optimization_barrier((x3, c2))
+    c3 = lax.ppermute(c2, "lon", swap("lon", 1))
+    spread, early, chain, finish = make_steps(lat_rows, lon_cols, blocks, members, channels, lat_devices)
     idx = jnp.stack([segment_index, lon_index, lat_index]).astype(jnp.int32)
     share = width // blocks // lat_devices
-    shape = jax.ShapeDtypeStruct
-    x_len = own + 2 * edge
-    c_len = own + edge
-    out, first_grad, gates, mine, *parts = pl.pallas_call(
+    lines = (share * channels // 128, 128)
+    blocks_type = (members, blocks, x_len, channels)
+    s1_type, slope_type, mid_type = (
+        shape((members * ns * cells, width), half_type),
+        shape(blocks_type, full_type),
+        shape(blocks_type, half_type),
+    )
+    (s0,) = call(
+        spread, "spread", (shape((members * nf * cells, width), half_type),), (x0, x1, x2, x3, forward), 8, 1.5
+    )
+    near_half, s0 = lax.optimization_barrier((near_half, s0))
+    far_half = lax.ppermute(near_half, "lon", swap("lon", 1))
+    s1, slope, mid = call(
+        early, "early", (s1_type, slope_type, mid_type), (idx, x0, x1, x2, x3, kernel, forward, s0), 12, 3.0
+    )
+    _, _, _, out, follow, gates, mine, *parts = call(
         chain,
-        out_shape=(
+        "chain",
+        (
+            s1_type,
+            slope_type,
+            mid_type,
             shape((members, own, channels), half_type),
             shape((members, own, channels), half_type),
-            shape((members, blocks, c_len, channels), half_type),
-            shape((share, channels), full_type),
+            shape((members * ns * cells, channels), half_type),
+            shape(lines, full_type),
         )
-        + (shape((share, channels), half_type),) * 3,
-        in_specs=[smem] + [vmem] * 9,
-        out_specs=(vmem,) * 7,
-        scratch_shapes=[
-            pltpu.VMEM((2 * width, channels), half_type),
-            pltpu.VMEM((members * nf * cells, width), half_type),
-            pltpu.VMEM((members * ns * cells, width), half_type),
-            pltpu.VMEM((members, blocks, x_len, channels), full_type),
-            pltpu.VMEM((members, blocks, x_len, channels), half_type),
+        + (shape(lines, half_type),) * 3,
+        (idx, x0, x1, x2, x3, c0, c1, c2, c3, kernel, near_half, far_half, forward, backward, s0, s1, slope, mid),
+        20,
+        6.0,
+        (
+            pltpu.VMEM((width, channels), half_type),
             pltpu.VMEM((members * ns * cells, channels), half_type),
             pltpu.VMEM((members * ns * cells * BASIS, channels), half_type),
-            pltpu.VMEM((members, blocks, x_len, channels), full_type),
-            pltpu.VMEM((width // blocks, channels), full_type),
-        ],
-        compiler_params=params,
-        cost_estimate=pl.CostEstimate(flops=6_000_000_000, bytes_accessed=10_000_000, transcendentals=2_000_000),
-        name="chain",
-    )(idx, block, mate, far, far_mate, kernel, near_half, far_half, forward, backward)
+            pltpu.VMEM(blocks_type, full_type),
+            pltpu.VMEM((width // blocks * channels // 128, 128), full_type),
+        ),
+        {15: 0, 16: 1, 17: 2},
+    )
     got = [lax.ppermute(part, "lat", swap("lat", bit)) for bit, part in zip((1, 2, 3), parts)]
-    grad = pl.pallas_call(
+    grad, out = call(
         finish,
-        out_shape=shape((members, own, channels), half_type),
-        in_specs=[smem] + [vmem] * 4,
-        out_specs=vmem,
-        scratch_shapes=[
-            pltpu.VMEM((members * ns * cells, channels), half_type),
+        "finish",
+        (shape((members, own, channels), half_type),) * 2,
+        (kernel, backward, gates, follow, out),
+        12,
+        2.0,
+        (
             pltpu.VMEM((members * ns * cells * BASIS, channels), half_type),
             pltpu.VMEM((members, x_len, channels), full_type),
-        ],
-        compiler_params=params,
-        cost_estimate=pl.CostEstimate(flops=2_000_000_000, bytes_accessed=5_000_000, transcendentals=0),
-        name="finish",
-    )(idx, kernel, backward, gates, first_grad)
+        ),
+    )
     total = mine
     for part in got:
         total = total + part.astype(full_type)

time: 65.9 us -> 76.3 us (1.16)
  starting transfers between devices: 15 us -> 21.8 us
  Pallas kernels: 18.1 us -> 20.7 us
  other arithmetic: 1.15 us -> 2.81 us
  local copies, waits for them, and re-layouts: 14.2 us -> 12.9 us
    ppermute x1, waiting for transfers between devices: 13.1 us -> 0.01 us  [whole_ring(): near_half = lax.ppermute(half, 'segment', swap('segment', 1))]
    ppermute x5 -> x10, waiting for transfers between devices: 0.97 us -> 11.4 us  [the longest x1 5.78 us: whole_ring(): c2 = lax.ppermute(c0, 'lon', swap('lon', 2))]
    ppermute x5 -> x10, starting transfers between devices: 8.47 us -> 14.4 us  [the longest x1 4.55 us: whole_ring(): lax.ppermute(jnp.concatenate([tail, coming[:, own - half_edge:]], axis=1)...]
    ppermute x3, waiting for transfers between devices: 2 us -> 4.92 us  [whole_ring(): lax.ppermute(part, 'lat', swap('lat', bit))]
    pallas_call x3 -> x5, Pallas kernels: 18.1 us -> 20.7 us  [call(): pl.pallas_call(body, out_shape=outs, in_specs=[smem if a.ndim == 1 else v...]
    mul x0 -> x1, other arithmetic: none -> 1.65 us  [whole_ring(): weight_grad = (total * grad_scale).reshape(1, share * channels)]
    ppermute x1, starting transfers between devices: 1.56 us -> 2.94 us  [whole_ring(): near_half = lax.ppermute(half, 'segment', swap('segment', 1))]
    unnamed x48 -> x66, local copies, waits for them, and re-layouts: 7.87 us -> 6.53 us
  transfers between devices with their start and end apart: 10 -> 15, of which waited for: 3 -> 3; matrix products, arithmetic and copies ran while one was open for 7% -> 7% of each run, Pallas kernels for 13% -> 19%
where the time goes in v2:
time: 76.3 us; the launch traced here: 75.9 us
  starting transfers between devices  21.8 us (29%)
  Pallas kernels  20.7 us (27%)
  waiting for transfers between devices  16.3 us (21%)
  local copies, waits for them, and re-layouts  12.9 us (17%)
  other arithmetic  2.81 us (4%)
  between operations  1.37 us (2%)
    pallas_call x5, Pallas kernels, call(): pl.pallas_call(body, out_shape=outs, in_specs=[smem if a.ndim == 1 else v...  20.7 us
    unnamed x66, local copies, waits for them, and re-layouts  6.53 us
    ppermute x1, waiting for transfers between devices, whole_ring(): c2 = lax.ppermute(c0, 'lon', swap('lon', 2))  5.78 us
    ppermute x1, waiting for transfers between devices, whole_ring(): after_y = lax.ppermute(head, ('lon', 'lat'), cross(down))  5.58 us
    ppermute x3, waiting for transfers between devices, whole_ring(): lax.ppermute(part, 'lat', swap('lat', bit))  4.92 us
    ppermute x1, starting transfers between devices, whole_ring(): lax.ppermute(jnp.concatenate([tail, coming[:, own - half_edge:]], axis=1)...  4.55 us
    ppermute x3, starting transfers between devices, whole_ring(): lax.ppermute(part, 'lat', swap('lat', bit))  4.39 us
    ppermute x1, starting transfers between devices, whole_ring(): before_y = lax.ppermute(tail, ('lon', 'lat'), cross(up))  3.43 us
  transfers between devices with their start and end apart: 15, of which 3 were waited for; matrix products, arithmetic and copies ran while one was open for 7% of the time, Pallas kernels for 19%

profile of v2, /device:TPU:0, one launch (start us, length us, event | category | flops | bytes accessed | tf_op | source)
XLA Modules:
  0.0 75.9 jit_solution(14747486761708114791)
XLA Ops:
  0.6 0.0 copy-start.22
  0.6 0.0 copy-start.26
  0.7 2.1 %constant_dynamic-slice_fusion = bf16[768,512]{1,0:T(8,128)(2,1)} fusion(bf16[1536,512]{1,0:T(8,128)(2,1)} %bitcast.42, s32[]{:T(128)S(6)} %select_n.38), kind=kLoop, calls=%fused_computation.57 | loop fusion | bytes 1572868 | tf_op jit(solution)/shard_map/dynamic_slice | solution.py:426
  2.8 2.9 %collective-permute-start.10 = (bf16[768,512]{1,0:T(8,128)(2,1)}, bf16[768,512]{1,0:T(8,128)(2,1)}, u32[]{:S(2)}, u32[]{:S(2)}) collective-permute-start(bf16[768,512]{1,0:T(8,128)(2,1)} %constant_dynamic-slice_fusion), channel_id=1, source_target_pairs={{0,1},{1,0},{2,3},{3,2},{4,5},{5,4},{6,7},{7,6},{8,9},{9,8},{10,11... | collective-permute-start | bytes 2359304 | tf_op jit(solution)/shard_map/ppermute | solution.py:427
  5.8 0.9 %reshape.80 = bf16[2,64,512]{2,1,0:T(8,128)(2,1)S(1)} reshape(bf16[2,16,4,512]{3,2,1,0:T(4,128)(2,1)} %param.8) | data formatting | bytes 262144 | tf_op jit(solution)/shard_map/reshape | solution.py:429
  6.7 1.6 %collective-permute-start.1 = (bf16[2,64,512]{2,1,0:T(8,128)(2,1)S(1)}, bf16[2,64,512]{2,1,0:T(8,128)(2,1)S(1)}, u32[]{:S(2)}, u32[]{:S(2)}) collective-permute-start(bf16[2,64,512]{2,1,0:T(8,128)(2,1)S(1)} %reshape.80), channel_id=1, source_target_pairs={{0,16},{8,24},{16,0},{24,8},{1,17},{9,25},{17,1},{25,9},{2,18},{10... | collective-permute-start | bytes 393224 | tf_op jit(solution)/shard_map/ppermute | solution.py:434
  8.3 3.4 %collective-permute-start = (bf16[2,32,512]{2,1,0:T(8,128)(2,1)S(1)}, bf16[2,32,512]{2,1,0:T(8,128)(2,1)S(1)}, u32[]{:S(2)}, u32[]{:S(2)}) collective-permute-start(bf16[2,32,512]{2,1,0:T(8,128)(2,1)S(1)} %get-tuple-element.51), channel_id=1, source_target_pairs={{0,18},{8,26},{16,2},{24,10},{2,20},{10,28},{18,4},{26,12},{4,22},... | collective-permute-start | bytes 196616 | tf_op jit(solution)/shard_map/ppermute | solution.py:436
  11.8 1.3 %collective-permute-start.4 = (bf16[2,48,512]{2,1,0:T(8,128)(2,1)S(1)}, bf16[2,48,512]{2,1,0:T(8,128)(2,1)S(1)}, u32[]{:S(2)}, u32[]{:S(2)}) collective-permute-start(bf16[2,48,512]{2,1,0:T(8,128)(2,1)S(1)} %pad_maximum_fusion.4), channel_id=1, source_target_pairs={{2,0},{4,2},{6,4},{3,1},{5,3},{7,5},{10,8},{12,10},{14,12},{11,9},... | collective-permute-start | bytes 294920 | tf_op jit(solution)/shard_map/ppermute | solution.py:439
  13.2 4.6 %collective-permute-start.3 = (bf16[2,48,512]{2,1,0:T(8,128)(2,1)S(1)}, bf16[2,48,512]{2,1,0:T(8,128)(2,1)S(1)}, u32[]{:S(2)}, u32[]{:S(2)}) collective-permute-start(bf16[2,48,512]{2,1,0:T(8,128)(2,1)S(1)} %pad_maximum_fusion.3), channel_id=1, source_target_pairs={{0,2},{2,4},{4,6},{1,3},{3,5},{5,7},{8,10},{10,12},{12,14},{9,11},... | collective-permute-start | bytes 294920 | tf_op jit(solution)/shard_map/ppermute | solution.py:438
  17.8 0.1 iota_add_fusion
  17.9 0.1 dynamic-slice_bitcast_fusion.7
  18.0 0.1 copy.40
  18.1 0.1 copy.34
  18.2 0.1 copy.35
  18.3 0.1 copy.36
  18.3 0.1 copy.37
  18.4 0.1 copy.38
  18.5 0.1 copy.39
  18.6 0.1 dynamic-slice_bitcast_fusion
  18.7 0.1 copy.47
  18.8 0.1 copy.41
  18.9 0.1 copy.42
  18.9 0.1 copy.43
  19.0 0.1 copy.44
  19.1 0.1 copy.45
  19.2 0.1 copy.46
  19.3 0.1 add.125
  19.4 0.1 fusion.12
  19.5 0.1 compare_and_fusion
  19.7 0.1 broadcast_in_dim.10
  19.8 0.1 add.127
  19.9 0.1 add.133
  20.0 0.7 fusion.5.place_ref
  20.7 0.1 broadcast_in_dim.12
  20.8 8.0 %maps.1 = (bf16[7,384,256]{2,1,0:T(8,128)(2,1)S(1)}, bf16[3,256,384]{2,1,0:T(8,128)(2,1)S(1)}) custom-call(s32[896,9]{1,0:T(8,128)S(1)} %fusion.5.place_ref, f32[896,27]{1,0:T(8,128)S(1)} %bitcast.41), custom_call_target="tpu_custom_call" | custom-call | flops 4000000000 | bytes 4000000 | tf_op jit(solution)/shard_map/maps/pallas_call | solution.py:459
  28.8 0.8 %copy-done.19 = bf16[3,256,384]{2,1,0:T(8,128)(2,1)} copy-done((bf16[3,256,384]{2,1,0:T(8,128)(2,1)}, bf16[3,256,384]{2,1,0:T(8,128)(2,1)S(1)}, u32[]{:S(2)}) %copy-start.19) | copy-done | bytes 589848
  29.6 1.3 %collective-permute-start.2 = (bf16[2,32,512]{2,1,0:T(8,128)(2,1)S(1)}, bf16[2,32,512]{2,1,0:T(8,128)(2,1)S(1)}, u32[]{:S(2)}, u32[]{:S(2)}) collective-permute-start(bf16[2,32,512]{2,1,0:T(8,128)(2,1)S(1)} %get-tuple-element.52), channel_id=1, source_target_pairs={{2,16},{10,24},{18,0},{26,8},{4,18},{12,26},{20,2},{28,10},{6,20},... | collective-permute-start | bytes 196616 | tf_op jit(solution)/shard_map/ppermute | solution.py:437
  31.0 0.1 collective-permute-start.5
  31.1 5.6 %collective-permute-done.2 = bf16[2,32,512]{2,1,0:T(8,128)(2,1)S(1)} collective-permute-done((bf16[2,32,512]{2,1,0:T(8,128)(2,1)S(1)}, bf16[2,32,512]{2,1,0:T(8,128)(2,1)S(1)}, u32[]{:S(2)}, u32[]{:S(2)}) %collective-permute-start.2) | collective-permute-done | bytes 65568 | tf_op jit(solution)/shard_map/ppermute | solution.py:437
  36.7 0.1 collective-permute-start.6
  36.8 0.0 copy-start.14
  36.8 1.6 %collective-permute-start.7 = (bf16[2,96,512]{2,1,0:T(8,128)(2,1)S(1)}, bf16[2,96,512]{2,1,0:T(8,128)(2,1)S(1)}, u32[]{:S(2)}, u32[]{:S(2)}) collective-permute-start(bf16[2,96,512]{2,1,0:T(8,128)(2,1)S(1)} %pad_maximum_fusion.2.c0), channel_id=1, source_target_pairs={{0,16},{8,24},{16,0},{24,8},{1,17},{9,25},{17,1},{25,9},{2,18},{10... | collective-permute-start | bytes 589832 | tf_op jit(solution)/shard_map/ppermute | solution.py:481
  38.4 5.8 %collective-permute-done.7.c2 = bf16[2,96,512]{2,1,0:T(8,128)(2,1)S(1)} collective-permute-done((bf16[2,96,512]{2,1,0:T(8,128)(2,1)S(1)}, bf16[2,96,512]{2,1,0:T(8,128)(2,1)S(1)}, u32[]{:S(2)}, u32[]{:S(2)}) %collective-permute-start.7) | collective-permute-done | bytes 196640 | tf_op jit(solution)/shard_map/ppermute | solution.py:481
  44.2 1.0 %spread.1.s0 = bf16[1024,1536]{1,0:T(8,128)(2,1)S(1)} custom-call(bf16[2,128,512]{2,1,0:T(8,128)(2,1)S(1)} %pad_maximum_fusion.1.x0, bf16[2,128,512]{2,1,0:T(8,128)(2,1)S(1)} %collective-permute-done.5.x1, bf16[2,128,512]{2,1,0:T(8,128)(2,1)S(1)} %pad_maximum_fusion.x2, bf16[2,128,512]{2,1,0:T(8,128)(2,1)S(1)} %collective-permute-done.6.x3, ...), custom_call_target="tpu_custom_call" | custom-call | flops 1500000000 | bytes 4000000 | tf_op jit(solution)/shard_map/spread/pallas_call | solution.py:459
  45.3 0.1 collective-permute-start.11
  45.4 0.1 pad_add_fusion.1.idx
  45.5 0.5 collective-permute-start.8
  45.9 0.1 collective-permute-start.9
  46.0 1.3 %copy-done.1 = bf16[7,384,256]{2,1,0:T(8,128)(2,1)S(1)} copy-done((bf16[7,384,256]{2,1,0:T(8,128)(2,1)S(1)}, bf16[7,384,256]{2,1,0:T(8,128)(2,1)}, u32[]{:S(2)}) %copy-start.1) | copy-done | bytes 1376280
  47.4 0.9 %copy-done.4 = bf16[2,128,512]{2,1,0:T(8,128)(2,1)S(1)} copy-done((bf16[2,128,512]{2,1,0:T(8,128)(2,1)S(1)}, bf16[2,128,512]{2,1,0:T(8,128)(2,1)}, u32[]{:S(2)}) %copy-start.4) | copy-done | bytes 262168
  48.3 1.4 %copy-done.6 = bf16[1,3,512,512]{3,2,1,0:T(8,128)(2,1)S(1)} copy-done((bf16[1,3,512,512]{3,2,1,0:T(8,128)(2,1)S(1)}, bf16[1,3,512,512]{3,2,1,0:T(8,128)(2,1)}, u32[]{:S(2)}) %copy-start.6) | copy-done | bytes 1572888
  49.7 0.9 %copy-done.9 = bf16[2,128,512]{2,1,0:T(8,128)(2,1)S(1)} copy-done((bf16[2,128,512]{2,1,0:T(8,128)(2,1)S(1)}, bf16[2,128,512]{2,1,0:T(8,128)(2,1)}, u32[]{:S(2)}) %copy-start.9) | copy-done | bytes 262168
  50.7 0.9 %copy-done.12 = bf16[2,128,512]{2,1,0:T(8,128)(2,1)S(1)} copy-done((bf16[2,128,512]{2,1,0:T(8,128)(2,1)S(1)}, bf16[2,128,512]{2,1,0:T(8,128)(2,1)}, u32[]{:S(2)}) %copy-start.12) | copy-done | bytes 262168
  51.6 0.0 copy-start.15
  51.7 3.5 %early.1 = (bf16[768,1536]{1,0:T(8,128)(2,1)S(1)}, f32[2,4,128,512]{3,2,1,0:T(8,128)S(1)}, bf16[2,4,128,512]{3,2,1,0:T(8,128)(2,1)S(1)}) custom-call(s32[3]{0:T(128)S(1)} %pad_add_fusion.1.idx, bf16[2,128,512]{2,1,0:T(8,128)(2,1)S(1)} %pad_maximum_fusion.1.x0, bf16[2,128,512]{2,1,0:T(8,128)(2,1)S(1)} %copy-done.9, bf16[2,128,512]{2,1,0:T(8,128)(2,1)S(1)} %copy-done.4, ...), custom_call_target="tpu_custom_call" | custom-call | flops 3000000000 | bytes 4000000 | tf_op jit(solution)/shard_map/early/pallas_call | solution.py:459
  55.3 6.3 %chain.1 = (bf16[768,1536]{1,0:T(8,128)(2,1)S(1)}, f32[2,4,128,512]{3,2,1,0:T(8,128)S(1)}, bf16[2,4,128,512]{3,2,1,0:T(8,128)(2,1)S(1)}, bf16[2,64,512]{2,1,0:T(...) custom-call(s32[3]{0:T(128)S(1)} %pad_add_fusion.1.idx, ...), custom_call_target="tpu_custom_call", output_to_operand_aliasing={{0}: (15, {}), {1}: (16, {}), {2}: (17, {})} | custom-call | flops 6000000000 | bytes 4000000 | tf_op jit(solution)/shard_map/chain/pallas_call | solution.py:459
  61.7 1.6 %collective-permute-start.12 = (bf16[384,128]{1,0:T(8,128)(2,1)}, bf16[384,128]{1,0:T(8,128)(2,1)S(1)}, u32[]{:S(2)}, u32[]{:S(2)}) collective-permute-start(bf16[384,128]{1,0:T(8,128)(2,1)} %get-tuple-element.46), channel_id=1, source_target_pairs={{0,2},{2,0},{4,6},{6,4},{1,3},{3,1},{5,7},{7,5},{8,10},{10,8},{12,... | collective-permute-start | bytes 294920 | tf_op jit(solution)/shard_map/ppermute | solution.py:528
  63.2 1.1 %collective-permute-start.13 = (bf16[384,128]{1,0:T(8,128)(2,1)}, bf16[384,128]{1,0:T(8,128)(2,1)S(1)}, u32[]{:S(2)}, u32[]{:S(2)}) collective-permute-start(bf16[384,128]{1,0:T(8,128)(2,1)} %get-tuple-element.47), channel_id=1, source_target_pairs={{0,4},{2,6},{4,0},{6,2},{1,5},{3,7},{5,1},{7,3},{8,12},{10,14},{12... | collective-permute-start | bytes 294920 | tf_op jit(solution)/shard_map/ppermute | solution.py:528
  64.3 1.8 %collective-permute-start.14 = (bf16[384,128]{1,0:T(8,128)(2,1)S(1)}, bf16[384,128]{1,0:T(8,128)(2,1)S(1)}, u32[]{:S(2)}, u32[]{:S(2)}) collective-permute-start(bf16[384,128]{1,0:T(8,128)(2,1)S(1)} %get-tuple-element.48), channel_id=1, source_target_pairs={{0,6},{2,4},{4,2},{6,0},{1,7},{3,5},{5,3},{7,1},{8,14},{10,12},{12... | collective-permute-start | bytes 294920 | tf_op jit(solution)/shard_map/ppermute | solution.py:528
  66.1 1.8 %finish.1 = (bf16[2,64,512]{2,1,0:T(8,128)(2,1)S(1)}, bf16[2,64,512]{2,1,0:T(8,128)(2,1)S(1)}) custom-call(bf16[1536,512]{1,0:T(8,128)(2,1)S(1)} %bitcast.45, bf16[3,256,384]{2,1,0:T(8,128)(2,1)S(1)} %copy-done.20, bf16[768,512]{1,0:T(8,128)(2,1)S(1)} %get-tuple-element.40.gates, bf16[2,64,512]{2,1,0:T(8,128)(2,1)S(1)} %get-tuple-element.41.next_ref, ...), custom_call_target="tpu_custom_call" | custom-call | flops 2000000000 | bytes 4000000 | tf_op jit(solution)/shard_map/finish/pallas_call | solution.py:459
  67.9 0.7 reshape.84
  68.6 0.7 reshape.85
  69.3 4.9 %collective-permute-done.13 = bf16[384,128]{1,0:T(8,128)(2,1)S(1)} collective-permute-done((bf16[384,128]{1,0:T(8,128)(2,1)}, bf16[384,128]{1,0:T(8,128)(2,1)S(1)}, u32[]{:S(2)}, u32[]{:S(2)}) %collective-permute-start.13) | collective-permute-done | bytes 98336 | tf_op jit(solution)/shard_map/ppermute | solution.py:528
  74.2 1.7 %add_multiply_fusion = f32[384,128]{1,0:T(8,128)} fusion(bf16[384,128]{1,0:T(8,128)(2,1)S(1)} %collective-permute-done.14, bf16[384,128]{1,0:T(8,128)(2,1)S(1)} %collective-permute-done.13, f32[384,128]{1,0:T(8,128)} %copy-done.16, bf16[384,128]{1,0:T(8,128)(2,1)S(1)} %collective-permute-done.12), kind=kLoop, calls=%fused_computation.22 | loop fusion | flops 344064 | bytes 688128 | tf_op jit(solution)/shard_map/mul | solution.py:544
  (88 shorter events, 0.3 us)
Async XLA Ops:
  0.6 17.1 %copy-start.22 = (s32[7,8]{1,0:T(8,128)S(1)}, s32[7,8]{1,0:T(8,128)}, u32[]{:S(2)}) copy-start(s32[7,8]{1,0:T(8,128)} %constant.84.clone) | copy-start | bytes 676
  0.6 18.8 %copy-start.26 = (s32[7]{0:T(128)S(1)}, s32[7]{0:T(128)}, u32[]{:S(2)}) copy-start(s32[7]{0:T(128)} %constant.91) | copy-start | bytes 88
  0.7 11.1 %copy-start.21 = (bf16[2,16,4,512]{3,2,1,0:T(4,128)(2,1)S(1)}, bf16[2,16,4,512]{3,2,1,0:T(4,128)(2,1)}, u32[]{:S(2)}) copy-start(bf16[2,16,4,512]{3,2,1,0:T(4,128)(2,1)} %param.9) | copy-start | bytes 393220
  0.7 17.2 %copy-start.23 = (f32[64,9,3]{0,2,1:T(4,128)S(1)}, f32[64,9,3]{0,2,1:T(4,128)}, u32[]{:S(2)}) copy-start(f32[64,9,3]{0,2,1:T(4,128)} %param.11) | copy-start | bytes 20740
  0.7 17.2 %copy-start.24 = (s32[64,9]{0,1:T(8,128)S(1)}, s32[64,9]{0,1:T(8,128)}, u32[]{:S(2)}) copy-start(s32[64,9]{0,1:T(8,128)} %param.13) | copy-start | bytes 6916
  0.7 17.2 %copy-start.25 = (s32[64,9]{0,1:T(8,128)S(1)}, s32[64,9]{0,1:T(8,128)}, u32[]{:S(2)}) copy-start(s32[64,9]{0,1:T(8,128)} %param.12) | copy-start | bytes 6916
  2.8 42.4 %collective-permute-start.10 = (bf16[768,512]{1,0:T(8,128)(2,1)}, bf16[768,512]{1,0:T(8,128)(2,1)}, u32[]{:S(2)}, u32[]{:S(2)}) collective-permute-start(bf16[768,512]{1,0:T(8,128)(2,1)} %constant_dynamic-slice_fusion), channel_id=1, source_target_pairs={{0,1},{1,0},{2,3},{3,2},{4,5},{5,4},{6,7},{7,6},{8,9},{9,8},{10,11... | collective-permute-start | bytes 2359304 | tf_op jit(solution)/shard_map/ppermute | solution.py:427
  6.7 30.0 %collective-permute-start.1 = (bf16[2,64,512]{2,1,0:T(8,128)(2,1)S(1)}, bf16[2,64,512]{2,1,0:T(8,128)(2,1)S(1)}, u32[]{:S(2)}, u32[]{:S(2)}) collective-permute-start(bf16[2,64,512]{2,1,0:T(8,128)(2,1)S(1)} %reshape.80), channel_id=1, source_target_pairs={{0,16},{8,24},{16,0},{24,8},{1,17},{9,25},{17,1},{25,9},{2,18},{10... | collective-permute-start | bytes 393224 | tf_op jit(solution)/shard_map/ppermute | solution.py:434
  8.3 22.8 %collective-permute-start = (bf16[2,32,512]{2,1,0:T(8,128)(2,1)S(1)}, bf16[2,32,512]{2,1,0:T(8,128)(2,1)S(1)}, u32[]{:S(2)}, u32[]{:S(2)}) collective-permute-start(bf16[2,32,512]{2,1,0:T(8,128)(2,1)S(1)} %get-tuple-element.51), channel_id=1, source_target_pairs={{0,18},{8,26},{16,2},{24,10},{2,20},{10,28},{18,4},{26,12},{4,22},... | collective-permute-start | bytes 196616 | tf_op jit(solution)/shard_map/ppermute | solution.py:436
  11.8 17.8 %collective-permute-start.4 = (bf16[2,48,512]{2,1,0:T(8,128)(2,1)S(1)}, bf16[2,48,512]{2,1,0:T(8,128)(2,1)S(1)}, u32[]{:S(2)}, u32[]{:S(2)}) collective-permute-start(bf16[2,48,512]{2,1,0:T(8,128)(2,1)S(1)} %pad_maximum_fusion.4), channel_id=1, source_target_pairs={{2,0},{4,2},{6,4},{3,1},{5,3},{7,5},{10,8},{12,10},{14,12},{11,9},... | collective-permute-start | bytes 294920 | tf_op jit(solution)/shard_map/ppermute | solution.py:439
  13.2 17.8 %collective-permute-start.3 = (bf16[2,48,512]{2,1,0:T(8,128)(2,1)S(1)}, bf16[2,48,512]{2,1,0:T(8,128)(2,1)S(1)}, u32[]{:S(2)}, u32[]{:S(2)}) collective-permute-start(bf16[2,48,512]{2,1,0:T(8,128)(2,1)S(1)} %pad_maximum_fusion.3), channel_id=1, source_target_pairs={{0,2},{2,4},{4,6},{1,3},{3,5},{5,7},{8,10},{10,12},{12,14},{9,11},... | collective-permute-start | bytes 294920 | tf_op jit(solution)/shard_map/ppermute | solution.py:438
  28.8 0.8 %copy-start.19 = (bf16[3,256,384]{2,1,0:T(8,128)(2,1)}, bf16[3,256,384]{2,1,0:T(8,128)(2,1)S(1)}, u32[]{:S(2)}) copy-start(bf16[3,256,384]{2,1,0:T(8,128)(2,1)S(1)} %get-tuple-element.29.backward) | copy-start | bytes 1769476
  29.6 15.6 %copy-start = (bf16[7,384,256]{2,1,0:T(8,128)(2,1)}, bf16[7,384,256]{2,1,0:T(8,128)(2,1)S(1)}, u32[]{:S(2)}) copy-start(bf16[7,384,256]{2,1,0:T(8,128)(2,1)S(1)} %get-tuple-element.34.forward) | copy-start | bytes 4128772
  29.6 7.0 %collective-permute-start.2 = (bf16[2,32,512]{2,1,0:T(8,128)(2,1)S(1)}, bf16[2,32,512]{2,1,0:T(8,128)(2,1)S(1)}, u32[]{:S(2)}, u32[]{:S(2)}) collective-permute-start(bf16[2,32,512]{2,1,0:T(8,128)(2,1)S(1)} %get-tuple-element.52), channel_id=1, source_target_pairs={{2,16},{10,24},{18,0},{26,8},{4,18},{12,26},{20,2},{28,10},{6,20},... | collective-permute-start | bytes 196616 | tf_op jit(solution)/shard_map/ppermute | solution.py:437
  31.0 13.2 %collective-permute-start.5 = (bf16[2,128,512]{2,1,0:T(8,128)(2,1)S(1)}, bf16[2,128,512]{2,1,0:T(8,128)(2,1)S(1)}, u32[]{:S(2)}, u32[]{:S(2)}) collective-permute-start(bf16[2,128,512]{2,1,0:T(8,128)(2,1)S(1)} %pad_maximum_fusion.1.x0), channel_id=1, source_target_pairs={{0,8},{8,0},{16,24},{24,16},{1,9},{9,1},{17,25},{25,17},{2,10},{10... | collective-permute-start | bytes 786440 | tf_op jit(solution)/shard_map/ppermute | solution.py:442
  36.7 8.5 %copy-start.3 = (bf16[2,128,512]{2,1,0:T(8,128)(2,1)}, bf16[2,128,512]{2,1,0:T(8,128)(2,1)S(1)}, u32[]{:S(2)}) copy-start(bf16[2,128,512]{2,1,0:T(8,128)(2,1)S(1)} %pad_maximum_fusion.x2) | copy-start | bytes 786436
  36.7 7.5 %collective-permute-start.6 = (bf16[2,128,512]{2,1,0:T(8,128)(2,1)S(1)}, bf16[2,128,512]{2,1,0:T(8,128)(2,1)S(1)}, u32[]{:S(2)}, u32[]{:S(2)}) collective-permute-start(bf16[2,128,512]{2,1,0:T(8,128)(2,1)S(1)} %pad_maximum_fusion.x2), channel_id=1, source_target_pairs={{0,8},{8,0},{16,24},{24,16},{1,9},{9,1},{17,25},{25,17},{2,10},{10... | collective-permute-start | bytes 786440 | tf_op jit(solution)/shard_map/ppermute | solution.py:480
  36.8 8.4 %copy-start.14 = (bf16[2,96,512]{2,1,0:T(8,128)(2,1)}, bf16[2,96,512]{2,1,0:T(8,128)(2,1)S(1)}, u32[]{:S(2)}) copy-start(bf16[2,96,512]{2,1,0:T(8,128)(2,1)S(1)} %pad_maximum_fusion.2.c0) | copy-start | bytes 589828
  36.8 7.4 %collective-permute-start.7 = (bf16[2,96,512]{2,1,0:T(8,128)(2,1)S(1)}, bf16[2,96,512]{2,1,0:T(8,128)(2,1)S(1)}, u32[]{:S(2)}, u32[]{:S(2)}) collective-permute-start(bf16[2,96,512]{2,1,0:T(8,128)(2,1)S(1)} %pad_maximum_fusion.2.c0), channel_id=1, source_target_pairs={{0,16},{8,24},{16,0},{24,8},{1,17},{9,25},{17,1},{25,9},{2,18},{10... | collective-permute-start | bytes 589832 | tf_op jit(solution)/shard_map/ppermute | solution.py:481
  44.2 1.0 %copy-start.17 = (bf16[2,96,512]{2,1,0:T(8,128)(2,1)}, bf16[2,96,512]{2,1,0:T(8,128)(2,1)S(1)}, u32[]{:S(2)}) copy-start(bf16[2,96,512]{2,1,0:T(8,128)(2,1)S(1)} %collective-permute-done.7.c2) | copy-start | bytes 589828
  44.2 1.0 %copy-start.11 = (bf16[2,128,512]{2,1,0:T(8,128)(2,1)}, bf16[2,128,512]{2,1,0:T(8,128)(2,1)S(1)}, u32[]{:S(2)}) copy-start(bf16[2,128,512]{2,1,0:T(8,128)(2,1)S(1)} %collective-permute-done.6.x3) | copy-start | bytes 786436
  44.2 1.1 %copy-start.8 = (bf16[2,128,512]{2,1,0:T(8,128)(2,1)}, bf16[2,128,512]{2,1,0:T(8,128)(2,1)S(1)}, u32[]{:S(2)}) copy-start(bf16[2,128,512]{2,1,0:T(8,128)(2,1)S(1)} %collective-permute-done.5.x1) | copy-start | bytes 786436
  45.3 10.0 %collective-permute-start.11 = (bf16[768,512]{1,0:T(8,128)(2,1)}, bf16[768,512]{1,0:T(8,128)(2,1)}, u32[]{:S(2)}, u32[]{:S(2)}) collective-permute-start(bf16[768,512]{1,0:T(8,128)(2,1)} %collective-permute-done.10.w_a), channel_id=1, source_target_pairs={{0,8},{8,0},{16,24},{24,16},{1,9},{9,1},{17,25},{25,17},{2,10},{10... | collective-permute-start | bytes 2359304 | tf_op jit(solution)/shard_map/ppermute | solution.py:499
  45.5 9.8 %collective-permute-start.8 = (bf16[2,96,512]{2,1,0:T(8,128)(2,1)}, bf16[2,96,512]{2,1,0:T(8,128)(2,1)S(1)}, u32[]{:S(2)}, u32[]{:S(2)}) collective-permute-start(bf16[2,96,512]{2,1,0:T(8,128)(2,1)} %copy-done.14), channel_id=1, source_target_pairs={{0,8},{8,0},{16,24},{24,16},{1,9},{9,1},{17,25},{25,17},{2,10},{10... | collective-permute-start | bytes 589832 | tf_op jit(solution)/shard_map/ppermute | solution.py:482
  45.9 9.3 %collective-permute-start.9 = (bf16[2,96,512]{2,1,0:T(8,128)(2,1)}, bf16[2,96,512]{2,1,0:T(8,128)(2,1)S(1)}, u32[]{:S(2)}, u32[]{:S(2)}) collective-permute-start(bf16[2,96,512]{2,1,0:T(8,128)(2,1)} %copy-done.17), channel_id=1, source_target_pairs={{0,8},{8,0},{16,24},{24,16},{1,9},{9,1},{17,25},{25,17},{2,10},{10... | collective-permute-start | bytes 589832 | tf_op jit(solution)/shard_map/ppermute | solution.py:484
  46.0 1.3 %copy-start.1 = (bf16[7,384,256]{2,1,0:T(8,128)(2,1)S(1)}, bf16[7,384,256]{2,1,0:T(8,128)(2,1)}, u32[]{:S(2)}) copy-start(bf16[7,384,256]{2,1,0:T(8,128)(2,1)} %copy-done) | copy-start | bytes 4128772
  47.4 0.9 %copy-start.4 = (bf16[2,128,512]{2,1,0:T(8,128)(2,1)S(1)}, bf16[2,128,512]{2,1,0:T(8,128)(2,1)}, u32[]{:S(2)}) copy-start(bf16[2,128,512]{2,1,0:T(8,128)(2,1)} %copy-done.3) | copy-start | bytes 786436
  48.3 1.4 %copy-start.6 = (bf16[1,3,512,512]{3,2,1,0:T(8,128)(2,1)S(1)}, bf16[1,3,512,512]{3,2,1,0:T(8,128)(2,1)}, u32[]{:S(2)}) copy-start(bf16[1,3,512,512]{3,2,1,0:T(8,128)(2,1)} %param.10) | copy-start | bytes 4718596
  49.7 0.9 %copy-start.9 = (bf16[2,128,512]{2,1,0:T(8,128)(2,1)S(1)}, bf16[2,128,512]{2,1,0:T(8,128)(2,1)}, u32[]{:S(2)}) copy-start(bf16[2,128,512]{2,1,0:T(8,128)(2,1)} %copy-done.8) | copy-start | bytes 786436
  50.7 0.9 %copy-start.12 = (bf16[2,128,512]{2,1,0:T(8,128)(2,1)S(1)}, bf16[2,128,512]{2,1,0:T(8,128)(2,1)}, u32[]{:S(2)}) copy-start(bf16[2,128,512]{2,1,0:T(8,128)(2,1)} %copy-done.11) | copy-start | bytes 786436
  51.6 3.6 %copy-start.2 = (bf16[7,384,256]{2,1,0:T(8,128)(2,1)S(1)}, bf16[7,384,256]{2,1,0:T(8,128)(2,1)}, u32[]{:S(2)}) copy-start(bf16[7,384,256]{2,1,0:T(8,128)(2,1)} %copy-done) | copy-start | bytes 4128772
  51.6 3.6 %copy-start.5 = (bf16[2,128,512]{2,1,0:T(8,128)(2,1)S(1)}, bf16[2,128,512]{2,1,0:T(8,128)(2,1)}, u32[]{:S(2)}) copy-start(bf16[2,128,512]{2,1,0:T(8,128)(2,1)} %copy-done.3) | copy-start | bytes 786436
  51.6 3.7 %copy-start.7 = (bf16[1,3,512,512]{3,2,1,0:T(8,128)(2,1)S(1)}, bf16[1,3,512,512]{3,2,1,0:T(8,128)(2,1)}, u32[]{:S(2)}) copy-start(bf16[1,3,512,512]{3,2,1,0:T(8,128)(2,1)} %param.10) | copy-start | bytes 4718596
  51.6 3.7 %copy-start.10 = (bf16[2,128,512]{2,1,0:T(8,128)(2,1)S(1)}, bf16[2,128,512]{2,1,0:T(8,128)(2,1)}, u32[]{:S(2)}) copy-start(bf16[2,128,512]{2,1,0:T(8,128)(2,1)} %copy-done.8) | copy-start | bytes 786436
  51.6 3.7 %copy-start.13 = (bf16[2,128,512]{2,1,0:T(8,128)(2,1)S(1)}, bf16[2,128,512]{2,1,0:T(8,128)(2,1)}, u32[]{:S(2)}) copy-start(bf16[2,128,512]{2,1,0:T(8,128)(2,1)} %copy-done.11) | copy-start | bytes 786436
  51.6 3.7 %copy-start.15 = (bf16[2,96,512]{2,1,0:T(8,128)(2,1)S(1)}, bf16[2,96,512]{2,1,0:T(8,128)(2,1)}, u32[]{:S(2)}) copy-start(bf16[2,96,512]{2,1,0:T(8,128)(2,1)} %copy-done.14) | copy-start | bytes 589828
  51.7 3.7 %copy-start.18 = (bf16[2,96,512]{2,1,0:T(8,128)(2,1)S(1)}, bf16[2,96,512]{2,1,0:T(8,128)(2,1)}, u32[]{:S(2)}) copy-start(bf16[2,96,512]{2,1,0:T(8,128)(2,1)} %copy-done.17) | copy-start | bytes 589828
  51.7 3.7 %copy-start.20 = (bf16[3,256,384]{2,1,0:T(8,128)(2,1)S(1)}, bf16[3,256,384]{2,1,0:T(8,128)(2,1)}, u32[]{:S(2)}) copy-start(bf16[3,256,384]{2,1,0:T(8,128)(2,1)} %copy-done.19) | copy-start | bytes 1769476
  61.7 6.2 %copy-start.16 = (f32[384,128]{1,0:T(8,128)}, f32[384,128]{1,0:T(8,128)S(1)}, u32[]{:S(2)}) copy-start(f32[384,128]{1,0:T(8,128)S(1)} %get-tuple-element.45) | copy-start | bytes 589828
  61.7 7.6 %collective-permute-start.12 = (bf16[384,128]{1,0:T(8,128)(2,1)}, bf16[384,128]{1,0:T(8,128)(2,1)S(1)}, u32[]{:S(2)}, u32[]{:S(2)}) collective-permute-start(bf16[384,128]{1,0:T(8,128)(2,1)} %get-tuple-element.46), channel_id=1, source_target_pairs={{0,2},{2,0},{4,6},{6,4},{1,3},{3,1},{5,7},{7,5},{8,10},{10,8},{12,... | collective-permute-start | bytes 294920 | tf_op jit(solution)/shard_map/ppermute | solution.py:528
  63.2 11.0 %collective-permute-start.13 = (bf16[384,128]{1,0:T(8,128)(2,1)}, bf16[384,128]{1,0:T(8,128)(2,1)S(1)}, u32[]{:S(2)}, u32[]{:S(2)}) collective-permute-start(bf16[384,128]{1,0:T(8,128)(2,1)} %get-tuple-element.47), channel_id=1, source_target_pairs={{0,4},{2,6},{4,0},{6,2},{1,5},{3,7},{5,1},{7,3},{8,12},{10,14},{12... | collective-permute-start | bytes 294920 | tf_op jit(solution)/shard_map/ppermute | solution.py:528
  64.3 9.9 %collective-permute-start.14 = (bf16[384,128]{1,0:T(8,128)(2,1)S(1)}, bf16[384,128]{1,0:T(8,128)(2,1)S(1)}, u32[]{:S(2)}, u32[]{:S(2)}) collective-permute-start(bf16[384,128]{1,0:T(8,128)(2,1)S(1)} %get-tuple-element.48), channel_id=1, source_target_pairs={{0,6},{2,4},{4,2},{6,0},{1,7},{3,5},{5,3},{7,1},{8,14},{10,12},{12... | collective-permute-start | bytes 294920 | tf_op jit(solution)/shard_map/ppermute | solution.py:528

commit v3 on v2

v3 whole, which is shorter than its diff:
```python
import functools
import math

import jax
import jax.numpy as jnp
from jax import lax
from jax.experimental import pallas as pl
from jax.experimental.pallas import tpu as pltpu
from jax.sharding import PartitionSpec as P

BASIS = 3
TAPS = 9
REACH = 2


def with_halo(array, sides, width):
    for axis, dim in sides:
        size, length = (lax.axis_size(axis), array.shape[dim])
        up = [(i, (i + 1) % size) for i in range(size)]
        down = [(j, i) for i, j in up]
        last = lax.slice_in_dim(array, length - width, length, axis=dim)
        first = lax.slice_in_dim(array, 0, width, axis=dim)
        before = lax.ppermute(last, axis, up)
        after = lax.ppermute(first, axis, down)
        array = jnp.concatenate([before, array, after], axis=dim)
    return array


def shifted(block, axis, distance):
    devices = range(lax.axis_size(axis))
    route = [(i - distance, i) for i in devices if i - distance in devices]
    return lax.ppermute(block, axis, route)


def widen(features):
    return with_halo(features, (("lon", 2), ("lat", 1)), REACH)


def pass_ahead(result):
    return shifted(result, "segment", 1)


def pass_behind(result):
    return shifted(result, "segment", -1)


def build_tables(basis_values, lat_step, lon_step, lat_rows, lon_cols, lat_index, lat_total):
    pad_rows = lat_rows + 2 * REACH
    pad_cols = lon_cols + 2 * REACH
    lat_padded = jnp.pad(lat_step, ((REACH, REACH), (0, 0)))
    lon_padded = jnp.pad(lon_step, ((REACH, REACH), (0, 0)))
    basis_padded = jnp.pad(basis_values, ((REACH, REACH), (0, 0), (0, 0)))
    row_start = lat_index * lat_rows
    lat_near = lax.dynamic_slice_in_dim(lat_padded, row_start, pad_rows, 0)
    lon_near = lax.dynamic_slice_in_dim(lon_padded, row_start, pad_rows, 0)
    basis_near = lax.dynamic_slice_in_dim(basis_padded, row_start, pad_rows, 0)
    lat_own = lat_near[REACH : REACH + lat_rows]
    lon_own = lon_near[REACH : REACH + lat_rows]
    basis_own = basis_near[REACH : REACH + lat_rows]
    own_rows = row_start + jnp.arange(lat_rows)
    inside = (own_rows[:, None] + lat_own >= 0) & (own_rows[:, None] + lat_own < lat_total)
    row_grid = jnp.arange(lat_rows)[:, None, None]
    col_grid = jnp.arange(lon_cols)[None, :, None]
    source = (row_grid + REACH + lat_own[:, None, :]) * pad_cols + (
        col_grid + REACH + lon_own[:, None, :]
    )
    tap_weight = jnp.where(inside[:, None, :, None], basis_own[:, None, :, :], 0.0)
    tap_weight = jnp.broadcast_to(tap_weight, (lat_rows, lon_cols, TAPS, BASIS))
    picker = (source[..., None] == jnp.arange(pad_rows * pad_cols)).astype(jnp.float32)
    forward_map = jnp.einsum("ijkb,ijks->bijs", tap_weight, picker, precision=lax.Precision.HIGHEST)
    forward_map = forward_map.reshape(BASIS, lat_rows * lon_cols, pad_rows * pad_cols)
    near_rows = row_start - REACH + jnp.arange(pad_rows)
    real_row = (near_rows >= 0) & (near_rows < lat_total)
    pad_row_grid = jnp.arange(pad_rows)[:, None, None]
    pad_col_grid = jnp.arange(pad_cols)[None, :, None]
    target_row = pad_row_grid - REACH + lat_near[:, None, :]
    target_col = pad_col_grid - REACH + lon_near[:, None, :]
    landed = (
        (target_row >= 0)
        & (target_row < lat_rows)
        & (target_col >= 0)
        & (target_col < lon_cols)
        & real_row[:, None, None]
    )
    target = target_row * lon_cols + target_col
    back_weight = jnp.where(landed[..., None], basis_near[:, None, :, :], 0.0)
    catcher = (target[..., None] == jnp.arange(lat_rows * lon_cols)).astype(jnp.float32)
    backward_map = jnp.einsum(
        "pqkb,pqkt->btpq", back_weight, catcher, precision=lax.Precision.HIGHEST
    )
    backward_map = backward_map.reshape(BASIS, lat_rows * lon_cols, pad_rows * pad_cols)
    return (forward_map, backward_map)


def per_device(inputs, cotangent, weights, basis_values, lat_step, lon_step):
    members, lat_rows, lon_cols, channels = inputs.shape
    pad_rows = lat_rows + 2 * REACH
    pad_cols = lon_cols + 2 * REACH
    cells = lat_rows * lon_cols
    lat_index = lax.axis_index("lat")
    lat_total = lat_rows * lax.axis_size("lat")
    segment_index = lax.axis_index("segment")
    depth = lax.axis_size("segment")
    grad_scale = 1.0 / math.sqrt(members * lat_total * lon_cols * lax.axis_size("lon"))
    forward_map, backward_map = build_tables(
        basis_values, lat_step, lon_step, lat_rows, lon_cols, lat_index, lat_total
    )
    kernel = weights[0]
    keep_spread = jnp.zeros((BASIS, members, cells, channels), jnp.bfloat16)
    keep_mixed = jnp.zeros((members, cells, channels), jnp.float32)
    keep_gate = jnp.zeros((members, cells, channels), jnp.bfloat16)
    section_out = jnp.zeros(inputs.shape, jnp.bfloat16)
    section_grad = jnp.zeros(inputs.shape, jnp.bfloat16)
    carry = inputs
    for tick_num in range(depth):
        layer_count = carry.shape[0]
        layer_padded = (
            widen(carry).reshape(layer_count, pad_rows * pad_cols, channels).astype(jnp.float32)
        )
        spread = jnp.einsum(
            "bts,msc->bmtc", forward_map, layer_padded, precision=lax.Precision.HIGHEST
        ).astype(jnp.bfloat16)
        layer_mixed = jnp.einsum(
            "bmtc,bcd->mtd", spread, kernel, preferred_element_type=jnp.float32
        )
        result = (
            carry.reshape(layer_count, cells, channels).astype(jnp.float32)
            + jax.nn.silu(layer_mixed)
        ).astype(jnp.bfloat16)
        spread, mixed, result = (spread, layer_mixed, result.reshape(carry.shape))
        here = segment_index == tick_num
        keep_spread = jnp.where(here, spread, keep_spread)
        keep_mixed = jnp.where(here, mixed, keep_mixed)
        section_out = jnp.where(here, result, section_out)
        if tick_num + 1 < depth:
            carry = pass_ahead(result)
    grad = cotangent
    for tick_num in range(depth):
        count = grad.shape[0]
        flat_grad = grad.reshape(count, cells, channels).astype(jnp.float32)
        sigma = jax.nn.sigmoid(keep_mixed)
        gate_grad = (flat_grad * sigma * (1.0 + keep_mixed * (1.0 - sigma))).astype(jnp.bfloat16)
        feature_grad = jnp.einsum(
            "mtd,bcd->bmtc", gate_grad, kernel, preferred_element_type=jnp.float32
        ).astype(jnp.bfloat16)
        padded = widen(feature_grad.reshape(BASIS * count, lat_rows, lon_cols, channels))
        padded = padded.reshape(BASIS, count, pad_rows * pad_cols, channels).astype(jnp.float32)
        pulled = jnp.einsum("bts,bmsc->mtc", backward_map, padded, precision=lax.Precision.HIGHEST)
        new_grad = (flat_grad + pulled).astype(jnp.bfloat16).reshape(grad.shape)
        gate_grad, new_grad = (gate_grad, new_grad)
        here = segment_index == depth - 1 - tick_num
        keep_gate = jnp.where(here, gate_grad, keep_gate)
        section_grad = jnp.where(here, new_grad, section_grad)
        if tick_num + 1 < depth:
            grad = pass_behind(new_grad)
    local_grad = (
        jnp.einsum("bmtc,mtd->bcd", keep_spread, keep_gate, preferred_element_type=jnp.float32)
        * grad_scale
    )
    owners = lax.axis_size("lon") * lax.axis_size("lat")
    grad_rows = local_grad.reshape(owners, -1)
    weight_grad = lax.psum_scatter(grad_rows, ("lon", "lat"), scatter_dimension=0, tiled=True)
    return (section_out[None], section_grad[None], weight_grad)


HALO = 8
BAND = 8


def swap(axis, bit):
    return [(i, i ^ bit) for i in range(lax.axis_size(axis))]


def window_plan(lat_rows):
    first = [(a, min(max(a - 4, -HALO), lat_rows + HALO - 16)) for a in range(-HALO, lat_rows + HALO, BAND)]
    second = [(a, a - 4) for a in range(-4, lat_rows + 4, BAND)]
    return first, second


def dot(a, b):
    return jnp.dot(a, b, preferred_element_type=jnp.float32)


def dot_nt(a, b):
    return lax.dot_general(a, b, (((1,), (1,)), ((), ())), preferred_element_type=jnp.float32)


def dot_tn(a, b):
    return lax.dot_general(a, b, (((0,), (0,)), ((), ())), preferred_element_type=jnp.float32)


def make_steps(lat_rows, lon_cols, blocks, members, channels, lat_devices):
    first, second = window_plan(lat_rows)
    nf, ns = len(first), len(second)
    lat_total = lat_rows * lat_devices
    ring = lon_cols * blocks
    band = BAND * lon_cols
    cells = blocks * band
    win = 16 * lon_cols
    own = lat_rows * lon_cols
    edge = HALO * lon_cols
    half_edge = edge // 2
    width = BASIS * channels
    lanes = 128
    pieces = channels // lanes
    halo = edge + half_edge
    state_parts = ((0, edge, 2 * own), (edge, own, 0), (edge + own, edge, 2 * own + halo))
    coming_parts = (
        (0, half_edge, 2 * own + edge),
        (half_edge, own, own),
        (half_edge + own, half_edge, 2 * own + halo + edge),
    )

    def take(blks, m, parts, low, high):
        found = []
        for r in blks:
            for start, size, at in parts:
                lo, hi = max(low, start), min(high, start + size)
                if lo < hi:
                    found.append(r[m, at + lo - start : at + hi - start, :])
        return jnp.concatenate(found, axis=0)

    def prep(idx, x, c, w, both, tail, head, half, sem):
        rows = half.shape[0]
        start = pl.multiple_of(idx[1] % 2 * rows, rows)
        copy = pltpu.make_async_copy(w.at[pl.ds(start, rows), :], half, sem)
        copy.start()
        for m in range(members):
            state = x[m].reshape(own, channels)
            coming = c[m].reshape(own, channels)
            both[m, :own, :] = state
            both[m, own:, :] = coming
            tail[m, :edge, :] = state[own - edge :]
            tail[m, edge:, :] = coming[own - half_edge :]
            head[m, :edge, :] = state[:edge]
            head[m, edge:, :] = coming[:half_edge]
        copy.wait()

    def maps(idx, lat_step, lon_step, basis, forward, again, backward, tab):
        lon, lat = idx[1], idx[2]
        base = lat * lat_rows
        tab[...] = jnp.zeros(tab.shape, jnp.float32)
        tab[0:TAPS, :] = lat_step[...].astype(jnp.float32)
        tab[TAPS : 2 * TAPS, :] = lon_step[...].astype(jnp.float32)
        for k in range(TAPS):
            tab[2 * TAPS + k * BASIS : 2 * TAPS + (k + 1) * BASIS, :] = basis[k]
        table = tab[...].astype(jnp.bfloat16)
        source = lax.broadcasted_iota(jnp.int32, (tab.shape[1], cells), 0)
        lane = lax.broadcasted_iota(jnp.int32, (1, cells), 1)
        block, rest = lane // band, lane % band
        row_in, col_in = rest // lon_cols, rest % lon_cols
        column_home = (block ^ lon) * lon_cols + col_in
        piece = 64
        spot = lax.broadcasted_iota(jnp.int32, (piece, cells), 0)
        for i, (a, start) in enumerate(first + second):
            row = row_in + (base + a)
            got = dot(table, (source == row).astype(jnp.bfloat16))
            step_lat = got[0:TAPS].astype(jnp.int32)
            step_lon = got[TAPS : 2 * TAPS].astype(jnp.int32)
            target = row + step_lat
            inside = (row >= 0) & (row < lat_total) & (target >= 0) & (target < lat_total)
            column = column_home + step_lon
            column = jnp.where(column < 0, column + ring, column)
            column = jnp.where(column >= ring, column - ring, column)
            local = target - (base + start)
            place = ((column // lon_cols) ^ lon) * win + local * lon_cols + column % lon_cols
            place = jnp.where(inside, place, -1)
            for p in range(0, blocks * win, piece):
                tables = [jnp.zeros((piece, cells), jnp.float32) for _ in range(BASIS)]
                for k in range(TAPS):
                    hit = spot == place[k : k + 1] - p
                    for b in range(BASIS):
                        at = 2 * TAPS + k * BASIS + b
                        tables[b] = tables[b] + jnp.where(hit, got[at : at + 1], 0.0)
                for b in range(BASIS):
                    span = slice(b * cells, (b + 1) * cells)
                    if i < nf:
                        forward[i, span, p : p + piece] = tables[b].T.astype(jnp.bfloat16)
                    else:
                        again[i - nf, span, p : p + piece] = tables[b].T.astype(jnp.bfloat16)
                        backward[i - nf, p : p + piece, span] = tables[b].astype(jnp.bfloat16)

    def put_spread(got, into, at):
        for b in range(BASIS):
            into[at : at + cells, b * channels : (b + 1) * channels] = got[b * cells : (b + 1) * cells]

    def spread(blk, forward, into):
        for m in range(members):
            for g, (a, start) in enumerate(first):
                o = (start + HALO) * lon_cols
                near = take(blk, m, state_parts, o, o + win)
                put_spread(dot(forward[g], near).astype(jnp.bfloat16), into, (m * nf + g) * cells)

    def first_section(blk, w, s0, s1, again, mid, slope):
        for m in range(members):
            total = dot(s0[m * nf * cells : (m + 1) * nf * cells, :], w[...])
            for g in range(nf):
                mixed = total[g * cells : (g + 1) * cells]
                sigma = jax.nn.sigmoid(mixed)
                here = take(blk, m, state_parts, g * band, (g + 1) * band)
                value = (here.astype(jnp.float32) + mixed * sigma).astype(jnp.bfloat16)
                mid[m, :, g * band : (g + 1) * band, :] = value.reshape(blocks, band, channels)
                if slope is not None:
                    tilt = (sigma * (1.0 + mixed * (1.0 - sigma))).astype(slope.dtype).reshape(blocks, band, channels)
                    low, high = max(g * band, half_edge), min((g + 1) * band, 3 * half_edge + own)
                    slope[m, :, low - half_edge : high - half_edge, :] = tilt[:, low - g * band : high - g * band]
            for g in range(ns):
                near = mid[m, :, g * band : g * band + win, :].reshape(blocks * win, channels)
                put_spread(dot(again[g], near).astype(jnp.bfloat16), s1, (m * ns + g) * cells)

    def columns_of(lon):
        return pl.ds(pl.multiple_of(lon * (width // blocks), 128), width // blocks)

    def early(idx, b0, b1, b2, b3, w_own, forward, again, s, left, slope, out, s0, mid):
        blk = (b0, b1, b2, b3)

        @pl.when(idx[0] == 0)
        def _():
            spread(blk, forward, s0)
            first_section(blk, w_own, s0, s, again, mid, slope)
            for m in range(members):
                size = (nf - 2) * cells
                left[m * size : (m + 1) * size, :] = s0[(m * nf + 1) * cells : (m * nf + nf - 1) * cells, columns_of(idx[1])]
                out[m, :, :] = mid[m, 0, edge : edge + own, :]

        @pl.when(idx[0] == 1)
        def _():
            spread(blk, forward, s)

    def own_part(g):
        return max(g * band, half_edge), min((g + 1) * band, half_edge + own)

    def apply_back(w, gates, feat):
        for b in range(BASIS):
            got = dot_nt(gates[...], w[b * channels : (b + 1) * channels, :]).astype(jnp.bfloat16)
            for i in range(members * ns):
                feat[(i * BASIS + b) * cells : (i * BASIS + b + 1) * cells, :] = got[i * cells : (i + 1) * cells]

    def chain(idx, b0, b1, b2, b3, w_own, w_a, w_b, again, backward, s, left0, slope, early_out,
              out_ref, next_ref, gate_ref, own_ref, p1, p2, p3, w, s1, mid, gates, feat, pull, grads):
        blk = (b0, b1, b2, b3)
        seg, lon, lat = idx[0], idx[1], idx[2]
        half = w_a.shape[0]
        core = lon % 2
        w[pl.ds(pl.multiple_of(core * half, half), half), :] = w_a[...]
        w[pl.ds(pl.multiple_of((1 - core) * half, half), half), :] = w_b[...]

        def coming_at(m, g):
            return take(blk, m, coming_parts, g * band, (g + 1) * band).astype(jnp.float32)

        def second_section(weight, spread_ref, into, last):
            for m in range(members):
                total = dot(spread_ref[m * ns * cells : (m + 1) * ns * cells, :], weight[...])
                for g in range(ns):
                    at = (m * ns + g) * cells
                    mixed = total[g * cells : (g + 1) * cells]
                    sigma = jax.nn.sigmoid(mixed)
                    into[at : at + cells, :] = (coming_at(m, g) * sigma * (1.0 + mixed * (1.0 - sigma))).astype(jnp.bfloat16)
                    if last:
                        low, high = own_part(g)
                        base = mid[m, 0, half_edge + low : half_edge + high, :]
                        local = slice(low - g * band, high - g * band)
                        base = (base.astype(jnp.float32) + mixed[local] * sigma[local]).astype(jnp.bfloat16)
                        out_ref[m, low - half_edge : high - half_edge, :] = base

        def store_grads(left, right):
            got = dot_tn(left, jnp.concatenate(right, axis=0))
            for c in range(pieces):
                grads[pl.ds(c, width // blocks, stride=pieces), :] = got[:, c * lanes : (c + 1) * lanes]

        @pl.when(seg == 0)
        def _():
            second_section(w, s, gates, False)
            out_ref[...] = early_out[...]
            apply_back(w, gates, feat)
            for m in range(members):
                for g in range(ns):
                    at = (m * ns + g) * cells * BASIS
                    got = dot(backward[g], feat[at : at + BASIS * cells, :]).reshape(blocks, win, channels)
                    if g == 0:
                        pull[m, :, :win, :] = got
                    else:
                        pull[m, :, g * band : (g + 1) * band, :] += got[:, :band]
                        pull[m, :, (g + 1) * band : g * band + win, :] = got[:, band:]
            right = []
            step = half_edge
            for m in range(members):
                for g in range(ns):
                    at = (m * ns + g) * cells
                    span = slice(half_edge + g * band, half_edge + (g + 1) * band)
                    value = (coming_at(m, g) + pull[m, :, span, :].reshape(cells, channels)).astype(jnp.bfloat16)
                    low, high = own_part(g)
                    next_ref[m, low - half_edge : high - half_edge, :] = value[low - g * band : high - g * band]
                    tilt = slope[m, :, g * band : (g + 1) * band, :].reshape(cells, channels)
                    gate_ref[at : at + cells, :] = (value.astype(jnp.float32) * tilt).astype(jnp.bfloat16)
                for g in range(1, nf - 1):
                    for q in range(blocks):
                        for o in range(0, band, step):
                            spot = half_edge + (g - 1) * band + o
                            turn, rest = spot // band, spot % band
                            at = (m * ns + turn) * cells + q * band + rest
                            right.append(gate_ref[at : at + step, :])
            store_grads(left0[...], right)

        @pl.when(seg == 1)
        def _():
            first_section(blk, w, s, s1, again, mid, None)
            second_section(w_own, s1, gate_ref, True)
            left, right = [], []
            for m in range(members):
                next_ref[m, :, :] = b0[m, own : 2 * own, :]
                for g in range(ns):
                    low, high = own_part(g)
                    for q in range(blocks):
                        at = (m * ns + g) * cells + q * band - g * band
                        left.append(s1[at + low : at + high, columns_of(lon)])
                        right.append(gate_ref[at + low : at + high, :])
            store_grads(jnp.concatenate(left, axis=0), right)

        share = width // blocks // lat_devices * pieces

        def rows_of(index):
            return grads[pl.ds(pl.multiple_of(index * share, share), share), :]

        own_ref[...] = rows_of(lat)
        for bit, ref in ((1, p1), (2, p2), (3, p3)):
            ref[...] = rows_of(lat ^ bit).astype(jnp.bfloat16)

    def finish(w_own, backward, gates, next_ref, last_ref, grad_ref, out_ref, feat, pull):
        apply_back(w_own, gates, feat)
        for m in range(members):
            for g in range(ns):
                at = (m * ns + g) * cells * BASIS
                got = dot(backward[g, 0:win, :], feat[at : at + BASIS * cells, :])
                if g == 0:
                    pull[m, :win, :] = got
                else:
                    pull[m, g * band : (g + 1) * band, :] += got[:band]
                    pull[m, (g + 1) * band : g * band + win, :] = got[band:]
            total = next_ref[m].astype(jnp.float32) + pull[m, edge : edge + own, :]
            grad_ref[m] = total.astype(jnp.bfloat16).reshape(lat_rows, lon_cols, channels)
            out_ref[m] = last_ref[m].reshape(lat_rows, lon_cols, channels)

    return prep, maps, early, chain, finish


def add_up(scale, mine, p1, p2, p3, out):
    out[...] = (mine[...] + p1[...].astype(jnp.float32) + p2[...].astype(jnp.float32) + p3[...].astype(jnp.float32)) * scale


def whole_ring(inputs, cotangent, weights, basis_values, lat_step, lon_step):
    members, lat_rows, lon_cols, channels = inputs.shape
    blocks = lax.axis_size("lon")
    lat_devices = lax.axis_size("lat")
    lat_total = lat_rows * lat_devices
    grad_scale = 1.0 / math.sqrt(members * lat_total * lon_cols * blocks)
    own = lat_rows * lon_cols
    edge = HALO * lon_cols
    half_edge = edge // 2
    halo = edge + half_edge
    width = BASIS * channels
    half_type, full_type = jnp.bfloat16, jnp.float32
    shape = jax.ShapeDtypeStruct
    first, second = window_plan(lat_rows)
    nf, ns = len(first), len(second)
    cells = blocks * BAND * lon_cols
    win = 16 * lon_cols
    vmem = pl.BlockSpec(memory_space=pltpu.VMEM)
    smem = pl.BlockSpec(memory_space=pltpu.SMEM)
    anywhere = pl.BlockSpec(memory_space=pltpu.HBM)

    def call(body, name, outs, ins, mib, gflops, scratch=(), far=()):
        return pl.pallas_call(
            body,
            out_shape=outs,
            in_specs=[smem if a.ndim == 1 else anywhere if i in far else vmem for i, a in enumerate(ins)],
            out_specs=(vmem,) * len(outs),
            scratch_shapes=list(scratch),
            compiler_params=pltpu.CompilerParams(vmem_limit_bytes=mib * 1024 * 1024),
            cost_estimate=pl.CostEstimate(flops=int(gflops * 1e9), bytes_accessed=4_000_000, transcendentals=0),
            name=name,
        )(*ins)

    prep, maps, early, chain, finish = make_steps(lat_rows, lon_cols, blocks, members, channels, lat_devices)
    idx = jnp.stack([lax.axis_index("segment"), lax.axis_index("lon"), lax.axis_index("lat")]).astype(jnp.int32)
    kernel = weights.reshape(width, channels)
    both, tail, head, half = call(
        prep,
        "prep",
        (
            shape((members, 2 * own, channels), half_type),
            shape((members, halo, channels), half_type),
            shape((members, halo, channels), half_type),
            shape((width // 2, channels), half_type),
        ),
        (idx, inputs, cotangent, kernel),
        4,
        0.5,
        (pltpu.SemaphoreType.DMA,),
        (3,),
    )
    up = [(i, i + 1) for i in range(lat_devices - 1)]
    down = [(i + 1, i) for i in range(lat_devices - 1)]
    near_half = lax.ppermute(half, "segment", swap("segment", 1))
    both_y = lax.ppermute(both, "lon", swap("lon", 2))
    before = lax.ppermute(tail, "lat", up)
    after = lax.ppermute(head, "lat", down)
    sides = jnp.concatenate([before, after], axis=1)
    sides_y = lax.ppermute(sides, "lon", swap("lon", 2))
    b0 = jnp.concatenate([both, sides], axis=1)
    b1 = lax.ppermute(b0, "lon", swap("lon", 1))
    forward, again, backward = call(
        maps,
        "maps",
        (
            shape((nf, BASIS * cells, blocks * win), half_type),
            shape((ns, BASIS * cells, blocks * win), half_type),
            shape((ns, blocks * win, BASIS * cells), half_type),
        ),
        (idx, lat_step.T, lon_step.T, jnp.transpose(basis_values, (1, 2, 0))),
        4,
        3.0,
        (pltpu.VMEM((48, lat_total), full_type),),
    )
    b2 = jnp.concatenate([both_y, sides_y], axis=1)
    b2, forward = lax.optimization_barrier((b2, forward))
    b3 = lax.ppermute(b2, "lon", swap("lon", 1))
    far_half = lax.ppermute(near_half, "lon", swap("lon", 1))
    s_type = (members * nf * cells, width)
    s, left, slope, early_out = call(
        early,
        "early",
        (
            shape(s_type, half_type),
            shape((members * (nf - 2) * cells, width // blocks), half_type),
            shape((members, blocks, own + edge, channels), half_type),
            shape((members, own, channels), half_type),
        ),
        (idx, b0, b1, b2, b3, kernel, forward, again),
        12,
        3.0,
        (pltpu.VMEM(s_type, half_type), pltpu.VMEM((members, blocks, own + 2 * edge, channels), half_type)),
    )
    lines = (width // blocks // lat_devices * channels // 128, 128)
    out, follow, gates, mine, *parts = call(
        chain,
        "chain",
        (
            shape((members, own, channels), half_type),
            shape((members, own, channels), half_type),
            shape((members * ns * cells, channels), half_type),
            shape(lines, full_type),
        )
        + (shape(lines, half_type),) * 3,
        (idx, b0, b1, b2, b3, kernel, near_half, far_half, again, backward, s, left, slope, early_out),
        18,
        6.0,
        (
            pltpu.VMEM((width, channels), half_type),
            pltpu.VMEM((members * ns * cells, width), half_type),
            pltpu.VMEM((members, blocks, own + 2 * edge, channels), half_type),
            pltpu.VMEM((members * ns * cells, channels), half_type),
            pltpu.VMEM((members * ns * cells * BASIS, channels), half_type),
            pltpu.VMEM((members, blocks, own + 2 * edge, channels), full_type),
            pltpu.VMEM((width // blocks * channels // 128, 128), full_type),
        ),
    )
    got = [lax.ppermute(part, "lat", swap("lat", bit)) for bit, part in zip((1, 2, 3), parts)]
    block = (members, lat_rows, lon_cols, channels)
    grad, out = call(
        finish,
        "finish",
        (shape(block, half_type),) * 2,
        (kernel, backward, gates, follow, out),
        10,
        2.0,
        (
            pltpu.VMEM((members * ns * cells * BASIS, channels), half_type),
            pltpu.VMEM((members, own + 2 * edge, channels), full_type),
        ),
    )
    (total,) = call(functools.partial(add_up, grad_scale), "add_up", (shape(lines, full_type),), (mine, *got), 2, 0.1)
    return (out[None], grad[None], total.reshape(1, lines[0] * lines[1]))


def fits_ring(mesh, inputs):
    sizes = dict(mesh.shape)
    rows, cols = inputs.shape[1] // sizes["lat"], inputs.shape[2] // sizes["lon"]
    return sizes["segment"] == 2 and sizes["lon"] == 4 and sizes["lat"] == 4 and rows == 16 and cols == 4


def solution(mesh):
    def apply(*args):
        body = whole_ring if fits_ring(mesh, args[0]) else per_device
        return jax.shard_map(
            body,
            mesh=mesh,
            in_specs=(
                P(None, "lat", "lon", None),
                P(None, "lat", "lon", None),
                P("segment", None, None, None),
                P(),
                P(),
                P(),
            ),
            out_specs=(
                P("segment", None, "lat", "lon", None),
                P("segment", None, "lat", "lon", None),
                P("segment", ("lon", "lat")),
            ),
            check_vma=False,
        )(*args)

    return apply
```

time: 76.3 us -> 51.8 us (0.68)
  local copies, waits for them, and re-layouts: 12.9 us -> 5.37 us
  starting transfers between devices: 21.8 us -> 15.2 us
  waiting for transfers between devices: 16.3 us -> 12.6 us
  Pallas kernels: 20.7 us -> 17.4 us
  other arithmetic: 2.81 us -> 0.12 us
    ppermute x10 -> x6, waiting for transfers between devices: 11.4 us -> 3.13 us  [the longest x1 1.79 us: whole_ring(): b3 = lax.ppermute(b2, 'lon', swap('lon', 1))]
    ppermute x10 -> x6, starting transfers between devices: 14.4 us -> 7.06 us  [the longest x1 3.47 us: whole_ring(): before = lax.ppermute(tail, 'lat', up)]
    ppermute x1, waiting for transfers between devices: 0.01 us -> 3.87 us  [whole_ring(): near_half = lax.ppermute(half, 'segment', swap('segment', 1))]
    pallas_call x5 -> x6, Pallas kernels: 20.7 us -> 17.4 us  [call(): pl.pallas_call(body, out_shape=outs, in_specs=[smem if a.ndim == 1 else a...]
    reshape x5 -> x0, local copies, waits for them, and re-layouts: 2.37 us -> none  [the longest x1 0.94 us: whole_ring(): state = inputs.reshape(members, own, channels)]
    dynamic_slice x1 -> x0, local copies, waits for them, and re-layouts: 2.13 us -> none  [whole_ring(): lax.dynamic_slice_in_dim(kernel, lon_index % 2 * (width // 2), width // 2...]
    mul x2 -> x0, other arithmetic: 1.66 us -> none  [the longest x1 1.65 us: whole_ring(): weight_grad = (total * grad_scale).reshape(1, share * channels)]
    another operation x18 -> x0, local copies, waits for them, and re-layouts: 1.34 us -> none  [tap_tables(): jnp.stack([table[a + HALO:a + HALO + BAND] for a, _ in plan])]
  transfers between devices with their start and end apart: 15 -> 11, of which waited for: 3 -> 4; matrix products, arithmetic and copies ran while one was open for 7% -> 0% of each run, Pallas kernels for 19% -> 22%
where the time goes in v3:
time: 51.8 us; the launch traced here: 51.5 us
  Pallas kernels  17.4 us (34%)
  starting transfers between devices  15.2 us (29%)
  waiting for transfers between devices  12.6 us (24%)
  local copies, waits for them, and re-layouts  5.37 us (10%)
  between operations  0.76 us (1%)
    pallas_call x6, Pallas kernels, call(): pl.pallas_call(body, out_shape=outs, in_specs=[smem if a.ndim == 1 else a...  17.4 us
    ppermute x3, waiting for transfers between devices, whole_ring(): lax.ppermute(part, 'lat', swap('lat', bit))  5.62 us
    unnamed x16, local copies, waits for them, and re-layouts  5.36 us
    ppermute x3, starting transfers between devices, whole_ring(): lax.ppermute(part, 'lat', swap('lat', bit))  5.16 us
    ppermute x1, waiting for transfers between devices, whole_ring(): near_half = lax.ppermute(half, 'segment', swap('segment', 1))  3.87 us
    ppermute x1, starting transfers between devices, whole_ring(): before = lax.ppermute(tail, 'lat', up)  3.47 us
    ppermute x1, starting transfers between devices, whole_ring(): near_half = lax.ppermute(half, 'segment', swap('segment', 1))  3 us
    ppermute x1, waiting for transfers between devices, whole_ring(): b3 = lax.ppermute(b2, 'lon', swap('lon', 1))  1.79 us
  transfers between devices with their start and end apart: 11, of which 4 were waited for; matrix products, arithmetic and copies ran while one was open for 0% of the time, Pallas kernels for 22%

profile of v3, /device:TPU:0, one launch (start us, length us, event | category | flops | bytes accessed | tf_op | source)
XLA Modules:
  0.0 51.5 jit_solution(11166791251271019896)
XLA Ops:
  0.6 0.1 pad_add_fusion.idx
  0.7 0.0 copy-start
  0.7 1.4 %copy-done = bf16[1,3,512,512]{3,2,1,0:T(8,128)(2,1)S(1)} copy-done((bf16[1,3,512,512]{3,2,1,0:T(8,128)(2,1)S(1)}, bf16[1,3,512,512]{3,2,1,0:T(8,128)(2,1)}, u32[]{:S(2)}) %copy-start) | copy-done | bytes 1572888
  2.1 0.0 copy-start.2
  2.1 0.9 %copy-done.2 = bf16[2,16,4,512]{3,2,1,0:T(4,128)(2,1)S(1)} copy-done((bf16[2,16,4,512]{3,2,1,0:T(4,128)(2,1)S(1)}, bf16[2,16,4,512]{3,2,1,0:T(4,128)(2,1)}, u32[]{:S(2)}) %copy-start.2) | copy-done | bytes 131096
  3.0 0.0 copy-start.3
  3.0 0.9 %copy-done.3 = bf16[2,16,4,512]{3,2,1,0:T(4,128)(2,1)S(1)} copy-done((bf16[2,16,4,512]{3,2,1,0:T(4,128)(2,1)S(1)}, bf16[2,16,4,512]{3,2,1,0:T(4,128)(2,1)}, u32[]{:S(2)}) %copy-start.3) | copy-done | bytes 131096
  3.9 0.7 %prep.1 = (bf16[2,128,512]{2,1,0:T(8,128)(2,1)S(1)}, bf16[2,48,512]{2,1,0:T(8,128)(2,1)S(1)}, bf16[2,48,512]{2,1,0:T(8,128)(2,1)S(1)}, bf16[768,512]{1,0:T(8,128)(2,1)S(1)}) custom-call(s32[3]{0:T(128)S(1)} %pad_add_fusion.idx, bf16[2,16,4,512]{3,2,1,0:T(4,128)(2,1)S(1)} %copy-done.2, bf16[2,16,4,512]{3,2,1,0:T(4,128)(2,1)S(1)} %copy-done.3, ...), custom_call_target="tpu_custom_call" | custom-call | flops 500000000 | bytes 4000000 | tf_op jit(solution)/shard_map/prep/pallas_call | solution.py:473
  4.6 3.0 %collective-permute-start.6 = (bf16[768,512]{1,0:T(8,128)(2,1)S(1)}, bf16[768,512]{1,0:T(8,128)(2,1)S(1)}, u32[]{:S(2)}, u32[]{:S(2)}) collective-permute-start(bf16[768,512]{1,0:T(8,128)(2,1)S(1)} %get-tuple-element.31), channel_id=1, source_target_pairs={{0,1},{1,0},{2,3},{3,2},{4,5},{5,4},{6,7},{7,6},{8,9},{9,8},{10,11... | collective-permute-start | bytes 2359304 | tf_op jit(solution)/shard_map/ppermute | solution.py:504
  7.6 3.5 %collective-permute-start = (bf16[2,48,512]{2,1,0:T(8,128)(2,1)S(1)}, bf16[2,48,512]{2,1,0:T(8,128)(2,1)S(1)}, u32[]{:S(2)}, u32[]{:S(2)}) collective-permute-start(bf16[2,48,512]{2,1,0:T(8,128)(2,1)S(1)} %get-tuple-element.27), channel_id=1, source_target_pairs={{0,2},{2,4},{4,6},{1,3},{3,5},{5,7},{8,10},{10,12},{12,14},{9,11},... | collective-permute-start | bytes 294920 | tf_op jit(solution)/shard_map/ppermute | solution.py:506
  11.1 1.3 %collective-permute-start.1 = (bf16[2,48,512]{2,1,0:T(8,128)(2,1)S(1)}, bf16[2,48,512]{2,1,0:T(8,128)(2,1)S(1)}, u32[]{:S(2)}, u32[]{:S(2)}) collective-permute-start(bf16[2,48,512]{2,1,0:T(8,128)(2,1)S(1)} %get-tuple-element.28), channel_id=1, source_target_pairs={{2,0},{4,2},{6,4},{3,1},{5,3},{7,5},{10,8},{12,10},{14,12},{11,9},... | collective-permute-start | bytes 294920 | tf_op jit(solution)/shard_map/ppermute | solution.py:507
  12.4 1.6 %collective-permute-start.3 = (bf16[2,128,512]{2,1,0:T(8,128)(2,1)S(1)}, bf16[2,128,512]{2,1,0:T(8,128)(2,1)S(1)}, u32[]{:S(2)}, u32[]{:S(2)}) collective-permute-start(bf16[2,128,512]{2,1,0:T(8,128)(2,1)S(1)} %get-tuple-element.26), channel_id=1, source_target_pairs={{0,16},{8,24},{16,0},{24,8},{1,17},{9,25},{17,1},{25,9},{2,18},{10... | collective-permute-start | bytes 786440 | tf_op jit(solution)/shard_map/ppermute | solution.py:505
  14.0 0.0 copy-start.4
  14.0 0.7 %copy-done.4 = f32[64,9,3]{0,2,1:T(4,128)S(1)} copy-done((f32[64,9,3]{0,2,1:T(4,128)S(1)}, f32[64,9,3]{0,2,1:T(4,128)}, u32[]{:S(2)}) %copy-start.4) | copy-done | bytes 6936
  14.7 0.0 copy-start.5
  14.7 0.7 %copy-done.5 = s32[64,9]{0,1:T(8,128)S(1)} copy-done((s32[64,9]{0,1:T(8,128)S(1)}, s32[64,9]{0,1:T(8,128)}, u32[]{:S(2)}) %copy-start.5) | copy-done | bytes 2328
  15.4 0.0 copy-start.6
  15.4 0.7 %copy-done.6 = s32[64,9]{0,1:T(8,128)S(1)} copy-done((s32[64,9]{0,1:T(8,128)S(1)}, s32[64,9]{0,1:T(8,128)}, u32[]{:S(2)}) %copy-start.6) | copy-done | bytes 2328
  16.1 0.0 copy-start.1
  16.1 4.4 %maps.1 = (bf16[4,384,256]{2,1,0:T(8,128)(2,1)S(1)}, bf16[3,384,256]{2,1,0:T(8,128)(2,1)S(1)}, bf16[3,256,384]{2,1,0:T(8,128)(2,1)S(1)}) custom-call(s32[3]{0:T(128)S(1)} %pad_add_fusion.idx, s32[9,64]{1,0:T(8,128)S(1)} %bitcast.15, s32[9,64]{1,0:T(8,128)S(1)} %bitcast.16, f32[9,3,64]{2,1,0:T(4,128)S(1)} %bitcast.14), custom_call_target="tpu_custom_call" | custom-call | flops 3000000000 | bytes 4000000 | tf_op jit(solution)/shard_map/maps/pallas_call | solution.py:473
  20.6 0.0 collective-permute-done
  20.6 0.0 collective-permute-done.1
  20.6 0.6 %collective-permute-start.4 = (bf16[2,96,512]{2,1,0:T(8,128)(2,1)S(1)}, bf16[2,96,512]{2,1,0:T(8,128)(2,1)S(1)}, u32[]{:S(2)}, u32[]{:S(2)}) collective-permute-start(bf16[2,96,512]{2,1,0:T(8,128)(2,1)S(1)} %pad_maximum_fusion.1), channel_id=1, source_target_pairs={{0,16},{8,24},{16,0},{24,8},{1,17},{9,25},{17,1},{25,9},{2,18},{10... | collective-permute-start | bytes 589832 | tf_op jit(solution)/shard_map/ppermute | solution.py:509
  21.2 0.1 collective-permute-start.2
  21.3 3.9 %collective-permute-done.6.w_a = bf16[768,512]{1,0:T(8,128)(2,1)S(1)} collective-permute-done((bf16[768,512]{1,0:T(8,128)(2,1)S(1)}, bf16[768,512]{1,0:T(8,128)(2,1)S(1)}, u32[]{:S(2)}, u32[]{:S(2)}) %collective-permute-start.6) | collective-permute-done | bytes 786464 | tf_op jit(solution)/shard_map/ppermute | solution.py:504
  25.1 0.0 collective-permute-start.7
  25.1 0.0 collective-permute-done.3
  25.1 1.3 %collective-permute-done.4 = bf16[2,96,512]{2,1,0:T(8,128)(2,1)S(1)} collective-permute-done((bf16[2,96,512]{2,1,0:T(8,128)(2,1)S(1)}, bf16[2,96,512]{2,1,0:T(8,128)(2,1)S(1)}, u32[]{:S(2)}, u32[]{:S(2)}) %collective-permute-start.4) | collective-permute-done | bytes 196640 | tf_op jit(solution)/shard_map/ppermute | solution.py:509
  26.5 0.1 collective-permute-start.5
  26.6 0.0 collective-permute-done.2.b1
  26.6 1.8 %collective-permute-done.5.b3 = bf16[2,224,512]{2,1,0:T(8,128)(2,1)S(1)} collective-permute-done((bf16[2,224,512]{2,1,0:T(8,128)(2,1)S(1)}, bf16[2,224,512]{2,1,0:T(8,128)(2,1)S(1)}, u32[]{:S(2)}, u32[]{:S(2)}) %collective-permute-start.5) | collective-permute-done | bytes 458784 | tf_op jit(solution)/shard_map/ppermute | solution.py:527
  28.4 0.0 copy-done.1
  28.4 4.3 %early.1 = (bf16[1024,1536]{1,0:T(8,128)(2,1)S(1)}, bf16[512,384]{1,0:T(8,128)(2,1)S(1)}, bf16[2,4,96,512]{3,2,1,0:T(8,128)(2,1)S(1)}, bf16[2,64,512]{2,1,0:T(8,128)(2,1)S(1)}) custom-call(s32[3]{0:T(128)S(1)} %pad_add_fusion.idx, bf16[2,224,512]{2,1,0:T(8,128)(2,1)S(1)} %constant_dynamic-update-slice_fusion.b0, ...), custom_call_target="tpu_custom_call" | custom-call | flops 3000000000 | bytes 4000000 | tf_op jit(solution)/shard_map/early/pallas_call | solution.py:473
  32.7 0.0 collective-permute-done.7.w_b
  32.7 4.8 %chain.1 = (bf16[2,64,512]{2,1,0:T(8,128)(2,1)S(1)}, bf16[2,64,512]{2,1,0:T(8,128)(2,1)S(1)}, bf16[768,512]{1,0:T(8,128)(2,1)S(1)}, f32[384,128]{1,0:T(8,128)S(1...) custom-call(s32[3]{0:T(128)S(1)} %pad_add_fusion.idx, ...), custom_call_target="tpu_custom_call" | custom-call | flops 6000000000 | bytes 4000000 | tf_op jit(solution)/shard_map/chain/pallas_call | solution.py:473
  37.5 2.6 %collective-permute-start.8 = (bf16[384,128]{1,0:T(8,128)(2,1)S(1)}, bf16[384,128]{1,0:T(8,128)(2,1)S(1)}, u32[]{:S(2)}, u32[]{:S(2)}) collective-permute-start(bf16[384,128]{1,0:T(8,128)(2,1)S(1)} %get-tuple-element.44), channel_id=1, source_target_pairs={{0,2},{2,0},{4,6},{6,4},{1,3},{3,1},{5,7},{7,5},{8,10},{10,8},{12,... | collective-permute-start | bytes 294920 | tf_op jit(solution)/shard_map/ppermute | solution.py:568
  40.0 2.6 %collective-permute-start.9 = (bf16[384,128]{1,0:T(8,128)(2,1)S(1)}, bf16[384,128]{1,0:T(8,128)(2,1)S(1)}, u32[]{:S(2)}, u32[]{:S(2)}) collective-permute-start(bf16[384,128]{1,0:T(8,128)(2,1)S(1)} %get-tuple-element.45), channel_id=1, source_target_pairs={{0,4},{2,6},{4,0},{6,2},{1,5},{3,7},{5,1},{7,3},{8,12},{10,14},{12... | collective-permute-start | bytes 294920 | tf_op jit(solution)/shard_map/ppermute | solution.py:568
  42.6 0.0 collective-permute-start.10
  42.6 2.5 %finish.1 = (bf16[2,16,4,512]{3,2,1,0:T(4,128)(2,1)}, bf16[2,16,4,512]{3,2,1,0:T(4,128)(2,1)}) custom-call(bf16[1536,512]{1,0:T(8,128)(2,1)S(1)} %bitcast.13, bf16[3,256,384]{2,1,0:T(8,128)(2,1)S(1)} %get-tuple-element.25.backward, bf16[768,512]{1,0:T(8,128)(2,1)S(1)} %get-tuple-element.38.gates, bf16[2,64,512]{2,1,0:T(8,128)(2,1)S(1)} %get-tuple-element.39.next_ref, ...), custom_call_target="tpu_custom_call" | custom-call | flops 2000000000 | bytes 4000000 | tf_op jit(solution)/shard_map/finish/pallas_call | solution.py:473
  45.1 0.0 collective-permute-done.8.p1
  45.1 5.6 %collective-permute-done.9.p2 = bf16[384,128]{1,0:T(8,128)(2,1)S(1)} collective-permute-done((bf16[384,128]{1,0:T(8,128)(2,1)S(1)}, bf16[384,128]{1,0:T(8,128)(2,1)S(1)}, u32[]{:S(2)}, u32[]{:S(2)}) %collective-permute-start.9) | collective-permute-done | bytes 98336 | tf_op jit(solution)/shard_map/ppermute | solution.py:568
  50.7 0.0 collective-permute-done.10.p3
  50.7 0.7 %add_up.1 = f32[384,128]{1,0:T(8,128)} custom-call(f32[384,128]{1,0:T(8,128)S(1)} %get-tuple-element.43.mine, bf16[384,128]{1,0:T(8,128)(2,1)S(1)} %collective-permute-done.8.p1, bf16[384,128]{1,0:T(8,128)(2,1)S(1)} %collective-permute-done.9.p2, bf16[384,128]{1,0:T(8,128)(2,1)S(1)} %collective-permute-done.10.p3), custom_call_target="tpu_custom_call" | custom-call | flops 100000000 | bytes 4000000 | tf_op jit(solution)/shard_map/add_up/pallas_call | solution.py:473
  (5 shorter events, 0.1 us)
Async XLA Ops:
  0.7 1.4 %copy-start = (bf16[1,3,512,512]{3,2,1,0:T(8,128)(2,1)S(1)}, bf16[1,3,512,512]{3,2,1,0:T(8,128)(2,1)}, u32[]{:S(2)}) copy-start(bf16[1,3,512,512]{3,2,1,0:T(8,128)(2,1)} %param.8) | copy-start | bytes 4718596
  2.1 0.9 %copy-start.2 = (bf16[2,16,4,512]{3,2,1,0:T(4,128)(2,1)S(1)}, bf16[2,16,4,512]{3,2,1,0:T(4,128)(2,1)}, u32[]{:S(2)}) copy-start(bf16[2,16,4,512]{3,2,1,0:T(4,128)(2,1)} %x.1) | copy-start | bytes 393220
  3.0 0.9 %copy-start.3 = (bf16[2,16,4,512]{3,2,1,0:T(4,128)(2,1)S(1)}, bf16[2,16,4,512]{3,2,1,0:T(4,128)(2,1)}, u32[]{:S(2)}) copy-start(bf16[2,16,4,512]{3,2,1,0:T(4,128)(2,1)} %c.1) | copy-start | bytes 393220
  4.6 20.5 %collective-permute-start.6 = (bf16[768,512]{1,0:T(8,128)(2,1)S(1)}, bf16[768,512]{1,0:T(8,128)(2,1)S(1)}, u32[]{:S(2)}, u32[]{:S(2)}) collective-permute-start(bf16[768,512]{1,0:T(8,128)(2,1)S(1)} %get-tuple-element.31), channel_id=1, source_target_pairs={{0,1},{1,0},{2,3},{3,2},{4,5},{5,4},{6,7},{7,6},{8,9},{9,8},{10,11... | collective-permute-start | bytes 2359304 | tf_op jit(solution)/shard_map/ppermute | solution.py:504
  7.6 13.0 %collective-permute-start = (bf16[2,48,512]{2,1,0:T(8,128)(2,1)S(1)}, bf16[2,48,512]{2,1,0:T(8,128)(2,1)S(1)}, u32[]{:S(2)}, u32[]{:S(2)}) collective-permute-start(bf16[2,48,512]{2,1,0:T(8,128)(2,1)S(1)} %get-tuple-element.27), channel_id=1, source_target_pairs={{0,2},{2,4},{4,6},{1,3},{3,5},{5,7},{8,10},{10,12},{12,14},{9,11},... | collective-permute-start | bytes 294920 | tf_op jit(solution)/shard_map/ppermute | solution.py:506
  11.1 9.5 %collective-permute-start.1 = (bf16[2,48,512]{2,1,0:T(8,128)(2,1)S(1)}, bf16[2,48,512]{2,1,0:T(8,128)(2,1)S(1)}, u32[]{:S(2)}, u32[]{:S(2)}) collective-permute-start(bf16[2,48,512]{2,1,0:T(8,128)(2,1)S(1)} %get-tuple-element.28), channel_id=1, source_target_pairs={{2,0},{4,2},{6,4},{3,1},{5,3},{7,5},{10,8},{12,10},{14,12},{11,9},... | collective-permute-start | bytes 294920 | tf_op jit(solution)/shard_map/ppermute | solution.py:507
  12.4 12.8 %collective-permute-start.3 = (bf16[2,128,512]{2,1,0:T(8,128)(2,1)S(1)}, bf16[2,128,512]{2,1,0:T(8,128)(2,1)S(1)}, u32[]{:S(2)}, u32[]{:S(2)}) collective-permute-start(bf16[2,128,512]{2,1,0:T(8,128)(2,1)S(1)} %get-tuple-element.26), channel_id=1, source_target_pairs={{0,16},{8,24},{16,0},{24,8},{1,17},{9,25},{17,1},{25,9},{2,18},{10... | collective-permute-start | bytes 786440 | tf_op jit(solution)/shard_map/ppermute | solution.py:505
  14.0 0.7 %copy-start.4 = (f32[64,9,3]{0,2,1:T(4,128)S(1)}, f32[64,9,3]{0,2,1:T(4,128)}, u32[]{:S(2)}) copy-start(f32[64,9,3]{0,2,1:T(4,128)} %param.9) | copy-start | bytes 20740
  14.7 0.7 %copy-start.5 = (s32[64,9]{0,1:T(8,128)S(1)}, s32[64,9]{0,1:T(8,128)}, u32[]{:S(2)}) copy-start(s32[64,9]{0,1:T(8,128)} %param.10) | copy-start | bytes 6916
  15.4 0.7 %copy-start.6 = (s32[64,9]{0,1:T(8,128)S(1)}, s32[64,9]{0,1:T(8,128)}, u32[]{:S(2)}) copy-start(s32[64,9]{0,1:T(8,128)} %param.11) | copy-start | bytes 6916
  16.1 12.3 %copy-start.1 = (bf16[1,3,512,512]{3,2,1,0:T(8,128)(2,1)S(1)}, bf16[1,3,512,512]{3,2,1,0:T(8,128)(2,1)}, u32[]{:S(2)}) copy-start(bf16[1,3,512,512]{3,2,1,0:T(8,128)(2,1)} %param.8) | copy-start | bytes 4718596
  20.6 5.9 %collective-permute-start.4 = (bf16[2,96,512]{2,1,0:T(8,128)(2,1)S(1)}, bf16[2,96,512]{2,1,0:T(8,128)(2,1)S(1)}, u32[]{:S(2)}, u32[]{:S(2)}) collective-permute-start(bf16[2,96,512]{2,1,0:T(8,128)(2,1)S(1)} %pad_maximum_fusion.1), channel_id=1, source_target_pairs={{0,16},{8,24},{16,0},{24,8},{1,17},{9,25},{17,1},{25,9},{2,18},{10... | collective-permute-start | bytes 589832 | tf_op jit(solution)/shard_map/ppermute | solution.py:509
  21.2 5.4 %collective-permute-start.2 = (bf16[2,224,512]{2,1,0:T(8,128)(2,1)S(1)}, bf16[2,224,512]{2,1,0:T(8,128)(2,1)S(1)}, u32[]{:S(2)}, u32[]{:S(2)}) collective-permute-start(bf16[2,224,512]{2,1,0:T(8,128)(2,1)S(1)} %constant_dynamic-update-slice_fusion.b0), channel_id=1, source_target_pairs={{0,8},{8,0},{16,24},{24,16},{1,9},{9,1},{17,25},{25,17},{2,10},{10... | collective-permute-start | bytes 1376264 | tf_op jit(solution)/shard_map/ppermute | solution.py:511
  25.1 7.5 %collective-permute-start.7 = (bf16[768,512]{1,0:T(8,128)(2,1)S(1)}, bf16[768,512]{1,0:T(8,128)(2,1)S(1)}, u32[]{:S(2)}, u32[]{:S(2)}) collective-permute-start(bf16[768,512]{1,0:T(8,128)(2,1)S(1)} %collective-permute-done.6.w_a), channel_id=1, source_target_pairs={{0,8},{8,0},{16,24},{24,16},{1,9},{9,1},{17,25},{25,17},{2,10},{10... | collective-permute-start | bytes 2359304 | tf_op jit(solution)/shard_map/ppermute | solution.py:528
  26.5 1.9 %collective-permute-start.5 = (bf16[2,224,512]{2,1,0:T(8,128)(2,1)S(1)}, bf16[2,224,512]{2,1,0:T(8,128)(2,1)S(1)}, u32[]{:S(2)}, u32[]{:S(2)}) collective-permute-start(bf16[2,224,512]{2,1,0:T(8,128)(2,1)S(1)} %pad_maximum_fusion.b2), channel_id=1, source_target_pairs={{0,8},{8,0},{16,24},{24,16},{1,9},{9,1},{17,25},{25,17},{2,10},{10... | collective-permute-start | bytes 1376264 | tf_op jit(solution)/shard_map/ppermute | solution.py:527
  37.5 7.6 %collective-permute-start.8 = (bf16[384,128]{1,0:T(8,128)(2,1)S(1)}, bf16[384,128]{1,0:T(8,128)(2,1)S(1)}, u32[]{:S(2)}, u32[]{:S(2)}) collective-permute-start(bf16[384,128]{1,0:T(8,128)(2,1)S(1)} %get-tuple-element.44), channel_id=1, source_target_pairs={{0,2},{2,0},{4,6},{6,4},{1,3},{3,1},{5,7},{7,5},{8,10},{10,8},{12,... | collective-permute-start | bytes 294920 | tf_op jit(solution)/shard_map/ppermute | solution.py:568
  40.0 10.7 %collective-permute-start.9 = (bf16[384,128]{1,0:T(8,128)(2,1)S(1)}, bf16[384,128]{1,0:T(8,128)(2,1)S(1)}, u32[]{:S(2)}, u32[]{:S(2)}) collective-permute-start(bf16[384,128]{1,0:T(8,128)(2,1)S(1)} %get-tuple-element.45), channel_id=1, source_target_pairs={{0,4},{2,6},{4,0},{6,2},{1,5},{3,7},{5,1},{7,3},{8,12},{10,14},{12... | collective-permute-start | bytes 294920 | tf_op jit(solution)/shard_map/ppermute | solution.py:568
  42.6 8.1 %collective-permute-start.10 = (bf16[384,128]{1,0:T(8,128)(2,1)S(1)}, bf16[384,128]{1,0:T(8,128)(2,1)S(1)}, u32[]{:S(2)}, u32[]{:S(2)}) collective-permute-start(bf16[384,128]{1,0:T(8,128)(2,1)S(1)} %get-tuple-element.46), channel_id=1, source_target_pairs={{0,6},{2,4},{4,2},{6,0},{1,7},{3,5},{5,3},{7,1},{8,14},{10,12},{12... | collective-permute-start | bytes 294920 | tf_op jit(solution)/shard_map/ppermute | solution.py:568

commit v4 on v3

--- a/solution.py
+++ b/solution.py
@@ -165,6 +165,7 @@
 
 HALO = 8
 BAND = 8
+PREP_MIB = 59.2
 
 
 def swap(axis, bit):
@@ -220,11 +221,19 @@
                     found.append(r[m, at + lo - start : at + hi - start, :])
         return jnp.concatenate(found, axis=0)
 
-    def prep(idx, x, c, w, both, tail, head, half, sem):
+    def take_half(idx, w, half, sem):
         rows = half.shape[0]
         start = pl.multiple_of(idx[1] % 2 * rows, rows)
-        copy = pltpu.make_async_copy(w.at[pl.ds(start, rows), :], half, sem)
-        copy.start()
+        move = pltpu.make_async_copy(w.at[pl.ds(start, rows), :], half, sem)
+        move.start()
+        move.wait()
+
+    def prep(x_in, c_in, both, tail, head, x, c, sems):
+        moves = [pltpu.make_async_copy(x_in, x, sems.at[0]), pltpu.make_async_copy(c_in, c, sems.at[1])]
+        for move in moves:
+            move.start()
+        moves[0].wait()
+        moves[1].wait()
         for m in range(members):
             state = x[m].reshape(own, channels)
             coming = c[m].reshape(own, channels)
@@ -234,7 +243,6 @@
             tail[m, edge:, :] = coming[own - half_edge :]
             head[m, :edge, :] = state[:edge]
             head[m, edge:, :] = coming[:half_edge]
-        copy.wait()
 
     def maps(idx, lat_step, lon_step, basis, forward, again, backward, tab):
         lon, lat = idx[1], idx[2]
@@ -441,7 +449,7 @@
             grad_ref[m] = total.astype(jnp.bfloat16).reshape(lat_rows, lon_cols, channels)
             out_ref[m] = last_ref[m].reshape(lat_rows, lon_cols, channels)
 
-    return prep, maps, early, chain, finish
+    return take_half, prep, maps, early, chain, finish
 
 
 def add_up(scale, mine, p1, p2, p3, out):
@@ -469,39 +477,50 @@
     smem = pl.BlockSpec(memory_space=pltpu.SMEM)
     anywhere = pl.BlockSpec(memory_space=pltpu.HBM)
 
-    def call(body, name, outs, ins, mib, gflops, scratch=(), far=()):
+    def call(body, name, outs, ins, mib, gflops, scratch=(), far=(), far_out=False):
         return pl.pallas_call(
             body,
             out_shape=outs,
             in_specs=[smem if a.ndim == 1 else anywhere if i in far else vmem for i, a in enumerate(ins)],
-            out_specs=(vmem,) * len(outs),
+            out_specs=(anywhere if far_out else vmem,) * len(outs),
             scratch_shapes=list(scratch),
-            compiler_params=pltpu.CompilerParams(vmem_limit_bytes=mib * 1024 * 1024),
+            compiler_params=pltpu.CompilerParams(vmem_limit_bytes=int(mib * 1024 * 1024)),
             cost_estimate=pl.CostEstimate(flops=int(gflops * 1e9), bytes_accessed=4_000_000, transcendentals=0),
             name=name,
         )(*ins)
 
-    prep, maps, early, chain, finish = make_steps(lat_rows, lon_cols, blocks, members, channels, lat_devices)
+    take_half, prep, maps, early, chain, finish = make_steps(lat_rows, lon_cols, blocks, members, channels, lat_devices)
     idx = jnp.stack([lax.axis_index("segment"), lax.axis_index("lon"), lax.axis_index("lat")]).astype(jnp.int32)
     kernel = weights.reshape(width, channels)
-    both, tail, head, half = call(
+    (half,) = call(
+        take_half,
+        "take_half",
+        (shape((width // 2, channels), half_type),),
+        (idx, kernel),
+        PREP_MIB,
+        0.5,
+        (pltpu.SemaphoreType.DMA,),
+        (1,),
+        True,
+    )
+    near_half = lax.ppermute(half, "segment", swap("segment", 1))
+    half, inputs, cotangent = lax.optimization_barrier((half, inputs, cotangent))
+    both, tail, head = call(
         prep,
         "prep",
         (
             shape((members, 2 * own, channels), half_type),
             shape((members, halo, channels), half_type),
             shape((members, halo, channels), half_type),
-            shape((width // 2, channels), half_type),
         ),
-        (idx, inputs, cotangent, kernel),
-        4,
+        (inputs, cotangent),
+        PREP_MIB,
         0.5,
-        (pltpu.SemaphoreType.DMA,),
-        (3,),
+        (pltpu.VMEM(inputs.shape, half_type), pltpu.VMEM(inputs.shape, half_type), pltpu.SemaphoreType.DMA((2,))),
+        (0, 1),
     )
     up = [(i, i + 1) for i in range(lat_devices - 1)]
     down = [(i + 1, i) for i in range(lat_devices - 1)]
-    near_half = lax.ppermute(half, "segment", swap("segment", 1))
     both_y = lax.ppermute(both, "lon", swap("lon", 2))
     before = lax.ppermute(tail, "lat", up)
     after = lax.ppermute(head, "lat", down)
@@ -509,6 +528,7 @@
     sides_y = lax.ppermute(sides, "lon", swap("lon", 2))
     b0 = jnp.concatenate([both, sides], axis=1)
     b1 = lax.ppermute(b0, "lon", swap("lon", 1))
+    b0, lat_step, lon_step, basis_values = lax.optimization_barrier((b0, lat_step, lon_step, basis_values))
     forward, again, backward = call(
         maps,
         "maps",
@@ -525,7 +545,6 @@
     b2 = jnp.concatenate([both_y, sides_y], axis=1)
     b2, forward = lax.optimization_barrier((b2, forward))
     b3 = lax.ppermute(b2, "lon", swap("lon", 1))
-    far_half = lax.ppermute(near_half, "lon", swap("lon", 1))
     s_type = (members * nf * cells, width)
     s, left, slope, early_out = call(
         early,
@@ -541,6 +560,8 @@
         3.0,
         (pltpu.VMEM(s_type, half_type), pltpu.VMEM((members, blocks, own + 2 * edge, channels), half_type)),
     )
+    near_half, s = lax.optimization_barrier((near_half, s))
+    far_half = lax.ppermute(near_half, "lon", swap("lon", 1))
     lines = (width // blocks // lat_devices * channels // 128, 128)
     out, follow, gates, mine, *parts = call(
         chain,
@@ -565,7 +586,7 @@
             pltpu.VMEM((width // blocks * channels // 128, 128), full_type),
         ),
     )
-    got = [lax.ppermute(part, "lat", swap("lat", bit)) for bit, part in zip((1, 2, 3), parts)]
+    got = [lax.ppermute(part, "lat", swap("lat", bit)) for bit, part in reversed(list(zip((1, 2, 3), parts)))]
     block = (members, lat_rows, lon_cols, channels)
     grad, out = call(
         finish,

time: 51.8 us -> 75.8 us (1.46)
  Pallas kernels: 17.4 us -> 44 us
  local copies, waits for them, and re-layouts: 5.37 us -> 1.04 us
  starting transfers between devices: 15.2 us -> 16.6 us
    pallas_call x6 -> x7, Pallas kernels: 17.4 us -> 44 us  [call(): pl.pallas_call(body, out_shape=outs, in_specs=[smem if a.ndim == 1 else a...]
    unnamed x16 -> x12, local copies, waits for them, and re-layouts: 5.36 us -> 1.03 us
    ppermute x1, waiting for transfers between devices: 3.87 us -> 0.01 us  [whole_ring(): near_half = lax.ppermute(half, 'segment', swap('segment', 1))]
    ppermute x1, waiting for transfers between devices: 0.01 us -> 2.82 us  [whole_ring(): after = lax.ppermute(head, 'lat', down)]
    ppermute x1, waiting for transfers between devices: 0.01 us -> 2.13 us  [whole_ring(): far_half = lax.ppermute(near_half, 'lon', swap('lon', 1))]
    ppermute x1, starting transfers between devices: 0.57 us -> 1.58 us  [whole_ring(): sides_y = lax.ppermute(sides, 'lon', swap('lon', 2))]
    ppermute x1, waiting for transfers between devices: 1.32 us -> 0.34 us  [whole_ring(): sides_y = lax.ppermute(sides, 'lon', swap('lon', 2))]
  transfers between devices with their start and end apart: 11 -> 11, of which waited for: 4 -> 6; matrix products, arithmetic and copies ran while one was open for 0% -> 1% of each run, Pallas kernels for 22% -> 17%
where the time goes in v4:
time: 75.8 us; the launch traced here: 75.6 us
  Pallas kernels  44 us (58%)
  starting transfers between devices  16.6 us (22%)
  waiting for transfers between devices  12.5 us (16%)
  local copies, waits for them, and re-layouts  1.04 us (1%)
  between operations  0.81 us (1%)
    pallas_call x7, Pallas kernels, call(): pl.pallas_call(body, out_shape=outs, in_specs=[smem if a.ndim == 1 else a...  44 us
    ppermute x3, waiting for transfers between devices, whole_ring(): lax.ppermute(part, 'lat', swap('lat', bit))  5.48 us
    ppermute x3, starting transfers between devices, whole_ring(): lax.ppermute(part, 'lat', swap('lat', bit))  5.11 us
    ppermute x1, starting transfers between devices, whole_ring(): before = lax.ppermute(tail, 'lat', up)  3.49 us
    ppermute x1, starting transfers between devices, whole_ring(): near_half = lax.ppermute(half, 'segment', swap('segment', 1))  3 us
    ppermute x1, waiting for transfers between devices, whole_ring(): after = lax.ppermute(head, 'lat', down)  2.82 us
    ppermute x1, waiting for transfers between devices, whole_ring(): far_half = lax.ppermute(near_half, 'lon', swap('lon', 1))  2.13 us
    ppermute x1, waiting for transfers between devices, whole_ring(): b3 = lax.ppermute(b2, 'lon', swap('lon', 1))  1.67 us
  transfers between devices with their start and end apart: 11, of which 6 were waited for; matrix products, arithmetic and copies ran while one was open for 1% of the time, Pallas kernels for 17%

profile of v4, /device:TPU:0, one launch (start us, length us, event | category | flops | bytes accessed | tf_op | source)
XLA Modules:
  0.0 75.6 jit_solution(14619393373156116869)
XLA Ops:
  0.6 0.0 copy-start.4
  0.6 0.0 copy-start.3
  0.7 0.0 copy-start.2
  0.7 0.7 pad_add_fusion.idx
  1.3 0.0 copy-start.1
  1.3 25.7 %take_half.1 = bf16[768,512]{1,0:T(8,128)(2,1)} custom-call(s32[3]{0:T(128)} %pad_add_fusion.idx, bf16[1536,512]{1,0:T(8,128)(2,1)} %bitcast.10), custom_call_target="tpu_custom_call" | custom-call | flops 500000000 | bytes 4000000 | tf_op jit(solution)/shard_map/take_half/pallas_call | solution.py:481
  27.1 3.0 %collective-permute-start.6 = (bf16[768,512]{1,0:T(8,128)(2,1)}, bf16[768,512]{1,0:T(8,128)(2,1)S(1)}, u32[]{:S(2)}, u32[]{:S(2)}) collective-permute-start(bf16[768,512]{1,0:T(8,128)(2,1)} %take_half.1), channel_id=1, source_target_pairs={{0,1},{1,0},{2,3},{3,2},{4,5},{5,4},{6,7},{7,6},{8,9},{9,8},{10,11... | collective-permute-start | bytes 2359304 | tf_op jit(solution)/shard_map/ppermute | solution.py:506
  30.1 1.8 %prep.1 = (bf16[2,128,512]{2,1,0:T(8,128)(2,1)}, bf16[2,48,512]{2,1,0:T(8,128)(2,1)}, bf16[2,48,512]{2,1,0:T(8,128)(2,1)}) custom-call(bf16[2,16,4,512]{3,2,1,0:T(4,128)(2,1)} %x_in, bf16[2,16,4,512]{3,2,1,0:T(4,128)(2,1)} %c_in), custom_call_target="tpu_custom_call" | custom-call | flops 500000000 | bytes 4000000 | tf_op jit(solution)/shard_map/prep/pallas_call | solution.py:481
  31.8 3.5 %collective-permute-start = (bf16[2,48,512]{2,1,0:T(8,128)(2,1)}, bf16[2,48,512]{2,1,0:T(8,128)(2,1)S(1)}, u32[]{:S(2)}, u32[]{:S(2)}) collective-permute-start(bf16[2,48,512]{2,1,0:T(8,128)(2,1)} %get-tuple-element.35), channel_id=1, source_target_pairs={{0,2},{2,4},{4,6},{1,3},{3,5},{5,7},{8,10},{10,12},{12,14},{9,11},... | collective-permute-start | bytes 294920 | tf_op jit(solution)/shard_map/ppermute | solution.py:525
  35.3 1.3 %collective-permute-start.1 = (bf16[2,48,512]{2,1,0:T(8,128)(2,1)}, bf16[2,48,512]{2,1,0:T(8,128)(2,1)S(1)}, u32[]{:S(2)}, u32[]{:S(2)}) collective-permute-start(bf16[2,48,512]{2,1,0:T(8,128)(2,1)} %get-tuple-element.36), channel_id=1, source_target_pairs={{2,0},{4,2},{6,4},{3,1},{5,3},{7,5},{10,8},{12,10},{14,12},{11,9},... | collective-permute-start | bytes 294920 | tf_op jit(solution)/shard_map/ppermute | solution.py:526
  36.6 1.6 %collective-permute-start.3 = (bf16[2,128,512]{2,1,0:T(8,128)(2,1)}, bf16[2,128,512]{2,1,0:T(8,128)(2,1)S(1)}, u32[]{:S(2)}, u32[]{:S(2)}) collective-permute-start(bf16[2,128,512]{2,1,0:T(8,128)(2,1)} %get-tuple-element.34), channel_id=1, source_target_pairs={{0,16},{8,24},{16,0},{24,8},{1,17},{9,25},{17,1},{25,9},{2,18},{10... | collective-permute-start | bytes 786440 | tf_op jit(solution)/shard_map/ppermute | solution.py:524
  38.2 1.0 %constant_dynamic-update-slice_fusion.2 = bf16[2,224,512]{2,1,0:T(8,128)(2,1)S(1)} fusion(bf16[2,128,512]{2,1,0:T(8,128)(2,1)} %get-tuple-element.34), kind=kLoop, calls=%fused_computation.4 | loop fusion | bytes 524288
  39.2 0.0 collective-permute-done
  39.2 2.8 %collective-permute-done.1 = bf16[2,48,512]{2,1,0:T(8,128)(2,1)S(1)} collective-permute-done((bf16[2,48,512]{2,1,0:T(8,128)(2,1)}, bf16[2,48,512]{2,1,0:T(8,128)(2,1)S(1)}, u32[]{:S(2)}, u32[]{:S(2)}) %collective-permute-start.1) | collective-permute-done | bytes 98336 | tf_op jit(solution)/shard_map/ppermute | solution.py:526
  42.1 1.6 %collective-permute-start.4 = (bf16[2,96,512]{2,1,0:T(8,128)(2,1)S(1)}, bf16[2,96,512]{2,1,0:T(8,128)(2,1)S(1)}, u32[]{:S(2)}, u32[]{:S(2)}) collective-permute-start(bf16[2,96,512]{2,1,0:T(8,128)(2,1)S(1)} %pad_maximum_fusion.1), channel_id=1, source_target_pairs={{0,16},{8,24},{16,0},{24,8},{1,17},{9,25},{17,1},{25,9},{2,18},{10... | collective-permute-start | bytes 589832 | tf_op jit(solution)/shard_map/ppermute | solution.py:528
  43.7 0.1 collective-permute-start.2
  43.8 0.0 copy-done.4
  43.8 0.0 copy-done.3
  43.8 0.0 copy-done.2
  43.8 0.0 copy-done.1
  43.8 0.0 copy-start
  43.8 4.4 %maps.1 = (bf16[4,384,256]{2,1,0:T(8,128)(2,1)S(1)}, bf16[3,384,256]{2,1,0:T(8,128)(2,1)S(1)}, bf16[3,256,384]{2,1,0:T(8,128)(2,1)S(1)}) custom-call(s32[3]{0:T(128)S(1)} %copy-done.1, s32[9,64]{1,0:T(8,128)S(1)} %bitcast.15, s32[9,64]{1,0:T(8,128)S(1)} %bitcast.16, f32[9,3,64]{2,1,0:T(4,128)S(1)} %bitcast.14), custom_call_target="tpu_custom_call" | custom-call | flops 3000000000 | bytes 4000000 | tf_op jit(solution)/shard_map/maps/pallas_call | solution.py:481
  48.3 0.0 collective-permute-done.3
  48.3 0.3 collective-permute-done.4
  48.6 0.2 collective-permute-start.5
  48.9 0.0 collective-permute-done.2.b1
  48.9 1.7 %collective-permute-done.5.b3 = bf16[2,224,512]{2,1,0:T(8,128)(2,1)S(1)} collective-permute-done((bf16[2,224,512]{2,1,0:T(8,128)(2,1)S(1)}, bf16[2,224,512]{2,1,0:T(8,128)(2,1)S(1)}, u32[]{:S(2)}, u32[]{:S(2)}) %collective-permute-start.5) | collective-permute-done | bytes 458784 | tf_op jit(solution)/shard_map/ppermute | solution.py:547
  50.5 0.0 copy-done
  50.5 4.2 %early.1 = (bf16[1024,1536]{1,0:T(8,128)(2,1)S(1)}, bf16[512,384]{1,0:T(8,128)(2,1)S(1)}, bf16[2,4,96,512]{3,2,1,0:T(8,128)(2,1)S(1)}, bf16[2,64,512]{2,1,0:T(8,128)(2,1)S(1)}) custom-call(s32[3]{0:T(128)S(1)} %copy-done.1, bf16[2,224,512]{2,1,0:T(8,128)(2,1)S(1)} %constant_dynamic-update-slice_fusion.b0, ...), custom_call_target="tpu_custom_call" | custom-call | flops 3000000000 | bytes 4000000 | tf_op jit(solution)/shard_map/early/pallas_call | solution.py:481
  54.8 0.0 collective-permute-done.6.w_a
  54.8 0.2 collective-permute-start.7
  55.0 2.1 %collective-permute-done.7.w_b = bf16[768,512]{1,0:T(8,128)(2,1)S(1)} collective-permute-done((bf16[768,512]{1,0:T(8,128)(2,1)S(1)}, bf16[768,512]{1,0:T(8,128)(2,1)S(1)}, u32[]{:S(2)}, u32[]{:S(2)}) %collective-permute-start.7) | collective-permute-done | bytes 786464 | tf_op jit(solution)/shard_map/ppermute | solution.py:564
  57.1 4.7 %chain.1 = (bf16[2,64,512]{2,1,0:T(8,128)(2,1)S(1)}, bf16[2,64,512]{2,1,0:T(8,128)(2,1)S(1)}, bf16[768,512]{1,0:T(8,128)(2,1)S(1)}, f32[384,128]{1,0:T(8,128)S(1...) custom-call(s32[3]{0:T(128)S(1)} %copy-done.1, ...), custom_call_target="tpu_custom_call" | custom-call | flops 6000000000 | bytes 4000000 | tf_op jit(solution)/shard_map/chain/pallas_call | solution.py:481
  61.8 4.5 %collective-permute-start.8 = (bf16[384,128]{1,0:T(8,128)(2,1)S(1)}, bf16[384,128]{1,0:T(8,128)(2,1)S(1)}, u32[]{:S(2)}, u32[]{:S(2)}) collective-permute-start(bf16[384,128]{1,0:T(8,128)(2,1)S(1)} %get-tuple-element.58), channel_id=1, source_target_pairs={{0,6},{2,4},{4,2},{6,0},{1,7},{3,5},{5,3},{7,1},{8,14},{10,12},{12... | collective-permute-start | bytes 294920 | tf_op jit(solution)/shard_map/ppermute | solution.py:589
  66.3 0.0 collective-permute-start.9
  66.3 0.6 collective-permute-start.10
  66.9 2.4 %finish.1 = (bf16[2,16,4,512]{3,2,1,0:T(4,128)(2,1)}, bf16[2,16,4,512]{3,2,1,0:T(4,128)(2,1)}) custom-call(bf16[1536,512]{1,0:T(8,128)(2,1)S(1)} %bitcast.13, bf16[3,256,384]{2,1,0:T(8,128)(2,1)S(1)} %get-tuple-element.40.backward, bf16[768,512]{1,0:T(8,128)(2,1)S(1)} %get-tuple-element.52.gates, bf16[2,64,512]{2,1,0:T(8,128)(2,1)S(1)} %get-tuple-element.53.next_ref, ...), custom_call_target="tpu_custom_call" | custom-call | flops 2000000000 | bytes 4000000 | tf_op jit(solution)/shard_map/finish/pallas_call | solution.py:481
  69.4 0.6 collective-permute-done.8.p1
  70.0 4.9 %collective-permute-done.9.p2 = bf16[384,128]{1,0:T(8,128)(2,1)S(1)} collective-permute-done((bf16[384,128]{1,0:T(8,128)(2,1)S(1)}, bf16[384,128]{1,0:T(8,128)(2,1)S(1)}, u32[]{:S(2)}, u32[]{:S(2)}) %collective-permute-start.9) | collective-permute-done | bytes 98336 | tf_op jit(solution)/shard_map/ppermute | solution.py:589
  74.9 0.0 collective-permute-done.10.p3
  74.9 0.7 add_up.1
  (4 shorter events, 0.1 us)
Async XLA Ops:
  0.6 43.1 %copy-start.4 = (s32[64,9]{0,1:T(8,128)S(1)}, s32[64,9]{0,1:T(8,128)}, u32[]{:S(2)}) copy-start(s32[64,9]{0,1:T(8,128)} %param.11) | copy-start | bytes 6916
  0.6 43.1 %copy-start.3 = (s32[64,9]{0,1:T(8,128)S(1)}, s32[64,9]{0,1:T(8,128)}, u32[]{:S(2)}) copy-start(s32[64,9]{0,1:T(8,128)} %param.10) | copy-start | bytes 6916
  0.7 43.1 %copy-start.2 = (f32[64,9,3]{0,2,1:T(4,128)S(1)}, f32[64,9,3]{0,2,1:T(4,128)}, u32[]{:S(2)}) copy-start(f32[64,9,3]{0,2,1:T(4,128)} %param.9) | copy-start | bytes 20740
  1.3 42.5 %copy-start.1 = (s32[3]{0:T(128)S(1)}, s32[3]{0:T(128)}, u32[]{:S(2)}) copy-start(s32[3]{0:T(128)} %pad_add_fusion.idx) | copy-start | bytes 40
  27.1 27.7 %collective-permute-start.6 = (bf16[768,512]{1,0:T(8,128)(2,1)}, bf16[768,512]{1,0:T(8,128)(2,1)S(1)}, u32[]{:S(2)}, u32[]{:S(2)}) collective-permute-start(bf16[768,512]{1,0:T(8,128)(2,1)} %take_half.1), channel_id=1, source_target_pairs={{0,1},{1,0},{2,3},{3,2},{4,5},{5,4},{6,7},{7,6},{8,9},{9,8},{10,11... | collective-permute-start | bytes 2359304 | tf_op jit(solution)/shard_map/ppermute | solution.py:506
  31.8 7.4 %collective-permute-start = (bf16[2,48,512]{2,1,0:T(8,128)(2,1)}, bf16[2,48,512]{2,1,0:T(8,128)(2,1)S(1)}, u32[]{:S(2)}, u32[]{:S(2)}) collective-permute-start(bf16[2,48,512]{2,1,0:T(8,128)(2,1)} %get-tuple-element.35), channel_id=1, source_target_pairs={{0,2},{2,4},{4,6},{1,3},{3,5},{5,7},{8,10},{10,12},{12,14},{9,11},... | collective-permute-start | bytes 294920 | tf_op jit(solution)/shard_map/ppermute | solution.py:525
  35.3 6.7 %collective-permute-start.1 = (bf16[2,48,512]{2,1,0:T(8,128)(2,1)}, bf16[2,48,512]{2,1,0:T(8,128)(2,1)S(1)}, u32[]{:S(2)}, u32[]{:S(2)}) collective-permute-start(bf16[2,48,512]{2,1,0:T(8,128)(2,1)} %get-tuple-element.36), channel_id=1, source_target_pairs={{2,0},{4,2},{6,4},{3,1},{5,3},{7,5},{10,8},{12,10},{14,12},{11,9},... | collective-permute-start | bytes 294920 | tf_op jit(solution)/shard_map/ppermute | solution.py:526
  36.6 11.6 %collective-permute-start.3 = (bf16[2,128,512]{2,1,0:T(8,128)(2,1)}, bf16[2,128,512]{2,1,0:T(8,128)(2,1)S(1)}, u32[]{:S(2)}, u32[]{:S(2)}) collective-permute-start(bf16[2,128,512]{2,1,0:T(8,128)(2,1)} %get-tuple-element.34), channel_id=1, source_target_pairs={{0,16},{8,24},{16,0},{24,8},{1,17},{9,25},{17,1},{25,9},{2,18},{10... | collective-permute-start | bytes 786440 | tf_op jit(solution)/shard_map/ppermute | solution.py:524
  42.1 6.5 %collective-permute-start.4 = (bf16[2,96,512]{2,1,0:T(8,128)(2,1)S(1)}, bf16[2,96,512]{2,1,0:T(8,128)(2,1)S(1)}, u32[]{:S(2)}, u32[]{:S(2)}) collective-permute-start(bf16[2,96,512]{2,1,0:T(8,128)(2,1)S(1)} %pad_maximum_fusion.1), channel_id=1, source_target_pairs={{0,16},{8,24},{16,0},{24,8},{1,17},{9,25},{17,1},{25,9},{2,18},{10... | collective-permute-start | bytes 589832 | tf_op jit(solution)/shard_map/ppermute | solution.py:528
  43.7 5.2 %collective-permute-start.2 = (bf16[2,224,512]{2,1,0:T(8,128)(2,1)S(1)}, bf16[2,224,512]{2,1,0:T(8,128)(2,1)S(1)}, u32[]{:S(2)}, u32[]{:S(2)}) collective-permute-start(bf16[2,224,512]{2,1,0:T(8,128)(2,1)S(1)} %constant_dynamic-update-slice_fusion.b0), channel_id=1, source_target_pairs={{0,8},{8,0},{16,24},{24,16},{1,9},{9,1},{17,25},{25,17},{2,10},{10... | collective-permute-start | bytes 1376264 | tf_op jit(solution)/shard_map/ppermute | solution.py:530
  43.8 6.7 %copy-start = (bf16[1,3,512,512]{3,2,1,0:T(8,128)(2,1)S(1)}, bf16[1,3,512,512]{3,2,1,0:T(8,128)(2,1)}, u32[]{:S(2)}) copy-start(bf16[1,3,512,512]{3,2,1,0:T(8,128)(2,1)} %param.8) | copy-start | bytes 4718596
  48.6 1.9 %collective-permute-start.5 = (bf16[2,224,512]{2,1,0:T(8,128)(2,1)S(1)}, bf16[2,224,512]{2,1,0:T(8,128)(2,1)S(1)}, u32[]{:S(2)}, u32[]{:S(2)}) collective-permute-start(bf16[2,224,512]{2,1,0:T(8,128)(2,1)S(1)} %pad_maximum_fusion.b2), channel_id=1, source_target_pairs={{0,8},{8,0},{16,24},{24,16},{1,9},{9,1},{17,25},{25,17},{2,10},{10... | collective-permute-start | bytes 1376264 | tf_op jit(solution)/shard_map/ppermute | solution.py:547
  54.8 2.4 %collective-permute-start.7 = (bf16[768,512]{1,0:T(8,128)(2,1)S(1)}, bf16[768,512]{1,0:T(8,128)(2,1)S(1)}, u32[]{:S(2)}, u32[]{:S(2)}) collective-permute-start(bf16[768,512]{1,0:T(8,128)(2,1)S(1)} %collective-permute-done.6.w_a), channel_id=1, source_target_pairs={{0,8},{8,0},{16,24},{24,16},{1,9},{9,1},{17,25},{25,17},{2,10},{10... | collective-permute-start | bytes 2359304 | tf_op jit(solution)/shard_map/ppermute | solution.py:564
  61.8 8.2 %collective-permute-start.8 = (bf16[384,128]{1,0:T(8,128)(2,1)S(1)}, bf16[384,128]{1,0:T(8,128)(2,1)S(1)}, u32[]{:S(2)}, u32[]{:S(2)}) collective-permute-start(bf16[384,128]{1,0:T(8,128)(2,1)S(1)} %get-tuple-element.58), channel_id=1, source_target_pairs={{0,6},{2,4},{4,2},{6,0},{1,7},{3,5},{5,3},{7,1},{8,14},{10,12},{12... | collective-permute-start | bytes 294920 | tf_op jit(solution)/shard_map/ppermute | solution.py:589
  66.3 8.6 %collective-permute-start.9 = (bf16[384,128]{1,0:T(8,128)(2,1)S(1)}, bf16[384,128]{1,0:T(8,128)(2,1)S(1)}, u32[]{:S(2)}, u32[]{:S(2)}) collective-permute-start(bf16[384,128]{1,0:T(8,128)(2,1)S(1)} %get-tuple-element.59), channel_id=1, source_target_pairs={{0,4},{2,6},{4,0},{6,2},{1,5},{3,7},{5,1},{7,3},{8,12},{10,14},{12... | collective-permute-start | bytes 294920 | tf_op jit(solution)/shard_map/ppermute | solution.py:589
  66.3 8.6 %collective-permute-start.10 = (bf16[384,128]{1,0:T(8,128)(2,1)S(1)}, bf16[384,128]{1,0:T(8,128)(2,1)S(1)}, u32[]{:S(2)}, u32[]{:S(2)}) collective-permute-start(bf16[384,128]{1,0:T(8,128)(2,1)S(1)} %get-tuple-element.60), channel_id=1, source_target_pairs={{0,2},{2,0},{4,6},{6,4},{1,3},{3,1},{5,7},{7,5},{8,10},{10,8},{12,... | collective-permute-start | bytes 294920 | tf_op jit(solution)/shard_map/ppermute | solution.py:589

commit v5 on v3

--- a/solution.py
+++ b/solution.py
@@ -220,24 +220,20 @@
                     found.append(r[m, at + lo - start : at + hi - start, :])
         return jnp.concatenate(found, axis=0)
 
-    def prep(idx, x, c, w, both, tail, head, half, sem):
-        rows = half.shape[0]
-        start = pl.multiple_of(idx[1] % 2 * rows, rows)
-        copy = pltpu.make_async_copy(w.at[pl.ds(start, rows), :], half, sem)
-        copy.start()
+    def prep(x, c, both):
         for m in range(members):
-            state = x[m].reshape(own, channels)
-            coming = c[m].reshape(own, channels)
-            both[m, :own, :] = state
-            both[m, own:, :] = coming
-            tail[m, :edge, :] = state[own - edge :]
-            tail[m, edge:, :] = coming[own - half_edge :]
-            head[m, :edge, :] = state[:edge]
-            head[m, edge:, :] = coming[:half_edge]
-        copy.wait()
-
-    def maps(idx, lat_step, lon_step, basis, forward, again, backward, tab):
-        lon, lat = idx[1], idx[2]
+            both[m, :own, :] = x[m].reshape(own, channels)
+            both[m, own:, :] = c[m].reshape(own, channels)
+
+    def edges(both, tail, head):
+        for m in range(members):
+            tail[m, :edge, :] = both[m, own - edge : own, :]
+            tail[m, edge:, :] = both[m, 2 * own - half_edge :, :]
+            head[m, :edge, :] = both[m, :edge, :]
+            head[m, edge:, :] = both[m, own : own + half_edge, :]
+
+    def maps(lat_step, lon_step, basis, forward, again, backward, tab):
+        lon, lat = lax.axis_index("lon"), lax.axis_index("lat")
         base = lat * lat_rows
         tab[...] = jnp.zeros(tab.shape, jnp.float32)
         tab[0:TAPS, :] = lat_step[...].astype(jnp.float32)
@@ -311,19 +307,19 @@
     def columns_of(lon):
         return pl.ds(pl.multiple_of(lon * (width // blocks), 128), width // blocks)
 
-    def early(idx, b0, b1, b2, b3, w_own, forward, again, s, left, slope, out, s0, mid):
+    def early(b0, b1, b2, b3, w_own, forward, again, s, left, slope, out, s0, mid):
         blk = (b0, b1, b2, b3)
 
-        @pl.when(idx[0] == 0)
+        @pl.when(lax.axis_index("segment") == 0)
         def _():
             spread(blk, forward, s0)
             first_section(blk, w_own, s0, s, again, mid, slope)
             for m in range(members):
                 size = (nf - 2) * cells
-                left[m * size : (m + 1) * size, :] = s0[(m * nf + 1) * cells : (m * nf + nf - 1) * cells, columns_of(idx[1])]
+                left[m * size : (m + 1) * size, :] = s0[(m * nf + 1) * cells : (m * nf + nf - 1) * cells, columns_of(lax.axis_index("lon"))]
                 out[m, :, :] = mid[m, 0, edge : edge + own, :]
 
-        @pl.when(idx[0] == 1)
+        @pl.when(lax.axis_index("segment") == 1)
         def _():
             spread(blk, forward, s)
 
@@ -336,10 +332,10 @@
             for i in range(members * ns):
                 feat[(i * BASIS + b) * cells : (i * BASIS + b + 1) * cells, :] = got[i * cells : (i + 1) * cells]
 
-    def chain(idx, b0, b1, b2, b3, w_own, w_a, w_b, again, backward, s, left0, slope, early_out,
+    def chain(b0, b1, b2, b3, w_own, w_a, w_b, again, backward, s, left0, slope, early_out,
               out_ref, next_ref, gate_ref, own_ref, p1, p2, p3, w, s1, mid, gates, feat, pull, grads):
         blk = (b0, b1, b2, b3)
-        seg, lon, lat = idx[0], idx[1], idx[2]
+        seg, lon, lat = lax.axis_index("segment"), lax.axis_index("lon"), lax.axis_index("lat")
         half = w_a.shape[0]
         core = lon % 2
         w[pl.ds(pl.multiple_of(core * half, half), half), :] = w_a[...]
@@ -441,7 +437,7 @@
             grad_ref[m] = total.astype(jnp.bfloat16).reshape(lat_rows, lon_cols, channels)
             out_ref[m] = last_ref[m].reshape(lat_rows, lon_cols, channels)
 
-    return prep, maps, early, chain, finish
+    return prep, edges, maps, early, chain, finish
 
 
 def add_up(scale, mine, p1, p2, p3, out):
@@ -466,49 +462,39 @@
     cells = blocks * BAND * lon_cols
     win = 16 * lon_cols
     vmem = pl.BlockSpec(memory_space=pltpu.VMEM)
-    smem = pl.BlockSpec(memory_space=pltpu.SMEM)
     anywhere = pl.BlockSpec(memory_space=pltpu.HBM)
 
     def call(body, name, outs, ins, mib, gflops, scratch=(), far=()):
         return pl.pallas_call(
             body,
             out_shape=outs,
-            in_specs=[smem if a.ndim == 1 else anywhere if i in far else vmem for i, a in enumerate(ins)],
+            in_specs=[anywhere if i in far else vmem for i, a in enumerate(ins)],
             out_specs=(vmem,) * len(outs),
             scratch_shapes=list(scratch),
-            compiler_params=pltpu.CompilerParams(vmem_limit_bytes=mib * 1024 * 1024),
+            compiler_params=pltpu.CompilerParams(vmem_limit_bytes=int(mib * 1024 * 1024)),
             cost_estimate=pl.CostEstimate(flops=int(gflops * 1e9), bytes_accessed=4_000_000, transcendentals=0),
             name=name,
         )(*ins)
 
-    prep, maps, early, chain, finish = make_steps(lat_rows, lon_cols, blocks, members, channels, lat_devices)
-    idx = jnp.stack([lax.axis_index("segment"), lax.axis_index("lon"), lax.axis_index("lat")]).astype(jnp.int32)
+    prep, edges, maps, early, chain, finish = make_steps(lat_rows, lon_cols, blocks, members, channels, lat_devices)
     kernel = weights.reshape(width, channels)
-    both, tail, head, half = call(
-        prep,
-        "prep",
-        (
-            shape((members, 2 * own, channels), half_type),
-            shape((members, halo, channels), half_type),
-            shape((members, halo, channels), half_type),
-            shape((width // 2, channels), half_type),
-        ),
-        (idx, inputs, cotangent, kernel),
-        4,
-        0.5,
-        (pltpu.SemaphoreType.DMA,),
-        (3,),
-    )
+    half = lax.dynamic_slice_in_dim(kernel, lax.axis_index("lon") % 2 * (width // 2), width // 2, 0)
+    near_half = lax.ppermute(half, "segment", swap("segment", 1))
+    half, inputs, cotangent = lax.optimization_barrier((half, inputs, cotangent))
+    (both,) = call(prep, "prep", (shape((members, 2 * own, channels), half_type),), (inputs, cotangent), 4, 0.5)
+    sides_type = shape((members, halo, channels), half_type)
+    tail, head = call(edges, "edges", (sides_type, sides_type), (both,), 4, 0.2)
     up = [(i, i + 1) for i in range(lat_devices - 1)]
     down = [(i + 1, i) for i in range(lat_devices - 1)]
-    near_half = lax.ppermute(half, "segment", swap("segment", 1))
     both_y = lax.ppermute(both, "lon", swap("lon", 2))
     before = lax.ppermute(tail, "lat", up)
     after = lax.ppermute(head, "lat", down)
     sides = jnp.concatenate([before, after], axis=1)
+    sides, both_y = lax.optimization_barrier((sides, both_y))
     sides_y = lax.ppermute(sides, "lon", swap("lon", 2))
     b0 = jnp.concatenate([both, sides], axis=1)
     b1 = lax.ppermute(b0, "lon", swap("lon", 1))
+    b0, lat_step, lon_step, basis_values = lax.optimization_barrier((b0, lat_step, lon_step, basis_values))
     forward, again, backward = call(
         maps,
         "maps",
@@ -517,7 +503,7 @@
             shape((ns, BASIS * cells, blocks * win), half_type),
             shape((ns, blocks * win, BASIS * cells), half_type),
         ),
-        (idx, lat_step.T, lon_step.T, jnp.transpose(basis_values, (1, 2, 0))),
+        (lat_step.T, lon_step.T, jnp.transpose(basis_values, (1, 2, 0))),
         4,
         3.0,
         (pltpu.VMEM((48, lat_total), full_type),),
@@ -525,6 +511,7 @@
     b2 = jnp.concatenate([both_y, sides_y], axis=1)
     b2, forward = lax.optimization_barrier((b2, forward))
     b3 = lax.ppermute(b2, "lon", swap("lon", 1))
+    near_half, _ = lax.optimization_barrier((near_half, b2))
     far_half = lax.ppermute(near_half, "lon", swap("lon", 1))
     s_type = (members * nf * cells, width)
     s, left, slope, early_out = call(
@@ -536,7 +523,7 @@
             shape((members, blocks, own + edge, channels), half_type),
             shape((members, own, channels), half_type),
         ),
-        (idx, b0, b1, b2, b3, kernel, forward, again),
+        (b0, b1, b2, b3, kernel, forward, again),
         12,
         3.0,
         (pltpu.VMEM(s_type, half_type), pltpu.VMEM((members, blocks, own + 2 * edge, channels), half_type)),
@@ -552,7 +539,7 @@
             shape(lines, full_type),
         )
         + (shape(lines, half_type),) * 3,
-        (idx, b0, b1, b2, b3, kernel, near_half, far_half, again, backward, s, left, slope, early_out),
+        (b0, b1, b2, b3, kernel, near_half, far_half, again, backward, s, left, slope, early_out),
         18,
         6.0,
         (
@@ -565,7 +552,7 @@
             pltpu.VMEM((width // blocks * channels // 128, 128), full_type),
         ),
     )
-    got = [lax.ppermute(part, "lat", swap("lat", bit)) for bit, part in zip((1, 2, 3), parts)]
+    got = [lax.ppermute(part, "lat", swap("lat", bit)) for bit, part in reversed(list(zip((1, 2, 3), parts)))]
     block = (members, lat_rows, lon_cols, channels)
     grad, out = call(
         finish,

time: 51.8 us -> 48.8 us (0.942)
  local copies, waits for them, and re-layouts: 5.37 us -> 1.28 us
  waiting for transfers between devices: 12.6 us -> 16.3 us
  Pallas kernels: 17.4 us -> 15.3 us
    unnamed x16 -> x12, local copies, waits for them, and re-layouts: 5.36 us -> 0.03 us
    ppermute x1, waiting for transfers between devices: 0.01 us -> 4.32 us  [whole_ring(): after = lax.ppermute(head, 'lat', down)]
    ppermute x1, waiting for transfers between devices: 0.01 us -> 2.43 us  [whole_ring(): b1 = lax.ppermute(b0, 'lon', swap('lon', 1))]
    ppermute x1, waiting for transfers between devices: 3.87 us -> 1.69 us  [whole_ring(): near_half = lax.ppermute(half, 'segment', swap('segment', 1))]
    pallas_call x6 -> x7, Pallas kernels: 17.4 us -> 15.3 us  [call(): pl.pallas_call(body, out_shape=outs, in_specs=[anywhere if i in far else...]
    ppermute x1, starting transfers between devices: 3 us -> 1.49 us  [whole_ring(): near_half = lax.ppermute(half, 'segment', swap('segment', 1))]
    ppermute x1, starting transfers between devices: 1.58 us -> 3.03 us  [whole_ring(): both_y = lax.ppermute(both, 'lon', swap('lon', 2))]
    dynamic_slice x0 -> x1, local copies, waits for them, and re-layouts: none -> 1.24 us  [whole_ring(): lax.dynamic_slice_in_dim(kernel, lax.axis_index('lon') % 2 * (width // 2)...]
  transfers between devices with their start and end apart: 11 -> 11, of which waited for: 4 -> 8; matrix products, arithmetic and copies ran while one was open for 0% -> 0% of each run, Pallas kernels for 22% -> 21%
where the time goes in v5:
time: 48.8 us; the launch traced here: 48.6 us
  waiting for transfers between devices  16.3 us (33%)
  Pallas kernels  15.3 us (31%)
  starting transfers between devices  14.8 us (30%)
  local copies, waits for them, and re-layouts  1.28 us (3%)
  between operations  0.82 us (2%)
    pallas_call x7, Pallas kernels, call(): pl.pallas_call(body, out_shape=outs, in_specs=[anywhere if i in far else...  15.3 us
    ppermute x3, waiting for transfers between devices, whole_ring(): lax.ppermute(part, 'lat', swap('lat', bit))  5.33 us
    ppermute x3, starting transfers between devices, whole_ring(): lax.ppermute(part, 'lat', swap('lat', bit))  4.45 us
    ppermute x1, waiting for transfers between devices, whole_ring(): after = lax.ppermute(head, 'lat', down)  4.32 us
    ppermute x1, starting transfers between devices, whole_ring(): before = lax.ppermute(tail, 'lat', up)  3.49 us
    ppermute x1, starting transfers between devices, whole_ring(): both_y = lax.ppermute(both, 'lon', swap('lon', 2))  3.03 us
    ppermute x1, waiting for transfers between devices, whole_ring(): b1 = lax.ppermute(b0, 'lon', swap('lon', 1))  2.43 us
    ppermute x1, waiting for transfers between devices, whole_ring(): near_half = lax.ppermute(half, 'segment', swap('segment', 1))  1.69 us
  transfers between devices with their start and end apart: 11, of which 8 were waited for; matrix products, arithmetic and copies ran while one was open for 0% of the time, Pallas kernels for 21%

profile of v5, /device:TPU:0, one launch (start us, length us, event | category | flops | bytes accessed | tf_op | source)
XLA Modules:
  0.0 48.6 jit_solution(2825678015164152245)
XLA Ops:
  0.6 0.0 copy-start.2
  0.6 0.0 copy-start.1
  0.7 1.2 %constant_dynamic-slice_fusion = bf16[768,512]{1,0:T(8,128)(2,1)S(1)} fusion(bf16[1536,512]{1,0:T(8,128)(2,1)} %bitcast.7, s32[]{:T(128)S(6)} %select_n.11), kind=kLoop, calls=%fused_computation.3 | loop fusion | bytes 1572868 | tf_op jit(solution)/shard_map/dynamic_slice | solution.py:481
  1.9 0.0 copy-done.2
  1.9 0.0 copy-done.1
  1.9 0.0 copy-start.3
  1.9 0.0 copy-start.4
  2.0 0.0 copy-start.5
  2.0 3.0 %collective-permute-start.2 = (bf16[2,128,512]{2,1,0:T(8,128)(2,1)S(1)}, bf16[2,128,512]{2,1,0:T(8,128)(2,1)S(1)}, u32[]{:S(2)}, u32[]{:S(2)}) collective-permute-start(bf16[2,128,512]{2,1,0:T(8,128)(2,1)S(1)} %prep.1.both), channel_id=1, source_target_pairs={{0,16},{8,24},{16,0},{24,8},{1,17},{9,25},{17,1},{25,9},{2,18},{10... | collective-permute-start | bytes 786440 | tf_op jit(solution)/shard_map/ppermute | solution.py:489
  5.0 1.5 %collective-permute-start.6 = (bf16[768,512]{1,0:T(8,128)(2,1)S(1)}, bf16[768,512]{1,0:T(8,128)(2,1)S(1)}, u32[]{:S(2)}, u32[]{:S(2)}) collective-permute-start(bf16[768,512]{1,0:T(8,128)(2,1)S(1)} %constant_dynamic-slice_fusion), channel_id=1, source_target_pairs={{0,1},{1,0},{2,3},{3,2},{4,5},{5,4},{6,7},{7,6},{8,9},{9,8},{10,11... | collective-permute-start | bytes 2359304 | tf_op jit(solution)/shard_map/ppermute | solution.py:482
  6.6 3.5 %collective-permute-start = (bf16[2,48,512]{2,1,0:T(8,128)(2,1)S(1)}, bf16[2,48,512]{2,1,0:T(8,128)(2,1)S(1)}, u32[]{:S(2)}, u32[]{:S(2)}) collective-permute-start(bf16[2,48,512]{2,1,0:T(8,128)(2,1)S(1)} %get-tuple-element.34), channel_id=1, source_target_pairs={{0,2},{2,4},{4,6},{1,3},{3,5},{5,7},{8,10},{10,12},{12,14},{9,11},... | collective-permute-start | bytes 294920 | tf_op jit(solution)/shard_map/ppermute | solution.py:490
  10.0 1.3 %collective-permute-start.1 = (bf16[2,48,512]{2,1,0:T(8,128)(2,1)S(1)}, bf16[2,48,512]{2,1,0:T(8,128)(2,1)S(1)}, u32[]{:S(2)}, u32[]{:S(2)}) collective-permute-start(bf16[2,48,512]{2,1,0:T(8,128)(2,1)S(1)} %get-tuple-element.35), channel_id=1, source_target_pairs={{2,0},{4,2},{6,4},{3,1},{5,3},{7,5},{10,8},{12,10},{14,12},{11,9},... | collective-permute-start | bytes 294920 | tf_op jit(solution)/shard_map/ppermute | solution.py:491
  11.3 0.9 %collective-permute-done = bf16[2,48,512]{2,1,0:T(8,128)(2,1)S(1)} collective-permute-done((bf16[2,48,512]{2,1,0:T(8,128)(2,1)S(1)}, bf16[2,48,512]{2,1,0:T(8,128)(2,1)S(1)}, u32[]{:S(2)}, u32[]{:S(2)}) %collective-permute-start) | collective-permute-done | bytes 98336 | tf_op jit(solution)/shard_map/ppermute | solution.py:490
  12.2 4.3 %collective-permute-done.1 = bf16[2,48,512]{2,1,0:T(8,128)(2,1)S(1)} collective-permute-done((bf16[2,48,512]{2,1,0:T(8,128)(2,1)S(1)}, bf16[2,48,512]{2,1,0:T(8,128)(2,1)S(1)}, u32[]{:S(2)}, u32[]{:S(2)}) %collective-permute-start.1) | collective-permute-done | bytes 98336 | tf_op jit(solution)/shard_map/ppermute | solution.py:491
  16.6 0.0 collective-permute-done.2
  16.6 0.6 %collective-permute-start.4 = (bf16[2,96,512]{2,1,0:T(8,128)(2,1)S(1)}, bf16[2,96,512]{2,1,0:T(8,128)(2,1)S(1)}, u32[]{:S(2)}, u32[]{:S(2)}) collective-permute-start(bf16[2,96,512]{2,1,0:T(8,128)(2,1)S(1)} %pad_maximum_fusion.2), channel_id=1, source_target_pairs={{0,16},{8,24},{16,0},{24,8},{1,17},{9,25},{17,1},{25,9},{2,18},{10... | collective-permute-start | bytes 589832 | tf_op jit(solution)/shard_map/ppermute | solution.py:494
  17.2 0.0 copy-done.3
  17.2 0.0 copy-done.4
  17.2 0.0 copy-done.5
  17.2 0.0 copy-start
  17.2 4.1 %maps.1 = (bf16[4,384,256]{2,1,0:T(8,128)(2,1)S(1)}, bf16[3,384,256]{2,1,0:T(8,128)(2,1)S(1)}, bf16[3,256,384]{2,1,0:T(8,128)(2,1)S(1)}) custom-call(s32[9,64]{1,0:T(8,128)S(1)} %bitcast.12, s32[9,64]{1,0:T(8,128)S(1)} %bitcast.13, f32[9,3,64]{2,1,0:T(4,128)S(1)} %bitcast.11), custom_call_target="tpu_custom_call" | custom-call | flops 3000000000 | bytes 4000000 | tf_op jit(solution)/shard_map/maps/pallas_call | solution.py:468
  21.4 0.9 %collective-permute-done.4 = bf16[2,96,512]{2,1,0:T(8,128)(2,1)S(1)} collective-permute-done((bf16[2,96,512]{2,1,0:T(8,128)(2,1)S(1)}, bf16[2,96,512]{2,1,0:T(8,128)(2,1)S(1)}, u32[]{:S(2)}, u32[]{:S(2)}) %collective-permute-start.4) | collective-permute-done | bytes 196640 | tf_op jit(solution)/shard_map/ppermute | solution.py:494
  22.4 1.7 %collective-permute-done.6.w_a = bf16[768,512]{1,0:T(8,128)(2,1)S(1)} collective-permute-done((bf16[768,512]{1,0:T(8,128)(2,1)S(1)}, bf16[768,512]{1,0:T(8,128)(2,1)S(1)}, u32[]{:S(2)}, u32[]{:S(2)}) %collective-permute-start.6) | collective-permute-done | bytes 786464 | tf_op jit(solution)/shard_map/ppermute | solution.py:482
  24.0 0.0 collective-permute-start.7
  24.0 0.5 %collective-permute-start.3 = (bf16[2,224,512]{2,1,0:T(8,128)(2,1)S(1)}, bf16[2,224,512]{2,1,0:T(8,128)(2,1)S(1)}, u32[]{:S(2)}, u32[]{:S(2)}) collective-permute-start(bf16[2,224,512]{2,1,0:T(8,128)(2,1)S(1)} %pad_maximum_fusion.b0), channel_id=1, source_target_pairs={{0,8},{8,0},{16,24},{24,16},{1,9},{9,1},{17,25},{25,17},{2,10},{10... | collective-permute-start | bytes 1376264 | tf_op jit(solution)/shard_map/ppermute | solution.py:496
  24.6 0.0 collective-permute-start.5
  24.6 2.4 %collective-permute-done.3.b1 = bf16[2,224,512]{2,1,0:T(8,128)(2,1)S(1)} collective-permute-done((bf16[2,224,512]{2,1,0:T(8,128)(2,1)S(1)}, bf16[2,224,512]{2,1,0:T(8,128)(2,1)S(1)}, u32[]{:S(2)}, u32[]{:S(2)}) %collective-permute-start.3) | collective-permute-done | bytes 458784 | tf_op jit(solution)/shard_map/ppermute | solution.py:496
  27.0 0.7 %collective-permute-done.5.b3 = bf16[2,224,512]{2,1,0:T(8,128)(2,1)S(1)} collective-permute-done((bf16[2,224,512]{2,1,0:T(8,128)(2,1)S(1)}, bf16[2,224,512]{2,1,0:T(8,128)(2,1)S(1)}, u32[]{:S(2)}, u32[]{:S(2)}) %collective-permute-start.5) | collective-permute-done | bytes 458784 | tf_op jit(solution)/shard_map/ppermute | solution.py:513
  27.6 0.0 copy-done
  27.6 3.8 %early.1 = (bf16[1024,1536]{1,0:T(8,128)(2,1)S(1)}, bf16[512,384]{1,0:T(8,128)(2,1)S(1)}, bf16[2,4,96,512]{3,2,1,0:T(8,128)(2,1)S(1)}, bf16[2,64,512]{2,1,0:T(8,128)(2,1)S(1)}) custom-call(bf16[2,224,512]{2,1,0:T(8,128)(2,1)S(1)} %pad_maximum_fusion.b0, bf16[2,224,512]{2,1,0:T(8,128)(2,1)S(1)} %collective-permute-done.3.b1, ...), custom_call_target="tpu_custom_call" | custom-call | flops 3000000000 | bytes 4000000 | tf_op jit(solution)/shard_map/early/pallas_call | solution.py:468
  31.4 0.0 collective-permute-done.7.w_b
  31.4 4.2 %chain.1 = (bf16[2,64,512]{2,1,0:T(8,128)(2,1)S(1)}, bf16[2,64,512]{2,1,0:T(8,128)(2,1)S(1)}, bf16[768,512]{1,0:T(8,128)(2,1)S(1)}, f32[384,128]{1,0:T(8,128)S(1...) custom-call(bf16[2,224,512]{2,1,0:T(8,128)(2,1)S(1)} %pad_maximum_fusion.b0, ...), custom_call_target="tpu_custom_call" | custom-call | flops 6000000000 | bytes 4000000 | tf_op jit(solution)/shard_map/chain/pallas_call | solution.py:468
  35.6 3.7 %collective-permute-start.8 = (bf16[384,128]{1,0:T(8,128)(2,1)S(1)}, bf16[384,128]{1,0:T(8,128)(2,1)S(1)}, u32[]{:S(2)}, u32[]{:S(2)}) collective-permute-start(bf16[384,128]{1,0:T(8,128)(2,1)S(1)} %get-tuple-element.58), channel_id=1, source_target_pairs={{0,6},{2,4},{4,2},{6,0},{1,7},{3,5},{5,3},{7,1},{8,14},{10,12},{12... | collective-permute-start | bytes 294920 | tf_op jit(solution)/shard_map/ppermute | solution.py:555
  39.3 0.0 collective-permute-start.9
  39.3 0.8 %collective-permute-start.10 = (bf16[384,128]{1,0:T(8,128)(2,1)S(1)}, bf16[384,128]{1,0:T(8,128)(2,1)S(1)}, u32[]{:S(2)}, u32[]{:S(2)}) collective-permute-start(bf16[384,128]{1,0:T(8,128)(2,1)S(1)} %get-tuple-element.60), channel_id=1, source_target_pairs={{0,2},{2,0},{4,6},{6,4},{1,3},{3,1},{5,7},{7,5},{8,10},{10,8},{12,... | collective-permute-start | bytes 294920 | tf_op jit(solution)/shard_map/ppermute | solution.py:555
  40.1 2.5 %finish.1 = (bf16[2,16,4,512]{3,2,1,0:T(4,128)(2,1)}, bf16[2,16,4,512]{3,2,1,0:T(4,128)(2,1)}) custom-call(bf16[1536,512]{1,0:T(8,128)(2,1)S(1)} %bitcast.10, bf16[3,256,384]{2,1,0:T(8,128)(2,1)S(1)} %get-tuple-element.40.backward, bf16[768,512]{1,0:T(8,128)(2,1)S(1)} %get-tuple-element.52.gates, bf16[2,64,512]{2,1,0:T(8,128)(2,1)S(1)} %get-tuple-element.53.next_ref, ...), custom_call_target="tpu_custom_call" | custom-call | flops 2000000000 | bytes 4000000 | tf_op jit(solution)/shard_map/finish/pallas_call | solution.py:468
  42.5 0.7 %collective-permute-done.8.p1 = bf16[384,128]{1,0:T(8,128)(2,1)S(1)} collective-permute-done((bf16[384,128]{1,0:T(8,128)(2,1)S(1)}, bf16[384,128]{1,0:T(8,128)(2,1)S(1)}, u32[]{:S(2)}, u32[]{:S(2)}) %collective-permute-start.8) | collective-permute-done | bytes 98336 | tf_op jit(solution)/shard_map/ppermute | solution.py:555
  43.2 4.6 %collective-permute-done.9.p2 = bf16[384,128]{1,0:T(8,128)(2,1)S(1)} collective-permute-done((bf16[384,128]{1,0:T(8,128)(2,1)S(1)}, bf16[384,128]{1,0:T(8,128)(2,1)S(1)}, u32[]{:S(2)}, u32[]{:S(2)}) %collective-permute-start.9) | collective-permute-done | bytes 98336 | tf_op jit(solution)/shard_map/ppermute | solution.py:555
  47.9 0.0 collective-permute-done.10.p3
  47.9 0.7 %add_up.1 = f32[384,128]{1,0:T(8,128)} custom-call(f32[384,128]{1,0:T(8,128)S(1)} %get-tuple-element.57.mine, bf16[384,128]{1,0:T(8,128)(2,1)S(1)} %collective-permute-done.8.p1, bf16[384,128]{1,0:T(8,128)(2,1)S(1)} %collective-permute-done.9.p2, bf16[384,128]{1,0:T(8,128)(2,1)S(1)} %collective-permute-done.10.p3), custom_call_target="tpu_custom_call" | custom-call | flops 100000000 | bytes 4000000 | tf_op jit(solution)/shard_map/add_up/pallas_call | solution.py:468
  (5 shorter events, 0.1 us)
Async XLA Ops:
  0.6 1.3 %copy-start.2 = (bf16[2,16,4,512]{3,2,1,0:T(4,128)(2,1)S(1)}, bf16[2,16,4,512]{3,2,1,0:T(4,128)(2,1)}, u32[]{:S(2)}) copy-start(bf16[2,16,4,512]{3,2,1,0:T(4,128)(2,1)} %c) | copy-start | bytes 393220
  0.6 1.3 %copy-start.1 = (bf16[2,16,4,512]{3,2,1,0:T(4,128)(2,1)S(1)}, bf16[2,16,4,512]{3,2,1,0:T(4,128)(2,1)}, u32[]{:S(2)}) copy-start(bf16[2,16,4,512]{3,2,1,0:T(4,128)(2,1)} %x) | copy-start | bytes 393220
  1.9 15.3 %copy-start.3 = (f32[64,9,3]{0,2,1:T(4,128)S(1)}, f32[64,9,3]{0,2,1:T(4,128)}, u32[]{:S(2)}) copy-start(f32[64,9,3]{0,2,1:T(4,128)} %param.9) | copy-start | bytes 20740
  1.9 15.3 %copy-start.4 = (s32[64,9]{0,1:T(8,128)S(1)}, s32[64,9]{0,1:T(8,128)}, u32[]{:S(2)}) copy-start(s32[64,9]{0,1:T(8,128)} %param.10) | copy-start | bytes 6916
  2.0 15.3 %copy-start.5 = (s32[64,9]{0,1:T(8,128)S(1)}, s32[64,9]{0,1:T(8,128)}, u32[]{:S(2)}) copy-start(s32[64,9]{0,1:T(8,128)} %param.11) | copy-start | bytes 6916
  2.0 14.6 %collective-permute-start.2 = (bf16[2,128,512]{2,1,0:T(8,128)(2,1)S(1)}, bf16[2,128,512]{2,1,0:T(8,128)(2,1)S(1)}, u32[]{:S(2)}, u32[]{:S(2)}) collective-permute-start(bf16[2,128,512]{2,1,0:T(8,128)(2,1)S(1)} %prep.1.both), channel_id=1, source_target_pairs={{0,16},{8,24},{16,0},{24,8},{1,17},{9,25},{17,1},{25,9},{2,18},{10... | collective-permute-start | bytes 786440 | tf_op jit(solution)/shard_map/ppermute | solution.py:489
  5.0 19.0 %collective-permute-start.6 = (bf16[768,512]{1,0:T(8,128)(2,1)S(1)}, bf16[768,512]{1,0:T(8,128)(2,1)S(1)}, u32[]{:S(2)}, u32[]{:S(2)}) collective-permute-start(bf16[768,512]{1,0:T(8,128)(2,1)S(1)} %constant_dynamic-slice_fusion), channel_id=1, source_target_pairs={{0,1},{1,0},{2,3},{3,2},{4,5},{5,4},{6,7},{7,6},{8,9},{9,8},{10,11... | collective-permute-start | bytes 2359304 | tf_op jit(solution)/shard_map/ppermute | solution.py:482
  6.6 5.7 %collective-permute-start = (bf16[2,48,512]{2,1,0:T(8,128)(2,1)S(1)}, bf16[2,48,512]{2,1,0:T(8,128)(2,1)S(1)}, u32[]{:S(2)}, u32[]{:S(2)}) collective-permute-start(bf16[2,48,512]{2,1,0:T(8,128)(2,1)S(1)} %get-tuple-element.34), channel_id=1, source_target_pairs={{0,2},{2,4},{4,6},{1,3},{3,5},{5,7},{8,10},{10,12},{12,14},{9,11},... | collective-permute-start | bytes 294920 | tf_op jit(solution)/shard_map/ppermute | solution.py:490
  10.0 6.5 %collective-permute-start.1 = (bf16[2,48,512]{2,1,0:T(8,128)(2,1)S(1)}, bf16[2,48,512]{2,1,0:T(8,128)(2,1)S(1)}, u32[]{:S(2)}, u32[]{:S(2)}) collective-permute-start(bf16[2,48,512]{2,1,0:T(8,128)(2,1)S(1)} %get-tuple-element.35), channel_id=1, source_target_pairs={{2,0},{4,2},{6,4},{3,1},{5,3},{7,5},{10,8},{12,10},{14,12},{11,9},... | collective-permute-start | bytes 294920 | tf_op jit(solution)/shard_map/ppermute | solution.py:491
  16.6 5.7 %collective-permute-start.4 = (bf16[2,96,512]{2,1,0:T(8,128)(2,1)S(1)}, bf16[2,96,512]{2,1,0:T(8,128)(2,1)S(1)}, u32[]{:S(2)}, u32[]{:S(2)}) collective-permute-start(bf16[2,96,512]{2,1,0:T(8,128)(2,1)S(1)} %pad_maximum_fusion.2), channel_id=1, source_target_pairs={{0,16},{8,24},{16,0},{24,8},{1,17},{9,25},{17,1},{25,9},{2,18},{10... | collective-permute-start | bytes 589832 | tf_op jit(solution)/shard_map/ppermute | solution.py:494
  17.2 10.4 %copy-start = (bf16[1,3,512,512]{3,2,1,0:T(8,128)(2,1)S(1)}, bf16[1,3,512,512]{3,2,1,0:T(8,128)(2,1)}, u32[]{:S(2)}) copy-start(bf16[1,3,512,512]{3,2,1,0:T(8,128)(2,1)} %param.8) | copy-start | bytes 4718596
  24.0 7.4 %collective-permute-start.7 = (bf16[768,512]{1,0:T(8,128)(2,1)S(1)}, bf16[768,512]{1,0:T(8,128)(2,1)S(1)}, u32[]{:S(2)}, u32[]{:S(2)}) collective-permute-start(bf16[768,512]{1,0:T(8,128)(2,1)S(1)} %collective-permute-done.6.w_a), channel_id=1, source_target_pairs={{0,8},{8,0},{16,24},{24,16},{1,9},{9,1},{17,25},{25,17},{2,10},{10... | collective-permute-start | bytes 2359304 | tf_op jit(solution)/shard_map/ppermute | solution.py:515
  24.0 2.9 %collective-permute-start.3 = (bf16[2,224,512]{2,1,0:T(8,128)(2,1)S(1)}, bf16[2,224,512]{2,1,0:T(8,128)(2,1)S(1)}, u32[]{:S(2)}, u32[]{:S(2)}) collective-permute-start(bf16[2,224,512]{2,1,0:T(8,128)(2,1)S(1)} %pad_maximum_fusion.b0), channel_id=1, source_target_pairs={{0,8},{8,0},{16,24},{24,16},{1,9},{9,1},{17,25},{25,17},{2,10},{10... | collective-permute-start | bytes 1376264 | tf_op jit(solution)/shard_map/ppermute | solution.py:496
  24.6 3.1 %collective-permute-start.5 = (bf16[2,224,512]{2,1,0:T(8,128)(2,1)S(1)}, bf16[2,224,512]{2,1,0:T(8,128)(2,1)S(1)}, u32[]{:S(2)}, u32[]{:S(2)}) collective-permute-start(bf16[2,224,512]{2,1,0:T(8,128)(2,1)S(1)} %pad_maximum_fusion.1.b2), channel_id=1, source_target_pairs={{0,8},{8,0},{16,24},{24,16},{1,9},{9,1},{17,25},{25,17},{2,10},{10... | collective-permute-start | bytes 1376264 | tf_op jit(solution)/shard_map/ppermute | solution.py:513
  35.6 7.6 %collective-permute-start.8 = (bf16[384,128]{1,0:T(8,128)(2,1)S(1)}, bf16[384,128]{1,0:T(8,128)(2,1)S(1)}, u32[]{:S(2)}, u32[]{:S(2)}) collective-permute-start(bf16[384,128]{1,0:T(8,128)(2,1)S(1)} %get-tuple-element.58), channel_id=1, source_target_pairs={{0,6},{2,4},{4,2},{6,0},{1,7},{3,5},{5,3},{7,1},{8,14},{10,12},{12... | collective-permute-start | bytes 294920 | tf_op jit(solution)/shard_map/ppermute | solution.py:555
  39.3 8.6 %collective-permute-start.9 = (bf16[384,128]{1,0:T(8,128)(2,1)S(1)}, bf16[384,128]{1,0:T(8,128)(2,1)S(1)}, u32[]{:S(2)}, u32[]{:S(2)}) collective-permute-start(bf16[384,128]{1,0:T(8,128)(2,1)S(1)} %get-tuple-element.59), channel_id=1, source_target_pairs={{0,4},{2,6},{4,0},{6,2},{1,5},{3,7},{5,1},{7,3},{8,12},{10,14},{12... | collective-permute-start | bytes 294920 | tf_op jit(solution)/shard_map/ppermute | solution.py:555
  39.3 8.6 %collective-permute-start.10 = (bf16[384,128]{1,0:T(8,128)(2,1)S(1)}, bf16[384,128]{1,0:T(8,128)(2,1)S(1)}, u32[]{:S(2)}, u32[]{:S(2)}) collective-permute-start(bf16[384,128]{1,0:T(8,128)(2,1)S(1)} %get-tuple-element.60), channel_id=1, source_target_pairs={{0,2},{2,0},{4,6},{6,4},{1,3},{3,1},{5,7},{7,5},{8,10},{10,8},{12,... | collective-permute-start | bytes 294920 | tf_op jit(solution)/shard_map/ppermute | solution.py:555

commit v6 on v5

--- a/solution.py
+++ b/solution.py
@@ -332,14 +332,17 @@
             for i in range(members * ns):
                 feat[(i * BASIS + b) * cells : (i * BASIS + b + 1) * cells, :] = got[i * cells : (i + 1) * cells]
 
-    def chain(b0, b1, b2, b3, w_own, w_a, w_b, again, backward, s, left0, slope, early_out,
+    def chain(b0, b1, b2, b3, w_own, near_half, far_half, ends, again, backward, s, left0, slope, early_out,
               out_ref, next_ref, gate_ref, own_ref, p1, p2, p3, w, s1, mid, gates, feat, pull, grads):
         blk = (b0, b1, b2, b3)
         seg, lon, lat = lax.axis_index("segment"), lax.axis_index("lon"), lax.axis_index("lat")
-        half = w_a.shape[0]
-        core = lon % 2
-        w[pl.ds(pl.multiple_of(core * half, half), half), :] = w_a[...]
-        w[pl.ds(pl.multiple_of((1 - core) * half, half), half), :] = w_b[...]
+        here = lon % 2 * (width // 2)
+        there = width // 2 - here
+        rows, rest = near_half.shape[0], ends.shape[0] // 2
+        for base, ref in ((here, near_half), (there, far_half)):
+            w[pl.ds(pl.multiple_of(base, 32), rows), :] = ref[...]
+        w[rows : rows + rest, :] = ends[:rest]
+        w[width - rest :, :] = ends[rest:]
 
         def coming_at(m, g):
             return take(blk, m, coming_parts, g * band, (g + 1) * band).astype(jnp.float32)
@@ -472,18 +475,22 @@
             out_specs=(vmem,) * len(outs),
             scratch_shapes=list(scratch),
             compiler_params=pltpu.CompilerParams(vmem_limit_bytes=int(mib * 1024 * 1024)),
-            cost_estimate=pl.CostEstimate(flops=int(gflops * 1e9), bytes_accessed=4_000_000, transcendentals=0),
+            cost_estimate=pl.CostEstimate(flops=int(gflops * 1e9), bytes_accessed=int(gflops * 1e6), transcendentals=0),
             name=name,
         )(*ins)
 
     prep, edges, maps, early, chain, finish = make_steps(lat_rows, lon_cols, blocks, members, channels, lat_devices)
     kernel = weights.reshape(width, channels)
-    half = lax.dynamic_slice_in_dim(kernel, lax.axis_index("lon") % 2 * (width // 2), width // 2, 0)
+    rest = width // 2 // 12
+    rows = width // 2 - rest
+    half = lax.dynamic_slice_in_dim(kernel, lax.axis_index("lon") % 2 * (width // 2), rows, 0)
+    ends = jnp.concatenate([kernel[rows : rows + rest], kernel[width - rest :]], axis=0)
     near_half = lax.ppermute(half, "segment", swap("segment", 1))
+    near_ends = lax.ppermute(ends, "segment", swap("segment", 1))
     half, inputs, cotangent = lax.optimization_barrier((half, inputs, cotangent))
-    (both,) = call(prep, "prep", (shape((members, 2 * own, channels), half_type),), (inputs, cotangent), 4, 0.5)
+    (both,) = call(prep, "prep", (shape((members, 2 * own, channels), half_type),), (inputs, cotangent), 4, 0.0)
     sides_type = shape((members, halo, channels), half_type)
-    tail, head = call(edges, "edges", (sides_type, sides_type), (both,), 4, 0.2)
+    tail, head = call(edges, "edges", (sides_type, sides_type), (both,), 4, 0.0)
     up = [(i, i + 1) for i in range(lat_devices - 1)]
     down = [(i + 1, i) for i in range(lat_devices - 1)]
     both_y = lax.ppermute(both, "lon", swap("lon", 2))
@@ -505,13 +512,12 @@
         ),
         (lat_step.T, lon_step.T, jnp.transpose(basis_values, (1, 2, 0))),
         4,
-        3.0,
+        0.0,
         (pltpu.VMEM((48, lat_total), full_type),),
     )
     b2 = jnp.concatenate([both_y, sides_y], axis=1)
-    b2, forward = lax.optimization_barrier((b2, forward))
+    b2, forward, near_half = lax.optimization_barrier((b2, forward, near_half))
     b3 = lax.ppermute(b2, "lon", swap("lon", 1))
-    near_half, _ = lax.optimization_barrier((near_half, b2))
     far_half = lax.ppermute(near_half, "lon", swap("lon", 1))
     s_type = (members * nf * cells, width)
     s, left, slope, early_out = call(
@@ -528,6 +534,7 @@
         3.0,
         (pltpu.VMEM(s_type, half_type), pltpu.VMEM((members, blocks, own + 2 * edge, channels), half_type)),
     )
+    near_ends, s = lax.optimization_barrier((near_ends, s))
     lines = (width // blocks // lat_devices * channels // 128, 128)
     out, follow, gates, mine, *parts = call(
         chain,
@@ -539,7 +546,7 @@
             shape(lines, full_type),
         )
         + (shape(lines, half_type),) * 3,
-        (b0, b1, b2, b3, kernel, near_half, far_half, again, backward, s, left, slope, early_out),
+        (b0, b1, b2, b3, kernel, near_half, far_half, near_ends, again, backward, s, left, slope, early_out),
         18,
         6.0,
         (

time: 48.8 us -> 47.2 us (0.967)
  waiting for transfers between devices: 16.3 us -> 12.1 us
  local copies, waits for them, and re-layouts: 1.28 us -> 3.01 us
  starting transfers between devices: 14.8 us -> 15.6 us
    ppermute x1, waiting for transfers between devices: 2.43 us -> 0.01 us  [whole_ring(): b1 = lax.ppermute(b0, 'lon', swap('lon', 1))]
    unnamed x12, local copies, waits for them, and re-layouts: 0.03 us -> 1.83 us
    ppermute x1, waiting for transfers between devices: 1.69 us -> 0.01 us  [whole_ring(): near_half = lax.ppermute(half, 'segment', swap('segment', 1))]
    ppermute x1, starting transfers between devices: 1.49 us -> 3 us  [whole_ring(): near_half = lax.ppermute(half, 'segment', swap('segment', 1))]
    ppermute x1, starting transfers between devices: 3.03 us -> 1.58 us  [whole_ring(): both_y = lax.ppermute(both, 'lon', swap('lon', 2))]
    ppermute x0 -> x1, starting transfers between devices: none -> 0.6 us  [whole_ring(): near_ends = lax.ppermute(ends, 'segment', swap('segment', 1))]
    ppermute x1, starting transfers between devices: 0.01 us -> 0.5 us  [whole_ring(): far_half = lax.ppermute(near_half, 'lon', swap('lon', 1))]
  transfers between devices with their start and end apart: 11 -> 12, of which waited for: 8 -> 7; matrix products, arithmetic and copies ran while one was open for 0% -> 0% of each run, Pallas kernels for 21% -> 22%
where the time goes in v6:
time: 47.2 us; the launch traced here: 47 us
  starting transfers between devices  15.6 us (33%)
  Pallas kernels  15.3 us (32%)
  waiting for transfers between devices  12.1 us (26%)
  local copies, waits for them, and re-layouts  3.01 us (6%)
  between operations  0.81 us (2%)
    pallas_call x7, Pallas kernels, call(): pl.pallas_call(body, out_shape=outs, in_specs=[anywhere if i in far else...  15.3 us
    ppermute x3, waiting for transfers between devices, whole_ring(): lax.ppermute(part, 'lat', swap('lat', bit))  4.88 us
    ppermute x3, starting transfers between devices, whole_ring(): lax.ppermute(part, 'lat', swap('lat', bit))  4.45 us
    ppermute x1, waiting for transfers between devices, whole_ring(): after = lax.ppermute(head, 'lat', down)  4.32 us
    ppermute x1, starting transfers between devices, whole_ring(): before = lax.ppermute(tail, 'lat', up)  3.49 us
    ppermute x1, starting transfers between devices, whole_ring(): near_half = lax.ppermute(half, 'segment', swap('segment', 1))  3 us
    unnamed x12, local copies, waits for them, and re-layouts  1.83 us
    ppermute x1, starting transfers between devices, whole_ring(): both_y = lax.ppermute(both, 'lon', swap('lon', 2))  1.58 us
  transfers between devices with their start and end apart: 12, of which 7 were waited for; matrix products, arithmetic and copies ran while one was open for 0% of the time, Pallas kernels for 22%

profile of v6, /device:TPU:0, one launch (start us, length us, event | category | flops | bytes accessed | tf_op | source)
XLA Modules:
  0.0 47.0 jit_solution(6234976475718709107)
XLA Ops:
  0.6 0.0 copy-start.3
  0.7 0.0 copy-start.4
  0.7 0.0 copy-start.5
  0.7 1.2 %constant_dynamic-slice_fusion = bf16[704,512]{1,0:T(8,128)(2,1)S(1)} fusion(bf16[1536,512]{1,0:T(8,128)(2,1)} %bitcast.7, s32[]{:T(128)S(6)} %select_n.11), kind=kLoop, calls=%fused_computation.4 | loop fusion | bytes 1441796 | tf_op jit(solution)/shard_map/dynamic_slice | solution.py:486
  1.9 0.0 copy-start
  1.9 3.0 %collective-permute-start.5 = (bf16[704,512]{1,0:T(8,128)(2,1)S(1)}, bf16[704,512]{1,0:T(8,128)(2,1)S(1)}, u32[]{:S(2)}, u32[]{:S(2)}) collective-permute-start(bf16[704,512]{1,0:T(8,128)(2,1)S(1)} %constant_dynamic-slice_fusion), channel_id=1, source_target_pairs={{0,1},{1,0},{2,3},{3,2},{4,5},{5,4},{6,7},{7,6},{8,9},{9,8},{10,11... | collective-permute-start | bytes 2162696 | tf_op jit(solution)/shard_map/ppermute | solution.py:488
  4.9 0.0 copy-start.1
  4.9 0.9 %copy-done.1 = bf16[2,16,4,512]{3,2,1,0:T(4,128)(2,1)S(1)} copy-done((bf16[2,16,4,512]{3,2,1,0:T(4,128)(2,1)S(1)}, bf16[2,16,4,512]{3,2,1,0:T(4,128)(2,1)}, u32[]{:S(2)}) %copy-start.1) | copy-done | bytes 131096
  5.8 0.0 copy-start.2
  5.8 0.9 %copy-done.2 = bf16[2,16,4,512]{3,2,1,0:T(4,128)(2,1)S(1)} copy-done((bf16[2,16,4,512]{3,2,1,0:T(4,128)(2,1)S(1)}, bf16[2,16,4,512]{3,2,1,0:T(4,128)(2,1)}, u32[]{:S(2)}) %copy-start.2) | copy-done | bytes 131096
  6.7 1.6 %collective-permute-start.2 = (bf16[2,128,512]{2,1,0:T(8,128)(2,1)S(1)}, bf16[2,128,512]{2,1,0:T(8,128)(2,1)S(1)}, u32[]{:S(2)}, u32[]{:S(2)}) collective-permute-start(bf16[2,128,512]{2,1,0:T(8,128)(2,1)S(1)} %prep.1.both), channel_id=1, source_target_pairs={{0,16},{8,24},{16,0},{24,8},{1,17},{9,25},{17,1},{25,9},{2,18},{10... | collective-permute-start | bytes 786440 | tf_op jit(solution)/shard_map/ppermute | solution.py:496
  8.3 3.5 %collective-permute-start = (bf16[2,48,512]{2,1,0:T(8,128)(2,1)S(1)}, bf16[2,48,512]{2,1,0:T(8,128)(2,1)S(1)}, u32[]{:S(2)}, u32[]{:S(2)}) collective-permute-start(bf16[2,48,512]{2,1,0:T(8,128)(2,1)S(1)} %get-tuple-element.36), channel_id=1, source_target_pairs={{0,2},{2,4},{4,6},{1,3},{3,5},{5,7},{8,10},{10,12},{12,14},{9,11},... | collective-permute-start | bytes 294920 | tf_op jit(solution)/shard_map/ppermute | solution.py:497
  11.8 1.3 %collective-permute-start.1 = (bf16[2,48,512]{2,1,0:T(8,128)(2,1)S(1)}, bf16[2,48,512]{2,1,0:T(8,128)(2,1)S(1)}, u32[]{:S(2)}, u32[]{:S(2)}) collective-permute-start(bf16[2,48,512]{2,1,0:T(8,128)(2,1)S(1)} %get-tuple-element.37), channel_id=1, source_target_pairs={{2,0},{4,2},{6,4},{3,1},{5,3},{7,5},{10,8},{12,10},{14,12},{11,9},... | collective-permute-start | bytes 294920 | tf_op jit(solution)/shard_map/ppermute | solution.py:498
  13.1 0.9 %collective-permute-done = bf16[2,48,512]{2,1,0:T(8,128)(2,1)S(1)} collective-permute-done((bf16[2,48,512]{2,1,0:T(8,128)(2,1)S(1)}, bf16[2,48,512]{2,1,0:T(8,128)(2,1)S(1)}, u32[]{:S(2)}, u32[]{:S(2)}) %collective-permute-start) | collective-permute-done | bytes 98336 | tf_op jit(solution)/shard_map/ppermute | solution.py:497
  14.0 4.3 %collective-permute-done.1 = bf16[2,48,512]{2,1,0:T(8,128)(2,1)S(1)} collective-permute-done((bf16[2,48,512]{2,1,0:T(8,128)(2,1)S(1)}, bf16[2,48,512]{2,1,0:T(8,128)(2,1)S(1)}, u32[]{:S(2)}, u32[]{:S(2)}) %collective-permute-start.1) | collective-permute-done | bytes 98336 | tf_op jit(solution)/shard_map/ppermute | solution.py:498
  18.3 0.0 collective-permute-done.2
  18.3 0.6 %collective-permute-start.4 = (bf16[2,96,512]{2,1,0:T(8,128)(2,1)S(1)}, bf16[2,96,512]{2,1,0:T(8,128)(2,1)S(1)}, u32[]{:S(2)}, u32[]{:S(2)}) collective-permute-start(bf16[2,96,512]{2,1,0:T(8,128)(2,1)S(1)} %pad_maximum_fusion.2), channel_id=1, source_target_pairs={{0,16},{8,24},{16,0},{24,8},{1,17},{9,25},{17,1},{25,9},{2,18},{10... | collective-permute-start | bytes 589832 | tf_op jit(solution)/shard_map/ppermute | solution.py:501
  19.0 0.1 collective-permute-start.3
  19.0 0.0 copy-done.3
  19.0 0.0 copy-done.4
  19.1 0.0 copy-done.5
  19.1 4.1 %maps.1 = (bf16[4,384,256]{2,1,0:T(8,128)(2,1)S(1)}, bf16[3,384,256]{2,1,0:T(8,128)(2,1)S(1)}, bf16[3,256,384]{2,1,0:T(8,128)(2,1)S(1)}) custom-call(s32[9,64]{1,0:T(8,128)S(1)} %bitcast.13, s32[9,64]{1,0:T(8,128)S(1)} %bitcast.14, f32[9,3,64]{2,1,0:T(4,128)S(1)} %bitcast.12), custom_call_target="tpu_custom_call" | custom-call | tf_op jit(solution)/shard_map/maps/pallas_call | solution.py:471
  23.2 0.9 %collective-permute-done.4 = bf16[2,96,512]{2,1,0:T(8,128)(2,1)S(1)} collective-permute-done((bf16[2,96,512]{2,1,0:T(8,128)(2,1)S(1)}, bf16[2,96,512]{2,1,0:T(8,128)(2,1)S(1)}, u32[]{:S(2)}, u32[]{:S(2)}) %collective-permute-start.4) | collective-permute-done | bytes 196640 | tf_op jit(solution)/shard_map/ppermute | solution.py:501
  24.1 0.0 collective-permute-done.5.near_half
  24.1 0.1 collective-permute-start.6
  24.2 0.5 %collective-permute-start.7 = (bf16[704,512]{1,0:T(8,128)(2,1)S(1)}, bf16[704,512]{1,0:T(8,128)(2,1)S(1)}, u32[]{:S(2)}, u32[]{:S(2)}) collective-permute-start(bf16[704,512]{1,0:T(8,128)(2,1)S(1)} %collective-permute-done.5.near_half), channel_id=1, source_target_pairs={{0,8},{8,0},{16,24},{24,16},{1,9},{9,1},{17,25},{25,17},{2,10},{10... | collective-permute-start | bytes 2162696 | tf_op jit(solution)/shard_map/ppermute | solution.py:521
  24.7 0.0 copy-done
  24.7 0.6 %collective-permute-start.8 = (bf16[128,512]{1,0:T(8,128)(2,1)S(1)}, bf16[128,512]{1,0:T(8,128)(2,1)S(1)}, u32[]{:S(2)}, u32[]{:S(2)}) collective-permute-start(bf16[128,512]{1,0:T(8,128)(2,1)S(1)} %pad_maximum_fusion.3), channel_id=1, source_target_pairs={{0,1},{1,0},{2,3},{3,2},{4,5},{5,4},{6,7},{7,6},{8,9},{9,8},{10,11... | collective-permute-start | bytes 393224 | tf_op jit(solution)/shard_map/ppermute | solution.py:489
  25.3 0.0 collective-permute-done.3.b1
  25.3 0.7 %collective-permute-done.6.b3 = bf16[2,224,512]{2,1,0:T(8,128)(2,1)S(1)} collective-permute-done((bf16[2,224,512]{2,1,0:T(8,128)(2,1)S(1)}, bf16[2,224,512]{2,1,0:T(8,128)(2,1)S(1)}, u32[]{:S(2)}, u32[]{:S(2)}) %collective-permute-start.6) | collective-permute-done | bytes 458784 | tf_op jit(solution)/shard_map/ppermute | solution.py:520
  26.0 3.8 %early.1 = (bf16[1024,1536]{1,0:T(8,128)(2,1)S(1)}, bf16[512,384]{1,0:T(8,128)(2,1)S(1)}, bf16[2,4,96,512]{3,2,1,0:T(8,128)(2,1)S(1)}, bf16[2,64,512]{2,1,0:T(8,128)(2,1)S(1)}) custom-call(bf16[2,224,512]{2,1,0:T(8,128)(2,1)S(1)} %pad_maximum_fusion.b0, bf16[2,224,512]{2,1,0:T(8,128)(2,1)S(1)} %collective-permute-done.3.b1, ...), custom_call_target="tpu_custom_call" | custom-call | flops 3000000000 | bytes 3000000 | tf_op jit(solution)/shard_map/early/pallas_call | solution.py:471
  29.8 0.5 %collective-permute-done.8.ends = bf16[128,512]{1,0:T(8,128)(2,1)S(1)} collective-permute-done((bf16[128,512]{1,0:T(8,128)(2,1)S(1)}, bf16[128,512]{1,0:T(8,128)(2,1)S(1)}, u32[]{:S(2)}, u32[]{:S(2)}) %collective-permute-start.8) | collective-permute-done | bytes 131104 | tf_op jit(solution)/shard_map/ppermute | solution.py:489
  30.3 0.0 collective-permute-done.7.far_half
  30.3 4.2 %chain.1 = (bf16[2,64,512]{2,1,0:T(8,128)(2,1)S(1)}, bf16[2,64,512]{2,1,0:T(8,128)(2,1)S(1)}, bf16[768,512]{1,0:T(8,128)(2,1)S(1)}, f32[384,128]{1,0:T(8,128)S(1...) custom-call(bf16[2,224,512]{2,1,0:T(8,128)(2,1)S(1)} %pad_maximum_fusion.b0, ...), custom_call_target="tpu_custom_call" | custom-call | flops 6000000000 | bytes 6000000 | tf_op jit(solution)/shard_map/chain/pallas_call | solution.py:471
  34.5 1.7 %collective-permute-start.9 = (bf16[384,128]{1,0:T(8,128)(2,1)S(1)}, bf16[384,128]{1,0:T(8,128)(2,1)S(1)}, u32[]{:S(2)}, u32[]{:S(2)}) collective-permute-start(bf16[384,128]{1,0:T(8,128)(2,1)S(1)} %get-tuple-element.62), channel_id=1, source_target_pairs={{0,6},{2,4},{4,2},{6,0},{1,7},{3,5},{5,3},{7,1},{8,14},{10,12},{12... | collective-permute-start | bytes 294920 | tf_op jit(solution)/shard_map/ppermute | solution.py:562
  36.2 1.4 %collective-permute-start.10 = (bf16[384,128]{1,0:T(8,128)(2,1)S(1)}, bf16[384,128]{1,0:T(8,128)(2,1)S(1)}, u32[]{:S(2)}, u32[]{:S(2)}) collective-permute-start(bf16[384,128]{1,0:T(8,128)(2,1)S(1)} %get-tuple-element.63), channel_id=1, source_target_pairs={{0,4},{2,6},{4,0},{6,2},{1,5},{3,7},{5,1},{7,3},{8,12},{10,14},{12... | collective-permute-start | bytes 294920 | tf_op jit(solution)/shard_map/ppermute | solution.py:562
  37.6 1.4 %collective-permute-start.11 = (bf16[384,128]{1,0:T(8,128)(2,1)S(1)}, bf16[384,128]{1,0:T(8,128)(2,1)S(1)}, u32[]{:S(2)}, u32[]{:S(2)}) collective-permute-start(bf16[384,128]{1,0:T(8,128)(2,1)S(1)} %get-tuple-element.64), channel_id=1, source_target_pairs={{0,2},{2,0},{4,6},{6,4},{1,3},{3,1},{5,7},{7,5},{8,10},{10,8},{12,... | collective-permute-start | bytes 294920 | tf_op jit(solution)/shard_map/ppermute | solution.py:562
  38.9 2.5 %finish.1 = (bf16[2,16,4,512]{3,2,1,0:T(4,128)(2,1)}, bf16[2,16,4,512]{3,2,1,0:T(4,128)(2,1)}) custom-call(bf16[1536,512]{1,0:T(8,128)(2,1)S(1)} %bitcast.11, bf16[3,256,384]{2,1,0:T(8,128)(2,1)S(1)} %get-tuple-element.42.backward, bf16[768,512]{1,0:T(8,128)(2,1)S(1)} %get-tuple-element.56.gates, bf16[2,64,512]{2,1,0:T(8,128)(2,1)S(1)} %get-tuple-element.57.next_ref, ...), custom_call_target="tpu_custom_call" | custom-call | flops 2000000000 | bytes 2000000 | tf_op jit(solution)/shard_map/finish/pallas_call | solution.py:471
  41.4 0.6 %collective-permute-done.9.p1 = bf16[384,128]{1,0:T(8,128)(2,1)S(1)} collective-permute-done((bf16[384,128]{1,0:T(8,128)(2,1)S(1)}, bf16[384,128]{1,0:T(8,128)(2,1)S(1)}, u32[]{:S(2)}, u32[]{:S(2)}) %collective-permute-start.9) | collective-permute-done | bytes 98336 | tf_op jit(solution)/shard_map/ppermute | solution.py:562
  41.9 4.3 %collective-permute-done.10.p2 = bf16[384,128]{1,0:T(8,128)(2,1)S(1)} collective-permute-done((bf16[384,128]{1,0:T(8,128)(2,1)S(1)}, bf16[384,128]{1,0:T(8,128)(2,1)S(1)}, u32[]{:S(2)}, u32[]{:S(2)}) %collective-permute-start.10) | collective-permute-done | bytes 98336 | tf_op jit(solution)/shard_map/ppermute | solution.py:562
  46.2 0.0 collective-permute-done.11.p3
  46.2 0.7 %add_up.1 = f32[384,128]{1,0:T(8,128)} custom-call(f32[384,128]{1,0:T(8,128)S(1)} %get-tuple-element.61.mine, bf16[384,128]{1,0:T(8,128)(2,1)S(1)} %collective-permute-done.9.p1, bf16[384,128]{1,0:T(8,128)(2,1)S(1)} %collective-permute-done.10.p2, bf16[384,128]{1,0:T(8,128)(2,1)S(1)} %collective-permute-done.11.p3), custom_call_target="tpu_custom_call" | custom-call | flops 100000000 | bytes 100000 | tf_op jit(solution)/shard_map/add_up/pallas_call | solution.py:471
  (7 shorter events, 0.1 us)
Async XLA Ops:
  0.6 18.4 %copy-start.3 = (f32[64,9,3]{0,2,1:T(4,128)S(1)}, f32[64,9,3]{0,2,1:T(4,128)}, u32[]{:S(2)}) copy-start(f32[64,9,3]{0,2,1:T(4,128)} %param.9) | copy-start | bytes 20740
  0.7 18.4 %copy-start.4 = (s32[64,9]{0,1:T(8,128)S(1)}, s32[64,9]{0,1:T(8,128)}, u32[]{:S(2)}) copy-start(s32[64,9]{0,1:T(8,128)} %param.10) | copy-start | bytes 6916
  0.7 18.4 %copy-start.5 = (s32[64,9]{0,1:T(8,128)S(1)}, s32[64,9]{0,1:T(8,128)}, u32[]{:S(2)}) copy-start(s32[64,9]{0,1:T(8,128)} %param.11) | copy-start | bytes 6916
  1.9 22.9 %copy-start = (bf16[1,3,512,512]{3,2,1,0:T(8,128)(2,1)S(1)}, bf16[1,3,512,512]{3,2,1,0:T(8,128)(2,1)}, u32[]{:S(2)}) copy-start(bf16[1,3,512,512]{3,2,1,0:T(8,128)(2,1)} %param.8) | copy-start | bytes 4718596
  1.9 22.3 %collective-permute-start.5 = (bf16[704,512]{1,0:T(8,128)(2,1)S(1)}, bf16[704,512]{1,0:T(8,128)(2,1)S(1)}, u32[]{:S(2)}, u32[]{:S(2)}) collective-permute-start(bf16[704,512]{1,0:T(8,128)(2,1)S(1)} %constant_dynamic-slice_fusion), channel_id=1, source_target_pairs={{0,1},{1,0},{2,3},{3,2},{4,5},{5,4},{6,7},{7,6},{8,9},{9,8},{10,11... | collective-permute-start | bytes 2162696 | tf_op jit(solution)/shard_map/ppermute | solution.py:488
  4.9 0.9 %copy-start.1 = (bf16[2,16,4,512]{3,2,1,0:T(4,128)(2,1)S(1)}, bf16[2,16,4,512]{3,2,1,0:T(4,128)(2,1)}, u32[]{:S(2)}) copy-start(bf16[2,16,4,512]{3,2,1,0:T(4,128)(2,1)} %x) | copy-start | bytes 393220
  5.8 0.9 %copy-start.2 = (bf16[2,16,4,512]{3,2,1,0:T(4,128)(2,1)S(1)}, bf16[2,16,4,512]{3,2,1,0:T(4,128)(2,1)}, u32[]{:S(2)}) copy-start(bf16[2,16,4,512]{3,2,1,0:T(4,128)(2,1)} %c) | copy-start | bytes 393220
  6.7 11.6 %collective-permute-start.2 = (bf16[2,128,512]{2,1,0:T(8,128)(2,1)S(1)}, bf16[2,128,512]{2,1,0:T(8,128)(2,1)S(1)}, u32[]{:S(2)}, u32[]{:S(2)}) collective-permute-start(bf16[2,128,512]{2,1,0:T(8,128)(2,1)S(1)} %prep.1.both), channel_id=1, source_target_pairs={{0,16},{8,24},{16,0},{24,8},{1,17},{9,25},{17,1},{25,9},{2,18},{10... | collective-permute-start | bytes 786440 | tf_op jit(solution)/shard_map/ppermute | solution.py:496
  8.3 5.7 %collective-permute-start = (bf16[2,48,512]{2,1,0:T(8,128)(2,1)S(1)}, bf16[2,48,512]{2,1,0:T(8,128)(2,1)S(1)}, u32[]{:S(2)}, u32[]{:S(2)}) collective-permute-start(bf16[2,48,512]{2,1,0:T(8,128)(2,1)S(1)} %get-tuple-element.36), channel_id=1, source_target_pairs={{0,2},{2,4},{4,6},{1,3},{3,5},{5,7},{8,10},{10,12},{12,14},{9,11},... | collective-permute-start | bytes 294920 | tf_op jit(solution)/shard_map/ppermute | solution.py:497
  11.8 6.5 %collective-permute-start.1 = (bf16[2,48,512]{2,1,0:T(8,128)(2,1)S(1)}, bf16[2,48,512]{2,1,0:T(8,128)(2,1)S(1)}, u32[]{:S(2)}, u32[]{:S(2)}) collective-permute-start(bf16[2,48,512]{2,1,0:T(8,128)(2,1)S(1)} %get-tuple-element.37), channel_id=1, source_target_pairs={{2,0},{4,2},{6,4},{3,1},{5,3},{7,5},{10,8},{12,10},{14,12},{11,9},... | collective-permute-start | bytes 294920 | tf_op jit(solution)/shard_map/ppermute | solution.py:498
  18.3 5.7 %collective-permute-start.4 = (bf16[2,96,512]{2,1,0:T(8,128)(2,1)S(1)}, bf16[2,96,512]{2,1,0:T(8,128)(2,1)S(1)}, u32[]{:S(2)}, u32[]{:S(2)}) collective-permute-start(bf16[2,96,512]{2,1,0:T(8,128)(2,1)S(1)} %pad_maximum_fusion.2), channel_id=1, source_target_pairs={{0,16},{8,24},{16,0},{24,8},{1,17},{9,25},{17,1},{25,9},{2,18},{10... | collective-permute-start | bytes 589832 | tf_op jit(solution)/shard_map/ppermute | solution.py:501
  19.0 6.4 %collective-permute-start.3 = (bf16[2,224,512]{2,1,0:T(8,128)(2,1)S(1)}, bf16[2,224,512]{2,1,0:T(8,128)(2,1)S(1)}, u32[]{:S(2)}, u32[]{:S(2)}) collective-permute-start(bf16[2,224,512]{2,1,0:T(8,128)(2,1)S(1)} %pad_maximum_fusion.b0), channel_id=1, source_target_pairs={{0,8},{8,0},{16,24},{24,16},{1,9},{9,1},{17,25},{25,17},{2,10},{10... | collective-permute-start | bytes 1376264 | tf_op jit(solution)/shard_map/ppermute | solution.py:503
  24.1 1.9 %collective-permute-start.6 = (bf16[2,224,512]{2,1,0:T(8,128)(2,1)S(1)}, bf16[2,224,512]{2,1,0:T(8,128)(2,1)S(1)}, u32[]{:S(2)}, u32[]{:S(2)}) collective-permute-start(bf16[2,224,512]{2,1,0:T(8,128)(2,1)S(1)} %pad_maximum_fusion.1.b2), channel_id=1, source_target_pairs={{0,8},{8,0},{16,24},{24,16},{1,9},{9,1},{17,25},{25,17},{2,10},{10... | collective-permute-start | bytes 1376264 | tf_op jit(solution)/shard_map/ppermute | solution.py:520
  24.2 6.1 %collective-permute-start.7 = (bf16[704,512]{1,0:T(8,128)(2,1)S(1)}, bf16[704,512]{1,0:T(8,128)(2,1)S(1)}, u32[]{:S(2)}, u32[]{:S(2)}) collective-permute-start(bf16[704,512]{1,0:T(8,128)(2,1)S(1)} %collective-permute-done.5.near_half), channel_id=1, source_target_pairs={{0,8},{8,0},{16,24},{24,16},{1,9},{9,1},{17,25},{25,17},{2,10},{10... | collective-permute-start | bytes 2162696 | tf_op jit(solution)/shard_map/ppermute | solution.py:521
  24.7 5.5 %collective-permute-start.8 = (bf16[128,512]{1,0:T(8,128)(2,1)S(1)}, bf16[128,512]{1,0:T(8,128)(2,1)S(1)}, u32[]{:S(2)}, u32[]{:S(2)}) collective-permute-start(bf16[128,512]{1,0:T(8,128)(2,1)S(1)} %pad_maximum_fusion.3), channel_id=1, source_target_pairs={{0,1},{1,0},{2,3},{3,2},{4,5},{5,4},{6,7},{7,6},{8,9},{9,8},{10,11... | collective-permute-start | bytes 393224 | tf_op jit(solution)/shard_map/ppermute | solution.py:489
  34.5 7.5 %collective-permute-start.9 = (bf16[384,128]{1,0:T(8,128)(2,1)S(1)}, bf16[384,128]{1,0:T(8,128)(2,1)S(1)}, u32[]{:S(2)}, u32[]{:S(2)}) collective-permute-start(bf16[384,128]{1,0:T(8,128)(2,1)S(1)} %get-tuple-element.62), channel_id=1, source_target_pairs={{0,6},{2,4},{4,2},{6,0},{1,7},{3,5},{5,3},{7,1},{8,14},{10,12},{12... | collective-permute-start | bytes 294920 | tf_op jit(solution)/shard_map/ppermute | solution.py:562
  36.2 10.1 %collective-permute-start.10 = (bf16[384,128]{1,0:T(8,128)(2,1)S(1)}, bf16[384,128]{1,0:T(8,128)(2,1)S(1)}, u32[]{:S(2)}, u32[]{:S(2)}) collective-permute-start(bf16[384,128]{1,0:T(8,128)(2,1)S(1)} %get-tuple-element.63), channel_id=1, source_target_pairs={{0,4},{2,6},{4,0},{6,2},{1,5},{3,7},{5,1},{7,3},{8,12},{10,14},{12... | collective-permute-start | bytes 294920 | tf_op jit(solution)/shard_map/ppermute | solution.py:562
  37.6 8.7 %collective-permute-start.11 = (bf16[384,128]{1,0:T(8,128)(2,1)S(1)}, bf16[384,128]{1,0:T(8,128)(2,1)S(1)}, u32[]{:S(2)}, u32[]{:S(2)}) collective-permute-start(bf16[384,128]{1,0:T(8,128)(2,1)S(1)} %get-tuple-element.64), channel_id=1, source_target_pairs={{0,2},{2,0},{4,6},{6,4},{1,3},{3,1},{5,7},{7,5},{8,10},{10,8},{12,... | collective-permute-start | bytes 294920 | tf_op jit(solution)/shard_map/ppermute | solution.py:562

commit v7 on v6

--- a/solution.py
+++ b/solution.py
@@ -220,10 +220,10 @@
                     found.append(r[m, at + lo - start : at + hi - start, :])
         return jnp.concatenate(found, axis=0)
 
-    def prep(x, c, both):
+    def prep(loaded, both):
         for m in range(members):
-            both[m, :own, :] = x[m].reshape(own, channels)
-            both[m, own:, :] = c[m].reshape(own, channels)
+            both[m, :own, :] = loaded[m].reshape(own, channels)
+            both[m, own:, :] = loaded[members + m].reshape(own, channels)
 
     def edges(both, tail, head):
         for m in range(members):
@@ -232,7 +232,8 @@
             head[m, :edge, :] = both[m, :edge, :]
             head[m, edge:, :] = both[m, own : own + half_edge, :]
 
-    def maps(lat_step, lon_step, basis, forward, again, backward, tab):
+    def maps(plan, lat_step, lon_step, basis, *outs):
+        forward, tab = outs[0], outs[-1]
         lon, lat = lax.axis_index("lon"), lax.axis_index("lat")
         base = lat * lat_rows
         tab[...] = jnp.zeros(tab.shape, jnp.float32)
@@ -248,7 +249,7 @@
         column_home = (block ^ lon) * lon_cols + col_in
         piece = 64
         spot = lax.broadcasted_iota(jnp.int32, (piece, cells), 0)
-        for i, (a, start) in enumerate(first + second):
+        for i, (a, start) in enumerate(plan):
             row = row_in + (base + a)
             got = dot(table, (source == row).astype(jnp.bfloat16))
             step_lat = got[0:TAPS].astype(jnp.int32)
@@ -270,11 +271,9 @@
                         tables[b] = tables[b] + jnp.where(hit, got[at : at + 1], 0.0)
                 for b in range(BASIS):
                     span = slice(b * cells, (b + 1) * cells)
-                    if i < nf:
-                        forward[i, span, p : p + piece] = tables[b].T.astype(jnp.bfloat16)
-                    else:
-                        again[i - nf, span, p : p + piece] = tables[b].T.astype(jnp.bfloat16)
-                        backward[i - nf, p : p + piece, span] = tables[b].astype(jnp.bfloat16)
+                    forward[i, span, p : p + piece] = tables[b].T.astype(jnp.bfloat16)
+                    if len(outs) == 3:
+                        outs[1][i, p : p + piece, span] = tables[b].astype(jnp.bfloat16)
 
     def put_spread(got, into, at):
         for b in range(BASIS):
@@ -485,10 +484,12 @@
     rows = width // 2 - rest
     half = lax.dynamic_slice_in_dim(kernel, lax.axis_index("lon") % 2 * (width // 2), rows, 0)
     ends = jnp.concatenate([kernel[rows : rows + rest], kernel[width - rest :]], axis=0)
-    near_half = lax.ppermute(half, "segment", swap("segment", 1))
     near_ends = lax.ppermute(ends, "segment", swap("segment", 1))
     half, inputs, cotangent = lax.optimization_barrier((half, inputs, cotangent))
-    (both,) = call(prep, "prep", (shape((members, 2 * own, channels), half_type),), (inputs, cotangent), 4, 0.0)
+    loaded = jnp.concatenate([inputs, cotangent], axis=0)
+    (both,) = call(prep, "prep", (shape((members, 2 * own, channels), half_type),), (loaded,), 4, 0.0)
+    half, both = lax.optimization_barrier((half, both))
+    near_half = lax.ppermute(half, "segment", swap("segment", 1))
     sides_type = shape((members, halo, channels), half_type)
     tail, head = call(edges, "edges", (sides_type, sides_type), (both,), 4, 0.0)
     up = [(i, i + 1) for i in range(lat_devices - 1)]
@@ -496,27 +497,35 @@
     both_y = lax.ppermute(both, "lon", swap("lon", 2))
     before = lax.ppermute(tail, "lat", up)
     after = lax.ppermute(head, "lat", down)
+    tables = (lat_step.T, lon_step.T, jnp.transpose(basis_values, (1, 2, 0)))
+    _, _, *tables = lax.optimization_barrier((tail, head, *tables))
+    (forward,) = call(
+        functools.partial(maps, first),
+        "maps_first",
+        (shape((nf, BASIS * cells, blocks * win), half_type),),
+        tables,
+        4,
+        0.0,
+        (pltpu.VMEM((48, lat_total), full_type),),
+    )
+    before, after, forward = lax.optimization_barrier((before, after, forward))
     sides = jnp.concatenate([before, after], axis=1)
     sides, both_y = lax.optimization_barrier((sides, both_y))
     sides_y = lax.ppermute(sides, "lon", swap("lon", 2))
     b0 = jnp.concatenate([both, sides], axis=1)
     b1 = lax.ppermute(b0, "lon", swap("lon", 1))
-    b0, lat_step, lon_step, basis_values = lax.optimization_barrier((b0, lat_step, lon_step, basis_values))
-    forward, again, backward = call(
-        maps,
-        "maps",
-        (
-            shape((nf, BASIS * cells, blocks * win), half_type),
-            shape((ns, BASIS * cells, blocks * win), half_type),
-            shape((ns, blocks * win, BASIS * cells), half_type),
-        ),
-        (lat_step.T, lon_step.T, jnp.transpose(basis_values, (1, 2, 0))),
+    b0, *tables = lax.optimization_barrier((b0, *tables))
+    again, backward = call(
+        functools.partial(maps, second),
+        "maps_again",
+        (shape((ns, BASIS * cells, blocks * win), half_type), shape((ns, blocks * win, BASIS * cells), half_type)),
+        tables,
         4,
         0.0,
         (pltpu.VMEM((48, lat_total), full_type),),
     )
     b2 = jnp.concatenate([both_y, sides_y], axis=1)
-    b2, forward, near_half = lax.optimization_barrier((b2, forward, near_half))
+    b2, again, near_half = lax.optimization_barrier((b2, again, near_half))
     b3 = lax.ppermute(b2, "lon", swap("lon", 1))
     far_half = lax.ppermute(near_half, "lon", swap("lon", 1))
     s_type = (members * nf * cells, width)

time: 47.2 us -> 46.6 us (0.987)
  local copies, waits for them, and re-layouts: 3.01 us -> 1.22 us
  other arithmetic: 0.09 us -> 1.2 us
    ppermute x1, waiting for transfers between devices: 0.87 us -> 3.12 us  [whole_ring(): sides_y = lax.ppermute(sides, 'lon', swap('lon', 2))]
    unnamed x12 -> x9, local copies, waits for them, and re-layouts: 1.83 us -> 0.04 us
    ppermute x1, waiting for transfers between devices: 4.32 us -> 2.74 us  [whole_ring(): after = lax.ppermute(head, 'lat', down)]
    concatenate x1, other arithmetic: 0.03 us -> 1.14 us  [whole_ring(): loaded = jnp.concatenate([inputs, cotangent], axis=0)]
    ppermute x1, waiting for transfers between devices: 0.89 us -> 0.01 us  [whole_ring(): before = lax.ppermute(tail, 'lat', up)]
    pallas_call x7 -> x8, Pallas kernels: 15.3 us -> 15.5 us  [call(): pl.pallas_call(body, out_shape=outs, in_specs=[anywhere if i in far else...]
  transfers between devices with their start and end apart: 12 -> 12, of which waited for: 7 -> 6; matrix products, arithmetic and copies ran while one was open for 0% -> 0% of each run, Pallas kernels for 22% -> 23%
where the time goes in v7:
time: 46.6 us; the launch traced here: 46.4 us
  starting transfers between devices  15.7 us (34%)
  Pallas kernels  15.5 us (33%)
  waiting for transfers between devices  11.9 us (26%)
  local copies, waits for them, and re-layouts  1.22 us (3%)
  other arithmetic  1.2 us (3%)
  between operations  0.83 us (2%)
    pallas_call x8, Pallas kernels, call(): pl.pallas_call(body, out_shape=outs, in_specs=[anywhere if i in far else...  15.5 us
    ppermute x3, waiting for transfers between devices, whole_ring(): lax.ppermute(part, 'lat', swap('lat', bit))  4.87 us
    ppermute x3, starting transfers between devices, whole_ring(): lax.ppermute(part, 'lat', swap('lat', bit))  4.45 us
    ppermute x1, starting transfers between devices, whole_ring(): before = lax.ppermute(tail, 'lat', up)  3.62 us
    ppermute x1, waiting for transfers between devices, whole_ring(): sides_y = lax.ppermute(sides, 'lon', swap('lon', 2))  3.12 us
    ppermute x1, starting transfers between devices, whole_ring(): near_half = lax.ppermute(half, 'segment', swap('segment', 1))  3 us
    ppermute x1, waiting for transfers between devices, whole_ring(): after = lax.ppermute(head, 'lat', down)  2.74 us
    ppermute x1, starting transfers between devices, whole_ring(): both_y = lax.ppermute(both, 'lon', swap('lon', 2))  1.52 us
  transfers between devices with their start and end apart: 12, of which 6 were waited for; matrix products, arithmetic and copies ran while one was open for 0% of the time, Pallas kernels for 23%

profile of v7, /device:TPU:0, one launch (start us, length us, event | category | flops | bytes accessed | tf_op | source)
XLA Modules:
  0.0 46.4 jit_solution(11065732052038116716)
XLA Ops:
  0.6 0.0 copy-start.3
  0.6 0.0 copy-start.2
  0.7 0.0 copy-start.1
  0.7 1.2 %constant_dynamic-slice_fusion = bf16[704,512]{1,0:T(8,128)(2,1)S(1)} fusion(bf16[1536,512]{1,0:T(8,128)(2,1)} %bitcast.7, s32[]{:T(128)S(6)} %select_n.11), kind=kLoop, calls=%fused_computation.6 | loop fusion | bytes 1441796 | tf_op jit(solution)/shard_map/dynamic_slice | solution.py:485
  1.8 1.1 %pad_maximum_fusion.1.loaded = bf16[4,16,4,512]{3,2,1,0:T(4,128)(2,1)S(1)} fusion(bf16[2,16,4,512]{3,2,1,0:T(4,128)(2,1)} %param.7, bf16[2,16,4,512]{3,2,1,0:T(4,128)(2,1)} %param.6), kind=kLoop, calls=%fused_computation.1 | loop fusion | flops 131072 | bytes 524288 | tf_op jit(solution)/shard_map/concatenate | solution.py:489
  3.0 3.0 %collective-permute-start.5 = (bf16[704,512]{1,0:T(8,128)(2,1)S(1)}, bf16[704,512]{1,0:T(8,128)(2,1)S(1)}, u32[]{:S(2)}, u32[]{:S(2)}) collective-permute-start(bf16[704,512]{1,0:T(8,128)(2,1)S(1)} %constant_dynamic-slice_fusion), channel_id=1, source_target_pairs={{0,1},{1,0},{2,3},{3,2},{4,5},{5,4},{6,7},{7,6},{8,9},{9,8},{10,11... | collective-permute-start | bytes 2162696 | tf_op jit(solution)/shard_map/ppermute | solution.py:492
  6.0 1.5 %collective-permute-start.2 = (bf16[2,128,512]{2,1,0:T(8,128)(2,1)S(1)}, bf16[2,128,512]{2,1,0:T(8,128)(2,1)S(1)}, u32[]{:S(2)}, u32[]{:S(2)}) collective-permute-start(bf16[2,128,512]{2,1,0:T(8,128)(2,1)S(1)} %prep.1.both), channel_id=1, source_target_pairs={{0,16},{8,24},{16,0},{24,8},{1,17},{9,25},{17,1},{25,9},{2,18},{10... | collective-permute-start | bytes 786440 | tf_op jit(solution)/shard_map/ppermute | solution.py:497
  7.6 0.0 copy-start
  7.6 3.6 %collective-permute-start = (bf16[2,48,512]{2,1,0:T(8,128)(2,1)S(1)}, bf16[2,48,512]{2,1,0:T(8,128)(2,1)S(1)}, u32[]{:S(2)}, u32[]{:S(2)}) collective-permute-start(bf16[2,48,512]{2,1,0:T(8,128)(2,1)S(1)} %get-tuple-element.46), channel_id=1, source_target_pairs={{0,2},{2,4},{4,6},{1,3},{3,5},{5,7},{8,10},{10,12},{12,14},{9,11},... | collective-permute-start | bytes 294920 | tf_op jit(solution)/shard_map/ppermute | solution.py:498
  11.2 1.3 %collective-permute-start.1 = (bf16[2,48,512]{2,1,0:T(8,128)(2,1)S(1)}, bf16[2,48,512]{2,1,0:T(8,128)(2,1)S(1)}, u32[]{:S(2)}, u32[]{:S(2)}) collective-permute-start(bf16[2,48,512]{2,1,0:T(8,128)(2,1)S(1)} %get-tuple-element.47), channel_id=1, source_target_pairs={{2,0},{4,2},{6,4},{3,1},{5,3},{7,5},{10,8},{12,10},{14,12},{11,9},... | collective-permute-start | bytes 294920 | tf_op jit(solution)/shard_map/ppermute | solution.py:499
  12.5 0.0 copy-done.3
  12.5 0.0 copy-done.2
  12.5 0.0 copy-done.1
  12.5 2.4 %maps_first.1.forward = bf16[4,384,256]{2,1,0:T(8,128)(2,1)S(1)} custom-call(s32[9,64]{1,0:T(8,128)S(1)} %bitcast.14, s32[9,64]{1,0:T(8,128)S(1)} %bitcast.16, f32[9,3,64]{2,1,0:T(4,128)S(1)} %bitcast.12), custom_call_target="tpu_custom_call" | custom-call | tf_op jit(solution)/shard_map/maps_first/pallas_call | solution.py:470
  15.0 0.0 collective-permute-done
  15.0 2.7 %collective-permute-done.1 = bf16[2,48,512]{2,1,0:T(8,128)(2,1)S(1)} collective-permute-done((bf16[2,48,512]{2,1,0:T(8,128)(2,1)S(1)}, bf16[2,48,512]{2,1,0:T(8,128)(2,1)S(1)}, u32[]{:S(2)}, u32[]{:S(2)}) %collective-permute-start.1) | collective-permute-done | bytes 98336 | tf_op jit(solution)/shard_map/ppermute | solution.py:499
  17.7 0.0 collective-permute-done.2
  17.7 0.6 %collective-permute-start.4 = (bf16[2,96,512]{2,1,0:T(8,128)(2,1)S(1)}, bf16[2,96,512]{2,1,0:T(8,128)(2,1)S(1)}, u32[]{:S(2)}, u32[]{:S(2)}) collective-permute-start(bf16[2,96,512]{2,1,0:T(8,128)(2,1)S(1)} %pad_maximum_fusion.2), channel_id=1, source_target_pairs={{0,16},{8,24},{16,0},{24,8},{1,17},{9,25},{17,1},{25,9},{2,18},{10... | collective-permute-start | bytes 589832 | tf_op jit(solution)/shard_map/ppermute | solution.py:514
  18.4 0.1 collective-permute-start.3
  18.4 1.9 %maps_again.1 = (bf16[3,384,256]{2,1,0:T(8,128)(2,1)S(1)}, bf16[3,256,384]{2,1,0:T(8,128)(2,1)S(1)}) custom-call(s32[9,64]{1,0:T(8,128)S(1)} %bitcast.15, s32[9,64]{1,0:T(8,128)S(1)} %bitcast.17, f32[9,3,64]{2,1,0:T(4,128)S(1)} %bitcast.13), custom_call_target="tpu_custom_call" | custom-call | tf_op jit(solution)/shard_map/maps_again/pallas_call | solution.py:470
  20.4 3.1 %collective-permute-done.4 = bf16[2,96,512]{2,1,0:T(8,128)(2,1)S(1)} collective-permute-done((bf16[2,96,512]{2,1,0:T(8,128)(2,1)S(1)}, bf16[2,96,512]{2,1,0:T(8,128)(2,1)S(1)}, u32[]{:S(2)}, u32[]{:S(2)}) %collective-permute-start.4) | collective-permute-done | bytes 196640 | tf_op jit(solution)/shard_map/ppermute | solution.py:514
  23.5 0.0 collective-permute-done.5.near_half
  23.5 0.1 collective-permute-start.6
  23.6 0.5 %collective-permute-start.7 = (bf16[704,512]{1,0:T(8,128)(2,1)S(1)}, bf16[704,512]{1,0:T(8,128)(2,1)S(1)}, u32[]{:S(2)}, u32[]{:S(2)}) collective-permute-start(bf16[704,512]{1,0:T(8,128)(2,1)S(1)} %collective-permute-done.5.near_half), channel_id=1, source_target_pairs={{0,8},{8,0},{16,24},{24,16},{1,9},{9,1},{17,25},{25,17},{2,10},{10... | collective-permute-start | bytes 2162696 | tf_op jit(solution)/shard_map/ppermute | solution.py:530
  24.1 0.0 copy-done
  24.1 0.6 %collective-permute-start.8 = (bf16[128,512]{1,0:T(8,128)(2,1)S(1)}, bf16[128,512]{1,0:T(8,128)(2,1)S(1)}, u32[]{:S(2)}, u32[]{:S(2)}) collective-permute-start(bf16[128,512]{1,0:T(8,128)(2,1)S(1)} %pad_maximum_fusion.3), channel_id=1, source_target_pairs={{0,1},{1,0},{2,3},{3,2},{4,5},{5,4},{6,7},{7,6},{8,9},{9,8},{10,11... | collective-permute-start | bytes 393224 | tf_op jit(solution)/shard_map/ppermute | solution.py:487
  24.7 0.0 collective-permute-done.3.b1
  24.7 0.7 %collective-permute-done.6.b3 = bf16[2,224,512]{2,1,0:T(8,128)(2,1)S(1)} collective-permute-done((bf16[2,224,512]{2,1,0:T(8,128)(2,1)S(1)}, bf16[2,224,512]{2,1,0:T(8,128)(2,1)S(1)}, u32[]{:S(2)}, u32[]{:S(2)}) %collective-permute-start.6) | collective-permute-done | bytes 458784 | tf_op jit(solution)/shard_map/ppermute | solution.py:529
  25.4 3.8 %early.1 = (bf16[1024,1536]{1,0:T(8,128)(2,1)S(1)}, bf16[512,384]{1,0:T(8,128)(2,1)S(1)}, bf16[2,4,96,512]{3,2,1,0:T(8,128)(2,1)S(1)}, bf16[2,64,512]{2,1,0:T(8,128)(2,1)S(1)}) custom-call(bf16[2,224,512]{2,1,0:T(8,128)(2,1)S(1)} %constant_dynamic-update-slice_fusion.b0, bf16[2,224,512]{2,1,0:T(8,128)(2,1)S(1)} %collective-permute-done.3.b1, ...), custom_call_target="tpu_custom_call" | custom-call | flops 3000000000 | bytes 3000000 | tf_op jit(solution)/shard_map/early/pallas_call | solution.py:470
  29.2 0.5 %collective-permute-done.8.ends = bf16[128,512]{1,0:T(8,128)(2,1)S(1)} collective-permute-done((bf16[128,512]{1,0:T(8,128)(2,1)S(1)}, bf16[128,512]{1,0:T(8,128)(2,1)S(1)}, u32[]{:S(2)}, u32[]{:S(2)}) %collective-permute-start.8) | collective-permute-done | bytes 131104 | tf_op jit(solution)/shard_map/ppermute | solution.py:487
  29.7 0.0 collective-permute-done.7.far_half
  29.7 4.2 %chain.1 = (bf16[2,64,512]{2,1,0:T(8,128)(2,1)S(1)}, bf16[2,64,512]{2,1,0:T(8,128)(2,1)S(1)}, bf16[768,512]{1,0:T(8,128)(2,1)S(1)}, f32[384,128]{1,0:T(8,128)S(1...) custom-call(bf16[2,224,512]{2,1,0:T(8,128)(2,1)S(1)} %constant_dynamic-update-slice_fusi, ...), custom_call_target="tpu_custom_call" | custom-call | flops 6000000000 | bytes 6000000 | tf_op jit(solution)/shard_map/chain/pallas_call | solution.py:470
  33.8 2.4 %collective-permute-start.9 = (bf16[384,128]{1,0:T(8,128)(2,1)S(1)}, bf16[384,128]{1,0:T(8,128)(2,1)S(1)}, u32[]{:S(2)}, u32[]{:S(2)}) collective-permute-start(bf16[384,128]{1,0:T(8,128)(2,1)S(1)} %get-tuple-element.78), channel_id=1, source_target_pairs={{0,6},{2,4},{4,2},{6,0},{1,7},{3,5},{5,3},{7,1},{8,14},{10,12},{12... | collective-permute-start | bytes 294920 | tf_op jit(solution)/shard_map/ppermute | solution.py:571
  36.3 0.7 %collective-permute-start.10 = (bf16[384,128]{1,0:T(8,128)(2,1)S(1)}, bf16[384,128]{1,0:T(8,128)(2,1)S(1)}, u32[]{:S(2)}, u32[]{:S(2)}) collective-permute-start(bf16[384,128]{1,0:T(8,128)(2,1)S(1)} %get-tuple-element.79), channel_id=1, source_target_pairs={{0,4},{2,6},{4,0},{6,2},{1,5},{3,7},{5,1},{7,3},{8,12},{10,14},{12... | collective-permute-start | bytes 294920 | tf_op jit(solution)/shard_map/ppermute | solution.py:571
  37.0 1.3 %collective-permute-start.11 = (bf16[384,128]{1,0:T(8,128)(2,1)S(1)}, bf16[384,128]{1,0:T(8,128)(2,1)S(1)}, u32[]{:S(2)}, u32[]{:S(2)}) collective-permute-start(bf16[384,128]{1,0:T(8,128)(2,1)S(1)} %get-tuple-element.80), channel_id=1, source_target_pairs={{0,2},{2,0},{4,6},{6,4},{1,3},{3,1},{5,7},{7,5},{8,10},{10,8},{12,... | collective-permute-start | bytes 294920 | tf_op jit(solution)/shard_map/ppermute | solution.py:571
  38.3 2.5 %finish.1 = (bf16[2,16,4,512]{3,2,1,0:T(4,128)(2,1)}, bf16[2,16,4,512]{3,2,1,0:T(4,128)(2,1)}) custom-call(bf16[1536,512]{1,0:T(8,128)(2,1)S(1)} %bitcast.11, bf16[3,256,384]{2,1,0:T(8,128)(2,1)S(1)} %get-tuple-element.57.backward, bf16[768,512]{1,0:T(8,128)(2,1)S(1)} %get-tuple-element.72.gates, bf16[2,64,512]{2,1,0:T(8,128)(2,1)S(1)} %get-tuple-element.73.next_ref, ...), custom_call_target="tpu_custom_call" | custom-call | flops 2000000000 | bytes 2000000 | tf_op jit(solution)/shard_map/finish/pallas_call | solution.py:470
  40.8 0.6 %collective-permute-done.9.p1 = bf16[384,128]{1,0:T(8,128)(2,1)S(1)} collective-permute-done((bf16[384,128]{1,0:T(8,128)(2,1)S(1)}, bf16[384,128]{1,0:T(8,128)(2,1)S(1)}, u32[]{:S(2)}, u32[]{:S(2)}) %collective-permute-start.9) | collective-permute-done | bytes 98336 | tf_op jit(solution)/shard_map/ppermute | solution.py:571
  41.3 4.3 %collective-permute-done.10.p2 = bf16[384,128]{1,0:T(8,128)(2,1)S(1)} collective-permute-done((bf16[384,128]{1,0:T(8,128)(2,1)S(1)}, bf16[384,128]{1,0:T(8,128)(2,1)S(1)}, u32[]{:S(2)}, u32[]{:S(2)}) %collective-permute-start.10) | collective-permute-done | bytes 98336 | tf_op jit(solution)/shard_map/ppermute | solution.py:571
  45.6 0.0 collective-permute-done.11.p3
  45.6 0.7 %add_up.1 = f32[384,128]{1,0:T(8,128)} custom-call(f32[384,128]{1,0:T(8,128)S(1)} %get-tuple-element.77.mine, bf16[384,128]{1,0:T(8,128)(2,1)S(1)} %collective-permute-done.9.p1, bf16[384,128]{1,0:T(8,128)(2,1)S(1)} %collective-permute-done.10.p2, bf16[384,128]{1,0:T(8,128)(2,1)S(1)} %collective-permute-done.11.p3), custom_call_target="tpu_custom_call" | custom-call | flops 100000000 | bytes 100000 | tf_op jit(solution)/shard_map/add_up/pallas_call | solution.py:470
  (8 shorter events, 0.1 us)
Async XLA Ops:
  0.6 11.9 %copy-start.3 = (s32[64,9]{0,1:T(8,128)S(1)}, s32[64,9]{0,1:T(8,128)}, u32[]{:S(2)}) copy-start(s32[64,9]{0,1:T(8,128)} %param.11) | copy-start | bytes 6916
  0.6 11.9 %copy-start.2 = (s32[64,9]{0,1:T(8,128)S(1)}, s32[64,9]{0,1:T(8,128)}, u32[]{:S(2)}) copy-start(s32[64,9]{0,1:T(8,128)} %param.10) | copy-start | bytes 6916
  0.7 11.9 %copy-start.1 = (f32[64,9,3]{0,2,1:T(4,128)S(1)}, f32[64,9,3]{0,2,1:T(4,128)}, u32[]{:S(2)}) copy-start(f32[64,9,3]{0,2,1:T(4,128)} %param.9) | copy-start | bytes 20740
  3.0 20.5 %collective-permute-start.5 = (bf16[704,512]{1,0:T(8,128)(2,1)S(1)}, bf16[704,512]{1,0:T(8,128)(2,1)S(1)}, u32[]{:S(2)}, u32[]{:S(2)}) collective-permute-start(bf16[704,512]{1,0:T(8,128)(2,1)S(1)} %constant_dynamic-slice_fusion), channel_id=1, source_target_pairs={{0,1},{1,0},{2,3},{3,2},{4,5},{5,4},{6,7},{7,6},{8,9},{9,8},{10,11... | collective-permute-start | bytes 2162696 | tf_op jit(solution)/shard_map/ppermute | solution.py:492
  6.0 11.7 %collective-permute-start.2 = (bf16[2,128,512]{2,1,0:T(8,128)(2,1)S(1)}, bf16[2,128,512]{2,1,0:T(8,128)(2,1)S(1)}, u32[]{:S(2)}, u32[]{:S(2)}) collective-permute-start(bf16[2,128,512]{2,1,0:T(8,128)(2,1)S(1)} %prep.1.both), channel_id=1, source_target_pairs={{0,16},{8,24},{16,0},{24,8},{1,17},{9,25},{17,1},{25,9},{2,18},{10... | collective-permute-start | bytes 786440 | tf_op jit(solution)/shard_map/ppermute | solution.py:497
  7.6 16.5 %copy-start = (bf16[1,3,512,512]{3,2,1,0:T(8,128)(2,1)S(1)}, bf16[1,3,512,512]{3,2,1,0:T(8,128)(2,1)}, u32[]{:S(2)}) copy-start(bf16[1,3,512,512]{3,2,1,0:T(8,128)(2,1)} %param.8) | copy-start | bytes 4718596
  7.6 7.4 %collective-permute-start = (bf16[2,48,512]{2,1,0:T(8,128)(2,1)S(1)}, bf16[2,48,512]{2,1,0:T(8,128)(2,1)S(1)}, u32[]{:S(2)}, u32[]{:S(2)}) collective-permute-start(bf16[2,48,512]{2,1,0:T(8,128)(2,1)S(1)} %get-tuple-element.46), channel_id=1, source_target_pairs={{0,2},{2,4},{4,6},{1,3},{3,5},{5,7},{8,10},{10,12},{12,14},{9,11},... | collective-permute-start | bytes 294920 | tf_op jit(solution)/shard_map/ppermute | solution.py:498
  11.2 6.5 %collective-permute-start.1 = (bf16[2,48,512]{2,1,0:T(8,128)(2,1)S(1)}, bf16[2,48,512]{2,1,0:T(8,128)(2,1)S(1)}, u32[]{:S(2)}, u32[]{:S(2)}) collective-permute-start(bf16[2,48,512]{2,1,0:T(8,128)(2,1)S(1)} %get-tuple-element.47), channel_id=1, source_target_pairs={{2,0},{4,2},{6,4},{3,1},{5,3},{7,5},{10,8},{12,10},{14,12},{11,9},... | collective-permute-start | bytes 294920 | tf_op jit(solution)/shard_map/ppermute | solution.py:499
  17.7 5.7 %collective-permute-start.4 = (bf16[2,96,512]{2,1,0:T(8,128)(2,1)S(1)}, bf16[2,96,512]{2,1,0:T(8,128)(2,1)S(1)}, u32[]{:S(2)}, u32[]{:S(2)}) collective-permute-start(bf16[2,96,512]{2,1,0:T(8,128)(2,1)S(1)} %pad_maximum_fusion.2), channel_id=1, source_target_pairs={{0,16},{8,24},{16,0},{24,8},{1,17},{9,25},{17,1},{25,9},{2,18},{10... | collective-permute-start | bytes 589832 | tf_op jit(solution)/shard_map/ppermute | solution.py:514
  18.4 6.4 %collective-permute-start.3 = (bf16[2,224,512]{2,1,0:T(8,128)(2,1)S(1)}, bf16[2,224,512]{2,1,0:T(8,128)(2,1)S(1)}, u32[]{:S(2)}, u32[]{:S(2)}) collective-permute-start(bf16[2,224,512]{2,1,0:T(8,128)(2,1)S(1)} %constant_dynamic-update-slice_fusion.b0), channel_id=1, source_target_pairs={{0,8},{8,0},{16,24},{24,16},{1,9},{9,1},{17,25},{25,17},{2,10},{10... | collective-permute-start | bytes 1376264 | tf_op jit(solution)/shard_map/ppermute | solution.py:516
  23.5 1.9 %collective-permute-start.6 = (bf16[2,224,512]{2,1,0:T(8,128)(2,1)S(1)}, bf16[2,224,512]{2,1,0:T(8,128)(2,1)S(1)}, u32[]{:S(2)}, u32[]{:S(2)}) collective-permute-start(bf16[2,224,512]{2,1,0:T(8,128)(2,1)S(1)} %pad_maximum_fusion.b2), channel_id=1, source_target_pairs={{0,8},{8,0},{16,24},{24,16},{1,9},{9,1},{17,25},{25,17},{2,10},{10... | collective-permute-start | bytes 1376264 | tf_op jit(solution)/shard_map/ppermute | solution.py:529
  23.6 6.1 %collective-permute-start.7 = (bf16[704,512]{1,0:T(8,128)(2,1)S(1)}, bf16[704,512]{1,0:T(8,128)(2,1)S(1)}, u32[]{:S(2)}, u32[]{:S(2)}) collective-permute-start(bf16[704,512]{1,0:T(8,128)(2,1)S(1)} %collective-permute-done.5.near_half), channel_id=1, source_target_pairs={{0,8},{8,0},{16,24},{24,16},{1,9},{9,1},{17,25},{25,17},{2,10},{10... | collective-permute-start | bytes 2162696 | tf_op jit(solution)/shard_map/ppermute | solution.py:530
  24.1 5.5 %collective-permute-start.8 = (bf16[128,512]{1,0:T(8,128)(2,1)S(1)}, bf16[128,512]{1,0:T(8,128)(2,1)S(1)}, u32[]{:S(2)}, u32[]{:S(2)}) collective-permute-start(bf16[128,512]{1,0:T(8,128)(2,1)S(1)} %pad_maximum_fusion.3), channel_id=1, source_target_pairs={{0,1},{1,0},{2,3},{3,2},{4,5},{5,4},{6,7},{7,6},{8,9},{9,8},{10,11... | collective-permute-start | bytes 393224 | tf_op jit(solution)/shard_map/ppermute | solution.py:487
  33.8 7.5 %collective-permute-start.9 = (bf16[384,128]{1,0:T(8,128)(2,1)S(1)}, bf16[384,128]{1,0:T(8,128)(2,1)S(1)}, u32[]{:S(2)}, u32[]{:S(2)}) collective-permute-start(bf16[384,128]{1,0:T(8,128)(2,1)S(1)} %get-tuple-element.78), channel_id=1, source_target_pairs={{0,6},{2,4},{4,2},{6,0},{1,7},{3,5},{5,3},{7,1},{8,14},{10,12},{12... | collective-permute-start | bytes 294920 | tf_op jit(solution)/shard_map/ppermute | solution.py:571
  36.3 9.4 %collective-permute-start.10 = (bf16[384,128]{1,0:T(8,128)(2,1)S(1)}, bf16[384,128]{1,0:T(8,128)(2,1)S(1)}, u32[]{:S(2)}, u32[]{:S(2)}) collective-permute-start(bf16[384,128]{1,0:T(8,128)(2,1)S(1)} %get-tuple-element.79), channel_id=1, source_target_pairs={{0,4},{2,6},{4,0},{6,2},{1,5},{3,7},{5,1},{7,3},{8,12},{10,14},{12... | collective-permute-start | bytes 294920 | tf_op jit(solution)/shard_map/ppermute | solution.py:571
  37.0 8.7 %collective-permute-start.11 = (bf16[384,128]{1,0:T(8,128)(2,1)S(1)}, bf16[384,128]{1,0:T(8,128)(2,1)S(1)}, u32[]{:S(2)}, u32[]{:S(2)}) collective-permute-start(bf16[384,128]{1,0:T(8,128)(2,1)S(1)} %get-tuple-element.80), channel_id=1, source_target_pairs={{0,2},{2,0},{4,6},{6,4},{1,3},{3,1},{5,7},{7,5},{8,10},{10,8},{12,... | collective-permute-start | bytes 294920 | tf_op jit(solution)/shard_map/ppermute | solution.py:571

commit v8 on v7

--- a/solution.py
+++ b/solution.py
@@ -204,20 +204,23 @@
     lanes = 128
     pieces = channels // lanes
     halo = edge + half_edge
-    state_parts = ((0, edge, 2 * own), (edge, own, 0), (edge + own, edge, 2 * own + halo))
-    coming_parts = (
-        (0, half_edge, 2 * own + edge),
-        (half_edge, own, own),
-        (half_edge + own, half_edge, 2 * own + halo + edge),
-    )
+    state_parts = ((0, edge, 0, 0), (edge, own, 0, None), (edge + own, edge, 0, 1))
+    coming_parts = ((0, half_edge, edge, 0), (half_edge, own, own, None), (half_edge + own, half_edge, edge, 1))
 
     def take(blks, m, parts, low, high):
         found = []
+        odd = lax.axis_index("lat") % 2
         for r in blks:
-            for start, size, at in parts:
+            for start, size, at, side in parts:
                 lo, hi = max(low, start), min(high, start + size)
-                if lo < hi:
+                if lo >= hi:
+                    continue
+                if side is None:
                     found.append(r[m, at + lo - start : at + hi - start, :])
+                else:
+                    slot = odd if side else 1 - odd
+                    first_row = pl.multiple_of(2 * own + at + lo - start + slot * halo, 16)
+                    found.append(r[m, pl.ds(first_row, hi - lo), :])
         return jnp.concatenate(found, axis=0)
 
     def prep(loaded, both):
@@ -225,12 +228,24 @@
             both[m, :own, :] = loaded[m].reshape(own, channels)
             both[m, own:, :] = loaded[members + m].reshape(own, channels)
 
-    def edges(both, tail, head):
-        for m in range(members):
-            tail[m, :edge, :] = both[m, own - edge : own, :]
-            tail[m, edge:, :] = both[m, 2 * own - half_edge :, :]
-            head[m, :edge, :] = both[m, :edge, :]
-            head[m, edge:, :] = both[m, own : own + half_edge, :]
+    def edges(both, toward, away):
+        tail = ((own - edge, own), (2 * own - half_edge, 2 * own))
+        head = ((0, edge), (own, own + half_edge))
+
+        def fill(spans, ref):
+            for m in range(members):
+                ref[m, :edge, :] = both[m, spans[0][0] : spans[0][1], :]
+                ref[m, edge:, :] = both[m, spans[1][0] : spans[1][1], :]
+
+        @pl.when(lax.axis_index("lat") % 2 == 0)
+        def _():
+            fill(tail, toward)
+            fill(head, away)
+
+        @pl.when(lax.axis_index("lat") % 2 == 1)
+        def _():
+            fill(head, toward)
+            fill(tail, away)
 
     def maps(plan, lat_step, lon_step, basis, *outs):
         forward, tab = outs[0], outs[-1]
@@ -291,7 +306,7 @@
             total = dot(s0[m * nf * cells : (m + 1) * nf * cells, :], w[...])
             for g in range(nf):
                 mixed = total[g * cells : (g + 1) * cells]
-                sigma = jax.nn.sigmoid(mixed)
+                sigma = 0.5 + 0.5 * jnp.tanh(0.5 * mixed)
                 here = take(blk, m, state_parts, g * band, (g + 1) * band)
                 value = (here.astype(jnp.float32) + mixed * sigma).astype(jnp.bfloat16)
                 mid[m, :, g * band : (g + 1) * band, :] = value.reshape(blocks, band, channels)
@@ -352,7 +367,7 @@
                 for g in range(ns):
                     at = (m * ns + g) * cells
                     mixed = total[g * cells : (g + 1) * cells]
-                    sigma = jax.nn.sigmoid(mixed)
+                    sigma = 0.5 + 0.5 * jnp.tanh(0.5 * mixed)
                     into[at : at + cells, :] = (coming_at(m, g) * sigma * (1.0 + mixed * (1.0 - sigma))).astype(jnp.bfloat16)
                     if last:
                         low, high = own_part(g)
@@ -491,14 +506,14 @@
     half, both = lax.optimization_barrier((half, both))
     near_half = lax.ppermute(half, "segment", swap("segment", 1))
     sides_type = shape((members, halo, channels), half_type)
-    tail, head = call(edges, "edges", (sides_type, sides_type), (both,), 4, 0.0)
-    up = [(i, i + 1) for i in range(lat_devices - 1)]
-    down = [(i + 1, i) for i in range(lat_devices - 1)]
+    toward, away = call(edges, "edges", (sides_type, sides_type), (both,), 4, 0.0)
     both_y = lax.ppermute(both, "lon", swap("lon", 2))
-    before = lax.ppermute(tail, "lat", up)
-    after = lax.ppermute(head, "lat", down)
+    near_pairs = [(i, i ^ 1) for i in range(lat_devices)]
+    far_pairs = [(i, j) for i in range(lat_devices) for j in [i + 1 if i % 2 else i - 1] if 0 <= j < lat_devices]
+    from_near = lax.ppermute(toward, "lat", near_pairs)
+    from_far = lax.ppermute(away, "lat", far_pairs)
     tables = (lat_step.T, lon_step.T, jnp.transpose(basis_values, (1, 2, 0)))
-    _, _, *tables = lax.optimization_barrier((tail, head, *tables))
+    _, _, *tables = lax.optimization_barrier((toward, away, *tables))
     (forward,) = call(
         functools.partial(maps, first),
         "maps_first",
@@ -508,8 +523,8 @@
         0.0,
         (pltpu.VMEM((48, lat_total), full_type),),
     )
-    before, after, forward = lax.optimization_barrier((before, after, forward))
-    sides = jnp.concatenate([before, after], axis=1)
+    from_near, from_far, forward = lax.optimization_barrier((from_near, from_far, forward))
+    sides = jnp.concatenate([from_near, from_far], axis=1)
     sides, both_y = lax.optimization_barrier((sides, both_y))
     sides_y = lax.ppermute(sides, "lon", swap("lon", 2))
     b0 = jnp.concatenate([both, sides], axis=1)

time: 46.6 us -> 45.6 us (0.979)
  waiting for transfers between devices: 11.9 us -> 11.2 us
  starting transfers between devices: 15.7 us -> 15.2 us
    ppermute x2, waiting for transfers between devices: 2.75 us -> 0.01 us  [the longest x1 0.01 us: whole_ring(): from_near = lax.ppermute(toward, 'lat', near_pairs)]
    ppermute x1, waiting for transfers between devices: 0.01 us -> 2.67 us  [whole_ring(): near_half = lax.ppermute(half, 'segment', swap('segment', 1))]
    ppermute x2, starting transfers between devices: 4.91 us -> 2.29 us  [the longest x1 1.64 us: whole_ring(): from_near = lax.ppermute(toward, 'lat', near_pairs)]
    ppermute x1, waiting for transfers between devices: 0.01 us -> 1.41 us  [whole_ring(): both_y = lax.ppermute(both, 'lon', swap('lon', 2))]
    ppermute x1, starting transfers between devices: 0.6 us -> 1.81 us  [whole_ring(): near_ends = lax.ppermute(ends, 'segment', swap('segment', 1))]
    ppermute x1, waiting for transfers between devices: 3.12 us -> 2.11 us  [whole_ring(): sides_y = lax.ppermute(sides, 'lon', swap('lon', 2))]
    ppermute x1, starting transfers between devices: 0.57 us -> 1.52 us  [whole_ring(): sides_y = lax.ppermute(sides, 'lon', swap('lon', 2))]
    ppermute x1, waiting for transfers between devices: 0.67 us -> 0.01 us  [whole_ring(): b3 = lax.ppermute(b2, 'lon', swap('lon', 1))]
  transfers between devices with their start and end apart: 12 -> 12, of which waited for: 6 -> 5; matrix products, arithmetic and copies ran while one was open for 0% -> 0% of each run, Pallas kernels for 23% -> 24%
where the time goes in v8:
time: 45.6 us; the launch traced here: 45.4 us
  Pallas kernels  15.8 us (35%)
  starting transfers between devices  15.2 us (33%)
  waiting for transfers between devices  11.2 us (25%)
  local copies, waits for them, and re-layouts  1.22 us (3%)
  other arithmetic  1.2 us (3%)
  between operations  0.83 us (2%)
    pallas_call x8, Pallas kernels, call(): pl.pallas_call(body, out_shape=outs, in_specs=[anywhere if i in far else...  15.8 us
    ppermute x3, waiting for transfers between devices, whole_ring(): lax.ppermute(part, 'lat', swap('lat', bit))  5.04 us
    ppermute x3, starting transfers between devices, whole_ring(): lax.ppermute(part, 'lat', swap('lat', bit))  4.45 us
    ppermute x1, starting transfers between devices, whole_ring(): near_half = lax.ppermute(half, 'segment', swap('segment', 1))  3 us
    ppermute x1, waiting for transfers between devices, whole_ring(): near_half = lax.ppermute(half, 'segment', swap('segment', 1))  2.67 us
    ppermute x1, waiting for transfers between devices, whole_ring(): sides_y = lax.ppermute(sides, 'lon', swap('lon', 2))  2.11 us
    ppermute x1, starting transfers between devices, whole_ring(): near_ends = lax.ppermute(ends, 'segment', swap('segment', 1))  1.81 us
    ppermute x1, starting transfers between devices, whole_ring(): from_near = lax.ppermute(toward, 'lat', near_pairs)  1.64 us
  transfers between devices with their start and end apart: 12, of which 5 were waited for; matrix products, arithmetic and copies ran while one was open for 0% of the time, Pallas kernels for 24%

profile of v8, /device:TPU:0, one launch (start us, length us, event | category | flops | bytes accessed | tf_op | source)
XLA Modules:
  0.0 45.4 jit_solution(11019346721945490584)
XLA Ops:
  0.6 0.0 copy-start.3
  0.6 0.0 copy-start.2
  0.7 0.0 copy-start.1
  0.7 1.2 %constant_dynamic-slice_fusion = bf16[704,512]{1,0:T(8,128)(2,1)S(1)} fusion(bf16[1536,512]{1,0:T(8,128)(2,1)} %bitcast.7, s32[]{:T(128)S(6)} %select_n.11), kind=kLoop, calls=%fused_computation.6 | loop fusion | bytes 1441796 | tf_op jit(solution)/shard_map/dynamic_slice | solution.py:500
  1.8 1.1 %pad_maximum_fusion.1.loaded = bf16[4,16,4,512]{3,2,1,0:T(4,128)(2,1)S(1)} fusion(bf16[2,16,4,512]{3,2,1,0:T(4,128)(2,1)} %param.7, bf16[2,16,4,512]{3,2,1,0:T(4,128)(2,1)} %param.6), kind=kLoop, calls=%fused_computation.1 | loop fusion | flops 131072 | bytes 524288 | tf_op jit(solution)/shard_map/concatenate | solution.py:504
  3.0 3.0 %collective-permute-start.5 = (bf16[704,512]{1,0:T(8,128)(2,1)S(1)}, bf16[704,512]{1,0:T(8,128)(2,1)S(1)}, u32[]{:S(2)}, u32[]{:S(2)}) collective-permute-start(bf16[704,512]{1,0:T(8,128)(2,1)S(1)} %constant_dynamic-slice_fusion), channel_id=1, source_target_pairs={{0,1},{1,0},{2,3},{3,2},{4,5},{5,4},{6,7},{7,6},{8,9},{9,8},{10,11... | collective-permute-start | bytes 2162696 | tf_op jit(solution)/shard_map/ppermute | solution.py:507
  6.0 1.5 %collective-permute-start.2 = (bf16[2,128,512]{2,1,0:T(8,128)(2,1)S(1)}, bf16[2,128,512]{2,1,0:T(8,128)(2,1)S(1)}, u32[]{:S(2)}, u32[]{:S(2)}) collective-permute-start(bf16[2,128,512]{2,1,0:T(8,128)(2,1)S(1)} %prep.1.both), channel_id=1, source_target_pairs={{0,16},{8,24},{16,0},{24,8},{1,17},{9,25},{17,1},{25,9},{2,18},{10... | collective-permute-start | bytes 786440 | tf_op jit(solution)/shard_map/ppermute | solution.py:510
  7.6 0.0 copy-start
  7.6 1.6 %collective-permute-start = (bf16[2,48,512]{2,1,0:T(8,128)(2,1)S(1)}, bf16[2,48,512]{2,1,0:T(8,128)(2,1)S(1)}, u32[]{:S(2)}, u32[]{:S(2)}) collective-permute-start(bf16[2,48,512]{2,1,0:T(8,128)(2,1)S(1)} %get-tuple-element.46), channel_id=1, source_target_pairs={{0,2},{2,0},{4,6},{6,4},{1,3},{3,1},{5,7},{7,5},{8,10},{10,8},{12,... | collective-permute-start | bytes 294920 | tf_op jit(solution)/shard_map/ppermute | solution.py:513
  9.2 0.7 %collective-permute-start.1 = (bf16[2,48,512]{2,1,0:T(8,128)(2,1)S(1)}, bf16[2,48,512]{2,1,0:T(8,128)(2,1)S(1)}, u32[]{:S(2)}, u32[]{:S(2)}) collective-permute-start(bf16[2,48,512]{2,1,0:T(8,128)(2,1)S(1)} %get-tuple-element.47), channel_id=1, source_target_pairs={{2,4},{4,2},{3,5},{5,3},{10,12},{12,10},{11,13},{13,11},{18,20},{2... | collective-permute-start | bytes 294920 | tf_op jit(solution)/shard_map/ppermute | solution.py:514
  9.9 0.0 copy-done.3
  9.9 0.0 copy-done.2
  9.9 0.0 copy-done.1
  9.9 2.4 %maps_first.1.forward = bf16[4,384,256]{2,1,0:T(8,128)(2,1)S(1)} custom-call(s32[9,64]{1,0:T(8,128)S(1)} %bitcast.14, s32[9,64]{1,0:T(8,128)S(1)} %bitcast.16, f32[9,3,64]{2,1,0:T(4,128)S(1)} %bitcast.12), custom_call_target="tpu_custom_call" | custom-call | tf_op jit(solution)/shard_map/maps_first/pallas_call | solution.py:485
  12.3 0.0 collective-permute-done
  12.4 0.0 collective-permute-done.1
  12.4 1.4 %collective-permute-done.2 = bf16[2,128,512]{2,1,0:T(8,128)(2,1)S(1)} collective-permute-done((bf16[2,128,512]{2,1,0:T(8,128)(2,1)S(1)}, bf16[2,128,512]{2,1,0:T(8,128)(2,1)S(1)}, u32[]{:S(2)}, u32[]{:S(2)}) %collective-permute-start.2) | collective-permute-done | bytes 262176 | tf_op jit(solution)/shard_map/ppermute | solution.py:510
  13.8 1.5 %collective-permute-start.4 = (bf16[2,96,512]{2,1,0:T(8,128)(2,1)S(1)}, bf16[2,96,512]{2,1,0:T(8,128)(2,1)S(1)}, u32[]{:S(2)}, u32[]{:S(2)}) collective-permute-start(bf16[2,96,512]{2,1,0:T(8,128)(2,1)S(1)} %pad_maximum_fusion.2), channel_id=1, source_target_pairs={{0,16},{8,24},{16,0},{24,8},{1,17},{9,25},{17,1},{25,9},{2,18},{10... | collective-permute-start | bytes 589832 | tf_op jit(solution)/shard_map/ppermute | solution.py:529
  15.4 0.1 collective-permute-start.3
  15.4 1.9 %maps_again.1 = (bf16[3,384,256]{2,1,0:T(8,128)(2,1)S(1)}, bf16[3,256,384]{2,1,0:T(8,128)(2,1)S(1)}) custom-call(s32[9,64]{1,0:T(8,128)S(1)} %bitcast.15, s32[9,64]{1,0:T(8,128)S(1)} %bitcast.17, f32[9,3,64]{2,1,0:T(4,128)S(1)} %bitcast.13), custom_call_target="tpu_custom_call" | custom-call | tf_op jit(solution)/shard_map/maps_again/pallas_call | solution.py:485
  17.4 2.1 %collective-permute-done.4 = bf16[2,96,512]{2,1,0:T(8,128)(2,1)S(1)} collective-permute-done((bf16[2,96,512]{2,1,0:T(8,128)(2,1)S(1)}, bf16[2,96,512]{2,1,0:T(8,128)(2,1)S(1)}, u32[]{:S(2)}, u32[]{:S(2)}) %collective-permute-start.4) | collective-permute-done | bytes 196640 | tf_op jit(solution)/shard_map/ppermute | solution.py:529
  19.5 2.7 %collective-permute-done.5.near_half = bf16[704,512]{1,0:T(8,128)(2,1)S(1)} collective-permute-done((bf16[704,512]{1,0:T(8,128)(2,1)S(1)}, bf16[704,512]{1,0:T(8,128)(2,1)S(1)}, u32[]{:S(2)}, u32[]{:S(2)}) %collective-permute-start.5) | collective-permute-done | bytes 720928 | tf_op jit(solution)/shard_map/ppermute | solution.py:507
  22.2 0.0 collective-permute-start.6
  22.2 0.5 %collective-permute-start.7 = (bf16[704,512]{1,0:T(8,128)(2,1)S(1)}, bf16[704,512]{1,0:T(8,128)(2,1)S(1)}, u32[]{:S(2)}, u32[]{:S(2)}) collective-permute-start(bf16[704,512]{1,0:T(8,128)(2,1)S(1)} %collective-permute-done.5.near_half), channel_id=1, source_target_pairs={{0,8},{8,0},{16,24},{24,16},{1,9},{9,1},{17,25},{25,17},{2,10},{10... | collective-permute-start | bytes 2162696 | tf_op jit(solution)/shard_map/ppermute | solution.py:545
  22.7 0.0 copy-done
  22.7 1.8 %collective-permute-start.8 = (bf16[128,512]{1,0:T(8,128)(2,1)S(1)}, bf16[128,512]{1,0:T(8,128)(2,1)S(1)}, u32[]{:S(2)}, u32[]{:S(2)}) collective-permute-start(bf16[128,512]{1,0:T(8,128)(2,1)S(1)} %pad_maximum_fusion.3), channel_id=1, source_target_pairs={{0,1},{1,0},{2,3},{3,2},{4,5},{5,4},{6,7},{7,6},{8,9},{9,8},{10,11... | collective-permute-start | bytes 393224 | tf_op jit(solution)/shard_map/ppermute | solution.py:502
  24.5 0.0 collective-permute-done.3.b1
  24.5 0.0 collective-permute-done.6.b3
  24.5 3.9 %early.1 = (bf16[1024,1536]{1,0:T(8,128)(2,1)S(1)}, bf16[512,384]{1,0:T(8,128)(2,1)S(1)}, bf16[2,4,96,512]{3,2,1,0:T(8,128)(2,1)S(1)}, bf16[2,64,512]{2,1,0:T(8,128)(2,1)S(1)}) custom-call(bf16[2,224,512]{2,1,0:T(8,128)(2,1)S(1)} %constant_dynamic-update-slice_fusion.b0, bf16[2,224,512]{2,1,0:T(8,128)(2,1)S(1)} %collective-permute-done.3.b1, ...), custom_call_target="tpu_custom_call" | custom-call | flops 3000000000 | bytes 3000000 | tf_op jit(solution)/shard_map/early/pallas_call | solution.py:485
  28.4 0.0 collective-permute-done.8.ends
  28.4 0.0 collective-permute-done.7.far_half
  28.5 4.3 %chain.1 = (bf16[2,64,512]{2,1,0:T(8,128)(2,1)S(1)}, bf16[2,64,512]{2,1,0:T(8,128)(2,1)S(1)}, bf16[768,512]{1,0:T(8,128)(2,1)S(1)}, f32[384,128]{1,0:T(8,128)S(1...) custom-call(bf16[2,224,512]{2,1,0:T(8,128)(2,1)S(1)} %constant_dynamic-update-slice_fusi, ...), custom_call_target="tpu_custom_call" | custom-call | flops 6000000000 | bytes 6000000 | tf_op jit(solution)/shard_map/chain/pallas_call | solution.py:485
  32.8 3.7 %collective-permute-start.9 = (bf16[384,128]{1,0:T(8,128)(2,1)S(1)}, bf16[384,128]{1,0:T(8,128)(2,1)S(1)}, u32[]{:S(2)}, u32[]{:S(2)}) collective-permute-start(bf16[384,128]{1,0:T(8,128)(2,1)S(1)} %get-tuple-element.78), channel_id=1, source_target_pairs={{0,6},{2,4},{4,2},{6,0},{1,7},{3,5},{5,3},{7,1},{8,14},{10,12},{12... | collective-permute-start | bytes 294920 | tf_op jit(solution)/shard_map/ppermute | solution.py:586
  36.4 0.0 collective-permute-start.10
  36.4 0.8 %collective-permute-start.11 = (bf16[384,128]{1,0:T(8,128)(2,1)S(1)}, bf16[384,128]{1,0:T(8,128)(2,1)S(1)}, u32[]{:S(2)}, u32[]{:S(2)}) collective-permute-start(bf16[384,128]{1,0:T(8,128)(2,1)S(1)} %get-tuple-element.80), channel_id=1, source_target_pairs={{0,2},{2,0},{4,6},{6,4},{1,3},{3,1},{5,7},{7,5},{8,10},{10,8},{12,... | collective-permute-start | bytes 294920 | tf_op jit(solution)/shard_map/ppermute | solution.py:586
  37.2 2.5 %finish.1 = (bf16[2,16,4,512]{3,2,1,0:T(4,128)(2,1)}, bf16[2,16,4,512]{3,2,1,0:T(4,128)(2,1)}) custom-call(bf16[1536,512]{1,0:T(8,128)(2,1)S(1)} %bitcast.11, bf16[3,256,384]{2,1,0:T(8,128)(2,1)S(1)} %get-tuple-element.57.backward, bf16[768,512]{1,0:T(8,128)(2,1)S(1)} %get-tuple-element.72.gates, bf16[2,64,512]{2,1,0:T(8,128)(2,1)S(1)} %get-tuple-element.73.next_ref, ...), custom_call_target="tpu_custom_call" | custom-call | flops 2000000000 | bytes 2000000 | tf_op jit(solution)/shard_map/finish/pallas_call | solution.py:485
  39.7 0.5 %collective-permute-done.9.p1 = bf16[384,128]{1,0:T(8,128)(2,1)S(1)} collective-permute-done((bf16[384,128]{1,0:T(8,128)(2,1)S(1)}, bf16[384,128]{1,0:T(8,128)(2,1)S(1)}, u32[]{:S(2)}, u32[]{:S(2)}) %collective-permute-start.9) | collective-permute-done | bytes 98336 | tf_op jit(solution)/shard_map/ppermute | solution.py:586
  40.2 4.6 %collective-permute-done.10.p2 = bf16[384,128]{1,0:T(8,128)(2,1)S(1)} collective-permute-done((bf16[384,128]{1,0:T(8,128)(2,1)S(1)}, bf16[384,128]{1,0:T(8,128)(2,1)S(1)}, u32[]{:S(2)}, u32[]{:S(2)}) %collective-permute-start.10) | collective-permute-done | bytes 98336 | tf_op jit(solution)/shard_map/ppermute | solution.py:586
  44.7 0.0 collective-permute-done.11.p3
  44.7 0.7 %add_up.1 = f32[384,128]{1,0:T(8,128)} custom-call(f32[384,128]{1,0:T(8,128)S(1)} %get-tuple-element.77.mine, bf16[384,128]{1,0:T(8,128)(2,1)S(1)} %collective-permute-done.9.p1, bf16[384,128]{1,0:T(8,128)(2,1)S(1)} %collective-permute-done.10.p2, bf16[384,128]{1,0:T(8,128)(2,1)S(1)} %collective-permute-done.11.p3), custom_call_target="tpu_custom_call" | custom-call | flops 100000000 | bytes 100000 | tf_op jit(solution)/shard_map/add_up/pallas_call | solution.py:485
  (8 shorter events, 0.1 us)
Async XLA Ops:
  0.6 9.3 %copy-start.3 = (s32[64,9]{0,1:T(8,128)S(1)}, s32[64,9]{0,1:T(8,128)}, u32[]{:S(2)}) copy-start(s32[64,9]{0,1:T(8,128)} %param.11) | copy-start | bytes 6916
  0.6 9.3 %copy-start.2 = (s32[64,9]{0,1:T(8,128)S(1)}, s32[64,9]{0,1:T(8,128)}, u32[]{:S(2)}) copy-start(s32[64,9]{0,1:T(8,128)} %param.10) | copy-start | bytes 6916
  0.7 9.3 %copy-start.1 = (f32[64,9,3]{0,2,1:T(4,128)S(1)}, f32[64,9,3]{0,2,1:T(4,128)}, u32[]{:S(2)}) copy-start(f32[64,9,3]{0,2,1:T(4,128)} %param.9) | copy-start | bytes 20740
  3.0 19.1 %collective-permute-start.5 = (bf16[704,512]{1,0:T(8,128)(2,1)S(1)}, bf16[704,512]{1,0:T(8,128)(2,1)S(1)}, u32[]{:S(2)}, u32[]{:S(2)}) collective-permute-start(bf16[704,512]{1,0:T(8,128)(2,1)S(1)} %constant_dynamic-slice_fusion), channel_id=1, source_target_pairs={{0,1},{1,0},{2,3},{3,2},{4,5},{5,4},{6,7},{7,6},{8,9},{9,8},{10,11... | collective-permute-start | bytes 2162696 | tf_op jit(solution)/shard_map/ppermute | solution.py:507
  6.0 7.8 %collective-permute-start.2 = (bf16[2,128,512]{2,1,0:T(8,128)(2,1)S(1)}, bf16[2,128,512]{2,1,0:T(8,128)(2,1)S(1)}, u32[]{:S(2)}, u32[]{:S(2)}) collective-permute-start(bf16[2,128,512]{2,1,0:T(8,128)(2,1)S(1)} %prep.1.both), channel_id=1, source_target_pairs={{0,16},{8,24},{16,0},{24,8},{1,17},{9,25},{17,1},{25,9},{2,18},{10... | collective-permute-start | bytes 786440 | tf_op jit(solution)/shard_map/ppermute | solution.py:510
  7.6 15.1 %copy-start = (bf16[1,3,512,512]{3,2,1,0:T(8,128)(2,1)S(1)}, bf16[1,3,512,512]{3,2,1,0:T(8,128)(2,1)}, u32[]{:S(2)}) copy-start(bf16[1,3,512,512]{3,2,1,0:T(8,128)(2,1)} %param.8) | copy-start | bytes 4718596
  7.6 4.8 %collective-permute-start = (bf16[2,48,512]{2,1,0:T(8,128)(2,1)S(1)}, bf16[2,48,512]{2,1,0:T(8,128)(2,1)S(1)}, u32[]{:S(2)}, u32[]{:S(2)}) collective-permute-start(bf16[2,48,512]{2,1,0:T(8,128)(2,1)S(1)} %get-tuple-element.46), channel_id=1, source_target_pairs={{0,2},{2,0},{4,6},{6,4},{1,3},{3,1},{5,7},{7,5},{8,10},{10,8},{12,... | collective-permute-start | bytes 294920 | tf_op jit(solution)/shard_map/ppermute | solution.py:513
  9.2 3.1 %collective-permute-start.1 = (bf16[2,48,512]{2,1,0:T(8,128)(2,1)S(1)}, bf16[2,48,512]{2,1,0:T(8,128)(2,1)S(1)}, u32[]{:S(2)}, u32[]{:S(2)}) collective-permute-start(bf16[2,48,512]{2,1,0:T(8,128)(2,1)S(1)} %get-tuple-element.47), channel_id=1, source_target_pairs={{2,4},{4,2},{3,5},{5,3},{10,12},{12,10},{11,13},{13,11},{18,20},{2... | collective-permute-start | bytes 294920 | tf_op jit(solution)/shard_map/ppermute | solution.py:514
  13.8 5.7 %collective-permute-start.4 = (bf16[2,96,512]{2,1,0:T(8,128)(2,1)S(1)}, bf16[2,96,512]{2,1,0:T(8,128)(2,1)S(1)}, u32[]{:S(2)}, u32[]{:S(2)}) collective-permute-start(bf16[2,96,512]{2,1,0:T(8,128)(2,1)S(1)} %pad_maximum_fusion.2), channel_id=1, source_target_pairs={{0,16},{8,24},{16,0},{24,8},{1,17},{9,25},{17,1},{25,9},{2,18},{10... | collective-permute-start | bytes 589832 | tf_op jit(solution)/shard_map/ppermute | solution.py:529
  15.4 9.2 %collective-permute-start.3 = (bf16[2,224,512]{2,1,0:T(8,128)(2,1)S(1)}, bf16[2,224,512]{2,1,0:T(8,128)(2,1)S(1)}, u32[]{:S(2)}, u32[]{:S(2)}) collective-permute-start(bf16[2,224,512]{2,1,0:T(8,128)(2,1)S(1)} %constant_dynamic-update-slice_fusion.b0), channel_id=1, source_target_pairs={{0,8},{8,0},{16,24},{24,16},{1,9},{9,1},{17,25},{25,17},{2,10},{10... | collective-permute-start | bytes 1376264 | tf_op jit(solution)/shard_map/ppermute | solution.py:531
  22.2 2.4 %collective-permute-start.6 = (bf16[2,224,512]{2,1,0:T(8,128)(2,1)S(1)}, bf16[2,224,512]{2,1,0:T(8,128)(2,1)S(1)}, u32[]{:S(2)}, u32[]{:S(2)}) collective-permute-start(bf16[2,224,512]{2,1,0:T(8,128)(2,1)S(1)} %pad_maximum_fusion.b2), channel_id=1, source_target_pairs={{0,8},{8,0},{16,24},{24,16},{1,9},{9,1},{17,25},{25,17},{2,10},{10... | collective-permute-start | bytes 1376264 | tf_op jit(solution)/shard_map/ppermute | solution.py:544
  22.2 6.3 %collective-permute-start.7 = (bf16[704,512]{1,0:T(8,128)(2,1)S(1)}, bf16[704,512]{1,0:T(8,128)(2,1)S(1)}, u32[]{:S(2)}, u32[]{:S(2)}) collective-permute-start(bf16[704,512]{1,0:T(8,128)(2,1)S(1)} %collective-permute-done.5.near_half), channel_id=1, source_target_pairs={{0,8},{8,0},{16,24},{24,16},{1,9},{9,1},{17,25},{25,17},{2,10},{10... | collective-permute-start | bytes 2162696 | tf_op jit(solution)/shard_map/ppermute | solution.py:545
  22.7 5.7 %collective-permute-start.8 = (bf16[128,512]{1,0:T(8,128)(2,1)S(1)}, bf16[128,512]{1,0:T(8,128)(2,1)S(1)}, u32[]{:S(2)}, u32[]{:S(2)}) collective-permute-start(bf16[128,512]{1,0:T(8,128)(2,1)S(1)} %pad_maximum_fusion.3), channel_id=1, source_target_pairs={{0,1},{1,0},{2,3},{3,2},{4,5},{5,4},{6,7},{7,6},{8,9},{9,8},{10,11... | collective-permute-start | bytes 393224 | tf_op jit(solution)/shard_map/ppermute | solution.py:502
  32.8 7.4 %collective-permute-start.9 = (bf16[384,128]{1,0:T(8,128)(2,1)S(1)}, bf16[384,128]{1,0:T(8,128)(2,1)S(1)}, u32[]{:S(2)}, u32[]{:S(2)}) collective-permute-start(bf16[384,128]{1,0:T(8,128)(2,1)S(1)} %get-tuple-element.78), channel_id=1, source_target_pairs={{0,6},{2,4},{4,2},{6,0},{1,7},{3,5},{5,3},{7,1},{8,14},{10,12},{12... | collective-permute-start | bytes 294920 | tf_op jit(solution)/shard_map/ppermute | solution.py:586
  36.4 8.3 %collective-permute-start.10 = (bf16[384,128]{1,0:T(8,128)(2,1)S(1)}, bf16[384,128]{1,0:T(8,128)(2,1)S(1)}, u32[]{:S(2)}, u32[]{:S(2)}) collective-permute-start(bf16[384,128]{1,0:T(8,128)(2,1)S(1)} %get-tuple-element.79), channel_id=1, source_target_pairs={{0,4},{2,6},{4,0},{6,2},{1,5},{3,7},{5,1},{7,3},{8,12},{10,14},{12... | collective-permute-start | bytes 294920 | tf_op jit(solution)/shard_map/ppermute | solution.py:586
  36.4 8.3 %collective-permute-start.11 = (bf16[384,128]{1,0:T(8,128)(2,1)S(1)}, bf16[384,128]{1,0:T(8,128)(2,1)S(1)}, u32[]{:S(2)}, u32[]{:S(2)}) collective-permute-start(bf16[384,128]{1,0:T(8,128)(2,1)S(1)} %get-tuple-element.80), channel_id=1, source_target_pairs={{0,2},{2,0},{4,6},{6,4},{1,3},{3,1},{5,7},{7,5},{8,10},{10,8},{12,... | collective-permute-start | bytes 294920 | tf_op jit(solution)/shard_map/ppermute | solution.py:586

commit v9 on v8

--- a/solution.py
+++ b/solution.py
@@ -302,10 +302,10 @@
                 put_spread(dot(forward[g], near).astype(jnp.bfloat16), into, (m * nf + g) * cells)
 
     def first_section(blk, w, s0, s1, again, mid, slope):
+        total = dot(s0[...], w[...])
         for m in range(members):
-            total = dot(s0[m * nf * cells : (m + 1) * nf * cells, :], w[...])
             for g in range(nf):
-                mixed = total[g * cells : (g + 1) * cells]
+                mixed = total[(m * nf + g) * cells : (m * nf + g + 1) * cells]
                 sigma = 0.5 + 0.5 * jnp.tanh(0.5 * mixed)
                 here = take(blk, m, state_parts, g * band, (g + 1) * band)
                 value = (here.astype(jnp.float32) + mixed * sigma).astype(jnp.bfloat16)
@@ -362,11 +362,11 @@
             return take(blk, m, coming_parts, g * band, (g + 1) * band).astype(jnp.float32)
 
         def second_section(weight, spread_ref, into, last):
+            total = dot(spread_ref[: members * ns * cells, :], weight[...])
             for m in range(members):
-                total = dot(spread_ref[m * ns * cells : (m + 1) * ns * cells, :], weight[...])
                 for g in range(ns):
                     at = (m * ns + g) * cells
-                    mixed = total[g * cells : (g + 1) * cells]
+                    mixed = total[at : at + cells]
                     sigma = 0.5 + 0.5 * jnp.tanh(0.5 * mixed)
                     into[at : at + cells, :] = (coming_at(m, g) * sigma * (1.0 + mixed * (1.0 - sigma))).astype(jnp.bfloat16)
                     if last:
@@ -495,16 +495,15 @@
 
     prep, edges, maps, early, chain, finish = make_steps(lat_rows, lon_cols, blocks, members, channels, lat_devices)
     kernel = weights.reshape(width, channels)
-    rest = width // 2 // 12
+    rest = width // 2 * 7 // 48
     rows = width // 2 - rest
     half = lax.dynamic_slice_in_dim(kernel, lax.axis_index("lon") % 2 * (width // 2), rows, 0)
     ends = jnp.concatenate([kernel[rows : rows + rest], kernel[width - rest :]], axis=0)
     near_ends = lax.ppermute(ends, "segment", swap("segment", 1))
+    near_half = lax.ppermute(half, "segment", swap("segment", 1))
     half, inputs, cotangent = lax.optimization_barrier((half, inputs, cotangent))
     loaded = jnp.concatenate([inputs, cotangent], axis=0)
     (both,) = call(prep, "prep", (shape((members, 2 * own, channels), half_type),), (loaded,), 4, 0.0)
-    half, both = lax.optimization_barrier((half, both))
-    near_half = lax.ppermute(half, "segment", swap("segment", 1))
     sides_type = shape((members, halo, channels), half_type)
     toward, away = call(edges, "edges", (sides_type, sides_type), (both,), 4, 0.0)
     both_y = lax.ppermute(both, "lon", swap("lon", 2))

time: 45.6 us -> 45.6 us (level)
  starting transfers between devices: 15.2 us -> 15.8 us
  waiting for transfers between devices: 11.2 us -> 10.7 us
    ppermute x1, waiting for transfers between devices: 2.67 us -> 0.36 us  [whole_ring(): near_half = lax.ppermute(half, 'segment', swap('segment', 1))]
    ppermute x1, waiting for transfers between devices: 0.01 us -> 1.98 us  [whole_ring(): near_ends = lax.ppermute(ends, 'segment', swap('segment', 1))]
    ppermute x3, starting transfers between devices: 4.45 us -> 5.03 us  [whole_ring(): lax.ppermute(part, 'lat', swap('lat', bit))]
  transfers between devices with their start and end apart: 12 -> 12, of which waited for: 5 -> 5; matrix products, arithmetic and copies ran while one was open for 0% -> 3% of each run, Pallas kernels for 24% -> 23%
where the time goes in v9:
time: 45.6 us; the launch traced here: 45.5 us
  starting transfers between devices  15.8 us (35%)
  Pallas kernels  15.7 us (34%)
  waiting for transfers between devices  10.7 us (23%)
  other arithmetic  1.24 us (3%)
  local copies, waits for them, and re-layouts  1.18 us (3%)
  between operations  0.81 us (2%)
    pallas_call x8, Pallas kernels, call(): pl.pallas_call(body, out_shape=outs, in_specs=[anywhere if i in far else...  15.7 us
    ppermute x3, starting transfers between devices, whole_ring(): lax.ppermute(part, 'lat', swap('lat', bit))  5.03 us
    ppermute x3, waiting for transfers between devices, whole_ring(): lax.ppermute(part, 'lat', swap('lat', bit))  4.86 us
    ppermute x1, starting transfers between devices, whole_ring(): near_half = lax.ppermute(half, 'segment', swap('segment', 1))  3 us
    ppermute x1, waiting for transfers between devices, whole_ring(): sides_y = lax.ppermute(sides, 'lon', swap('lon', 2))  2.12 us
    ppermute x1, waiting for transfers between devices, whole_ring(): near_ends = lax.ppermute(ends, 'segment', swap('segment', 1))  1.98 us
    ppermute x1, starting transfers between devices, whole_ring(): near_ends = lax.ppermute(ends, 'segment', swap('segment', 1))  1.81 us
    ppermute x1, starting transfers between devices, whole_ring(): from_near = lax.ppermute(toward, 'lat', near_pairs)  1.64 us
  transfers between devices with their start and end apart: 12, of which 5 were waited for; matrix products, arithmetic and copies ran while one was open for 3% of the time, Pallas kernels for 23%

profile of v9, /device:TPU:0, one launch (start us, length us, event | category | flops | bytes accessed | tf_op | source)
XLA Modules:
  0.0 45.5 jit_solution(6475793769881524831)
XLA Ops:
  0.6 0.0 copy-start.3
  0.6 0.0 copy-start.2
  0.7 0.0 copy-start.1
  0.7 1.1 %constant_dynamic-slice_fusion = bf16[656,512]{1,0:T(8,128)(2,1)S(1)} fusion(bf16[1536,512]{1,0:T(8,128)(2,1)} %bitcast.7, s32[]{:T(128)S(6)} %select_n.11), kind=kLoop, calls=%fused_computation.5 | loop fusion | bytes 1343492 | tf_op jit(solution)/shard_map/dynamic_slice | solution.py:500
  1.8 3.0 %collective-permute-start.5 = (bf16[656,512]{1,0:T(8,128)(2,1)S(1)}, bf16[656,512]{1,0:T(8,128)(2,1)S(1)}, u32[]{:S(2)}, u32[]{:S(2)}) collective-permute-start(bf16[656,512]{1,0:T(8,128)(2,1)S(1)} %constant_dynamic-slice_fusion), channel_id=1, source_target_pairs={{0,1},{1,0},{2,3},{3,2},{4,5},{5,4},{6,7},{7,6},{8,9},{9,8},{10,11... | collective-permute-start | bytes 2015240 | tf_op jit(solution)/shard_map/ppermute | solution.py:503
  4.8 1.1 %pad_maximum_fusion.2.loaded = bf16[4,16,4,512]{3,2,1,0:T(4,128)(2,1)S(1)} fusion(bf16[2,16,4,512]{3,2,1,0:T(4,128)(2,1)} %param.7, bf16[2,16,4,512]{3,2,1,0:T(4,128)(2,1)} %param.6), kind=kLoop, calls=%fused_computation.2 | loop fusion | flops 131072 | bytes 524288 | tf_op jit(solution)/shard_map/concatenate | solution.py:505
  6.0 1.6 %collective-permute-start.2 = (bf16[2,128,512]{2,1,0:T(8,128)(2,1)S(1)}, bf16[2,128,512]{2,1,0:T(8,128)(2,1)S(1)}, u32[]{:S(2)}, u32[]{:S(2)}) collective-permute-start(bf16[2,128,512]{2,1,0:T(8,128)(2,1)S(1)} %prep.1.both), channel_id=1, source_target_pairs={{0,16},{8,24},{16,0},{24,8},{1,17},{9,25},{17,1},{25,9},{2,18},{10... | collective-permute-start | bytes 786440 | tf_op jit(solution)/shard_map/ppermute | solution.py:509
  7.6 0.0 copy-start
  7.6 1.6 %collective-permute-start = (bf16[2,48,512]{2,1,0:T(8,128)(2,1)S(1)}, bf16[2,48,512]{2,1,0:T(8,128)(2,1)S(1)}, u32[]{:S(2)}, u32[]{:S(2)}) collective-permute-start(bf16[2,48,512]{2,1,0:T(8,128)(2,1)S(1)} %get-tuple-element.41), channel_id=1, source_target_pairs={{0,2},{2,0},{4,6},{6,4},{1,3},{3,1},{5,7},{7,5},{8,10},{10,8},{12,... | collective-permute-start | bytes 294920 | tf_op jit(solution)/shard_map/ppermute | solution.py:512
  9.3 0.7 %collective-permute-start.1 = (bf16[2,48,512]{2,1,0:T(8,128)(2,1)S(1)}, bf16[2,48,512]{2,1,0:T(8,128)(2,1)S(1)}, u32[]{:S(2)}, u32[]{:S(2)}) collective-permute-start(bf16[2,48,512]{2,1,0:T(8,128)(2,1)S(1)} %get-tuple-element.42), channel_id=1, source_target_pairs={{2,4},{4,2},{3,5},{5,3},{10,12},{12,10},{11,13},{13,11},{18,20},{2... | collective-permute-start | bytes 294920 | tf_op jit(solution)/shard_map/ppermute | solution.py:513
  9.9 0.0 copy-done.3
  9.9 0.0 copy-done.2
  9.9 0.0 copy-done.1
  10.0 2.4 %maps_first.1.forward = bf16[4,384,256]{2,1,0:T(8,128)(2,1)S(1)} custom-call(s32[9,64]{1,0:T(8,128)S(1)} %bitcast.14, s32[9,64]{1,0:T(8,128)S(1)} %bitcast.16, f32[9,3,64]{2,1,0:T(4,128)S(1)} %bitcast.12), custom_call_target="tpu_custom_call" | custom-call | tf_op jit(solution)/shard_map/maps_first/pallas_call | solution.py:485
  12.4 0.0 collective-permute-done
  12.4 0.0 collective-permute-done.1
  12.4 1.4 %collective-permute-done.2 = bf16[2,128,512]{2,1,0:T(8,128)(2,1)S(1)} collective-permute-done((bf16[2,128,512]{2,1,0:T(8,128)(2,1)S(1)}, bf16[2,128,512]{2,1,0:T(8,128)(2,1)S(1)}, u32[]{:S(2)}, u32[]{:S(2)}) %collective-permute-start.2) | collective-permute-done | bytes 262176 | tf_op jit(solution)/shard_map/ppermute | solution.py:509
  13.8 1.5 %collective-permute-start.4 = (bf16[2,96,512]{2,1,0:T(8,128)(2,1)S(1)}, bf16[2,96,512]{2,1,0:T(8,128)(2,1)S(1)}, u32[]{:S(2)}, u32[]{:S(2)}) collective-permute-start(bf16[2,96,512]{2,1,0:T(8,128)(2,1)S(1)} %pad_maximum_fusion.4), channel_id=1, source_target_pairs={{0,16},{8,24},{16,0},{24,8},{1,17},{9,25},{17,1},{25,9},{2,18},{10... | collective-permute-start | bytes 589832 | tf_op jit(solution)/shard_map/ppermute | solution.py:528
  15.4 0.1 collective-permute-start.3
  15.5 1.9 %maps_again.1 = (bf16[3,384,256]{2,1,0:T(8,128)(2,1)S(1)}, bf16[3,256,384]{2,1,0:T(8,128)(2,1)S(1)}) custom-call(s32[9,64]{1,0:T(8,128)S(1)} %bitcast.15, s32[9,64]{1,0:T(8,128)S(1)} %bitcast.17, f32[9,3,64]{2,1,0:T(4,128)S(1)} %bitcast.13), custom_call_target="tpu_custom_call" | custom-call | tf_op jit(solution)/shard_map/maps_again/pallas_call | solution.py:485
  17.4 2.1 %collective-permute-done.4 = bf16[2,96,512]{2,1,0:T(8,128)(2,1)S(1)} collective-permute-done((bf16[2,96,512]{2,1,0:T(8,128)(2,1)S(1)}, bf16[2,96,512]{2,1,0:T(8,128)(2,1)S(1)}, u32[]{:S(2)}, u32[]{:S(2)}) %collective-permute-start.4) | collective-permute-done | bytes 196640 | tf_op jit(solution)/shard_map/ppermute | solution.py:528
  19.5 0.4 collective-permute-done.5.near_half
  19.9 0.0 collective-permute-start.6
  19.9 0.5 %collective-permute-start.7 = (bf16[656,512]{1,0:T(8,128)(2,1)S(1)}, bf16[656,512]{1,0:T(8,128)(2,1)S(1)}, u32[]{:S(2)}, u32[]{:S(2)}) collective-permute-start(bf16[656,512]{1,0:T(8,128)(2,1)S(1)} %collective-permute-done.5.near_half), channel_id=1, source_target_pairs={{0,8},{8,0},{16,24},{24,16},{1,9},{9,1},{17,25},{25,17},{2,10},{10... | collective-permute-start | bytes 2015240 | tf_op jit(solution)/shard_map/ppermute | solution.py:544
  20.4 0.0 copy-done
  20.5 1.8 %collective-permute-start.8 = (bf16[224,512]{1,0:T(8,128)(2,1)S(1)}, bf16[224,512]{1,0:T(8,128)(2,1)S(1)}, u32[]{:S(2)}, u32[]{:S(2)}) collective-permute-start(bf16[224,512]{1,0:T(8,128)(2,1)S(1)} %pad_maximum_fusion.3), channel_id=1, source_target_pairs={{0,1},{1,0},{2,3},{3,2},{4,5},{5,4},{6,7},{7,6},{8,9},{9,8},{10,11... | collective-permute-start | bytes 688136 | tf_op jit(solution)/shard_map/ppermute | solution.py:502
  22.3 0.0 collective-permute-done.3.b1
  22.3 0.0 collective-permute-done.6.b3
  22.3 3.8 %early.1 = (bf16[1024,1536]{1,0:T(8,128)(2,1)S(1)}, bf16[512,384]{1,0:T(8,128)(2,1)S(1)}, bf16[2,4,96,512]{3,2,1,0:T(8,128)(2,1)S(1)}, bf16[2,64,512]{2,1,0:T(8,128)(2,1)S(1)}) custom-call(bf16[2,224,512]{2,1,0:T(8,128)(2,1)S(1)} %pad_maximum_fusion.b0, bf16[2,224,512]{2,1,0:T(8,128)(2,1)S(1)} %collective-permute-done.3.b1, ...), custom_call_target="tpu_custom_call" | custom-call | flops 3000000000 | bytes 3000000 | tf_op jit(solution)/shard_map/early/pallas_call | solution.py:485
  26.1 2.0 %collective-permute-done.8.ends = bf16[224,512]{1,0:T(8,128)(2,1)S(1)} collective-permute-done((bf16[224,512]{1,0:T(8,128)(2,1)S(1)}, bf16[224,512]{1,0:T(8,128)(2,1)S(1)}, u32[]{:S(2)}, u32[]{:S(2)}) %collective-permute-start.8) | collective-permute-done | bytes 229408 | tf_op jit(solution)/shard_map/ppermute | solution.py:502
  28.0 0.0 collective-permute-done.7.far_half
  28.0 4.4 %chain.1 = (bf16[2,64,512]{2,1,0:T(8,128)(2,1)S(1)}, bf16[2,64,512]{2,1,0:T(8,128)(2,1)S(1)}, bf16[768,512]{1,0:T(8,128)(2,1)S(1)}, f32[384,128]{1,0:T(8,128)S(1...) custom-call(bf16[2,224,512]{2,1,0:T(8,128)(2,1)S(1)} %pad_maximum_fusion.b0, ...), custom_call_target="tpu_custom_call" | custom-call | flops 6000000000 | bytes 6000000 | tf_op jit(solution)/shard_map/chain/pallas_call | solution.py:485
  32.4 3.9 %collective-permute-start.9 = (bf16[384,128]{1,0:T(8,128)(2,1)S(1)}, bf16[384,128]{1,0:T(8,128)(2,1)S(1)}, u32[]{:S(2)}, u32[]{:S(2)}) collective-permute-start(bf16[384,128]{1,0:T(8,128)(2,1)S(1)} %get-tuple-element.72), channel_id=1, source_target_pairs={{0,6},{2,4},{4,2},{6,0},{1,7},{3,5},{5,3},{7,1},{8,14},{10,12},{12... | collective-permute-start | bytes 294920 | tf_op jit(solution)/shard_map/ppermute | solution.py:585
  36.3 0.6 %collective-permute-start.10 = (bf16[384,128]{1,0:T(8,128)(2,1)S(1)}, bf16[384,128]{1,0:T(8,128)(2,1)S(1)}, u32[]{:S(2)}, u32[]{:S(2)}) collective-permute-start(bf16[384,128]{1,0:T(8,128)(2,1)S(1)} %get-tuple-element.73), channel_id=1, source_target_pairs={{0,4},{2,6},{4,0},{6,2},{1,5},{3,7},{5,1},{7,3},{8,12},{10,14},{12... | collective-permute-start | bytes 294920 | tf_op jit(solution)/shard_map/ppermute | solution.py:585
  36.9 0.5 %collective-permute-start.11 = (bf16[384,128]{1,0:T(8,128)(2,1)S(1)}, bf16[384,128]{1,0:T(8,128)(2,1)S(1)}, u32[]{:S(2)}, u32[]{:S(2)}) collective-permute-start(bf16[384,128]{1,0:T(8,128)(2,1)S(1)} %get-tuple-element.74), channel_id=1, source_target_pairs={{0,2},{2,0},{4,6},{6,4},{1,3},{3,1},{5,7},{7,5},{8,10},{10,8},{12,... | collective-permute-start | bytes 294920 | tf_op jit(solution)/shard_map/ppermute | solution.py:585
  37.4 2.5 %finish.1 = (bf16[2,16,4,512]{3,2,1,0:T(4,128)(2,1)}, bf16[2,16,4,512]{3,2,1,0:T(4,128)(2,1)}) custom-call(bf16[1536,512]{1,0:T(8,128)(2,1)S(1)} %bitcast.11, bf16[3,256,384]{2,1,0:T(8,128)(2,1)S(1)} %get-tuple-element.52.backward, bf16[768,512]{1,0:T(8,128)(2,1)S(1)} %get-tuple-element.66.gates, bf16[2,64,512]{2,1,0:T(8,128)(2,1)S(1)} %get-tuple-element.67.next_ref, ...), custom_call_target="tpu_custom_call" | custom-call | flops 2000000000 | bytes 2000000 | tf_op jit(solution)/shard_map/finish/pallas_call | solution.py:485
  39.9 0.0 collective-permute-done.9.p1
  39.9 4.9 %collective-permute-done.10.p2 = bf16[384,128]{1,0:T(8,128)(2,1)S(1)} collective-permute-done((bf16[384,128]{1,0:T(8,128)(2,1)S(1)}, bf16[384,128]{1,0:T(8,128)(2,1)S(1)}, u32[]{:S(2)}, u32[]{:S(2)}) %collective-permute-start.10) | collective-permute-done | bytes 98336 | tf_op jit(solution)/shard_map/ppermute | solution.py:585
  44.7 0.0 collective-permute-done.11.p3
  44.8 0.7 %add_up.1 = f32[384,128]{1,0:T(8,128)} custom-call(f32[384,128]{1,0:T(8,128)S(1)} %get-tuple-element.71.mine, bf16[384,128]{1,0:T(8,128)(2,1)S(1)} %collective-permute-done.9.p1, bf16[384,128]{1,0:T(8,128)(2,1)S(1)} %collective-permute-done.10.p2, bf16[384,128]{1,0:T(8,128)(2,1)S(1)} %collective-permute-done.11.p3), custom_call_target="tpu_custom_call" | custom-call | flops 100000000 | bytes 100000 | tf_op jit(solution)/shard_map/add_up/pallas_call | solution.py:485
  (7 shorter events, 0.2 us)
Async XLA Ops:
  0.6 9.3 %copy-start.3 = (s32[64,9]{0,1:T(8,128)S(1)}, s32[64,9]{0,1:T(8,128)}, u32[]{:S(2)}) copy-start(s32[64,9]{0,1:T(8,128)} %param.11) | copy-start | bytes 6916
  0.6 9.3 %copy-start.2 = (s32[64,9]{0,1:T(8,128)S(1)}, s32[64,9]{0,1:T(8,128)}, u32[]{:S(2)}) copy-start(s32[64,9]{0,1:T(8,128)} %param.10) | copy-start | bytes 6916
  0.7 9.3 %copy-start.1 = (f32[64,9,3]{0,2,1:T(4,128)S(1)}, f32[64,9,3]{0,2,1:T(4,128)}, u32[]{:S(2)}) copy-start(f32[64,9,3]{0,2,1:T(4,128)} %param.9) | copy-start | bytes 20740
  1.8 18.1 %collective-permute-start.5 = (bf16[656,512]{1,0:T(8,128)(2,1)S(1)}, bf16[656,512]{1,0:T(8,128)(2,1)S(1)}, u32[]{:S(2)}, u32[]{:S(2)}) collective-permute-start(bf16[656,512]{1,0:T(8,128)(2,1)S(1)} %constant_dynamic-slice_fusion), channel_id=1, source_target_pairs={{0,1},{1,0},{2,3},{3,2},{4,5},{5,4},{6,7},{7,6},{8,9},{9,8},{10,11... | collective-permute-start | bytes 2015240 | tf_op jit(solution)/shard_map/ppermute | solution.py:503
  6.0 7.8 %collective-permute-start.2 = (bf16[2,128,512]{2,1,0:T(8,128)(2,1)S(1)}, bf16[2,128,512]{2,1,0:T(8,128)(2,1)S(1)}, u32[]{:S(2)}, u32[]{:S(2)}) collective-permute-start(bf16[2,128,512]{2,1,0:T(8,128)(2,1)S(1)} %prep.1.both), channel_id=1, source_target_pairs={{0,16},{8,24},{16,0},{24,8},{1,17},{9,25},{17,1},{25,9},{2,18},{10... | collective-permute-start | bytes 786440 | tf_op jit(solution)/shard_map/ppermute | solution.py:509
  7.6 12.8 %copy-start = (bf16[1,3,512,512]{3,2,1,0:T(8,128)(2,1)S(1)}, bf16[1,3,512,512]{3,2,1,0:T(8,128)(2,1)}, u32[]{:S(2)}) copy-start(bf16[1,3,512,512]{3,2,1,0:T(8,128)(2,1)} %param.8) | copy-start | bytes 4718596
  7.6 4.8 %collective-permute-start = (bf16[2,48,512]{2,1,0:T(8,128)(2,1)S(1)}, bf16[2,48,512]{2,1,0:T(8,128)(2,1)S(1)}, u32[]{:S(2)}, u32[]{:S(2)}) collective-permute-start(bf16[2,48,512]{2,1,0:T(8,128)(2,1)S(1)} %get-tuple-element.41), channel_id=1, source_target_pairs={{0,2},{2,0},{4,6},{6,4},{1,3},{3,1},{5,7},{7,5},{8,10},{10,8},{12,... | collective-permute-start | bytes 294920 | tf_op jit(solution)/shard_map/ppermute | solution.py:512
  9.3 3.1 %collective-permute-start.1 = (bf16[2,48,512]{2,1,0:T(8,128)(2,1)S(1)}, bf16[2,48,512]{2,1,0:T(8,128)(2,1)S(1)}, u32[]{:S(2)}, u32[]{:S(2)}) collective-permute-start(bf16[2,48,512]{2,1,0:T(8,128)(2,1)S(1)} %get-tuple-element.42), channel_id=1, source_target_pairs={{2,4},{4,2},{3,5},{5,3},{10,12},{12,10},{11,13},{13,11},{18,20},{2... | collective-permute-start | bytes 294920 | tf_op jit(solution)/shard_map/ppermute | solution.py:513
  13.8 5.7 %collective-permute-start.4 = (bf16[2,96,512]{2,1,0:T(8,128)(2,1)S(1)}, bf16[2,96,512]{2,1,0:T(8,128)(2,1)S(1)}, u32[]{:S(2)}, u32[]{:S(2)}) collective-permute-start(bf16[2,96,512]{2,1,0:T(8,128)(2,1)S(1)} %pad_maximum_fusion.4), channel_id=1, source_target_pairs={{0,16},{8,24},{16,0},{24,8},{1,17},{9,25},{17,1},{25,9},{2,18},{10... | collective-permute-start | bytes 589832 | tf_op jit(solution)/shard_map/ppermute | solution.py:528
  15.4 6.9 %collective-permute-start.3 = (bf16[2,224,512]{2,1,0:T(8,128)(2,1)S(1)}, bf16[2,224,512]{2,1,0:T(8,128)(2,1)S(1)}, u32[]{:S(2)}, u32[]{:S(2)}) collective-permute-start(bf16[2,224,512]{2,1,0:T(8,128)(2,1)S(1)} %pad_maximum_fusion.b0), channel_id=1, source_target_pairs={{0,8},{8,0},{16,24},{24,16},{1,9},{9,1},{17,25},{25,17},{2,10},{10... | collective-permute-start | bytes 1376264 | tf_op jit(solution)/shard_map/ppermute | solution.py:530
  19.9 2.4 %collective-permute-start.6 = (bf16[2,224,512]{2,1,0:T(8,128)(2,1)S(1)}, bf16[2,224,512]{2,1,0:T(8,128)(2,1)S(1)}, u32[]{:S(2)}, u32[]{:S(2)}) collective-permute-start(bf16[2,224,512]{2,1,0:T(8,128)(2,1)S(1)} %pad_maximum_fusion.1.b2), channel_id=1, source_target_pairs={{0,8},{8,0},{16,24},{24,16},{1,9},{9,1},{17,25},{25,17},{2,10},{10... | collective-permute-start | bytes 1376264 | tf_op jit(solution)/shard_map/ppermute | solution.py:543
  19.9 8.1 %collective-permute-start.7 = (bf16[656,512]{1,0:T(8,128)(2,1)S(1)}, bf16[656,512]{1,0:T(8,128)(2,1)S(1)}, u32[]{:S(2)}, u32[]{:S(2)}) collective-permute-start(bf16[656,512]{1,0:T(8,128)(2,1)S(1)} %collective-permute-done.5.near_half), channel_id=1, source_target_pairs={{0,8},{8,0},{16,24},{24,16},{1,9},{9,1},{17,25},{25,17},{2,10},{10... | collective-permute-start | bytes 2015240 | tf_op jit(solution)/shard_map/ppermute | solution.py:544
  20.5 7.6 %collective-permute-start.8 = (bf16[224,512]{1,0:T(8,128)(2,1)S(1)}, bf16[224,512]{1,0:T(8,128)(2,1)S(1)}, u32[]{:S(2)}, u32[]{:S(2)}) collective-permute-start(bf16[224,512]{1,0:T(8,128)(2,1)S(1)} %pad_maximum_fusion.3), channel_id=1, source_target_pairs={{0,1},{1,0},{2,3},{3,2},{4,5},{5,4},{6,7},{7,6},{8,9},{9,8},{10,11... | collective-permute-start | bytes 688136 | tf_op jit(solution)/shard_map/ppermute | solution.py:502
  32.4 7.5 %collective-permute-start.9 = (bf16[384,128]{1,0:T(8,128)(2,1)S(1)}, bf16[384,128]{1,0:T(8,128)(2,1)S(1)}, u32[]{:S(2)}, u32[]{:S(2)}) collective-permute-start(bf16[384,128]{1,0:T(8,128)(2,1)S(1)} %get-tuple-element.72), channel_id=1, source_target_pairs={{0,6},{2,4},{4,2},{6,0},{1,7},{3,5},{5,3},{7,1},{8,14},{10,12},{12... | collective-permute-start | bytes 294920 | tf_op jit(solution)/shard_map/ppermute | solution.py:585
  36.3 8.4 %collective-permute-start.10 = (bf16[384,128]{1,0:T(8,128)(2,1)S(1)}, bf16[384,128]{1,0:T(8,128)(2,1)S(1)}, u32[]{:S(2)}, u32[]{:S(2)}) collective-permute-start(bf16[384,128]{1,0:T(8,128)(2,1)S(1)} %get-tuple-element.73), channel_id=1, source_target_pairs={{0,4},{2,6},{4,0},{6,2},{1,5},{3,7},{5,1},{7,3},{8,12},{10,14},{12... | collective-permute-start | bytes 294920 | tf_op jit(solution)/shard_map/ppermute | solution.py:585
  36.9 7.8 %collective-permute-start.11 = (bf16[384,128]{1,0:T(8,128)(2,1)S(1)}, bf16[384,128]{1,0:T(8,128)(2,1)S(1)}, u32[]{:S(2)}, u32[]{:S(2)}) collective-permute-start(bf16[384,128]{1,0:T(8,128)(2,1)S(1)} %get-tuple-element.74), channel_id=1, source_target_pairs={{0,2},{2,0},{4,6},{6,4},{1,3},{3,1},{5,7},{7,5},{8,10},{10,8},{12,... | collective-permute-start | bytes 294920 | tf_op jit(solution)/shard_map/ppermute | solution.py:585

commit v10 on v9

--- a/solution.py
+++ b/solution.py
@@ -301,8 +301,7 @@
                 near = take(blk, m, state_parts, o, o + win)
                 put_spread(dot(forward[g], near).astype(jnp.bfloat16), into, (m * nf + g) * cells)
 
-    def first_section(blk, w, s0, s1, again, mid, slope):
-        total = dot(s0[...], w[...])
+    def first_section(blk, total, s1, again, mid, slope):
         for m in range(members):
             for g in range(nf):
                 mixed = total[(m * nf + g) * cells : (m * nf + g + 1) * cells]
@@ -327,7 +326,7 @@
         @pl.when(lax.axis_index("segment") == 0)
         def _():
             spread(blk, forward, s0)
-            first_section(blk, w_own, s0, s, again, mid, slope)
+            first_section(blk, dot(s0[...], w_own[...]), s, again, mid, slope)
             for m in range(members):
                 size = (nf - 2) * cells
                 left[m * size : (m + 1) * size, :] = s0[(m * nf + 1) * cells : (m * nf + nf - 1) * cells, columns_of(lax.axis_index("lon"))]
@@ -336,6 +335,24 @@
         @pl.when(lax.axis_index("segment") == 1)
         def _():
             spread(blk, forward, s)
+
+    def partial(s, near_half, far_half, w, part):
+        rows = near_half.shape[0]
+        here = lax.axis_index("lon") % 2 * (width // 2)
+        for base, ref in ((here, near_half), (width // 2 - here, far_half)):
+            w[pl.ds(pl.multiple_of(base, 32), rows), :] = ref[...]
+        for i in range(2):
+            late = slice(i * (width // 2) + rows, (i + 1) * (width // 2))
+            w[late, :] = jnp.zeros((width // 2 - rows, channels), w.dtype)
+
+        @pl.when(lax.axis_index("segment") == 0)
+        def _():
+            size = members * ns * cells
+            part[:size, :] = dot(s[:size, :], w[...])
+
+        @pl.when(lax.axis_index("segment") == 1)
+        def _():
+            part[...] = dot(s[...], w[...])
 
     def own_part(g):
         return max(g * band, half_edge), min((g + 1) * band, half_edge + own)
@@ -346,23 +363,31 @@
             for i in range(members * ns):
                 feat[(i * BASIS + b) * cells : (i * BASIS + b + 1) * cells, :] = got[i * cells : (i + 1) * cells]
 
-    def chain(b0, b1, b2, b3, w_own, near_half, far_half, ends, again, backward, s, left0, slope, early_out,
-              out_ref, next_ref, gate_ref, own_ref, p1, p2, p3, w, s1, mid, gates, feat, pull, grads):
+    def chain(b0, b1, b2, b3, w_own, w_in, part, ends, again, backward, s, left0, slope, early_out, w,
+              out_ref, next_ref, gate_ref, own_ref, p1, p2, p3, late, s1, mid, gates, feat, pull, grads):
         blk = (b0, b1, b2, b3)
         seg, lon, lat = lax.axis_index("segment"), lax.axis_index("lon"), lax.axis_index("lat")
-        here = lon % 2 * (width // 2)
-        there = width // 2 - here
-        rows, rest = near_half.shape[0], ends.shape[0] // 2
-        for base, ref in ((here, near_half), (there, far_half)):
-            w[pl.ds(pl.multiple_of(base, 32), rows), :] = ref[...]
-        w[rows : rows + rest, :] = ends[:rest]
-        w[width - rest :, :] = ends[rest:]
+        rest = ends.shape[0] // 2
+        rows = width // 2 - rest
+        aligned = rows // lanes * lanes
+        span = width // 2 - aligned
+        for i in range(2):
+            piece = ends[i * rest : (i + 1) * rest, :]
+            w[i * (width // 2) + rows : (i + 1) * (width // 2), :] = piece
+            late[i * span : (i + 1) * span - rest, :] = jnp.zeros((span - rest, channels), late.dtype)
+            late[(i + 1) * span - rest : (i + 1) * span, :] = piece
+
+        def complete(size):
+            total = part[:size, :]
+            for i in range(2):
+                at = i * (width // 2) + aligned
+                total = total + dot(s[:size, at : at + span], late[i * span : (i + 1) * span, :])
+            return total
 
         def coming_at(m, g):
             return take(blk, m, coming_parts, g * band, (g + 1) * band).astype(jnp.float32)
 
-        def second_section(weight, spread_ref, into, last):
-            total = dot(spread_ref[: members * ns * cells, :], weight[...])
+        def second_section(total, into, last):
             for m in range(members):
                 for g in range(ns):
                     at = (m * ns + g) * cells
@@ -383,7 +408,7 @@
 
         @pl.when(seg == 0)
         def _():
-            second_section(w, s, gates, False)
+            second_section(complete(members * ns * cells), gates, False)
             out_ref[...] = early_out[...]
             apply_back(w, gates, feat)
             for m in range(members):
@@ -417,8 +442,8 @@
 
         @pl.when(seg == 1)
         def _():
-            first_section(blk, w, s, s1, again, mid, None)
-            second_section(w_own, s1, gate_ref, True)
+            first_section(blk, complete(members * nf * cells), s1, again, mid, None)
+            second_section(dot(s1[...], w_own[...]), gate_ref, True)
             left, right = [], []
             for m in range(members):
                 next_ref[m, :, :] = b0[m, own : 2 * own, :]
@@ -454,7 +479,7 @@
             grad_ref[m] = total.astype(jnp.bfloat16).reshape(lat_rows, lon_cols, channels)
             out_ref[m] = last_ref[m].reshape(lat_rows, lon_cols, channels)
 
-    return prep, edges, maps, early, chain, finish
+    return prep, edges, maps, early, partial, chain, finish
 
 
 def add_up(scale, mine, p1, p2, p3, out):
@@ -479,23 +504,23 @@
     cells = blocks * BAND * lon_cols
     win = 16 * lon_cols
     vmem = pl.BlockSpec(memory_space=pltpu.VMEM)
-    anywhere = pl.BlockSpec(memory_space=pltpu.HBM)
-
-    def call(body, name, outs, ins, mib, gflops, scratch=(), far=()):
+
+    def call(body, name, outs, ins, mib, gflops, scratch=(), aliases={}):
         return pl.pallas_call(
             body,
             out_shape=outs,
-            in_specs=[anywhere if i in far else vmem for i, a in enumerate(ins)],
+            in_specs=[vmem] * len(ins),
             out_specs=(vmem,) * len(outs),
             scratch_shapes=list(scratch),
+            input_output_aliases=aliases,
             compiler_params=pltpu.CompilerParams(vmem_limit_bytes=int(mib * 1024 * 1024)),
             cost_estimate=pl.CostEstimate(flops=int(gflops * 1e9), bytes_accessed=int(gflops * 1e6), transcendentals=0),
             name=name,
         )(*ins)
 
-    prep, edges, maps, early, chain, finish = make_steps(lat_rows, lon_cols, blocks, members, channels, lat_devices)
+    prep, edges, maps, early, partial, chain, finish = make_steps(lat_rows, lon_cols, blocks, members, channels, lat_devices)
     kernel = weights.reshape(width, channels)
-    rest = width // 2 * 7 // 48
+    rest = width // 2 * 5 // 48
     rows = width // 2 - rest
     half = lax.dynamic_slice_in_dim(kernel, lax.axis_index("lon") % 2 * (width // 2), rows, 0)
     ends = jnp.concatenate([kernel[rows : rows + rest], kernel[width - rest :]], axis=0)
@@ -557,23 +582,33 @@
         3.0,
         (pltpu.VMEM(s_type, half_type), pltpu.VMEM((members, blocks, own + 2 * edge, channels), half_type)),
     )
-    near_ends, s = lax.optimization_barrier((near_ends, s))
+    w_type = shape((width, channels), half_type)
+    w, part = call(
+        partial,
+        "partial",
+        (w_type, shape((s_type[0], channels), full_type)),
+        (s, near_half, far_half),
+        8,
+        1.5,
+    )
+    near_ends, part = lax.optimization_barrier((near_ends, part))
     lines = (width // blocks // lat_devices * channels // 128, 128)
-    out, follow, gates, mine, *parts = call(
+    _, out, follow, gates, mine, *parts = call(
         chain,
         "chain",
         (
+            w_type,
             shape((members, own, channels), half_type),
             shape((members, own, channels), half_type),
             shape((members * ns * cells, channels), half_type),
             shape(lines, full_type),
         )
         + (shape(lines, half_type),) * 3,
-        (b0, b1, b2, b3, kernel, near_half, far_half, near_ends, again, backward, s, left, slope, early_out),
+        (b0, b1, b2, b3, kernel, w, part, near_ends, again, backward, s, left, slope, early_out),
         18,
         6.0,
         (
-            pltpu.VMEM((width, channels), half_type),
+            pltpu.VMEM((2 * (width // 2 - (width // 2 - rest) // 128 * 128), channels), half_type),
             pltpu.VMEM((members * ns * cells, width), half_type),
             pltpu.VMEM((members, blocks, own + 2 * edge, channels), half_type),
             pltpu.VMEM((members * ns * cells, channels), half_type),
@@ -581,6 +616,7 @@
             pltpu.VMEM((members, blocks, own + 2 * edge, channels), full_type),
             pltpu.VMEM((width // blocks * channels // 128, 128), full_type),
         ),
+        {5: 0},
     )
     got = [lax.ppermute(part, "lat", swap("lat", bit)) for bit, part in reversed(list(zip((1, 2, 3), parts)))]
     block = (members, lat_rows, lon_cols, channels)

time: 45.6 us -> 45.2 us (level)
  Pallas kernels: 15.7 us -> 16.3 us
  starting transfers between devices: 15.8 us -> 15.2 us
    ppermute x1, waiting for transfers between devices: 1.98 us -> 0.01 us  [whole_ring(): near_ends = lax.ppermute(ends, 'segment', swap('segment', 1))]
    ppermute x3, waiting for transfers between devices: 4.86 us -> 5.66 us  [whole_ring(): lax.ppermute(part, 'lat', swap('lat', bit))]
    ppermute x1, waiting for transfers between devices: 0.36 us -> 1.07 us  [whole_ring(): near_half = lax.ppermute(half, 'segment', swap('segment', 1))]
    pallas_call x8 -> x9, Pallas kernels: 15.7 us -> 16.3 us  [call(): pl.pallas_call(body, out_shape=outs, in_specs=[vmem] * len(ins), out_spec...]
    ppermute x3, starting transfers between devices: 5.03 us -> 4.45 us  [whole_ring(): lax.ppermute(part, 'lat', swap('lat', bit))]
  transfers between devices with their start and end apart: 12 -> 12, of which waited for: 5 -> 4; matrix products, arithmetic and copies ran while one was open for 3% -> 3% of each run, Pallas kernels for 23% -> 27%
where the time goes in v10:
time: 45.2 us; the launch traced here: 45.1 us
  Pallas kernels  16.3 us (36%)
  starting transfers between devices  15.2 us (34%)
  waiting for transfers between devices  10.3 us (23%)
  other arithmetic  1.23 us (3%)
  local copies, waits for them, and re-layouts  1.19 us (3%)
  between operations  0.83 us (2%)
    pallas_call x9, Pallas kernels, call(): pl.pallas_call(body, out_shape=outs, in_specs=[vmem] * len(ins), out_spec...  16.3 us
    ppermute x3, waiting for transfers between devices, whole_ring(): lax.ppermute(part, 'lat', swap('lat', bit))  5.66 us
    ppermute x3, starting transfers between devices, whole_ring(): lax.ppermute(part, 'lat', swap('lat', bit))  4.45 us
    ppermute x1, starting transfers between devices, whole_ring(): near_half = lax.ppermute(half, 'segment', swap('segment', 1))  3 us
    ppermute x1, waiting for transfers between devices, whole_ring(): sides_y = lax.ppermute(sides, 'lon', swap('lon', 2))  2.12 us
    ppermute x1, starting transfers between devices, whole_ring(): near_ends = lax.ppermute(ends, 'segment', swap('segment', 1))  1.81 us
    ppermute x1, starting transfers between devices, whole_ring(): from_near = lax.ppermute(toward, 'lat', near_pairs)  1.64 us
    ppermute x1, starting transfers between devices, whole_ring(): both_y = lax.ppermute(both, 'lon', swap('lon', 2))  1.58 us
  transfers between devices with their start and end apart: 12, of which 4 were waited for; matrix products, arithmetic and copies ran while one was open for 3% of the time, Pallas kernels for 27%

profile of v10, /device:TPU:0, one launch (start us, length us, event | category | flops | bytes accessed | tf_op | source)
XLA Modules:
  0.0 45.1 jit_solution(1156657180800861981)
XLA Ops:
  0.6 0.0 copy-start.3
  0.6 0.0 copy-start.2
  0.7 0.0 copy-start.1
  0.7 1.2 %constant_dynamic-slice_fusion = bf16[688,512]{1,0:T(8,128)(2,1)S(1)} fusion(bf16[1536,512]{1,0:T(8,128)(2,1)} %bitcast.7, s32[]{:T(128)S(6)} %select_n.11), kind=kLoop, calls=%fused_computation.5 | loop fusion | bytes 1409028 | tf_op jit(solution)/shard_map/dynamic_slice | solution.py:525
  1.8 3.0 %collective-permute-start.5 = (bf16[688,512]{1,0:T(8,128)(2,1)S(1)}, bf16[688,512]{1,0:T(8,128)(2,1)S(1)}, u32[]{:S(2)}, u32[]{:S(2)}) collective-permute-start(bf16[688,512]{1,0:T(8,128)(2,1)S(1)} %constant_dynamic-slice_fusion), channel_id=1, source_target_pairs={{0,1},{1,0},{2,3},{3,2},{4,5},{5,4},{6,7},{7,6},{8,9},{9,8},{10,11... | collective-permute-start | bytes 2113544 | tf_op jit(solution)/shard_map/ppermute | solution.py:528
  4.8 1.1 %pad_maximum_fusion.2.loaded = bf16[4,16,4,512]{3,2,1,0:T(4,128)(2,1)S(1)} fusion(bf16[2,16,4,512]{3,2,1,0:T(4,128)(2,1)} %param.7, bf16[2,16,4,512]{3,2,1,0:T(4,128)(2,1)} %param.6), kind=kLoop, calls=%fused_computation.2 | loop fusion | flops 131072 | bytes 524288 | tf_op jit(solution)/shard_map/concatenate | solution.py:530
  6.0 1.6 %collective-permute-start.2 = (bf16[2,128,512]{2,1,0:T(8,128)(2,1)S(1)}, bf16[2,128,512]{2,1,0:T(8,128)(2,1)S(1)}, u32[]{:S(2)}, u32[]{:S(2)}) collective-permute-start(bf16[2,128,512]{2,1,0:T(8,128)(2,1)S(1)} %prep.1.both), channel_id=1, source_target_pairs={{0,16},{8,24},{16,0},{24,8},{1,17},{9,25},{17,1},{25,9},{2,18},{10... | collective-permute-start | bytes 786440 | tf_op jit(solution)/shard_map/ppermute | solution.py:534
  7.6 0.0 copy-start
  7.6 1.6 %collective-permute-start = (bf16[2,48,512]{2,1,0:T(8,128)(2,1)S(1)}, bf16[2,48,512]{2,1,0:T(8,128)(2,1)S(1)}, u32[]{:S(2)}, u32[]{:S(2)}) collective-permute-start(bf16[2,48,512]{2,1,0:T(8,128)(2,1)S(1)} %get-tuple-element.43), channel_id=1, source_target_pairs={{0,2},{2,0},{4,6},{6,4},{1,3},{3,1},{5,7},{7,5},{8,10},{10,8},{12,... | collective-permute-start | bytes 294920 | tf_op jit(solution)/shard_map/ppermute | solution.py:537
  9.3 0.7 %collective-permute-start.1 = (bf16[2,48,512]{2,1,0:T(8,128)(2,1)S(1)}, bf16[2,48,512]{2,1,0:T(8,128)(2,1)S(1)}, u32[]{:S(2)}, u32[]{:S(2)}) collective-permute-start(bf16[2,48,512]{2,1,0:T(8,128)(2,1)S(1)} %get-tuple-element.44), channel_id=1, source_target_pairs={{2,4},{4,2},{3,5},{5,3},{10,12},{12,10},{11,13},{13,11},{18,20},{2... | collective-permute-start | bytes 294920 | tf_op jit(solution)/shard_map/ppermute | solution.py:538
  9.9 0.0 copy-done.3
  10.0 0.0 copy-done.2
  10.0 0.0 copy-done.1
  10.0 2.4 %maps_first.1.forward = bf16[4,384,256]{2,1,0:T(8,128)(2,1)S(1)} custom-call(s32[9,64]{1,0:T(8,128)S(1)} %bitcast.14, s32[9,64]{1,0:T(8,128)S(1)} %bitcast.16, f32[9,3,64]{2,1,0:T(4,128)S(1)} %bitcast.12), custom_call_target="tpu_custom_call" | custom-call | tf_op jit(solution)/shard_map/maps_first/pallas_call | solution.py:509
  12.4 0.0 collective-permute-done
  12.4 0.0 collective-permute-done.1
  12.4 1.4 %collective-permute-done.2 = bf16[2,128,512]{2,1,0:T(8,128)(2,1)S(1)} collective-permute-done((bf16[2,128,512]{2,1,0:T(8,128)(2,1)S(1)}, bf16[2,128,512]{2,1,0:T(8,128)(2,1)S(1)}, u32[]{:S(2)}, u32[]{:S(2)}) %collective-permute-start.2) | collective-permute-done | bytes 262176 | tf_op jit(solution)/shard_map/ppermute | solution.py:534
  13.9 1.5 %collective-permute-start.4 = (bf16[2,96,512]{2,1,0:T(8,128)(2,1)S(1)}, bf16[2,96,512]{2,1,0:T(8,128)(2,1)S(1)}, u32[]{:S(2)}, u32[]{:S(2)}) collective-permute-start(bf16[2,96,512]{2,1,0:T(8,128)(2,1)S(1)} %pad_maximum_fusion.3), channel_id=1, source_target_pairs={{0,16},{8,24},{16,0},{24,8},{1,17},{9,25},{17,1},{25,9},{2,18},{10... | collective-permute-start | bytes 589832 | tf_op jit(solution)/shard_map/ppermute | solution.py:553
  15.4 0.1 collective-permute-start.3
  15.5 1.9 %maps_again.1 = (bf16[3,384,256]{2,1,0:T(8,128)(2,1)S(1)}, bf16[3,256,384]{2,1,0:T(8,128)(2,1)S(1)}) custom-call(s32[9,64]{1,0:T(8,128)S(1)} %bitcast.15, s32[9,64]{1,0:T(8,128)S(1)} %bitcast.17, f32[9,3,64]{2,1,0:T(4,128)S(1)} %bitcast.13), custom_call_target="tpu_custom_call" | custom-call | tf_op jit(solution)/shard_map/maps_again/pallas_call | solution.py:509
  17.4 2.1 %collective-permute-done.4 = bf16[2,96,512]{2,1,0:T(8,128)(2,1)S(1)} collective-permute-done((bf16[2,96,512]{2,1,0:T(8,128)(2,1)S(1)}, bf16[2,96,512]{2,1,0:T(8,128)(2,1)S(1)}, u32[]{:S(2)}, u32[]{:S(2)}) %collective-permute-start.4) | collective-permute-done | bytes 196640 | tf_op jit(solution)/shard_map/ppermute | solution.py:553
  19.6 1.1 %collective-permute-done.5.near_half = bf16[688,512]{1,0:T(8,128)(2,1)S(1)} collective-permute-done((bf16[688,512]{1,0:T(8,128)(2,1)S(1)}, bf16[688,512]{1,0:T(8,128)(2,1)S(1)}, u32[]{:S(2)}, u32[]{:S(2)}) %collective-permute-start.5) | collective-permute-done | bytes 704544 | tf_op jit(solution)/shard_map/ppermute | solution.py:528
  20.6 0.0 collective-permute-start.6
  20.6 0.5 %collective-permute-start.7 = (bf16[688,512]{1,0:T(8,128)(2,1)S(1)}, bf16[688,512]{1,0:T(8,128)(2,1)S(1)}, u32[]{:S(2)}, u32[]{:S(2)}) collective-permute-start(bf16[688,512]{1,0:T(8,128)(2,1)S(1)} %collective-permute-done.5.near_half), channel_id=1, source_target_pairs={{0,8},{8,0},{16,24},{24,16},{1,9},{9,1},{17,25},{25,17},{2,10},{10... | collective-permute-start | bytes 2113544 | tf_op jit(solution)/shard_map/ppermute | solution.py:569
  21.1 0.0 copy-done
  21.2 1.8 %collective-permute-start.8 = (bf16[160,512]{1,0:T(8,128)(2,1)S(1)}, bf16[160,512]{1,0:T(8,128)(2,1)S(1)}, u32[]{:S(2)}, u32[]{:S(2)}) collective-permute-start(bf16[160,512]{1,0:T(8,128)(2,1)S(1)} %pad_maximum_fusion.4), channel_id=1, source_target_pairs={{0,1},{1,0},{2,3},{3,2},{4,5},{5,4},{6,7},{7,6},{8,9},{9,8},{10,11... | collective-permute-start | bytes 491528 | tf_op jit(solution)/shard_map/ppermute | solution.py:527
  23.0 0.0 collective-permute-done.3.b1
  23.0 0.0 collective-permute-done.6.b3
  23.0 3.8 %early.1 = (bf16[1024,1536]{1,0:T(8,128)(2,1)S(1)}, bf16[512,384]{1,0:T(8,128)(2,1)S(1)}, bf16[2,4,96,512]{3,2,1,0:T(8,128)(2,1)S(1)}, bf16[2,64,512]{2,1,0:T(8,128)(2,1)S(1)}) custom-call(bf16[2,224,512]{2,1,0:T(8,128)(2,1)S(1)} %pad_maximum_fusion.b0, bf16[2,224,512]{2,1,0:T(8,128)(2,1)S(1)} %collective-permute-done.3.b1, ...), custom_call_target="tpu_custom_call" | custom-call | flops 3000000000 | bytes 3000000 | tf_op jit(solution)/shard_map/early/pallas_call | solution.py:509
  26.8 0.0 collective-permute-done.7.far_half
  26.8 1.5 %partial.1 = (bf16[1536,512]{1,0:T(8,128)(2,1)S(1)}, f32[1024,512]{1,0:T(8,128)S(1)}) custom-call(bf16[1024,1536]{1,0:T(8,128)(2,1)S(1)} %get-tuple-element.61.s, bf16[688,512]{1,0:T(8,128)(2,1)S(1)} %collective-permute-done.5.near_half, bf16[688,512]{1,0:T(8,128)(2,1)S(1)} %collective-permute-done.7.far_half), custom_call_target="tpu_custom_call" | custom-call | flops 1500000000 | bytes 1500000 | tf_op jit(solution)/shard_map/partial/pallas_call | solution.py:509
  28.3 0.0 collective-permute-done.8.ends
  28.3 3.5 %chain.1 = (bf16[1536,512]{1,0:T(8,128)(2,1)S(1)}, bf16[2,64,512]{2,1,0:T(8,128)(2,1)S(1)}, bf16[2,64,512]{2,1,0:T(8,128)(2,1)S(1)}, bf16[768,512]{1,0:T(8,128)(...) custom-call(bf16[2,224,512]{2,1,0:T(8,128)(2,1)S(1)} %pad_maximum_fu, ...), custom_call_target="tpu_custom_call", output_to_operand_aliasing={{0}: (5, {})} | custom-call | flops 6000000000 | bytes 6000000 | tf_op jit(solution)/shard_map/chain/pallas_call | solution.py:509
  31.8 3.7 %collective-permute-start.9 = (bf16[384,128]{1,0:T(8,128)(2,1)S(1)}, bf16[384,128]{1,0:T(8,128)(2,1)S(1)}, u32[]{:S(2)}, u32[]{:S(2)}) collective-permute-start(bf16[384,128]{1,0:T(8,128)(2,1)S(1)} %get-tuple-element.76), channel_id=1, source_target_pairs={{0,6},{2,4},{4,2},{6,0},{1,7},{3,5},{5,3},{7,1},{8,14},{10,12},{12... | collective-permute-start | bytes 294920 | tf_op jit(solution)/shard_map/ppermute | solution.py:621
  35.5 0.0 collective-permute-start.10
  35.5 0.8 %collective-permute-start.11 = (bf16[384,128]{1,0:T(8,128)(2,1)S(1)}, bf16[384,128]{1,0:T(8,128)(2,1)S(1)}, u32[]{:S(2)}, u32[]{:S(2)}) collective-permute-start(bf16[384,128]{1,0:T(8,128)(2,1)S(1)} %get-tuple-element.78), channel_id=1, source_target_pairs={{0,2},{2,0},{4,6},{6,4},{1,3},{3,1},{5,7},{7,5},{8,10},{10,8},{12,... | collective-permute-start | bytes 294920 | tf_op jit(solution)/shard_map/ppermute | solution.py:621
  36.2 2.5 %finish.1 = (bf16[2,16,4,512]{3,2,1,0:T(4,128)(2,1)}, bf16[2,16,4,512]{3,2,1,0:T(4,128)(2,1)}) custom-call(bf16[1536,512]{1,0:T(8,128)(2,1)S(1)} %bitcast.11, bf16[3,256,384]{2,1,0:T(8,128)(2,1)S(1)} %get-tuple-element.54.backward, bf16[768,512]{1,0:T(8,128)(2,1)S(1)} %get-tuple-element.70.gates, bf16[2,64,512]{2,1,0:T(8,128)(2,1)S(1)} %get-tuple-element.71.next_ref, ...), custom_call_target="tpu_custom_call" | custom-call | flops 2000000000 | bytes 2000000 | tf_op jit(solution)/shard_map/finish/pallas_call | solution.py:509
  38.7 0.0 collective-permute-done.9.p1
  38.7 5.7 %collective-permute-done.10.p2 = bf16[384,128]{1,0:T(8,128)(2,1)S(1)} collective-permute-done((bf16[384,128]{1,0:T(8,128)(2,1)S(1)}, bf16[384,128]{1,0:T(8,128)(2,1)S(1)}, u32[]{:S(2)}, u32[]{:S(2)}) %collective-permute-start.10) | collective-permute-done | bytes 98336 | tf_op jit(solution)/shard_map/ppermute | solution.py:621
  44.3 0.0 collective-permute-done.11.p3
  44.4 0.7 %add_up.1 = f32[384,128]{1,0:T(8,128)} custom-call(f32[384,128]{1,0:T(8,128)S(1)} %get-tuple-element.75.mine, bf16[384,128]{1,0:T(8,128)(2,1)S(1)} %collective-permute-done.9.p1, bf16[384,128]{1,0:T(8,128)(2,1)S(1)} %collective-permute-done.10.p2, bf16[384,128]{1,0:T(8,128)(2,1)S(1)} %collective-permute-done.11.p3), custom_call_target="tpu_custom_call" | custom-call | flops 100000000 | bytes 100000 | tf_op jit(solution)/shard_map/add_up/pallas_call | solution.py:509
  (7 shorter events, 0.1 us)
Async XLA Ops:
  0.6 9.3 %copy-start.3 = (s32[64,9]{0,1:T(8,128)S(1)}, s32[64,9]{0,1:T(8,128)}, u32[]{:S(2)}) copy-start(s32[64,9]{0,1:T(8,128)} %param.11) | copy-start | bytes 6916
  0.6 9.3 %copy-start.2 = (s32[64,9]{0,1:T(8,128)S(1)}, s32[64,9]{0,1:T(8,128)}, u32[]{:S(2)}) copy-start(s32[64,9]{0,1:T(8,128)} %param.10) | copy-start | bytes 6916
  0.7 9.3 %copy-start.1 = (f32[64,9,3]{0,2,1:T(4,128)S(1)}, f32[64,9,3]{0,2,1:T(4,128)}, u32[]{:S(2)}) copy-start(f32[64,9,3]{0,2,1:T(4,128)} %param.9) | copy-start | bytes 20740
  1.8 18.8 %collective-permute-start.5 = (bf16[688,512]{1,0:T(8,128)(2,1)S(1)}, bf16[688,512]{1,0:T(8,128)(2,1)S(1)}, u32[]{:S(2)}, u32[]{:S(2)}) collective-permute-start(bf16[688,512]{1,0:T(8,128)(2,1)S(1)} %constant_dynamic-slice_fusion), channel_id=1, source_target_pairs={{0,1},{1,0},{2,3},{3,2},{4,5},{5,4},{6,7},{7,6},{8,9},{9,8},{10,11... | collective-permute-start | bytes 2113544 | tf_op jit(solution)/shard_map/ppermute | solution.py:528
  6.0 7.8 %collective-permute-start.2 = (bf16[2,128,512]{2,1,0:T(8,128)(2,1)S(1)}, bf16[2,128,512]{2,1,0:T(8,128)(2,1)S(1)}, u32[]{:S(2)}, u32[]{:S(2)}) collective-permute-start(bf16[2,128,512]{2,1,0:T(8,128)(2,1)S(1)} %prep.1.both), channel_id=1, source_target_pairs={{0,16},{8,24},{16,0},{24,8},{1,17},{9,25},{17,1},{25,9},{2,18},{10... | collective-permute-start | bytes 786440 | tf_op jit(solution)/shard_map/ppermute | solution.py:534
  7.6 13.5 %copy-start = (bf16[1,3,512,512]{3,2,1,0:T(8,128)(2,1)S(1)}, bf16[1,3,512,512]{3,2,1,0:T(8,128)(2,1)}, u32[]{:S(2)}) copy-start(bf16[1,3,512,512]{3,2,1,0:T(8,128)(2,1)} %param.8) | copy-start | bytes 4718596
  7.6 4.8 %collective-permute-start = (bf16[2,48,512]{2,1,0:T(8,128)(2,1)S(1)}, bf16[2,48,512]{2,1,0:T(8,128)(2,1)S(1)}, u32[]{:S(2)}, u32[]{:S(2)}) collective-permute-start(bf16[2,48,512]{2,1,0:T(8,128)(2,1)S(1)} %get-tuple-element.43), channel_id=1, source_target_pairs={{0,2},{2,0},{4,6},{6,4},{1,3},{3,1},{5,7},{7,5},{8,10},{10,8},{12,... | collective-permute-start | bytes 294920 | tf_op jit(solution)/shard_map/ppermute | solution.py:537
  9.3 3.1 %collective-permute-start.1 = (bf16[2,48,512]{2,1,0:T(8,128)(2,1)S(1)}, bf16[2,48,512]{2,1,0:T(8,128)(2,1)S(1)}, u32[]{:S(2)}, u32[]{:S(2)}) collective-permute-start(bf16[2,48,512]{2,1,0:T(8,128)(2,1)S(1)} %get-tuple-element.44), channel_id=1, source_target_pairs={{2,4},{4,2},{3,5},{5,3},{10,12},{12,10},{11,13},{13,11},{18,20},{2... | collective-permute-start | bytes 294920 | tf_op jit(solution)/shard_map/ppermute | solution.py:538
  13.9 5.7 %collective-permute-start.4 = (bf16[2,96,512]{2,1,0:T(8,128)(2,1)S(1)}, bf16[2,96,512]{2,1,0:T(8,128)(2,1)S(1)}, u32[]{:S(2)}, u32[]{:S(2)}) collective-permute-start(bf16[2,96,512]{2,1,0:T(8,128)(2,1)S(1)} %pad_maximum_fusion.3), channel_id=1, source_target_pairs={{0,16},{8,24},{16,0},{24,8},{1,17},{9,25},{17,1},{25,9},{2,18},{10... | collective-permute-start | bytes 589832 | tf_op jit(solution)/shard_map/ppermute | solution.py:553
  15.4 7.6 %collective-permute-start.3 = (bf16[2,224,512]{2,1,0:T(8,128)(2,1)S(1)}, bf16[2,224,512]{2,1,0:T(8,128)(2,1)S(1)}, u32[]{:S(2)}, u32[]{:S(2)}) collective-permute-start(bf16[2,224,512]{2,1,0:T(8,128)(2,1)S(1)} %pad_maximum_fusion.b0), channel_id=1, source_target_pairs={{0,8},{8,0},{16,24},{24,16},{1,9},{9,1},{17,25},{25,17},{2,10},{10... | collective-permute-start | bytes 1376264 | tf_op jit(solution)/shard_map/ppermute | solution.py:555
  20.6 2.4 %collective-permute-start.6 = (bf16[2,224,512]{2,1,0:T(8,128)(2,1)S(1)}, bf16[2,224,512]{2,1,0:T(8,128)(2,1)S(1)}, u32[]{:S(2)}, u32[]{:S(2)}) collective-permute-start(bf16[2,224,512]{2,1,0:T(8,128)(2,1)S(1)} %pad_maximum_fusion.1.b2), channel_id=1, source_target_pairs={{0,8},{8,0},{16,24},{24,16},{1,9},{9,1},{17,25},{25,17},{2,10},{10... | collective-permute-start | bytes 1376264 | tf_op jit(solution)/shard_map/ppermute | solution.py:568
  20.6 6.2 %collective-permute-start.7 = (bf16[688,512]{1,0:T(8,128)(2,1)S(1)}, bf16[688,512]{1,0:T(8,128)(2,1)S(1)}, u32[]{:S(2)}, u32[]{:S(2)}) collective-permute-start(bf16[688,512]{1,0:T(8,128)(2,1)S(1)} %collective-permute-done.5.near_half), channel_id=1, source_target_pairs={{0,8},{8,0},{16,24},{24,16},{1,9},{9,1},{17,25},{25,17},{2,10},{10... | collective-permute-start | bytes 2113544 | tf_op jit(solution)/shard_map/ppermute | solution.py:569
  21.2 7.1 %collective-permute-start.8 = (bf16[160,512]{1,0:T(8,128)(2,1)S(1)}, bf16[160,512]{1,0:T(8,128)(2,1)S(1)}, u32[]{:S(2)}, u32[]{:S(2)}) collective-permute-start(bf16[160,512]{1,0:T(8,128)(2,1)S(1)} %pad_maximum_fusion.4), channel_id=1, source_target_pairs={{0,1},{1,0},{2,3},{3,2},{4,5},{5,4},{6,7},{7,6},{8,9},{9,8},{10,11... | collective-permute-start | bytes 491528 | tf_op jit(solution)/shard_map/ppermute | solution.py:527
  31.8 6.9 %collective-permute-start.9 = (bf16[384,128]{1,0:T(8,128)(2,1)S(1)}, bf16[384,128]{1,0:T(8,128)(2,1)S(1)}, u32[]{:S(2)}, u32[]{:S(2)}) collective-permute-start(bf16[384,128]{1,0:T(8,128)(2,1)S(1)} %get-tuple-element.76), channel_id=1, source_target_pairs={{0,6},{2,4},{4,2},{6,0},{1,7},{3,5},{5,3},{7,1},{8,14},{10,12},{12... | collective-permute-start | bytes 294920 | tf_op jit(solution)/shard_map/ppermute | solution.py:621
  35.5 8.9 %collective-permute-start.10 = (bf16[384,128]{1,0:T(8,128)(2,1)S(1)}, bf16[384,128]{1,0:T(8,128)(2,1)S(1)}, u32[]{:S(2)}, u32[]{:S(2)}) collective-permute-start(bf16[384,128]{1,0:T(8,128)(2,1)S(1)} %get-tuple-element.77), channel_id=1, source_target_pairs={{0,4},{2,6},{4,0},{6,2},{1,5},{3,7},{5,1},{7,3},{8,12},{10,14},{12... | collective-permute-start | bytes 294920 | tf_op jit(solution)/shard_map/ppermute | solution.py:621
  35.5 8.9 %collective-permute-start.11 = (bf16[384,128]{1,0:T(8,128)(2,1)S(1)}, bf16[384,128]{1,0:T(8,128)(2,1)S(1)}, u32[]{:S(2)}, u32[]{:S(2)}) collective-permute-start(bf16[384,128]{1,0:T(8,128)(2,1)S(1)} %get-tuple-element.78), channel_id=1, source_target_pairs={{0,2},{2,0},{4,6},{6,4},{1,3},{3,1},{5,7},{7,5},{8,10},{10,8},{12,... | collective-permute-start | bytes 294920 | tf_op jit(solution)/shard_map/ppermute | solution.py:621

commit v11 on v10

--- a/solution.py
+++ b/solution.py
@@ -364,7 +364,7 @@
                 feat[(i * BASIS + b) * cells : (i * BASIS + b + 1) * cells, :] = got[i * cells : (i + 1) * cells]
 
     def chain(b0, b1, b2, b3, w_own, w_in, part, ends, again, backward, s, left0, slope, early_out, w,
-              out_ref, next_ref, gate_ref, own_ref, p1, p2, p3, late, s1, mid, gates, feat, pull, grads):
+              out_ref, next_ref, gate_ref, parts, late, s1, mid, gates, feat, pull, grads):
         blk = (b0, b1, b2, b3)
         seg, lon, lat = lax.axis_index("segment"), lax.axis_index("lon"), lax.axis_index("lat")
         rest = ends.shape[0] // 2
@@ -460,9 +460,8 @@
         def rows_of(index):
             return grads[pl.ds(pl.multiple_of(index * share, share), share), :]
 
-        own_ref[...] = rows_of(lat)
-        for bit, ref in ((1, p1), (2, p2), (3, p3)):
-            ref[...] = rows_of(lat ^ bit).astype(jnp.bfloat16)
+        for index in range(lat_devices):
+            parts[index] = rows_of(index).astype(jnp.bfloat16)
 
     def finish(w_own, backward, gates, next_ref, last_ref, grad_ref, out_ref, feat, pull):
         apply_back(w_own, gates, feat)
@@ -482,8 +481,11 @@
     return prep, edges, maps, early, partial, chain, finish
 
 
-def add_up(scale, mine, p1, p2, p3, out):
-    out[...] = (mine[...] + p1[...].astype(jnp.float32) + p2[...].astype(jnp.float32) + p3[...].astype(jnp.float32)) * scale
+def add_up(scale, parts, out):
+    total = parts[0].astype(jnp.float32)
+    for index in range(1, parts.shape[0]):
+        total = total + parts[index].astype(jnp.float32)
+    out[...] = total * scale
 
 
 def whole_ring(inputs, cotangent, weights, basis_values, lat_step, lon_step):
@@ -520,7 +522,7 @@
 
     prep, edges, maps, early, partial, chain, finish = make_steps(lat_rows, lon_cols, blocks, members, channels, lat_devices)
     kernel = weights.reshape(width, channels)
-    rest = width // 2 * 5 // 48
+    rest = width // 2 // 8
     rows = width // 2 - rest
     half = lax.dynamic_slice_in_dim(kernel, lax.axis_index("lon") % 2 * (width // 2), rows, 0)
     ends = jnp.concatenate([kernel[rows : rows + rest], kernel[width - rest :]], axis=0)
@@ -593,7 +595,7 @@
     )
     near_ends, part = lax.optimization_barrier((near_ends, part))
     lines = (width // blocks // lat_devices * channels // 128, 128)
-    _, out, follow, gates, mine, *parts = call(
+    _, out, follow, gates, parts = call(
         chain,
         "chain",
         (
@@ -601,9 +603,8 @@
             shape((members, own, channels), half_type),
             shape((members, own, channels), half_type),
             shape((members * ns * cells, channels), half_type),
-            shape(lines, full_type),
-        )
-        + (shape(lines, half_type),) * 3,
+            shape((lat_devices,) + lines, half_type),
+        ),
         (b0, b1, b2, b3, kernel, w, part, near_ends, again, backward, s, left, slope, early_out),
         18,
         6.0,
@@ -618,7 +619,7 @@
         ),
         {5: 0},
     )
-    got = [lax.ppermute(part, "lat", swap("lat", bit)) for bit, part in reversed(list(zip((1, 2, 3), parts)))]
+    got = lax.all_to_all(parts, "lat", 0, 0, tiled=True)
     block = (members, lat_rows, lon_cols, channels)
     grad, out = call(
         finish,
@@ -632,7 +633,7 @@
             pltpu.VMEM((members, own + 2 * edge, channels), full_type),
         ),
     )
-    (total,) = call(functools.partial(add_up, grad_scale), "add_up", (shape(lines, full_type),), (mine, *got), 2, 0.1)
+    (total,) = call(functools.partial(add_up, grad_scale), "add_up", (shape(lines, full_type),), (got,), 2, 0.1)
     return (out[None], grad[None], total.reshape(1, lines[0] * lines[1]))
 
 

time: 45.2 us -> 50.5 us (1.12)
  waiting for transfers between devices: 10.3 us -> 12.5 us
  local copies, waits for them, and re-layouts: 1.19 us -> 2.74 us
  Pallas kernels: 16.3 us -> 17.1 us
  starting transfers between devices: 15.2 us -> 15.8 us
    all_to_all x0 -> x1, waiting for transfers between devices: none -> 8.28 us  [whole_ring(): got = lax.all_to_all(parts, 'lat', 0, 0, tiled=True)]
    ppermute x3 -> x0, waiting for transfers between devices: 5.66 us -> none  [whole_ring(): lax.ppermute(part, 'lat', swap('lat', bit))]
    all_to_all x0 -> x1, starting transfers between devices: none -> 5.05 us  [whole_ring(): got = lax.all_to_all(parts, 'lat', 0, 0, tiled=True)]
    ppermute x3 -> x0, starting transfers between devices: 4.45 us -> none  [whole_ring(): lax.ppermute(part, 'lat', swap('lat', bit))]
    unnamed x8 -> x12, local copies, waits for them, and re-layouts: 0.02 us -> 1.58 us
    pallas_call x9, Pallas kernels: 16.3 us -> 17.1 us  [call(): pl.pallas_call(body, out_shape=outs, in_specs=[vmem] * len(ins), out_spec...]
  transfers between devices with their start and end apart: 12 -> 10, of which waited for: 4 -> 4; matrix products, arithmetic and copies ran while one was open for 3% -> 2% of each run, Pallas kernels for 27% -> 24%
where the time goes in v11:
time: 50.5 us; the launch traced here: 50.2 us
  Pallas kernels  17.1 us (34%)
  starting transfers between devices  15.8 us (31%)
  waiting for transfers between devices  12.5 us (25%)
  local copies, waits for them, and re-layouts  2.74 us (5%)
  other arithmetic  1.23 us (2%)
  between operations  0.82 us (2%)
    pallas_call x9, Pallas kernels, call(): pl.pallas_call(body, out_shape=outs, in_specs=[vmem] * len(ins), out_spec...  17.1 us
    all_to_all x1, waiting for transfers between devices, whole_ring(): got = lax.all_to_all(parts, 'lat', 0, 0, tiled=True)  8.28 us
    all_to_all x1, starting transfers between devices, whole_ring(): got = lax.all_to_all(parts, 'lat', 0, 0, tiled=True)  5.05 us
    ppermute x1, starting transfers between devices, whole_ring(): near_half = lax.ppermute(half, 'segment', swap('segment', 1))  3 us
    ppermute x1, waiting for transfers between devices, whole_ring(): sides_y = lax.ppermute(sides, 'lon', swap('lon', 2))  2.12 us
    ppermute x1, starting transfers between devices, whole_ring(): near_ends = lax.ppermute(ends, 'segment', swap('segment', 1))  1.81 us
    ppermute x1, starting transfers between devices, whole_ring(): from_near = lax.ppermute(toward, 'lat', near_pairs)  1.64 us
    ppermute x1, starting transfers between devices, whole_ring(): both_y = lax.ppermute(both, 'lon', swap('lon', 2))  1.58 us
  transfers between devices with their start and end apart: 10, of which 4 were waited for; matrix products, arithmetic and copies ran while one was open for 2% of the time, Pallas kernels for 24%

profile of v11, /device:TPU:0, one launch (start us, length us, event | category | flops | bytes accessed | tf_op | source)
XLA Modules:
  0.0 50.2 jit_solution(15470015436144960976)
XLA Ops:
  0.6 0.0 copy-start.3
  0.6 0.0 copy-start.2
  0.7 0.0 copy-start.1
  0.7 1.1 %constant_dynamic-slice_fusion = bf16[672,512]{1,0:T(8,128)(2,1)S(1)} fusion(bf16[1536,512]{1,0:T(8,128)(2,1)} %bitcast.7, s32[]{:T(128)S(6)} %select_n.11), kind=kLoop, calls=%fused_computation.5 | loop fusion | bytes 1376260 | tf_op jit(solution)/shard_map/dynamic_slice | solution.py:527
  1.8 3.0 %collective-permute-start.5 = (bf16[672,512]{1,0:T(8,128)(2,1)S(1)}, bf16[672,512]{1,0:T(8,128)(2,1)S(1)}, u32[]{:S(2)}, u32[]{:S(2)}) collective-permute-start(bf16[672,512]{1,0:T(8,128)(2,1)S(1)} %constant_dynamic-slice_fusion), channel_id=1, source_target_pairs={{0,1},{1,0},{2,3},{3,2},{4,5},{5,4},{6,7},{7,6},{8,9},{9,8},{10,11... | collective-permute-start | bytes 2064392 | tf_op jit(solution)/shard_map/ppermute | solution.py:530
  4.8 1.1 %pad_maximum_fusion.2.loaded = bf16[4,16,4,512]{3,2,1,0:T(4,128)(2,1)S(1)} fusion(bf16[2,16,4,512]{3,2,1,0:T(4,128)(2,1)} %param.7, bf16[2,16,4,512]{3,2,1,0:T(4,128)(2,1)} %param.6), kind=kLoop, calls=%fused_computation.2 | loop fusion | flops 131072 | bytes 524288 | tf_op jit(solution)/shard_map/concatenate | solution.py:532
  6.0 1.6 %collective-permute-start.2 = (bf16[2,128,512]{2,1,0:T(8,128)(2,1)S(1)}, bf16[2,128,512]{2,1,0:T(8,128)(2,1)S(1)}, u32[]{:S(2)}, u32[]{:S(2)}) collective-permute-start(bf16[2,128,512]{2,1,0:T(8,128)(2,1)S(1)} %prep.1.both), channel_id=1, source_target_pairs={{0,16},{8,24},{16,0},{24,8},{1,17},{9,25},{17,1},{25,9},{2,18},{10... | collective-permute-start | bytes 786440 | tf_op jit(solution)/shard_map/ppermute | solution.py:536
  7.6 0.0 copy-start
  7.6 1.6 %collective-permute-start = (bf16[2,48,512]{2,1,0:T(8,128)(2,1)S(1)}, bf16[2,48,512]{2,1,0:T(8,128)(2,1)S(1)}, u32[]{:S(2)}, u32[]{:S(2)}) collective-permute-start(bf16[2,48,512]{2,1,0:T(8,128)(2,1)S(1)} %get-tuple-element.40), channel_id=1, source_target_pairs={{0,2},{2,0},{4,6},{6,4},{1,3},{3,1},{5,7},{7,5},{8,10},{10,8},{12,... | collective-permute-start | bytes 294920 | tf_op jit(solution)/shard_map/ppermute | solution.py:539
  9.3 0.7 %collective-permute-start.1 = (bf16[2,48,512]{2,1,0:T(8,128)(2,1)S(1)}, bf16[2,48,512]{2,1,0:T(8,128)(2,1)S(1)}, u32[]{:S(2)}, u32[]{:S(2)}) collective-permute-start(bf16[2,48,512]{2,1,0:T(8,128)(2,1)S(1)} %get-tuple-element.41), channel_id=1, source_target_pairs={{2,4},{4,2},{3,5},{5,3},{10,12},{12,10},{11,13},{13,11},{18,20},{2... | collective-permute-start | bytes 294920 | tf_op jit(solution)/shard_map/ppermute | solution.py:540
  9.9 0.0 copy-done.3
  9.9 0.0 copy-done.2
  10.0 0.0 copy-done.1
  10.0 2.4 %maps_first.1.forward = bf16[4,384,256]{2,1,0:T(8,128)(2,1)S(1)} custom-call(s32[9,64]{1,0:T(8,128)S(1)} %bitcast.14, s32[9,64]{1,0:T(8,128)S(1)} %bitcast.16, f32[9,3,64]{2,1,0:T(4,128)S(1)} %bitcast.12), custom_call_target="tpu_custom_call" | custom-call | tf_op jit(solution)/shard_map/maps_first/pallas_call | solution.py:511
  12.4 0.0 collective-permute-done
  12.4 0.0 collective-permute-done.1
  12.4 1.4 %collective-permute-done.2 = bf16[2,128,512]{2,1,0:T(8,128)(2,1)S(1)} collective-permute-done((bf16[2,128,512]{2,1,0:T(8,128)(2,1)S(1)}, bf16[2,128,512]{2,1,0:T(8,128)(2,1)S(1)}, u32[]{:S(2)}, u32[]{:S(2)}) %collective-permute-start.2) | collective-permute-done | bytes 262176 | tf_op jit(solution)/shard_map/ppermute | solution.py:536
  13.8 1.5 %collective-permute-start.4 = (bf16[2,96,512]{2,1,0:T(8,128)(2,1)S(1)}, bf16[2,96,512]{2,1,0:T(8,128)(2,1)S(1)}, u32[]{:S(2)}, u32[]{:S(2)}) collective-permute-start(bf16[2,96,512]{2,1,0:T(8,128)(2,1)S(1)} %pad_maximum_fusion.3), channel_id=1, source_target_pairs={{0,16},{8,24},{16,0},{24,8},{1,17},{9,25},{17,1},{25,9},{2,18},{10... | collective-permute-start | bytes 589832 | tf_op jit(solution)/shard_map/ppermute | solution.py:555
  15.4 0.1 collective-permute-start.3
  15.5 1.9 %maps_again.1 = (bf16[3,384,256]{2,1,0:T(8,128)(2,1)S(1)}, bf16[3,256,384]{2,1,0:T(8,128)(2,1)S(1)}) custom-call(s32[9,64]{1,0:T(8,128)S(1)} %bitcast.15, s32[9,64]{1,0:T(8,128)S(1)} %bitcast.17, f32[9,3,64]{2,1,0:T(4,128)S(1)} %bitcast.13), custom_call_target="tpu_custom_call" | custom-call | tf_op jit(solution)/shard_map/maps_again/pallas_call | solution.py:511
  17.4 2.1 %collective-permute-done.4 = bf16[2,96,512]{2,1,0:T(8,128)(2,1)S(1)} collective-permute-done((bf16[2,96,512]{2,1,0:T(8,128)(2,1)S(1)}, bf16[2,96,512]{2,1,0:T(8,128)(2,1)S(1)}, u32[]{:S(2)}, u32[]{:S(2)}) %collective-permute-start.4) | collective-permute-done | bytes 196640 | tf_op jit(solution)/shard_map/ppermute | solution.py:555
  19.6 0.7 %collective-permute-done.5.near_half = bf16[672,512]{1,0:T(8,128)(2,1)S(1)} collective-permute-done((bf16[672,512]{1,0:T(8,128)(2,1)S(1)}, bf16[672,512]{1,0:T(8,128)(2,1)S(1)}, u32[]{:S(2)}, u32[]{:S(2)}) %collective-permute-start.5) | collective-permute-done | bytes 688160 | tf_op jit(solution)/shard_map/ppermute | solution.py:530
  20.3 0.0 collective-permute-start.6
  20.3 0.5 %collective-permute-start.7 = (bf16[672,512]{1,0:T(8,128)(2,1)S(1)}, bf16[672,512]{1,0:T(8,128)(2,1)S(1)}, u32[]{:S(2)}, u32[]{:S(2)}) collective-permute-start(bf16[672,512]{1,0:T(8,128)(2,1)S(1)} %collective-permute-done.5.near_half), channel_id=1, source_target_pairs={{0,8},{8,0},{16,24},{24,16},{1,9},{9,1},{17,25},{25,17},{2,10},{10... | collective-permute-start | bytes 2064392 | tf_op jit(solution)/shard_map/ppermute | solution.py:571
  20.8 0.0 copy-done
  20.8 1.8 %collective-permute-start.8 = (bf16[192,512]{1,0:T(8,128)(2,1)S(1)}, bf16[192,512]{1,0:T(8,128)(2,1)S(1)}, u32[]{:S(2)}, u32[]{:S(2)}) collective-permute-start(bf16[192,512]{1,0:T(8,128)(2,1)S(1)} %pad_maximum_fusion.4), channel_id=1, source_target_pairs={{0,1},{1,0},{2,3},{3,2},{4,5},{5,4},{6,7},{7,6},{8,9},{9,8},{10,11... | collective-permute-start | bytes 589832 | tf_op jit(solution)/shard_map/ppermute | solution.py:529
  22.6 0.0 collective-permute-done.3.b1
  22.6 0.0 collective-permute-done.6.b3
  22.6 3.8 %early.1 = (bf16[1024,1536]{1,0:T(8,128)(2,1)S(1)}, bf16[512,384]{1,0:T(8,128)(2,1)S(1)}, bf16[2,4,96,512]{3,2,1,0:T(8,128)(2,1)S(1)}, bf16[2,64,512]{2,1,0:T(8,128)(2,1)S(1)}) custom-call(bf16[2,224,512]{2,1,0:T(8,128)(2,1)S(1)} %pad_maximum_fusion.b0, bf16[2,224,512]{2,1,0:T(8,128)(2,1)S(1)} %collective-permute-done.3.b1, ...), custom_call_target="tpu_custom_call" | custom-call | flops 3000000000 | bytes 3000000 | tf_op jit(solution)/shard_map/early/pallas_call | solution.py:511
  26.4 0.0 collective-permute-done.7.far_half
  26.4 1.5 %partial.1 = (bf16[1536,512]{1,0:T(8,128)(2,1)S(1)}, f32[1024,512]{1,0:T(8,128)S(1)}) custom-call(bf16[1024,1536]{1,0:T(8,128)(2,1)S(1)} %get-tuple-element.58.s, bf16[672,512]{1,0:T(8,128)(2,1)S(1)} %collective-permute-done.5.near_half, bf16[672,512]{1,0:T(8,128)(2,1)S(1)} %collective-permute-done.7.far_half), custom_call_target="tpu_custom_call" | custom-call | flops 1500000000 | bytes 1500000 | tf_op jit(solution)/shard_map/partial/pallas_call | solution.py:511
  27.9 0.0 collective-permute-done.8.ends
  27.9 4.2 %chain.1 = (bf16[1536,512]{1,0:T(8,128)(2,1)S(1)}, bf16[2,64,512]{2,1,0:T(8,128)(2,1)S(1)}, bf16[2,64,512]{2,1,0:T(8,128)(2,1)S(1)}, bf16[768,512]{1,0:T(8,128)(2,1)S(1)}, bf16[4,384,128]{2,1,0:T(8,128)(2,1)}) custom-call(bf16[2,224,512]{2,1,0:T(8,128)(2,1)S(1)} %pad_maximum_fusion.b0, ...), custom_call_target="tpu_custom_call", output_to_operand_aliasing={{0}: (5, {})} | custom-call | flops 6000000000 | bytes 6000000 | tf_op jit(solution)/shard_map/chain/pallas_call | solution.py:511
  32.2 0.0 copy-start.4
  32.2 0.7 %copy-done.4 = bf16[2,64,512]{2,1,0:T(8,128)(2,1)} copy-done((bf16[2,64,512]{2,1,0:T(8,128)(2,1)}, bf16[2,64,512]{2,1,0:T(8,128)(2,1)S(1)}, u32[]{:S(2)}) %copy-start.4) | copy-done | bytes 131096
  32.8 5.1 %all-to-all-start = ((bf16[4,384,128]{2,1,0:T(8,128)(2,1)}), bf16[4,384,128]{2,1,0:T(8,128)(2,1)S(1)}, u32[]{:S(2)}, u32[]{:S(2)}) async-start(bf16[4,384,128]{2,1,0:T(8,128)(2,1)} %get-tuple-element.72), calls=%async_computation | async-start | bytes 786432 | tf_op jit(solution)/shard_map/all_to_all | solution.py:622
  37.9 0.0 copy-start.5
  37.9 0.9 %copy-done.5 = bf16[2,64,512]{2,1,0:T(8,128)(2,1)S(1)} copy-done((bf16[2,64,512]{2,1,0:T(8,128)(2,1)S(1)}, bf16[2,64,512]{2,1,0:T(8,128)(2,1)}, u32[]{:S(2)}) %copy-start.5) | copy-done | bytes 131096
  38.8 2.5 %finish.1 = (bf16[2,16,4,512]{3,2,1,0:T(4,128)(2,1)}, bf16[2,16,4,512]{3,2,1,0:T(4,128)(2,1)}) custom-call(bf16[1536,512]{1,0:T(8,128)(2,1)S(1)} %bitcast.11, bf16[3,256,384]{2,1,0:T(8,128)(2,1)S(1)} %get-tuple-element.51.backward, bf16[768,512]{1,0:T(8,128)(2,1)S(1)} %get-tuple-element.67.gates, bf16[2,64,512]{2,1,0:T(8,128)(2,1)S(1)} %copy-done.5, ...), custom_call_target="tpu_custom_call" | custom-call | flops 2000000000 | bytes 2000000 | tf_op jit(solution)/shard_map/finish/pallas_call | solution.py:511
  41.2 8.3 %all-to-all-done.parts = bf16[4,384,128]{2,1,0:T(8,128)(2,1)S(1)} async-done(((bf16[4,384,128]{2,1,0:T(8,128)(2,1)}), bf16[4,384,128]{2,1,0:T(8,128)(2,1)S(1)}, u32[]{:S(2)}, u32[]{:S(2)}) %all-to-all-start) | async-done | bytes 393248 | tf_op jit(solution)/shard_map/all_to_all | solution.py:622
  49.5 0.7 %add_up.1 = f32[384,128]{1,0:T(8,128)} custom-call(bf16[4,384,128]{2,1,0:T(8,128)(2,1)S(1)} %all-to-all-done.parts), custom_call_target="tpu_custom_call" | custom-call | flops 100000000 | bytes 100000 | tf_op jit(solution)/shard_map/add_up/pallas_call | solution.py:511
  (7 shorter events, 0.2 us)
Async XLA Ops:
  0.6 9.3 %copy-start.3 = (s32[64,9]{0,1:T(8,128)S(1)}, s32[64,9]{0,1:T(8,128)}, u32[]{:S(2)}) copy-start(s32[64,9]{0,1:T(8,128)} %param.11) | copy-start | bytes 6916
  0.6 9.3 %copy-start.2 = (s32[64,9]{0,1:T(8,128)S(1)}, s32[64,9]{0,1:T(8,128)}, u32[]{:S(2)}) copy-start(s32[64,9]{0,1:T(8,128)} %param.10) | copy-start | bytes 6916
  0.7 9.3 %copy-start.1 = (f32[64,9,3]{0,2,1:T(4,128)S(1)}, f32[64,9,3]{0,2,1:T(4,128)}, u32[]{:S(2)}) copy-start(f32[64,9,3]{0,2,1:T(4,128)} %param.9) | copy-start | bytes 20740
  1.8 18.4 %collective-permute-start.5 = (bf16[672,512]{1,0:T(8,128)(2,1)S(1)}, bf16[672,512]{1,0:T(8,128)(2,1)S(1)}, u32[]{:S(2)}, u32[]{:S(2)}) collective-permute-start(bf16[672,512]{1,0:T(8,128)(2,1)S(1)} %constant_dynamic-slice_fusion), channel_id=1, source_target_pairs={{0,1},{1,0},{2,3},{3,2},{4,5},{5,4},{6,7},{7,6},{8,9},{9,8},{10,11... | collective-permute-start | bytes 2064392 | tf_op jit(solution)/shard_map/ppermute | solution.py:530
  6.0 7.8 %collective-permute-start.2 = (bf16[2,128,512]{2,1,0:T(8,128)(2,1)S(1)}, bf16[2,128,512]{2,1,0:T(8,128)(2,1)S(1)}, u32[]{:S(2)}, u32[]{:S(2)}) collective-permute-start(bf16[2,128,512]{2,1,0:T(8,128)(2,1)S(1)} %prep.1.both), channel_id=1, source_target_pairs={{0,16},{8,24},{16,0},{24,8},{1,17},{9,25},{17,1},{25,9},{2,18},{10... | collective-permute-start | bytes 786440 | tf_op jit(solution)/shard_map/ppermute | solution.py:536
  7.6 13.2 %copy-start = (bf16[1,3,512,512]{3,2,1,0:T(8,128)(2,1)S(1)}, bf16[1,3,512,512]{3,2,1,0:T(8,128)(2,1)}, u32[]{:S(2)}) copy-start(bf16[1,3,512,512]{3,2,1,0:T(8,128)(2,1)} %param.8) | copy-start | bytes 4718596
  7.6 4.8 %collective-permute-start = (bf16[2,48,512]{2,1,0:T(8,128)(2,1)S(1)}, bf16[2,48,512]{2,1,0:T(8,128)(2,1)S(1)}, u32[]{:S(2)}, u32[]{:S(2)}) collective-permute-start(bf16[2,48,512]{2,1,0:T(8,128)(2,1)S(1)} %get-tuple-element.40), channel_id=1, source_target_pairs={{0,2},{2,0},{4,6},{6,4},{1,3},{3,1},{5,7},{7,5},{8,10},{10,8},{12,... | collective-permute-start | bytes 294920 | tf_op jit(solution)/shard_map/ppermute | solution.py:539
  9.3 3.1 %collective-permute-start.1 = (bf16[2,48,512]{2,1,0:T(8,128)(2,1)S(1)}, bf16[2,48,512]{2,1,0:T(8,128)(2,1)S(1)}, u32[]{:S(2)}, u32[]{:S(2)}) collective-permute-start(bf16[2,48,512]{2,1,0:T(8,128)(2,1)S(1)} %get-tuple-element.41), channel_id=1, source_target_pairs={{2,4},{4,2},{3,5},{5,3},{10,12},{12,10},{11,13},{13,11},{18,20},{2... | collective-permute-start | bytes 294920 | tf_op jit(solution)/shard_map/ppermute | solution.py:540
  13.8 5.7 %collective-permute-start.4 = (bf16[2,96,512]{2,1,0:T(8,128)(2,1)S(1)}, bf16[2,96,512]{2,1,0:T(8,128)(2,1)S(1)}, u32[]{:S(2)}, u32[]{:S(2)}) collective-permute-start(bf16[2,96,512]{2,1,0:T(8,128)(2,1)S(1)} %pad_maximum_fusion.3), channel_id=1, source_target_pairs={{0,16},{8,24},{16,0},{24,8},{1,17},{9,25},{17,1},{25,9},{2,18},{10... | collective-permute-start | bytes 589832 | tf_op jit(solution)/shard_map/ppermute | solution.py:555
  15.4 7.2 %collective-permute-start.3 = (bf16[2,224,512]{2,1,0:T(8,128)(2,1)S(1)}, bf16[2,224,512]{2,1,0:T(8,128)(2,1)S(1)}, u32[]{:S(2)}, u32[]{:S(2)}) collective-permute-start(bf16[2,224,512]{2,1,0:T(8,128)(2,1)S(1)} %pad_maximum_fusion.b0), channel_id=1, source_target_pairs={{0,8},{8,0},{16,24},{24,16},{1,9},{9,1},{17,25},{25,17},{2,10},{10... | collective-permute-start | bytes 1376264 | tf_op jit(solution)/shard_map/ppermute | solution.py:557
  20.3 2.4 %collective-permute-start.6 = (bf16[2,224,512]{2,1,0:T(8,128)(2,1)S(1)}, bf16[2,224,512]{2,1,0:T(8,128)(2,1)S(1)}, u32[]{:S(2)}, u32[]{:S(2)}) collective-permute-start(bf16[2,224,512]{2,1,0:T(8,128)(2,1)S(1)} %pad_maximum_fusion.1.b2), channel_id=1, source_target_pairs={{0,8},{8,0},{16,24},{24,16},{1,9},{9,1},{17,25},{25,17},{2,10},{10... | collective-permute-start | bytes 1376264 | tf_op jit(solution)/shard_map/ppermute | solution.py:570
  20.3 6.2 %collective-permute-start.7 = (bf16[672,512]{1,0:T(8,128)(2,1)S(1)}, bf16[672,512]{1,0:T(8,128)(2,1)S(1)}, u32[]{:S(2)}, u32[]{:S(2)}) collective-permute-start(bf16[672,512]{1,0:T(8,128)(2,1)S(1)} %collective-permute-done.5.near_half), channel_id=1, source_target_pairs={{0,8},{8,0},{16,24},{24,16},{1,9},{9,1},{17,25},{25,17},{2,10},{10... | collective-permute-start | bytes 2064392 | tf_op jit(solution)/shard_map/ppermute | solution.py:571
  20.8 7.1 %collective-permute-start.8 = (bf16[192,512]{1,0:T(8,128)(2,1)S(1)}, bf16[192,512]{1,0:T(8,128)(2,1)S(1)}, u32[]{:S(2)}, u32[]{:S(2)}) collective-permute-start(bf16[192,512]{1,0:T(8,128)(2,1)S(1)} %pad_maximum_fusion.4), channel_id=1, source_target_pairs={{0,1},{1,0},{2,3},{3,2},{4,5},{5,4},{6,7},{7,6},{8,9},{9,8},{10,11... | collective-permute-start | bytes 589832 | tf_op jit(solution)/shard_map/ppermute | solution.py:529
  32.2 0.7 %copy-start.4 = (bf16[2,64,512]{2,1,0:T(8,128)(2,1)}, bf16[2,64,512]{2,1,0:T(8,128)(2,1)S(1)}, u32[]{:S(2)}) copy-start(bf16[2,64,512]{2,1,0:T(8,128)(2,1)S(1)} %get-tuple-element.68.next_ref) | copy-start | bytes 393220
  32.8 16.7 %all-to-all-start = ((bf16[4,384,128]{2,1,0:T(8,128)(2,1)}), bf16[4,384,128]{2,1,0:T(8,128)(2,1)S(1)}, u32[]{:S(2)}, u32[]{:S(2)}) async-start(bf16[4,384,128]{2,1,0:T(8,128)(2,1)} %get-tuple-element.72), calls=%async_computation | async-start | bytes 786432 | tf_op jit(solution)/shard_map/all_to_all | solution.py:622
  37.9 0.9 %copy-start.5 = (bf16[2,64,512]{2,1,0:T(8,128)(2,1)S(1)}, bf16[2,64,512]{2,1,0:T(8,128)(2,1)}, u32[]{:S(2)}) copy-start(bf16[2,64,512]{2,1,0:T(8,128)(2,1)} %copy-done.4) | copy-start | bytes 393220

commit v12 on v10

--- a/solution.py
+++ b/solution.py
@@ -345,11 +345,6 @@
             late = slice(i * (width // 2) + rows, (i + 1) * (width // 2))
             w[late, :] = jnp.zeros((width // 2 - rows, channels), w.dtype)
 
-        @pl.when(lax.axis_index("segment") == 0)
-        def _():
-            size = members * ns * cells
-            part[:size, :] = dot(s[:size, :], w[...])
-
         @pl.when(lax.axis_index("segment") == 1)
         def _():
             part[...] = dot(s[...], w[...])
@@ -377,11 +372,11 @@
             late[i * span : (i + 1) * span - rest, :] = jnp.zeros((span - rest, channels), late.dtype)
             late[(i + 1) * span - rest : (i + 1) * span, :] = piece
 
-        def complete(size):
-            total = part[:size, :]
+        def complete():
+            total = part[...]
             for i in range(2):
                 at = i * (width // 2) + aligned
-                total = total + dot(s[:size, at : at + span], late[i * span : (i + 1) * span, :])
+                total = total + dot(s[:, at : at + span], late[i * span : (i + 1) * span, :])
             return total
 
         def coming_at(m, g):
@@ -408,18 +403,22 @@
 
         @pl.when(seg == 0)
         def _():
-            second_section(complete(members * ns * cells), gates, False)
+            second_section(dot(s[: members * ns * cells, :], w[...]), gates, False)
             out_ref[...] = early_out[...]
             apply_back(w, gates, feat)
             for m in range(members):
                 for g in range(ns):
                     at = (m * ns + g) * cells * BASIS
-                    got = dot(backward[g], feat[at : at + BASIS * cells, :]).reshape(blocks, win, channels)
-                    if g == 0:
-                        pull[m, :, :win, :] = got
-                    else:
-                        pull[m, :, g * band : (g + 1) * band, :] += got[:, :band]
-                        pull[m, :, (g + 1) * band : g * band + win, :] = got[:, band:]
+                    low = max(g * band, half_edge)
+                    high = min(g * band + win, 3 * half_edge + own)
+                    local = range(0, blocks * win, win)
+                    rows = [backward[g, q + low - g * band : q + high - g * band, :] for q in local]
+                    got = dot(jnp.concatenate(rows, axis=0), feat[at : at + BASIS * cells, :])
+                    got = got.reshape(blocks, high - low, channels)
+                    turn = low if g == 0 else (g + 1) * band
+                    if g > 0:
+                        pull[m, :, low:turn, :] += got[:, : turn - low]
+                    pull[m, :, turn:high, :] = got[:, turn - low :]
             right = []
             step = half_edge
             for m in range(members):
@@ -442,7 +441,7 @@
 
         @pl.when(seg == 1)
         def _():
-            first_section(blk, complete(members * nf * cells), s1, again, mid, None)
+            first_section(blk, complete(), s1, again, mid, None)
             second_section(dot(s1[...], w_own[...]), gate_ref, True)
             left, right = [], []
             for m in range(members):

time: 45.2 us -> 44.7 us (0.989)
  Pallas kernels: 16.3 us -> 15.6 us
    pallas_call x9, Pallas kernels: 16.3 us -> 15.6 us  [call(): pl.pallas_call(body, out_shape=outs, in_specs=[vmem] * len(ins), out_spec...]
  transfers between devices with their start and end apart: 12 -> 12, of which waited for: 4 -> 6; matrix products, arithmetic and copies ran while one was open for 3% -> 3% of each run, Pallas kernels for 27% -> 24%
where the time goes in v12:
time: 44.7 us; the launch traced here: 44.5 us
  Pallas kernels  15.6 us (35%)
  starting transfers between devices  15.3 us (34%)
  waiting for transfers between devices  10.3 us (23%)
  other arithmetic  1.23 us (3%)
  local copies, waits for them, and re-layouts  1.19 us (3%)
  between operations  0.82 us (2%)
    pallas_call x9, Pallas kernels, call(): pl.pallas_call(body, out_shape=outs, in_specs=[vmem] * len(ins), out_spec...  15.6 us
    ppermute x3, waiting for transfers between devices, whole_ring(): lax.ppermute(part, 'lat', swap('lat', bit))  5.27 us
    ppermute x3, starting transfers between devices, whole_ring(): lax.ppermute(part, 'lat', swap('lat', bit))  4.56 us
    ppermute x1, starting transfers between devices, whole_ring(): near_half = lax.ppermute(half, 'segment', swap('segment', 1))  3 us
    ppermute x1, waiting for transfers between devices, whole_ring(): sides_y = lax.ppermute(sides, 'lon', swap('lon', 2))  2.12 us
    ppermute x1, starting transfers between devices, whole_ring(): near_ends = lax.ppermute(ends, 'segment', swap('segment', 1))  1.81 us
    ppermute x1, starting transfers between devices, whole_ring(): from_near = lax.ppermute(toward, 'lat', near_pairs)  1.64 us
    ppermute x1, starting transfers between devices, whole_ring(): both_y = lax.ppermute(both, 'lon', swap('lon', 2))  1.58 us
  transfers between devices with their start and end apart: 12, of which 6 were waited for; matrix products, arithmetic and copies ran while one was open for 3% of the time, Pallas kernels for 24%

profile of v12, /device:TPU:0, one launch (start us, length us, event | category | flops | bytes accessed | tf_op | source)
XLA Modules:
  0.0 44.5 jit_solution(11070187300485283037)
XLA Ops:
  0.6 0.0 copy-start.3
  0.6 0.0 copy-start.2
  0.7 0.0 copy-start.1
  0.7 1.2 %constant_dynamic-slice_fusion = bf16[688,512]{1,0:T(8,128)(2,1)S(1)} fusion(bf16[1536,512]{1,0:T(8,128)(2,1)} %bitcast.7, s32[]{:T(128)S(6)} %select_n.11), kind=kLoop, calls=%fused_computation.5 | loop fusion | bytes 1409028 | tf_op jit(solution)/shard_map/dynamic_slice | solution.py:524
  1.8 3.0 %collective-permute-start.5 = (bf16[688,512]{1,0:T(8,128)(2,1)S(1)}, bf16[688,512]{1,0:T(8,128)(2,1)S(1)}, u32[]{:S(2)}, u32[]{:S(2)}) collective-permute-start(bf16[688,512]{1,0:T(8,128)(2,1)S(1)} %constant_dynamic-slice_fusion), channel_id=1, source_target_pairs={{0,1},{1,0},{2,3},{3,2},{4,5},{5,4},{6,7},{7,6},{8,9},{9,8},{10,11... | collective-permute-start | bytes 2113544 | tf_op jit(solution)/shard_map/ppermute | solution.py:527
  4.8 1.1 %pad_maximum_fusion.2.loaded = bf16[4,16,4,512]{3,2,1,0:T(4,128)(2,1)S(1)} fusion(bf16[2,16,4,512]{3,2,1,0:T(4,128)(2,1)} %param.7, bf16[2,16,4,512]{3,2,1,0:T(4,128)(2,1)} %param.6), kind=kLoop, calls=%fused_computation.2 | loop fusion | flops 131072 | bytes 524288 | tf_op jit(solution)/shard_map/concatenate | solution.py:529
  6.0 1.6 %collective-permute-start.2 = (bf16[2,128,512]{2,1,0:T(8,128)(2,1)S(1)}, bf16[2,128,512]{2,1,0:T(8,128)(2,1)S(1)}, u32[]{:S(2)}, u32[]{:S(2)}) collective-permute-start(bf16[2,128,512]{2,1,0:T(8,128)(2,1)S(1)} %prep.1.both), channel_id=1, source_target_pairs={{0,16},{8,24},{16,0},{24,8},{1,17},{9,25},{17,1},{25,9},{2,18},{10... | collective-permute-start | bytes 786440 | tf_op jit(solution)/shard_map/ppermute | solution.py:533
  7.6 0.0 copy-start
  7.6 1.6 %collective-permute-start = (bf16[2,48,512]{2,1,0:T(8,128)(2,1)S(1)}, bf16[2,48,512]{2,1,0:T(8,128)(2,1)S(1)}, u32[]{:S(2)}, u32[]{:S(2)}) collective-permute-start(bf16[2,48,512]{2,1,0:T(8,128)(2,1)S(1)} %get-tuple-element.43), channel_id=1, source_target_pairs={{0,2},{2,0},{4,6},{6,4},{1,3},{3,1},{5,7},{7,5},{8,10},{10,8},{12,... | collective-permute-start | bytes 294920 | tf_op jit(solution)/shard_map/ppermute | solution.py:536
  9.3 0.7 %collective-permute-start.1 = (bf16[2,48,512]{2,1,0:T(8,128)(2,1)S(1)}, bf16[2,48,512]{2,1,0:T(8,128)(2,1)S(1)}, u32[]{:S(2)}, u32[]{:S(2)}) collective-permute-start(bf16[2,48,512]{2,1,0:T(8,128)(2,1)S(1)} %get-tuple-element.44), channel_id=1, source_target_pairs={{2,4},{4,2},{3,5},{5,3},{10,12},{12,10},{11,13},{13,11},{18,20},{2... | collective-permute-start | bytes 294920 | tf_op jit(solution)/shard_map/ppermute | solution.py:537
  9.9 0.0 copy-done.3
  10.0 0.0 copy-done.2
  10.0 0.0 copy-done.1
  10.0 2.4 %maps_first.1.forward = bf16[4,384,256]{2,1,0:T(8,128)(2,1)S(1)} custom-call(s32[9,64]{1,0:T(8,128)S(1)} %bitcast.14, s32[9,64]{1,0:T(8,128)S(1)} %bitcast.16, f32[9,3,64]{2,1,0:T(4,128)S(1)} %bitcast.12), custom_call_target="tpu_custom_call" | custom-call | tf_op jit(solution)/shard_map/maps_first/pallas_call | solution.py:508
  12.4 0.0 collective-permute-done
  12.4 0.0 collective-permute-done.1
  12.4 1.4 %collective-permute-done.2 = bf16[2,128,512]{2,1,0:T(8,128)(2,1)S(1)} collective-permute-done((bf16[2,128,512]{2,1,0:T(8,128)(2,1)S(1)}, bf16[2,128,512]{2,1,0:T(8,128)(2,1)S(1)}, u32[]{:S(2)}, u32[]{:S(2)}) %collective-permute-start.2) | collective-permute-done | bytes 262176 | tf_op jit(solution)/shard_map/ppermute | solution.py:533
  13.9 1.5 %collective-permute-start.4 = (bf16[2,96,512]{2,1,0:T(8,128)(2,1)S(1)}, bf16[2,96,512]{2,1,0:T(8,128)(2,1)S(1)}, u32[]{:S(2)}, u32[]{:S(2)}) collective-permute-start(bf16[2,96,512]{2,1,0:T(8,128)(2,1)S(1)} %pad_maximum_fusion.3), channel_id=1, source_target_pairs={{0,16},{8,24},{16,0},{24,8},{1,17},{9,25},{17,1},{25,9},{2,18},{10... | collective-permute-start | bytes 589832 | tf_op jit(solution)/shard_map/ppermute | solution.py:552
  15.4 0.1 collective-permute-start.3
  15.5 1.9 %maps_again.1 = (bf16[3,384,256]{2,1,0:T(8,128)(2,1)S(1)}, bf16[3,256,384]{2,1,0:T(8,128)(2,1)S(1)}) custom-call(s32[9,64]{1,0:T(8,128)S(1)} %bitcast.15, s32[9,64]{1,0:T(8,128)S(1)} %bitcast.17, f32[9,3,64]{2,1,0:T(4,128)S(1)} %bitcast.13), custom_call_target="tpu_custom_call" | custom-call | tf_op jit(solution)/shard_map/maps_again/pallas_call | solution.py:508
  17.4 2.1 %collective-permute-done.4 = bf16[2,96,512]{2,1,0:T(8,128)(2,1)S(1)} collective-permute-done((bf16[2,96,512]{2,1,0:T(8,128)(2,1)S(1)}, bf16[2,96,512]{2,1,0:T(8,128)(2,1)S(1)}, u32[]{:S(2)}, u32[]{:S(2)}) %collective-permute-start.4) | collective-permute-done | bytes 196640 | tf_op jit(solution)/shard_map/ppermute | solution.py:552
  19.6 1.1 %collective-permute-done.5.near_half = bf16[688,512]{1,0:T(8,128)(2,1)S(1)} collective-permute-done((bf16[688,512]{1,0:T(8,128)(2,1)S(1)}, bf16[688,512]{1,0:T(8,128)(2,1)S(1)}, u32[]{:S(2)}, u32[]{:S(2)}) %collective-permute-start.5) | collective-permute-done | bytes 704544 | tf_op jit(solution)/shard_map/ppermute | solution.py:527
  20.6 0.0 collective-permute-start.6
  20.6 0.5 %collective-permute-start.7 = (bf16[688,512]{1,0:T(8,128)(2,1)S(1)}, bf16[688,512]{1,0:T(8,128)(2,1)S(1)}, u32[]{:S(2)}, u32[]{:S(2)}) collective-permute-start(bf16[688,512]{1,0:T(8,128)(2,1)S(1)} %collective-permute-done.5.near_half), channel_id=1, source_target_pairs={{0,8},{8,0},{16,24},{24,16},{1,9},{9,1},{17,25},{25,17},{2,10},{10... | collective-permute-start | bytes 2113544 | tf_op jit(solution)/shard_map/ppermute | solution.py:568
  21.1 0.0 copy-done
  21.2 1.8 %collective-permute-start.8 = (bf16[160,512]{1,0:T(8,128)(2,1)S(1)}, bf16[160,512]{1,0:T(8,128)(2,1)S(1)}, u32[]{:S(2)}, u32[]{:S(2)}) collective-permute-start(bf16[160,512]{1,0:T(8,128)(2,1)S(1)} %pad_maximum_fusion.4), channel_id=1, source_target_pairs={{0,1},{1,0},{2,3},{3,2},{4,5},{5,4},{6,7},{7,6},{8,9},{9,8},{10,11... | collective-permute-start | bytes 491528 | tf_op jit(solution)/shard_map/ppermute | solution.py:526
  23.0 0.0 collective-permute-done.3.b1
  23.0 0.0 collective-permute-done.6.b3
  23.0 3.8 %early.1 = (bf16[1024,1536]{1,0:T(8,128)(2,1)S(1)}, bf16[512,384]{1,0:T(8,128)(2,1)S(1)}, bf16[2,4,96,512]{3,2,1,0:T(8,128)(2,1)S(1)}, bf16[2,64,512]{2,1,0:T(8,128)(2,1)S(1)}) custom-call(bf16[2,224,512]{2,1,0:T(8,128)(2,1)S(1)} %pad_maximum_fusion.b0, bf16[2,224,512]{2,1,0:T(8,128)(2,1)S(1)} %collective-permute-done.3.b1, ...), custom_call_target="tpu_custom_call" | custom-call | flops 3000000000 | bytes 3000000 | tf_op jit(solution)/shard_map/early/pallas_call | solution.py:508
  26.8 0.0 collective-permute-done.7.far_half
  26.8 0.1 partial.1
  26.9 0.4 collective-permute-done.8.ends
  27.3 4.2 %chain.1 = (bf16[1536,512]{1,0:T(8,128)(2,1)S(1)}, bf16[2,64,512]{2,1,0:T(8,128)(2,1)S(1)}, bf16[2,64,512]{2,1,0:T(8,128)(2,1)S(1)}, bf16[768,512]{1,0:T(8,128)(...) custom-call(bf16[2,224,512]{2,1,0:T(8,128)(2,1)S(1)} %pad_maximum_fu, ...), custom_call_target="tpu_custom_call", output_to_operand_aliasing={{0}: (5, {})} | custom-call | flops 6000000000 | bytes 6000000 | tf_op jit(solution)/shard_map/chain/pallas_call | solution.py:508
  31.5 3.9 %collective-permute-start.9 = (bf16[384,128]{1,0:T(8,128)(2,1)S(1)}, bf16[384,128]{1,0:T(8,128)(2,1)S(1)}, u32[]{:S(2)}, u32[]{:S(2)}) collective-permute-start(bf16[384,128]{1,0:T(8,128)(2,1)S(1)} %get-tuple-element.76), channel_id=1, source_target_pairs={{0,6},{2,4},{4,2},{6,0},{1,7},{3,5},{5,3},{7,1},{8,14},{10,12},{12... | collective-permute-start | bytes 294920 | tf_op jit(solution)/shard_map/ppermute | solution.py:620
  35.4 0.0 collective-permute-start.10
  35.4 0.6 %collective-permute-start.11 = (bf16[384,128]{1,0:T(8,128)(2,1)S(1)}, bf16[384,128]{1,0:T(8,128)(2,1)S(1)}, u32[]{:S(2)}, u32[]{:S(2)}) collective-permute-start(bf16[384,128]{1,0:T(8,128)(2,1)S(1)} %get-tuple-element.78), channel_id=1, source_target_pairs={{0,2},{2,0},{4,6},{6,4},{1,3},{3,1},{5,7},{7,5},{8,10},{10,8},{12,... | collective-permute-start | bytes 294920 | tf_op jit(solution)/shard_map/ppermute | solution.py:620
  36.1 2.5 %finish.1 = (bf16[2,16,4,512]{3,2,1,0:T(4,128)(2,1)}, bf16[2,16,4,512]{3,2,1,0:T(4,128)(2,1)}) custom-call(bf16[1536,512]{1,0:T(8,128)(2,1)S(1)} %bitcast.11, bf16[3,256,384]{2,1,0:T(8,128)(2,1)S(1)} %get-tuple-element.54.backward, bf16[768,512]{1,0:T(8,128)(2,1)S(1)} %get-tuple-element.70.gates, bf16[2,64,512]{2,1,0:T(8,128)(2,1)S(1)} %get-tuple-element.71.next_ref, ...), custom_call_target="tpu_custom_call" | custom-call | flops 2000000000 | bytes 2000000 | tf_op jit(solution)/shard_map/finish/pallas_call | solution.py:508
  38.5 0.2 collective-permute-done.9.p1
  38.7 5.1 %collective-permute-done.10.p2 = bf16[384,128]{1,0:T(8,128)(2,1)S(1)} collective-permute-done((bf16[384,128]{1,0:T(8,128)(2,1)S(1)}, bf16[384,128]{1,0:T(8,128)(2,1)S(1)}, u32[]{:S(2)}, u32[]{:S(2)}) %collective-permute-start.10) | collective-permute-done | bytes 98336 | tf_op jit(solution)/shard_map/ppermute | solution.py:620
  43.8 0.0 collective-permute-done.11.p3
  43.8 0.7 %add_up.1 = f32[384,128]{1,0:T(8,128)} custom-call(f32[384,128]{1,0:T(8,128)S(1)} %get-tuple-element.75.mine, bf16[384,128]{1,0:T(8,128)(2,1)S(1)} %collective-permute-done.9.p1, bf16[384,128]{1,0:T(8,128)(2,1)S(1)} %collective-permute-done.10.p2, bf16[384,128]{1,0:T(8,128)(2,1)S(1)} %collective-permute-done.11.p3), custom_call_target="tpu_custom_call" | custom-call | flops 100000000 | bytes 100000 | tf_op jit(solution)/shard_map/add_up/pallas_call | solution.py:508
  (7 shorter events, 0.1 us)
Async XLA Ops:
  0.6 9.3 %copy-start.3 = (s32[64,9]{0,1:T(8,128)S(1)}, s32[64,9]{0,1:T(8,128)}, u32[]{:S(2)}) copy-start(s32[64,9]{0,1:T(8,128)} %param.11) | copy-start | bytes 6916
  0.6 9.3 %copy-start.2 = (s32[64,9]{0,1:T(8,128)S(1)}, s32[64,9]{0,1:T(8,128)}, u32[]{:S(2)}) copy-start(s32[64,9]{0,1:T(8,128)} %param.10) | copy-start | bytes 6916
  0.7 9.3 %copy-start.1 = (f32[64,9,3]{0,2,1:T(4,128)S(1)}, f32[64,9,3]{0,2,1:T(4,128)}, u32[]{:S(2)}) copy-start(f32[64,9,3]{0,2,1:T(4,128)} %param.9) | copy-start | bytes 20740
  1.8 18.8 %collective-permute-start.5 = (bf16[688,512]{1,0:T(8,128)(2,1)S(1)}, bf16[688,512]{1,0:T(8,128)(2,1)S(1)}, u32[]{:S(2)}, u32[]{:S(2)}) collective-permute-start(bf16[688,512]{1,0:T(8,128)(2,1)S(1)} %constant_dynamic-slice_fusion), channel_id=1, source_target_pairs={{0,1},{1,0},{2,3},{3,2},{4,5},{5,4},{6,7},{7,6},{8,9},{9,8},{10,11... | collective-permute-start | bytes 2113544 | tf_op jit(solution)/shard_map/ppermute | solution.py:527
  6.0 7.8 %collective-permute-start.2 = (bf16[2,128,512]{2,1,0:T(8,128)(2,1)S(1)}, bf16[2,128,512]{2,1,0:T(8,128)(2,1)S(1)}, u32[]{:S(2)}, u32[]{:S(2)}) collective-permute-start(bf16[2,128,512]{2,1,0:T(8,128)(2,1)S(1)} %prep.1.both), channel_id=1, source_target_pairs={{0,16},{8,24},{16,0},{24,8},{1,17},{9,25},{17,1},{25,9},{2,18},{10... | collective-permute-start | bytes 786440 | tf_op jit(solution)/shard_map/ppermute | solution.py:533
  7.6 13.5 %copy-start = (bf16[1,3,512,512]{3,2,1,0:T(8,128)(2,1)S(1)}, bf16[1,3,512,512]{3,2,1,0:T(8,128)(2,1)}, u32[]{:S(2)}) copy-start(bf16[1,3,512,512]{3,2,1,0:T(8,128)(2,1)} %param.8) | copy-start | bytes 4718596
  7.6 4.8 %collective-permute-start = (bf16[2,48,512]{2,1,0:T(8,128)(2,1)S(1)}, bf16[2,48,512]{2,1,0:T(8,128)(2,1)S(1)}, u32[]{:S(2)}, u32[]{:S(2)}) collective-permute-start(bf16[2,48,512]{2,1,0:T(8,128)(2,1)S(1)} %get-tuple-element.43), channel_id=1, source_target_pairs={{0,2},{2,0},{4,6},{6,4},{1,3},{3,1},{5,7},{7,5},{8,10},{10,8},{12,... | collective-permute-start | bytes 294920 | tf_op jit(solution)/shard_map/ppermute | solution.py:536
  9.3 3.1 %collective-permute-start.1 = (bf16[2,48,512]{2,1,0:T(8,128)(2,1)S(1)}, bf16[2,48,512]{2,1,0:T(8,128)(2,1)S(1)}, u32[]{:S(2)}, u32[]{:S(2)}) collective-permute-start(bf16[2,48,512]{2,1,0:T(8,128)(2,1)S(1)} %get-tuple-element.44), channel_id=1, source_target_pairs={{2,4},{4,2},{3,5},{5,3},{10,12},{12,10},{11,13},{13,11},{18,20},{2... | collective-permute-start | bytes 294920 | tf_op jit(solution)/shard_map/ppermute | solution.py:537
  13.9 5.7 %collective-permute-start.4 = (bf16[2,96,512]{2,1,0:T(8,128)(2,1)S(1)}, bf16[2,96,512]{2,1,0:T(8,128)(2,1)S(1)}, u32[]{:S(2)}, u32[]{:S(2)}) collective-permute-start(bf16[2,96,512]{2,1,0:T(8,128)(2,1)S(1)} %pad_maximum_fusion.3), channel_id=1, source_target_pairs={{0,16},{8,24},{16,0},{24,8},{1,17},{9,25},{17,1},{25,9},{2,18},{10... | collective-permute-start | bytes 589832 | tf_op jit(solution)/shard_map/ppermute | solution.py:552
  15.4 7.6 %collective-permute-start.3 = (bf16[2,224,512]{2,1,0:T(8,128)(2,1)S(1)}, bf16[2,224,512]{2,1,0:T(8,128)(2,1)S(1)}, u32[]{:S(2)}, u32[]{:S(2)}) collective-permute-start(bf16[2,224,512]{2,1,0:T(8,128)(2,1)S(1)} %pad_maximum_fusion.b0), channel_id=1, source_target_pairs={{0,8},{8,0},{16,24},{24,16},{1,9},{9,1},{17,25},{25,17},{2,10},{10... | collective-permute-start | bytes 1376264 | tf_op jit(solution)/shard_map/ppermute | solution.py:554
  20.6 2.4 %collective-permute-start.6 = (bf16[2,224,512]{2,1,0:T(8,128)(2,1)S(1)}, bf16[2,224,512]{2,1,0:T(8,128)(2,1)S(1)}, u32[]{:S(2)}, u32[]{:S(2)}) collective-permute-start(bf16[2,224,512]{2,1,0:T(8,128)(2,1)S(1)} %pad_maximum_fusion.1.b2), channel_id=1, source_target_pairs={{0,8},{8,0},{16,24},{24,16},{1,9},{9,1},{17,25},{25,17},{2,10},{10... | collective-permute-start | bytes 1376264 | tf_op jit(solution)/shard_map/ppermute | solution.py:567
  20.6 6.2 %collective-permute-start.7 = (bf16[688,512]{1,0:T(8,128)(2,1)S(1)}, bf16[688,512]{1,0:T(8,128)(2,1)S(1)}, u32[]{:S(2)}, u32[]{:S(2)}) collective-permute-start(bf16[688,512]{1,0:T(8,128)(2,1)S(1)} %collective-permute-done.5.near_half), channel_id=1, source_target_pairs={{0,8},{8,0},{16,24},{24,16},{1,9},{9,1},{17,25},{25,17},{2,10},{10... | collective-permute-start | bytes 2113544 | tf_op jit(solution)/shard_map/ppermute | solution.py:568
  21.2 6.2 %collective-permute-start.8 = (bf16[160,512]{1,0:T(8,128)(2,1)S(1)}, bf16[160,512]{1,0:T(8,128)(2,1)S(1)}, u32[]{:S(2)}, u32[]{:S(2)}) collective-permute-start(bf16[160,512]{1,0:T(8,128)(2,1)S(1)} %pad_maximum_fusion.4), channel_id=1, source_target_pairs={{0,1},{1,0},{2,3},{3,2},{4,5},{5,4},{6,7},{7,6},{8,9},{9,8},{10,11... | collective-permute-start | bytes 491528 | tf_op jit(solution)/shard_map/ppermute | solution.py:526
  31.5 7.2 %collective-permute-start.9 = (bf16[384,128]{1,0:T(8,128)(2,1)S(1)}, bf16[384,128]{1,0:T(8,128)(2,1)S(1)}, u32[]{:S(2)}, u32[]{:S(2)}) collective-permute-start(bf16[384,128]{1,0:T(8,128)(2,1)S(1)} %get-tuple-element.76), channel_id=1, source_target_pairs={{0,6},{2,4},{4,2},{6,0},{1,7},{3,5},{5,3},{7,1},{8,14},{10,12},{12... | collective-permute-start | bytes 294920 | tf_op jit(solution)/shard_map/ppermute | solution.py:620
  35.4 8.4 %collective-permute-start.10 = (bf16[384,128]{1,0:T(8,128)(2,1)S(1)}, bf16[384,128]{1,0:T(8,128)(2,1)S(1)}, u32[]{:S(2)}, u32[]{:S(2)}) collective-permute-start(bf16[384,128]{1,0:T(8,128)(2,1)S(1)} %get-tuple-element.77), channel_id=1, source_target_pairs={{0,4},{2,6},{4,0},{6,2},{1,5},{3,7},{5,1},{7,3},{8,12},{10,14},{12... | collective-permute-start | bytes 294920 | tf_op jit(solution)/shard_map/ppermute | solution.py:620
  35.4 8.4 %collective-permute-start.11 = (bf16[384,128]{1,0:T(8,128)(2,1)S(1)}, bf16[384,128]{1,0:T(8,128)(2,1)S(1)}, u32[]{:S(2)}, u32[]{:S(2)}) collective-permute-start(bf16[384,128]{1,0:T(8,128)(2,1)S(1)} %get-tuple-element.78), channel_id=1, source_target_pairs={{0,2},{2,0},{4,6},{6,4},{1,3},{3,1},{5,7},{7,5},{8,10},{10,8},{12,... | collective-permute-start | bytes 294920 | tf_op jit(solution)/shard_map/ppermute | solution.py:620

commit v13 on v12

--- a/solution.py
+++ b/solution.py
@@ -519,7 +519,7 @@
 
     prep, edges, maps, early, partial, chain, finish = make_steps(lat_rows, lon_cols, blocks, members, channels, lat_devices)
     kernel = weights.reshape(width, channels)
-    rest = width // 2 * 5 // 48
+    rest = width // 2 // 12
     rows = width // 2 - rest
     half = lax.dynamic_slice_in_dim(kernel, lax.axis_index("lon") % 2 * (width // 2), rows, 0)
     ends = jnp.concatenate([kernel[rows : rows + rest], kernel[width - rest :]], axis=0)

time: 44.7 us -> 44.6 us (level)
  transfers between devices with their start and end apart: 12 -> 12, of which waited for: 6 -> 5; matrix products, arithmetic and copies ran while one was open for 3% -> 3% of each run, Pallas kernels for 24% -> 24%
where the time goes in v13:
time: 44.6 us; the launch traced here: 44.4 us
  Pallas kernels  15.7 us (35%)
  starting transfers between devices  15.2 us (34%)
  waiting for transfers between devices  10.2 us (23%)
  other arithmetic  1.23 us (3%)
  local copies, waits for them, and re-layouts  1.19 us (3%)
  between operations  0.83 us (2%)
    pallas_call x9, Pallas kernels, call(): pl.pallas_call(body, out_shape=outs, in_specs=[vmem] * len(ins), out_spec...  15.7 us
    ppermute x3, waiting for transfers between devices, whole_ring(): lax.ppermute(part, 'lat', swap('lat', bit))  5.28 us
    ppermute x3, starting transfers between devices, whole_ring(): lax.ppermute(part, 'lat', swap('lat', bit))  4.45 us
    ppermute x1, starting transfers between devices, whole_ring(): near_half = lax.ppermute(half, 'segment', swap('segment', 1))  3 us
    ppermute x1, waiting for transfers between devices, whole_ring(): sides_y = lax.ppermute(sides, 'lon', swap('lon', 2))  2.12 us
    ppermute x1, starting transfers between devices, whole_ring(): near_ends = lax.ppermute(ends, 'segment', swap('segment', 1))  1.81 us
    ppermute x1, starting transfers between devices, whole_ring(): from_near = lax.ppermute(toward, 'lat', near_pairs)  1.64 us
    ppermute x1, starting transfers between devices, whole_ring(): both_y = lax.ppermute(both, 'lon', swap('lon', 2))  1.58 us
  transfers between devices with their start and end apart: 12, of which 5 were waited for; matrix products, arithmetic and copies ran while one was open for 3% of the time, Pallas kernels for 24%

profile of v13, /device:TPU:0, one launch (start us, length us, event | category | flops | bytes accessed | tf_op | source)
XLA Modules:
  0.0 44.4 jit_solution(14683475174965844095)
XLA Ops:
  0.6 0.0 copy-start.3
  0.6 0.0 copy-start.2
  0.7 0.0 copy-start.1
  0.7 1.2 %constant_dynamic-slice_fusion = bf16[704,512]{1,0:T(8,128)(2,1)S(1)} fusion(bf16[1536,512]{1,0:T(8,128)(2,1)} %bitcast.7, s32[]{:T(128)S(6)} %select_n.11), kind=kLoop, calls=%fused_computation.5 | loop fusion | bytes 1441796 | tf_op jit(solution)/shard_map/dynamic_slice | solution.py:524
  1.8 3.0 %collective-permute-start.5 = (bf16[704,512]{1,0:T(8,128)(2,1)S(1)}, bf16[704,512]{1,0:T(8,128)(2,1)S(1)}, u32[]{:S(2)}, u32[]{:S(2)}) collective-permute-start(bf16[704,512]{1,0:T(8,128)(2,1)S(1)} %constant_dynamic-slice_fusion), channel_id=1, source_target_pairs={{0,1},{1,0},{2,3},{3,2},{4,5},{5,4},{6,7},{7,6},{8,9},{9,8},{10,11... | collective-permute-start | bytes 2162696 | tf_op jit(solution)/shard_map/ppermute | solution.py:527
  4.8 1.1 %pad_maximum_fusion.2.loaded = bf16[4,16,4,512]{3,2,1,0:T(4,128)(2,1)S(1)} fusion(bf16[2,16,4,512]{3,2,1,0:T(4,128)(2,1)} %param.7, bf16[2,16,4,512]{3,2,1,0:T(4,128)(2,1)} %param.6), kind=kLoop, calls=%fused_computation.2 | loop fusion | flops 131072 | bytes 524288 | tf_op jit(solution)/shard_map/concatenate | solution.py:529
  6.0 1.6 %collective-permute-start.2 = (bf16[2,128,512]{2,1,0:T(8,128)(2,1)S(1)}, bf16[2,128,512]{2,1,0:T(8,128)(2,1)S(1)}, u32[]{:S(2)}, u32[]{:S(2)}) collective-permute-start(bf16[2,128,512]{2,1,0:T(8,128)(2,1)S(1)} %prep.1.both), channel_id=1, source_target_pairs={{0,16},{8,24},{16,0},{24,8},{1,17},{9,25},{17,1},{25,9},{2,18},{10... | collective-permute-start | bytes 786440 | tf_op jit(solution)/shard_map/ppermute | solution.py:533
  7.6 0.0 copy-start
  7.6 1.6 %collective-permute-start = (bf16[2,48,512]{2,1,0:T(8,128)(2,1)S(1)}, bf16[2,48,512]{2,1,0:T(8,128)(2,1)S(1)}, u32[]{:S(2)}, u32[]{:S(2)}) collective-permute-start(bf16[2,48,512]{2,1,0:T(8,128)(2,1)S(1)} %get-tuple-element.43), channel_id=1, source_target_pairs={{0,2},{2,0},{4,6},{6,4},{1,3},{3,1},{5,7},{7,5},{8,10},{10,8},{12,... | collective-permute-start | bytes 294920 | tf_op jit(solution)/shard_map/ppermute | solution.py:536
  9.3 0.7 %collective-permute-start.1 = (bf16[2,48,512]{2,1,0:T(8,128)(2,1)S(1)}, bf16[2,48,512]{2,1,0:T(8,128)(2,1)S(1)}, u32[]{:S(2)}, u32[]{:S(2)}) collective-permute-start(bf16[2,48,512]{2,1,0:T(8,128)(2,1)S(1)} %get-tuple-element.44), channel_id=1, source_target_pairs={{2,4},{4,2},{3,5},{5,3},{10,12},{12,10},{11,13},{13,11},{18,20},{2... | collective-permute-start | bytes 294920 | tf_op jit(solution)/shard_map/ppermute | solution.py:537
  9.9 0.0 copy-done.3
  10.0 0.0 copy-done.2
  10.0 0.0 copy-done.1
  10.0 2.4 %maps_first.1.forward = bf16[4,384,256]{2,1,0:T(8,128)(2,1)S(1)} custom-call(s32[9,64]{1,0:T(8,128)S(1)} %bitcast.14, s32[9,64]{1,0:T(8,128)S(1)} %bitcast.16, f32[9,3,64]{2,1,0:T(4,128)S(1)} %bitcast.12), custom_call_target="tpu_custom_call" | custom-call | tf_op jit(solution)/shard_map/maps_first/pallas_call | solution.py:508
  12.4 0.0 collective-permute-done
  12.4 0.0 collective-permute-done.1
  12.4 1.4 %collective-permute-done.2 = bf16[2,128,512]{2,1,0:T(8,128)(2,1)S(1)} collective-permute-done((bf16[2,128,512]{2,1,0:T(8,128)(2,1)S(1)}, bf16[2,128,512]{2,1,0:T(8,128)(2,1)S(1)}, u32[]{:S(2)}, u32[]{:S(2)}) %collective-permute-start.2) | collective-permute-done | bytes 262176 | tf_op jit(solution)/shard_map/ppermute | solution.py:533
  13.9 1.5 %collective-permute-start.4 = (bf16[2,96,512]{2,1,0:T(8,128)(2,1)S(1)}, bf16[2,96,512]{2,1,0:T(8,128)(2,1)S(1)}, u32[]{:S(2)}, u32[]{:S(2)}) collective-permute-start(bf16[2,96,512]{2,1,0:T(8,128)(2,1)S(1)} %pad_maximum_fusion.3), channel_id=1, source_target_pairs={{0,16},{8,24},{16,0},{24,8},{1,17},{9,25},{17,1},{25,9},{2,18},{10... | collective-permute-start | bytes 589832 | tf_op jit(solution)/shard_map/ppermute | solution.py:552
  15.4 0.1 collective-permute-start.3
  15.5 1.9 %maps_again.1 = (bf16[3,384,256]{2,1,0:T(8,128)(2,1)S(1)}, bf16[3,256,384]{2,1,0:T(8,128)(2,1)S(1)}) custom-call(s32[9,64]{1,0:T(8,128)S(1)} %bitcast.15, s32[9,64]{1,0:T(8,128)S(1)} %bitcast.17, f32[9,3,64]{2,1,0:T(4,128)S(1)} %bitcast.13), custom_call_target="tpu_custom_call" | custom-call | tf_op jit(solution)/shard_map/maps_again/pallas_call | solution.py:508
  17.4 2.1 %collective-permute-done.4 = bf16[2,96,512]{2,1,0:T(8,128)(2,1)S(1)} collective-permute-done((bf16[2,96,512]{2,1,0:T(8,128)(2,1)S(1)}, bf16[2,96,512]{2,1,0:T(8,128)(2,1)S(1)}, u32[]{:S(2)}, u32[]{:S(2)}) %collective-permute-start.4) | collective-permute-done | bytes 196640 | tf_op jit(solution)/shard_map/ppermute | solution.py:552
  19.6 1.4 %collective-permute-done.5.near_half = bf16[704,512]{1,0:T(8,128)(2,1)S(1)} collective-permute-done((bf16[704,512]{1,0:T(8,128)(2,1)S(1)}, bf16[704,512]{1,0:T(8,128)(2,1)S(1)}, u32[]{:S(2)}, u32[]{:S(2)}) %collective-permute-start.5) | collective-permute-done | bytes 720928 | tf_op jit(solution)/shard_map/ppermute | solution.py:527
  21.0 0.0 collective-permute-start.6
  21.0 0.5 %collective-permute-start.7 = (bf16[704,512]{1,0:T(8,128)(2,1)S(1)}, bf16[704,512]{1,0:T(8,128)(2,1)S(1)}, u32[]{:S(2)}, u32[]{:S(2)}) collective-permute-start(bf16[704,512]{1,0:T(8,128)(2,1)S(1)} %collective-permute-done.5.near_half), channel_id=1, source_target_pairs={{0,8},{8,0},{16,24},{24,16},{1,9},{9,1},{17,25},{25,17},{2,10},{10... | collective-permute-start | bytes 2162696 | tf_op jit(solution)/shard_map/ppermute | solution.py:568
  21.5 0.0 copy-done
  21.5 1.8 %collective-permute-start.8 = (bf16[128,512]{1,0:T(8,128)(2,1)S(1)}, bf16[128,512]{1,0:T(8,128)(2,1)S(1)}, u32[]{:S(2)}, u32[]{:S(2)}) collective-permute-start(bf16[128,512]{1,0:T(8,128)(2,1)S(1)} %pad_maximum_fusion.4), channel_id=1, source_target_pairs={{0,1},{1,0},{2,3},{3,2},{4,5},{5,4},{6,7},{7,6},{8,9},{9,8},{10,11... | collective-permute-start | bytes 393224 | tf_op jit(solution)/shard_map/ppermute | solution.py:526
  23.3 0.0 collective-permute-done.3.b1
  23.3 0.0 collective-permute-done.6.b3
  23.3 3.8 %early.1 = (bf16[1024,1536]{1,0:T(8,128)(2,1)S(1)}, bf16[512,384]{1,0:T(8,128)(2,1)S(1)}, bf16[2,4,96,512]{3,2,1,0:T(8,128)(2,1)S(1)}, bf16[2,64,512]{2,1,0:T(8,128)(2,1)S(1)}) custom-call(bf16[2,224,512]{2,1,0:T(8,128)(2,1)S(1)} %pad_maximum_fusion.b0, bf16[2,224,512]{2,1,0:T(8,128)(2,1)S(1)} %collective-permute-done.3.b1, ...), custom_call_target="tpu_custom_call" | custom-call | flops 3000000000 | bytes 3000000 | tf_op jit(solution)/shard_map/early/pallas_call | solution.py:508
  27.2 0.0 collective-permute-done.7.far_half
  27.2 0.1 partial.1
  27.3 0.0 collective-permute-done.8.ends
  27.3 4.2 %chain.1 = (bf16[1536,512]{1,0:T(8,128)(2,1)S(1)}, bf16[2,64,512]{2,1,0:T(8,128)(2,1)S(1)}, bf16[2,64,512]{2,1,0:T(8,128)(2,1)S(1)}, bf16[768,512]{1,0:T(8,128)(...) custom-call(bf16[2,224,512]{2,1,0:T(8,128)(2,1)S(1)} %pad_maximum_fu, ...), custom_call_target="tpu_custom_call", output_to_operand_aliasing={{0}: (5, {})} | custom-call | flops 6000000000 | bytes 6000000 | tf_op jit(solution)/shard_map/chain/pallas_call | solution.py:508
  31.5 3.6 %collective-permute-start.9 = (bf16[384,128]{1,0:T(8,128)(2,1)S(1)}, bf16[384,128]{1,0:T(8,128)(2,1)S(1)}, u32[]{:S(2)}, u32[]{:S(2)}) collective-permute-start(bf16[384,128]{1,0:T(8,128)(2,1)S(1)} %get-tuple-element.76), channel_id=1, source_target_pairs={{0,6},{2,4},{4,2},{6,0},{1,7},{3,5},{5,3},{7,1},{8,14},{10,12},{12... | collective-permute-start | bytes 294920 | tf_op jit(solution)/shard_map/ppermute | solution.py:620
  35.1 0.0 collective-permute-start.10
  35.1 0.8 %collective-permute-start.11 = (bf16[384,128]{1,0:T(8,128)(2,1)S(1)}, bf16[384,128]{1,0:T(8,128)(2,1)S(1)}, u32[]{:S(2)}, u32[]{:S(2)}) collective-permute-start(bf16[384,128]{1,0:T(8,128)(2,1)S(1)} %get-tuple-element.78), channel_id=1, source_target_pairs={{0,2},{2,0},{4,6},{6,4},{1,3},{3,1},{5,7},{7,5},{8,10},{10,8},{12,... | collective-permute-start | bytes 294920 | tf_op jit(solution)/shard_map/ppermute | solution.py:620
  35.9 2.5 %finish.1 = (bf16[2,16,4,512]{3,2,1,0:T(4,128)(2,1)}, bf16[2,16,4,512]{3,2,1,0:T(4,128)(2,1)}) custom-call(bf16[1536,512]{1,0:T(8,128)(2,1)S(1)} %bitcast.11, bf16[3,256,384]{2,1,0:T(8,128)(2,1)S(1)} %get-tuple-element.54.backward, bf16[768,512]{1,0:T(8,128)(2,1)S(1)} %get-tuple-element.70.gates, bf16[2,64,512]{2,1,0:T(8,128)(2,1)S(1)} %get-tuple-element.71.next_ref, ...), custom_call_target="tpu_custom_call" | custom-call | flops 2000000000 | bytes 2000000 | tf_op jit(solution)/shard_map/finish/pallas_call | solution.py:508
  38.4 0.1 collective-permute-done.9.p1
  38.5 5.2 %collective-permute-done.10.p2 = bf16[384,128]{1,0:T(8,128)(2,1)S(1)} collective-permute-done((bf16[384,128]{1,0:T(8,128)(2,1)S(1)}, bf16[384,128]{1,0:T(8,128)(2,1)S(1)}, u32[]{:S(2)}, u32[]{:S(2)}) %collective-permute-start.10) | collective-permute-done | bytes 98336 | tf_op jit(solution)/shard_map/ppermute | solution.py:620
  43.7 0.0 collective-permute-done.11.p3
  43.7 0.7 %add_up.1 = f32[384,128]{1,0:T(8,128)} custom-call(f32[384,128]{1,0:T(8,128)S(1)} %get-tuple-element.75.mine, bf16[384,128]{1,0:T(8,128)(2,1)S(1)} %collective-permute-done.9.p1, bf16[384,128]{1,0:T(8,128)(2,1)S(1)} %collective-permute-done.10.p2, bf16[384,128]{1,0:T(8,128)(2,1)S(1)} %collective-permute-done.11.p3), custom_call_target="tpu_custom_call" | custom-call | flops 100000000 | bytes 100000 | tf_op jit(solution)/shard_map/add_up/pallas_call | solution.py:508
  (7 shorter events, 0.1 us)
Async XLA Ops:
  0.6 9.3 %copy-start.3 = (s32[64,9]{0,1:T(8,128)S(1)}, s32[64,9]{0,1:T(8,128)}, u32[]{:S(2)}) copy-start(s32[64,9]{0,1:T(8,128)} %param.11) | copy-start | bytes 6916
  0.6 9.3 %copy-start.2 = (s32[64,9]{0,1:T(8,128)S(1)}, s32[64,9]{0,1:T(8,128)}, u32[]{:S(2)}) copy-start(s32[64,9]{0,1:T(8,128)} %param.10) | copy-start | bytes 6916
  0.7 9.3 %copy-start.1 = (f32[64,9,3]{0,2,1:T(4,128)S(1)}, f32[64,9,3]{0,2,1:T(4,128)}, u32[]{:S(2)}) copy-start(f32[64,9,3]{0,2,1:T(4,128)} %param.9) | copy-start | bytes 20740
  1.8 19.1 %collective-permute-start.5 = (bf16[704,512]{1,0:T(8,128)(2,1)S(1)}, bf16[704,512]{1,0:T(8,128)(2,1)S(1)}, u32[]{:S(2)}, u32[]{:S(2)}) collective-permute-start(bf16[704,512]{1,0:T(8,128)(2,1)S(1)} %constant_dynamic-slice_fusion), channel_id=1, source_target_pairs={{0,1},{1,0},{2,3},{3,2},{4,5},{5,4},{6,7},{7,6},{8,9},{9,8},{10,11... | collective-permute-start | bytes 2162696 | tf_op jit(solution)/shard_map/ppermute | solution.py:527
  6.0 7.8 %collective-permute-start.2 = (bf16[2,128,512]{2,1,0:T(8,128)(2,1)S(1)}, bf16[2,128,512]{2,1,0:T(8,128)(2,1)S(1)}, u32[]{:S(2)}, u32[]{:S(2)}) collective-permute-start(bf16[2,128,512]{2,1,0:T(8,128)(2,1)S(1)} %prep.1.both), channel_id=1, source_target_pairs={{0,16},{8,24},{16,0},{24,8},{1,17},{9,25},{17,1},{25,9},{2,18},{10... | collective-permute-start | bytes 786440 | tf_op jit(solution)/shard_map/ppermute | solution.py:533
  7.6 13.9 %copy-start = (bf16[1,3,512,512]{3,2,1,0:T(8,128)(2,1)S(1)}, bf16[1,3,512,512]{3,2,1,0:T(8,128)(2,1)}, u32[]{:S(2)}) copy-start(bf16[1,3,512,512]{3,2,1,0:T(8,128)(2,1)} %param.8) | copy-start | bytes 4718596
  7.6 4.8 %collective-permute-start = (bf16[2,48,512]{2,1,0:T(8,128)(2,1)S(1)}, bf16[2,48,512]{2,1,0:T(8,128)(2,1)S(1)}, u32[]{:S(2)}, u32[]{:S(2)}) collective-permute-start(bf16[2,48,512]{2,1,0:T(8,128)(2,1)S(1)} %get-tuple-element.43), channel_id=1, source_target_pairs={{0,2},{2,0},{4,6},{6,4},{1,3},{3,1},{5,7},{7,5},{8,10},{10,8},{12,... | collective-permute-start | bytes 294920 | tf_op jit(solution)/shard_map/ppermute | solution.py:536
  9.3 3.1 %collective-permute-start.1 = (bf16[2,48,512]{2,1,0:T(8,128)(2,1)S(1)}, bf16[2,48,512]{2,1,0:T(8,128)(2,1)S(1)}, u32[]{:S(2)}, u32[]{:S(2)}) collective-permute-start(bf16[2,48,512]{2,1,0:T(8,128)(2,1)S(1)} %get-tuple-element.44), channel_id=1, source_target_pairs={{2,4},{4,2},{3,5},{5,3},{10,12},{12,10},{11,13},{13,11},{18,20},{2... | collective-permute-start | bytes 294920 | tf_op jit(solution)/shard_map/ppermute | solution.py:537
  13.9 5.7 %collective-permute-start.4 = (bf16[2,96,512]{2,1,0:T(8,128)(2,1)S(1)}, bf16[2,96,512]{2,1,0:T(8,128)(2,1)S(1)}, u32[]{:S(2)}, u32[]{:S(2)}) collective-permute-start(bf16[2,96,512]{2,1,0:T(8,128)(2,1)S(1)} %pad_maximum_fusion.3), channel_id=1, source_target_pairs={{0,16},{8,24},{16,0},{24,8},{1,17},{9,25},{17,1},{25,9},{2,18},{10... | collective-permute-start | bytes 589832 | tf_op jit(solution)/shard_map/ppermute | solution.py:552
  15.4 7.9 %collective-permute-start.3 = (bf16[2,224,512]{2,1,0:T(8,128)(2,1)S(1)}, bf16[2,224,512]{2,1,0:T(8,128)(2,1)S(1)}, u32[]{:S(2)}, u32[]{:S(2)}) collective-permute-start(bf16[2,224,512]{2,1,0:T(8,128)(2,1)S(1)} %pad_maximum_fusion.b0), channel_id=1, source_target_pairs={{0,8},{8,0},{16,24},{24,16},{1,9},{9,1},{17,25},{25,17},{2,10},{10... | collective-permute-start | bytes 1376264 | tf_op jit(solution)/shard_map/ppermute | solution.py:554
  21.0 2.4 %collective-permute-start.6 = (bf16[2,224,512]{2,1,0:T(8,128)(2,1)S(1)}, bf16[2,224,512]{2,1,0:T(8,128)(2,1)S(1)}, u32[]{:S(2)}, u32[]{:S(2)}) collective-permute-start(bf16[2,224,512]{2,1,0:T(8,128)(2,1)S(1)} %pad_maximum_fusion.1.b2), channel_id=1, source_target_pairs={{0,8},{8,0},{16,24},{24,16},{1,9},{9,1},{17,25},{25,17},{2,10},{10... | collective-permute-start | bytes 1376264 | tf_op jit(solution)/shard_map/ppermute | solution.py:567
  21.0 6.2 %collective-permute-start.7 = (bf16[704,512]{1,0:T(8,128)(2,1)S(1)}, bf16[704,512]{1,0:T(8,128)(2,1)S(1)}, u32[]{:S(2)}, u32[]{:S(2)}) collective-permute-start(bf16[704,512]{1,0:T(8,128)(2,1)S(1)} %collective-permute-done.5.near_half), channel_id=1, source_target_pairs={{0,8},{8,0},{16,24},{24,16},{1,9},{9,1},{17,25},{25,17},{2,10},{10... | collective-permute-start | bytes 2162696 | tf_op jit(solution)/shard_map/ppermute | solution.py:568
  21.5 5.8 %collective-permute-start.8 = (bf16[128,512]{1,0:T(8,128)(2,1)S(1)}, bf16[128,512]{1,0:T(8,128)(2,1)S(1)}, u32[]{:S(2)}, u32[]{:S(2)}) collective-permute-start(bf16[128,512]{1,0:T(8,128)(2,1)S(1)} %pad_maximum_fusion.4), channel_id=1, source_target_pairs={{0,1},{1,0},{2,3},{3,2},{4,5},{5,4},{6,7},{7,6},{8,9},{9,8},{10,11... | collective-permute-start | bytes 393224 | tf_op jit(solution)/shard_map/ppermute | solution.py:526
  31.5 7.0 %collective-permute-start.9 = (bf16[384,128]{1,0:T(8,128)(2,1)S(1)}, bf16[384,128]{1,0:T(8,128)(2,1)S(1)}, u32[]{:S(2)}, u32[]{:S(2)}) collective-permute-start(bf16[384,128]{1,0:T(8,128)(2,1)S(1)} %get-tuple-element.76), channel_id=1, source_target_pairs={{0,6},{2,4},{4,2},{6,0},{1,7},{3,5},{5,3},{7,1},{8,14},{10,12},{12... | collective-permute-start | bytes 294920 | tf_op jit(solution)/shard_map/ppermute | solution.py:620
  35.1 8.5 %collective-permute-start.10 = (bf16[384,128]{1,0:T(8,128)(2,1)S(1)}, bf16[384,128]{1,0:T(8,128)(2,1)S(1)}, u32[]{:S(2)}, u32[]{:S(2)}) collective-permute-start(bf16[384,128]{1,0:T(8,128)(2,1)S(1)} %get-tuple-element.77), channel_id=1, source_target_pairs={{0,4},{2,6},{4,0},{6,2},{1,5},{3,7},{5,1},{7,3},{8,12},{10,14},{12... | collective-permute-start | bytes 294920 | tf_op jit(solution)/shard_map/ppermute | solution.py:620
  35.1 8.5 %collective-permute-start.11 = (bf16[384,128]{1,0:T(8,128)(2,1)S(1)}, bf16[384,128]{1,0:T(8,128)(2,1)S(1)}, u32[]{:S(2)}, u32[]{:S(2)}) collective-permute-start(bf16[384,128]{1,0:T(8,128)(2,1)S(1)} %get-tuple-element.78), channel_id=1, source_target_pairs={{0,2},{2,0},{4,6},{6,4},{1,3},{3,1},{5,7},{7,5},{8,10},{10,8},{12,... | collective-permute-start | bytes 294920 | tf_op jit(solution)/shard_map/ppermute | solution.py:620

commit v14 on v12

--- a/solution.py
+++ b/solution.py
@@ -617,7 +617,7 @@
         ),
         {5: 0},
     )
-    got = [lax.ppermute(part, "lat", swap("lat", bit)) for bit, part in reversed(list(zip((1, 2, 3), parts)))]
+    got = [lax.ppermute(parts[bit - 1], "lat", swap("lat", bit)) for bit in (2, 3, 1)]
     block = (members, lat_rows, lon_cols, channels)
     grad, out = call(
         finish,

time: 44.7 us -> 43.7 us (0.978)
  waiting for transfers between devices: 10.3 us -> 9.18 us
    ppermute x3, waiting for transfers between devices: 5.27 us -> 4.14 us  [whole_ring(): lax.ppermute(parts[bit - 1], 'lat', swap('lat', bit))]
  transfers between devices with their start and end apart: 12 -> 12, of which waited for: 6 -> 6; matrix products, arithmetic and copies ran while one was open for 3% -> 3% of each run, Pallas kernels for 24% -> 25%
where the time goes in v14:
time: 43.7 us; the launch traced here: 43.5 us
  Pallas kernels  15.6 us (36%)
  starting transfers between devices  15.5 us (35%)
  waiting for transfers between devices  9.18 us (21%)
  other arithmetic  1.23 us (3%)
  local copies, waits for them, and re-layouts  1.19 us (3%)
  between operations  0.82 us (2%)
    pallas_call x9, Pallas kernels, call(): pl.pallas_call(body, out_shape=outs, in_specs=[vmem] * len(ins), out_spec...  15.6 us
    ppermute x3, starting transfers between devices, whole_ring(): lax.ppermute(parts[bit - 1], 'lat', swap('lat', bit))  4.67 us
    ppermute x3, waiting for transfers between devices, whole_ring(): lax.ppermute(parts[bit - 1], 'lat', swap('lat', bit))  4.14 us
    ppermute x1, starting transfers between devices, whole_ring(): near_half = lax.ppermute(half, 'segment', swap('segment', 1))  3 us
    ppermute x1, waiting for transfers between devices, whole_ring(): sides_y = lax.ppermute(sides, 'lon', swap('lon', 2))  2.12 us
    ppermute x1, starting transfers between devices, whole_ring(): near_ends = lax.ppermute(ends, 'segment', swap('segment', 1))  1.81 us
    ppermute x1, starting transfers between devices, whole_ring(): from_near = lax.ppermute(toward, 'lat', near_pairs)  1.64 us
    ppermute x1, starting transfers between devices, whole_ring(): both_y = lax.ppermute(both, 'lon', swap('lon', 2))  1.58 us
  transfers between devices with their start and end apart: 12, of which 6 were waited for; matrix products, arithmetic and copies ran while one was open for 3% of the time, Pallas kernels for 25%

profile of v14, /device:TPU:0, one launch (start us, length us, event | category | flops | bytes accessed | tf_op | source)
XLA Modules:
  0.0 43.5 jit_solution(17272841457431358395)
XLA Ops:
  0.6 0.0 copy-start.3
  0.6 0.0 copy-start.2
  0.7 0.0 copy-start.1
  0.7 1.2 %constant_dynamic-slice_fusion = bf16[688,512]{1,0:T(8,128)(2,1)S(1)} fusion(bf16[1536,512]{1,0:T(8,128)(2,1)} %bitcast.7, s32[]{:T(128)S(6)} %select_n.11), kind=kLoop, calls=%fused_computation.5 | loop fusion | bytes 1409028 | tf_op jit(solution)/shard_map/dynamic_slice | solution.py:524
  1.8 3.0 %collective-permute-start.5 = (bf16[688,512]{1,0:T(8,128)(2,1)S(1)}, bf16[688,512]{1,0:T(8,128)(2,1)S(1)}, u32[]{:S(2)}, u32[]{:S(2)}) collective-permute-start(bf16[688,512]{1,0:T(8,128)(2,1)S(1)} %constant_dynamic-slice_fusion), channel_id=1, source_target_pairs={{0,1},{1,0},{2,3},{3,2},{4,5},{5,4},{6,7},{7,6},{8,9},{9,8},{10,11... | collective-permute-start | bytes 2113544 | tf_op jit(solution)/shard_map/ppermute | solution.py:527
  4.8 1.1 %pad_maximum_fusion.2.loaded = bf16[4,16,4,512]{3,2,1,0:T(4,128)(2,1)S(1)} fusion(bf16[2,16,4,512]{3,2,1,0:T(4,128)(2,1)} %param.7, bf16[2,16,4,512]{3,2,1,0:T(4,128)(2,1)} %param.6), kind=kLoop, calls=%fused_computation.2 | loop fusion | flops 131072 | bytes 524288 | tf_op jit(solution)/shard_map/concatenate | solution.py:529
  6.0 1.6 %collective-permute-start.2 = (bf16[2,128,512]{2,1,0:T(8,128)(2,1)S(1)}, bf16[2,128,512]{2,1,0:T(8,128)(2,1)S(1)}, u32[]{:S(2)}, u32[]{:S(2)}) collective-permute-start(bf16[2,128,512]{2,1,0:T(8,128)(2,1)S(1)} %prep.1.both), channel_id=1, source_target_pairs={{0,16},{8,24},{16,0},{24,8},{1,17},{9,25},{17,1},{25,9},{2,18},{10... | collective-permute-start | bytes 786440 | tf_op jit(solution)/shard_map/ppermute | solution.py:533
  7.6 0.0 copy-start
  7.6 1.6 %collective-permute-start = (bf16[2,48,512]{2,1,0:T(8,128)(2,1)S(1)}, bf16[2,48,512]{2,1,0:T(8,128)(2,1)S(1)}, u32[]{:S(2)}, u32[]{:S(2)}) collective-permute-start(bf16[2,48,512]{2,1,0:T(8,128)(2,1)S(1)} %get-tuple-element.43), channel_id=1, source_target_pairs={{0,2},{2,0},{4,6},{6,4},{1,3},{3,1},{5,7},{7,5},{8,10},{10,8},{12,... | collective-permute-start | bytes 294920 | tf_op jit(solution)/shard_map/ppermute | solution.py:536
  9.3 0.7 %collective-permute-start.1 = (bf16[2,48,512]{2,1,0:T(8,128)(2,1)S(1)}, bf16[2,48,512]{2,1,0:T(8,128)(2,1)S(1)}, u32[]{:S(2)}, u32[]{:S(2)}) collective-permute-start(bf16[2,48,512]{2,1,0:T(8,128)(2,1)S(1)} %get-tuple-element.44), channel_id=1, source_target_pairs={{2,4},{4,2},{3,5},{5,3},{10,12},{12,10},{11,13},{13,11},{18,20},{2... | collective-permute-start | bytes 294920 | tf_op jit(solution)/shard_map/ppermute | solution.py:537
  9.9 0.0 copy-done.3
  10.0 0.0 copy-done.2
  10.0 0.0 copy-done.1
  10.0 2.4 %maps_first.1.forward = bf16[4,384,256]{2,1,0:T(8,128)(2,1)S(1)} custom-call(s32[9,64]{1,0:T(8,128)S(1)} %bitcast.14, s32[9,64]{1,0:T(8,128)S(1)} %bitcast.16, f32[9,3,64]{2,1,0:T(4,128)S(1)} %bitcast.12), custom_call_target="tpu_custom_call" | custom-call | tf_op jit(solution)/shard_map/maps_first/pallas_call | solution.py:508
  12.4 0.0 collective-permute-done
  12.4 0.0 collective-permute-done.1
  12.4 1.4 %collective-permute-done.2 = bf16[2,128,512]{2,1,0:T(8,128)(2,1)S(1)} collective-permute-done((bf16[2,128,512]{2,1,0:T(8,128)(2,1)S(1)}, bf16[2,128,512]{2,1,0:T(8,128)(2,1)S(1)}, u32[]{:S(2)}, u32[]{:S(2)}) %collective-permute-start.2) | collective-permute-done | bytes 262176 | tf_op jit(solution)/shard_map/ppermute | solution.py:533
  13.9 1.5 %collective-permute-start.4 = (bf16[2,96,512]{2,1,0:T(8,128)(2,1)S(1)}, bf16[2,96,512]{2,1,0:T(8,128)(2,1)S(1)}, u32[]{:S(2)}, u32[]{:S(2)}) collective-permute-start(bf16[2,96,512]{2,1,0:T(8,128)(2,1)S(1)} %pad_maximum_fusion.3), channel_id=1, source_target_pairs={{0,16},{8,24},{16,0},{24,8},{1,17},{9,25},{17,1},{25,9},{2,18},{10... | collective-permute-start | bytes 589832 | tf_op jit(solution)/shard_map/ppermute | solution.py:552
  15.4 0.1 collective-permute-start.3
  15.5 1.9 %maps_again.1 = (bf16[3,384,256]{2,1,0:T(8,128)(2,1)S(1)}, bf16[3,256,384]{2,1,0:T(8,128)(2,1)S(1)}) custom-call(s32[9,64]{1,0:T(8,128)S(1)} %bitcast.15, s32[9,64]{1,0:T(8,128)S(1)} %bitcast.17, f32[9,3,64]{2,1,0:T(4,128)S(1)} %bitcast.13), custom_call_target="tpu_custom_call" | custom-call | tf_op jit(solution)/shard_map/maps_again/pallas_call | solution.py:508
  17.4 2.1 %collective-permute-done.4 = bf16[2,96,512]{2,1,0:T(8,128)(2,1)S(1)} collective-permute-done((bf16[2,96,512]{2,1,0:T(8,128)(2,1)S(1)}, bf16[2,96,512]{2,1,0:T(8,128)(2,1)S(1)}, u32[]{:S(2)}, u32[]{:S(2)}) %collective-permute-start.4) | collective-permute-done | bytes 196640 | tf_op jit(solution)/shard_map/ppermute | solution.py:552
  19.6 1.1 %collective-permute-done.5.near_half = bf16[688,512]{1,0:T(8,128)(2,1)S(1)} collective-permute-done((bf16[688,512]{1,0:T(8,128)(2,1)S(1)}, bf16[688,512]{1,0:T(8,128)(2,1)S(1)}, u32[]{:S(2)}, u32[]{:S(2)}) %collective-permute-start.5) | collective-permute-done | bytes 704544 | tf_op jit(solution)/shard_map/ppermute | solution.py:527
  20.6 0.0 collective-permute-start.6
  20.6 0.5 %collective-permute-start.7 = (bf16[688,512]{1,0:T(8,128)(2,1)S(1)}, bf16[688,512]{1,0:T(8,128)(2,1)S(1)}, u32[]{:S(2)}, u32[]{:S(2)}) collective-permute-start(bf16[688,512]{1,0:T(8,128)(2,1)S(1)} %collective-permute-done.5.near_half), channel_id=1, source_target_pairs={{0,8},{8,0},{16,24},{24,16},{1,9},{9,1},{17,25},{25,17},{2,10},{10... | collective-permute-start | bytes 2113544 | tf_op jit(solution)/shard_map/ppermute | solution.py:568
  21.1 0.0 copy-done
  21.2 1.8 %collective-permute-start.8 = (bf16[160,512]{1,0:T(8,128)(2,1)S(1)}, bf16[160,512]{1,0:T(8,128)(2,1)S(1)}, u32[]{:S(2)}, u32[]{:S(2)}) collective-permute-start(bf16[160,512]{1,0:T(8,128)(2,1)S(1)} %pad_maximum_fusion.4), channel_id=1, source_target_pairs={{0,1},{1,0},{2,3},{3,2},{4,5},{5,4},{6,7},{7,6},{8,9},{9,8},{10,11... | collective-permute-start | bytes 491528 | tf_op jit(solution)/shard_map/ppermute | solution.py:526
  23.0 0.0 collective-permute-done.3.b1
  23.0 0.0 collective-permute-done.6.b3
  23.0 3.8 %early.1 = (bf16[1024,1536]{1,0:T(8,128)(2,1)S(1)}, bf16[512,384]{1,0:T(8,128)(2,1)S(1)}, bf16[2,4,96,512]{3,2,1,0:T(8,128)(2,1)S(1)}, bf16[2,64,512]{2,1,0:T(8,128)(2,1)S(1)}) custom-call(bf16[2,224,512]{2,1,0:T(8,128)(2,1)S(1)} %pad_maximum_fusion.b0, bf16[2,224,512]{2,1,0:T(8,128)(2,1)S(1)} %collective-permute-done.3.b1, ...), custom_call_target="tpu_custom_call" | custom-call | flops 3000000000 | bytes 3000000 | tf_op jit(solution)/shard_map/early/pallas_call | solution.py:508
  26.8 0.0 collective-permute-done.7.far_half
  26.8 0.1 partial.1
  26.9 0.4 collective-permute-done.8.ends
  27.3 4.2 %chain.1 = (bf16[1536,512]{1,0:T(8,128)(2,1)S(1)}, bf16[2,64,512]{2,1,0:T(8,128)(2,1)S(1)}, bf16[2,64,512]{2,1,0:T(8,128)(2,1)S(1)}, bf16[768,512]{1,0:T(8,128)(...) custom-call(bf16[2,224,512]{2,1,0:T(8,128)(2,1)S(1)} %pad_maximum_fu, ...), custom_call_target="tpu_custom_call", output_to_operand_aliasing={{0}: (5, {})} | custom-call | flops 6000000000 | bytes 6000000 | tf_op jit(solution)/shard_map/chain/pallas_call | solution.py:508
  31.5 3.8 %collective-permute-start.9 = (bf16[384,128]{1,0:T(8,128)(2,1)S(1)}, bf16[384,128]{1,0:T(8,128)(2,1)S(1)}, u32[]{:S(2)}, u32[]{:S(2)}) collective-permute-start(bf16[384,128]{1,0:T(8,128)(2,1)S(1)} %get-tuple-element.76), channel_id=1, source_target_pairs={{0,4},{2,6},{4,0},{6,2},{1,5},{3,7},{5,1},{7,3},{8,12},{10,14},{12... | collective-permute-start | bytes 294920 | tf_op jit(solution)/shard_map/ppermute | solution.py:620
  35.3 0.9 %collective-permute-start.10 = (bf16[384,128]{1,0:T(8,128)(2,1)S(1)}, bf16[384,128]{1,0:T(8,128)(2,1)S(1)}, u32[]{:S(2)}, u32[]{:S(2)}) collective-permute-start(bf16[384,128]{1,0:T(8,128)(2,1)S(1)} %get-tuple-element.77), channel_id=1, source_target_pairs={{0,6},{2,4},{4,2},{6,0},{1,7},{3,5},{5,3},{7,1},{8,14},{10,12},{12... | collective-permute-start | bytes 294920 | tf_op jit(solution)/shard_map/ppermute | solution.py:620
  36.2 0.0 collective-permute-start.11
  36.2 2.5 %finish.1 = (bf16[2,16,4,512]{3,2,1,0:T(4,128)(2,1)}, bf16[2,16,4,512]{3,2,1,0:T(4,128)(2,1)}) custom-call(bf16[1536,512]{1,0:T(8,128)(2,1)S(1)} %bitcast.11, bf16[3,256,384]{2,1,0:T(8,128)(2,1)S(1)} %get-tuple-element.54.backward, bf16[768,512]{1,0:T(8,128)(2,1)S(1)} %get-tuple-element.70.gates, bf16[2,64,512]{2,1,0:T(8,128)(2,1)S(1)} %get-tuple-element.71.next_ref, ...), custom_call_target="tpu_custom_call" | custom-call | flops 2000000000 | bytes 2000000 | tf_op jit(solution)/shard_map/finish/pallas_call | solution.py:508
  38.6 3.8 %collective-permute-done.9.p1 = bf16[384,128]{1,0:T(8,128)(2,1)S(1)} collective-permute-done((bf16[384,128]{1,0:T(8,128)(2,1)S(1)}, bf16[384,128]{1,0:T(8,128)(2,1)S(1)}, u32[]{:S(2)}, u32[]{:S(2)}) %collective-permute-start.9) | collective-permute-done | bytes 98336 | tf_op jit(solution)/shard_map/ppermute | solution.py:620
  42.5 0.0 collective-permute-done.10.p2
  42.5 0.3 collective-permute-done.11.p3
  42.8 0.7 %add_up.1 = f32[384,128]{1,0:T(8,128)} custom-call(f32[384,128]{1,0:T(8,128)S(1)} %get-tuple-element.75.mine, bf16[384,128]{1,0:T(8,128)(2,1)S(1)} %collective-permute-done.9.p1, bf16[384,128]{1,0:T(8,128)(2,1)S(1)} %collective-permute-done.10.p2, bf16[384,128]{1,0:T(8,128)(2,1)S(1)} %collective-permute-done.11.p3), custom_call_target="tpu_custom_call" | custom-call | flops 100000000 | bytes 100000 | tf_op jit(solution)/shard_map/add_up/pallas_call | solution.py:508
  (7 shorter events, 0.1 us)
Async XLA Ops:
  0.6 9.3 %copy-start.3 = (s32[64,9]{0,1:T(8,128)S(1)}, s32[64,9]{0,1:T(8,128)}, u32[]{:S(2)}) copy-start(s32[64,9]{0,1:T(8,128)} %param.11) | copy-start | bytes 6916
  0.6 9.3 %copy-start.2 = (s32[64,9]{0,1:T(8,128)S(1)}, s32[64,9]{0,1:T(8,128)}, u32[]{:S(2)}) copy-start(s32[64,9]{0,1:T(8,128)} %param.10) | copy-start | bytes 6916
  0.7 9.3 %copy-start.1 = (f32[64,9,3]{0,2,1:T(4,128)S(1)}, f32[64,9,3]{0,2,1:T(4,128)}, u32[]{:S(2)}) copy-start(f32[64,9,3]{0,2,1:T(4,128)} %param.9) | copy-start | bytes 20740
  1.8 18.8 %collective-permute-start.5 = (bf16[688,512]{1,0:T(8,128)(2,1)S(1)}, bf16[688,512]{1,0:T(8,128)(2,1)S(1)}, u32[]{:S(2)}, u32[]{:S(2)}) collective-permute-start(bf16[688,512]{1,0:T(8,128)(2,1)S(1)} %constant_dynamic-slice_fusion), channel_id=1, source_target_pairs={{0,1},{1,0},{2,3},{3,2},{4,5},{5,4},{6,7},{7,6},{8,9},{9,8},{10,11... | collective-permute-start | bytes 2113544 | tf_op jit(solution)/shard_map/ppermute | solution.py:527
  6.0 7.8 %collective-permute-start.2 = (bf16[2,128,512]{2,1,0:T(8,128)(2,1)S(1)}, bf16[2,128,512]{2,1,0:T(8,128)(2,1)S(1)}, u32[]{:S(2)}, u32[]{:S(2)}) collective-permute-start(bf16[2,128,512]{2,1,0:T(8,128)(2,1)S(1)} %prep.1.both), channel_id=1, source_target_pairs={{0,16},{8,24},{16,0},{24,8},{1,17},{9,25},{17,1},{25,9},{2,18},{10... | collective-permute-start | bytes 786440 | tf_op jit(solution)/shard_map/ppermute | solution.py:533
  7.6 13.5 %copy-start = (bf16[1,3,512,512]{3,2,1,0:T(8,128)(2,1)S(1)}, bf16[1,3,512,512]{3,2,1,0:T(8,128)(2,1)}, u32[]{:S(2)}) copy-start(bf16[1,3,512,512]{3,2,1,0:T(8,128)(2,1)} %param.8) | copy-start | bytes 4718596
  7.6 4.8 %collective-permute-start = (bf16[2,48,512]{2,1,0:T(8,128)(2,1)S(1)}, bf16[2,48,512]{2,1,0:T(8,128)(2,1)S(1)}, u32[]{:S(2)}, u32[]{:S(2)}) collective-permute-start(bf16[2,48,512]{2,1,0:T(8,128)(2,1)S(1)} %get-tuple-element.43), channel_id=1, source_target_pairs={{0,2},{2,0},{4,6},{6,4},{1,3},{3,1},{5,7},{7,5},{8,10},{10,8},{12,... | collective-permute-start | bytes 294920 | tf_op jit(solution)/shard_map/ppermute | solution.py:536
  9.3 3.1 %collective-permute-start.1 = (bf16[2,48,512]{2,1,0:T(8,128)(2,1)S(1)}, bf16[2,48,512]{2,1,0:T(8,128)(2,1)S(1)}, u32[]{:S(2)}, u32[]{:S(2)}) collective-permute-start(bf16[2,48,512]{2,1,0:T(8,128)(2,1)S(1)} %get-tuple-element.44), channel_id=1, source_target_pairs={{2,4},{4,2},{3,5},{5,3},{10,12},{12,10},{11,13},{13,11},{18,20},{2... | collective-permute-start | bytes 294920 | tf_op jit(solution)/shard_map/ppermute | solution.py:537
  13.9 5.7 %collective-permute-start.4 = (bf16[2,96,512]{2,1,0:T(8,128)(2,1)S(1)}, bf16[2,96,512]{2,1,0:T(8,128)(2,1)S(1)}, u32[]{:S(2)}, u32[]{:S(2)}) collective-permute-start(bf16[2,96,512]{2,1,0:T(8,128)(2,1)S(1)} %pad_maximum_fusion.3), channel_id=1, source_target_pairs={{0,16},{8,24},{16,0},{24,8},{1,17},{9,25},{17,1},{25,9},{2,18},{10... | collective-permute-start | bytes 589832 | tf_op jit(solution)/shard_map/ppermute | solution.py:552
  15.4 7.6 %collective-permute-start.3 = (bf16[2,224,512]{2,1,0:T(8,128)(2,1)S(1)}, bf16[2,224,512]{2,1,0:T(8,128)(2,1)S(1)}, u32[]{:S(2)}, u32[]{:S(2)}) collective-permute-start(bf16[2,224,512]{2,1,0:T(8,128)(2,1)S(1)} %pad_maximum_fusion.b0), channel_id=1, source_target_pairs={{0,8},{8,0},{16,24},{24,16},{1,9},{9,1},{17,25},{25,17},{2,10},{10... | collective-permute-start | bytes 1376264 | tf_op jit(solution)/shard_map/ppermute | solution.py:554
  20.6 2.4 %collective-permute-start.6 = (bf16[2,224,512]{2,1,0:T(8,128)(2,1)S(1)}, bf16[2,224,512]{2,1,0:T(8,128)(2,1)S(1)}, u32[]{:S(2)}, u32[]{:S(2)}) collective-permute-start(bf16[2,224,512]{2,1,0:T(8,128)(2,1)S(1)} %pad_maximum_fusion.1.b2), channel_id=1, source_target_pairs={{0,8},{8,0},{16,24},{24,16},{1,9},{9,1},{17,25},{25,17},{2,10},{10... | collective-permute-start | bytes 1376264 | tf_op jit(solution)/shard_map/ppermute | solution.py:567
  20.6 6.2 %collective-permute-start.7 = (bf16[688,512]{1,0:T(8,128)(2,1)S(1)}, bf16[688,512]{1,0:T(8,128)(2,1)S(1)}, u32[]{:S(2)}, u32[]{:S(2)}) collective-permute-start(bf16[688,512]{1,0:T(8,128)(2,1)S(1)} %collective-permute-done.5.near_half), channel_id=1, source_target_pairs={{0,8},{8,0},{16,24},{24,16},{1,9},{9,1},{17,25},{25,17},{2,10},{10... | collective-permute-start | bytes 2113544 | tf_op jit(solution)/shard_map/ppermute | solution.py:568
  21.2 6.2 %collective-permute-start.8 = (bf16[160,512]{1,0:T(8,128)(2,1)S(1)}, bf16[160,512]{1,0:T(8,128)(2,1)S(1)}, u32[]{:S(2)}, u32[]{:S(2)}) collective-permute-start(bf16[160,512]{1,0:T(8,128)(2,1)S(1)} %pad_maximum_fusion.4), channel_id=1, source_target_pairs={{0,1},{1,0},{2,3},{3,2},{4,5},{5,4},{6,7},{7,6},{8,9},{9,8},{10,11... | collective-permute-start | bytes 491528 | tf_op jit(solution)/shard_map/ppermute | solution.py:526
  31.5 10.9 %collective-permute-start.9 = (bf16[384,128]{1,0:T(8,128)(2,1)S(1)}, bf16[384,128]{1,0:T(8,128)(2,1)S(1)}, u32[]{:S(2)}, u32[]{:S(2)}) collective-permute-start(bf16[384,128]{1,0:T(8,128)(2,1)S(1)} %get-tuple-element.76), channel_id=1, source_target_pairs={{0,4},{2,6},{4,0},{6,2},{1,5},{3,7},{5,1},{7,3},{8,12},{10,14},{12... | collective-permute-start | bytes 294920 | tf_op jit(solution)/shard_map/ppermute | solution.py:620
  35.3 7.2 %collective-permute-start.10 = (bf16[384,128]{1,0:T(8,128)(2,1)S(1)}, bf16[384,128]{1,0:T(8,128)(2,1)S(1)}, u32[]{:S(2)}, u32[]{:S(2)}) collective-permute-start(bf16[384,128]{1,0:T(8,128)(2,1)S(1)} %get-tuple-element.77), channel_id=1, source_target_pairs={{0,6},{2,4},{4,2},{6,0},{1,7},{3,5},{5,3},{7,1},{8,14},{10,12},{12... | collective-permute-start | bytes 294920 | tf_op jit(solution)/shard_map/ppermute | solution.py:620
  36.2 6.6 %collective-permute-start.11 = (bf16[384,128]{1,0:T(8,128)(2,1)S(1)}, bf16[384,128]{1,0:T(8,128)(2,1)S(1)}, u32[]{:S(2)}, u32[]{:S(2)}) collective-permute-start(bf16[384,128]{1,0:T(8,128)(2,1)S(1)} %get-tuple-element.78), channel_id=1, source_target_pairs={{0,2},{2,0},{4,6},{6,4},{1,3},{3,1},{5,7},{7,5},{8,10},{10,8},{12,... | collective-permute-start | bytes 294920 | tf_op jit(solution)/shard_map/ppermute | solution.py:620

commit v15 on v14

--- a/solution.py
+++ b/solution.py
@@ -617,7 +617,7 @@
         ),
         {5: 0},
     )
-    got = [lax.ppermute(parts[bit - 1], "lat", swap("lat", bit)) for bit in (2, 3, 1)]
+    got = [lax.ppermute(parts[bit - 1], "lat", swap("lat", bit)) for bit in (2, 1, 3)]
     block = (members, lat_rows, lon_cols, channels)
     grad, out = call(
         finish,

time: 43.7 us -> 43.4 us (level)
  waiting for transfers between devices: 9.18 us -> 8.24 us
  starting transfers between devices: 15.5 us -> 16.1 us
    ppermute x3, waiting for transfers between devices: 4.14 us -> 3.19 us  [whole_ring(): lax.ppermute(parts[bit - 1], 'lat', swap('lat', bit))]
    ppermute x3, starting transfers between devices: 4.67 us -> 5.3 us  [whole_ring(): lax.ppermute(parts[bit - 1], 'lat', swap('lat', bit))]
  transfers between devices with their start and end apart: 12 -> 12, of which waited for: 6 -> 7; matrix products, arithmetic and copies ran while one was open for 3% -> 3% of each run, Pallas kernels for 25% -> 25%
where the time goes in v15:
time: 43.4 us; the launch traced here: 43.2 us
  starting transfers between devices  16.1 us (37%)
  Pallas kernels  15.6 us (36%)
  waiting for transfers between devices  8.24 us (19%)
  other arithmetic  1.23 us (3%)
  local copies, waits for them, and re-layouts  1.19 us (3%)
  between operations  0.82 us (2%)
    pallas_call x9, Pallas kernels, call(): pl.pallas_call(body, out_shape=outs, in_specs=[vmem] * len(ins), out_spec...  15.6 us
    ppermute x3, starting transfers between devices, whole_ring(): lax.ppermute(parts[bit - 1], 'lat', swap('lat', bit))  5.3 us
    ppermute x3, waiting for transfers between devices, whole_ring(): lax.ppermute(parts[bit - 1], 'lat', swap('lat', bit))  3.19 us
    ppermute x1, starting transfers between devices, whole_ring(): near_half = lax.ppermute(half, 'segment', swap('segment', 1))  3 us
    ppermute x1, waiting for transfers between devices, whole_ring(): sides_y = lax.ppermute(sides, 'lon', swap('lon', 2))  2.12 us
    ppermute x1, starting transfers between devices, whole_ring(): near_ends = lax.ppermute(ends, 'segment', swap('segment', 1))  1.81 us
    ppermute x1, starting transfers between devices, whole_ring(): from_near = lax.ppermute(toward, 'lat', near_pairs)  1.64 us
    ppermute x1, starting transfers between devices, whole_ring(): both_y = lax.ppermute(both, 'lon', swap('lon', 2))  1.58 us
  transfers between devices with their start and end apart: 12, of which 7 were waited for; matrix products, arithmetic and copies ran while one was open for 3% of the time, Pallas kernels for 25%

profile of v15, /device:TPU:0, one launch (start us, length us, event | category | flops | bytes accessed | tf_op | source)
XLA Modules:
  0.0 43.2 jit_solution(13294367464821527876)
XLA Ops:
  0.6 0.0 copy-start.3
  0.6 0.0 copy-start.2
  0.7 0.0 copy-start.1
  0.7 1.2 %constant_dynamic-slice_fusion = bf16[688,512]{1,0:T(8,128)(2,1)S(1)} fusion(bf16[1536,512]{1,0:T(8,128)(2,1)} %bitcast.7, s32[]{:T(128)S(6)} %select_n.11), kind=kLoop, calls=%fused_computation.5 | loop fusion | bytes 1409028 | tf_op jit(solution)/shard_map/dynamic_slice | solution.py:524
  1.8 3.0 %collective-permute-start.5 = (bf16[688,512]{1,0:T(8,128)(2,1)S(1)}, bf16[688,512]{1,0:T(8,128)(2,1)S(1)}, u32[]{:S(2)}, u32[]{:S(2)}) collective-permute-start(bf16[688,512]{1,0:T(8,128)(2,1)S(1)} %constant_dynamic-slice_fusion), channel_id=1, source_target_pairs={{0,1},{1,0},{2,3},{3,2},{4,5},{5,4},{6,7},{7,6},{8,9},{9,8},{10,11... | collective-permute-start | bytes 2113544 | tf_op jit(solution)/shard_map/ppermute | solution.py:527
  4.8 1.1 %pad_maximum_fusion.2.loaded = bf16[4,16,4,512]{3,2,1,0:T(4,128)(2,1)S(1)} fusion(bf16[2,16,4,512]{3,2,1,0:T(4,128)(2,1)} %param.7, bf16[2,16,4,512]{3,2,1,0:T(4,128)(2,1)} %param.6), kind=kLoop, calls=%fused_computation.2 | loop fusion | flops 131072 | bytes 524288 | tf_op jit(solution)/shard_map/concatenate | solution.py:529
  6.0 1.6 %collective-permute-start.2 = (bf16[2,128,512]{2,1,0:T(8,128)(2,1)S(1)}, bf16[2,128,512]{2,1,0:T(8,128)(2,1)S(1)}, u32[]{:S(2)}, u32[]{:S(2)}) collective-permute-start(bf16[2,128,512]{2,1,0:T(8,128)(2,1)S(1)} %prep.1.both), channel_id=1, source_target_pairs={{0,16},{8,24},{16,0},{24,8},{1,17},{9,25},{17,1},{25,9},{2,18},{10... | collective-permute-start | bytes 786440 | tf_op jit(solution)/shard_map/ppermute | solution.py:533
  7.6 0.0 copy-start
  7.6 1.6 %collective-permute-start = (bf16[2,48,512]{2,1,0:T(8,128)(2,1)S(1)}, bf16[2,48,512]{2,1,0:T(8,128)(2,1)S(1)}, u32[]{:S(2)}, u32[]{:S(2)}) collective-permute-start(bf16[2,48,512]{2,1,0:T(8,128)(2,1)S(1)} %get-tuple-element.43), channel_id=1, source_target_pairs={{0,2},{2,0},{4,6},{6,4},{1,3},{3,1},{5,7},{7,5},{8,10},{10,8},{12,... | collective-permute-start | bytes 294920 | tf_op jit(solution)/shard_map/ppermute | solution.py:536
  9.3 0.7 %collective-permute-start.1 = (bf16[2,48,512]{2,1,0:T(8,128)(2,1)S(1)}, bf16[2,48,512]{2,1,0:T(8,128)(2,1)S(1)}, u32[]{:S(2)}, u32[]{:S(2)}) collective-permute-start(bf16[2,48,512]{2,1,0:T(8,128)(2,1)S(1)} %get-tuple-element.44), channel_id=1, source_target_pairs={{2,4},{4,2},{3,5},{5,3},{10,12},{12,10},{11,13},{13,11},{18,20},{2... | collective-permute-start | bytes 294920 | tf_op jit(solution)/shard_map/ppermute | solution.py:537
  9.9 0.0 copy-done.3
  10.0 0.0 copy-done.2
  10.0 0.0 copy-done.1
  10.0 2.4 %maps_first.1.forward = bf16[4,384,256]{2,1,0:T(8,128)(2,1)S(1)} custom-call(s32[9,64]{1,0:T(8,128)S(1)} %bitcast.14, s32[9,64]{1,0:T(8,128)S(1)} %bitcast.16, f32[9,3,64]{2,1,0:T(4,128)S(1)} %bitcast.12), custom_call_target="tpu_custom_call" | custom-call | tf_op jit(solution)/shard_map/maps_first/pallas_call | solution.py:508
  12.4 0.0 collective-permute-done
  12.4 0.0 collective-permute-done.1
  12.4 1.4 %collective-permute-done.2 = bf16[2,128,512]{2,1,0:T(8,128)(2,1)S(1)} collective-permute-done((bf16[2,128,512]{2,1,0:T(8,128)(2,1)S(1)}, bf16[2,128,512]{2,1,0:T(8,128)(2,1)S(1)}, u32[]{:S(2)}, u32[]{:S(2)}) %collective-permute-start.2) | collective-permute-done | bytes 262176 | tf_op jit(solution)/shard_map/ppermute | solution.py:533
  13.9 1.5 %collective-permute-start.4 = (bf16[2,96,512]{2,1,0:T(8,128)(2,1)S(1)}, bf16[2,96,512]{2,1,0:T(8,128)(2,1)S(1)}, u32[]{:S(2)}, u32[]{:S(2)}) collective-permute-start(bf16[2,96,512]{2,1,0:T(8,128)(2,1)S(1)} %pad_maximum_fusion.3), channel_id=1, source_target_pairs={{0,16},{8,24},{16,0},{24,8},{1,17},{9,25},{17,1},{25,9},{2,18},{10... | collective-permute-start | bytes 589832 | tf_op jit(solution)/shard_map/ppermute | solution.py:552
  15.4 0.1 collective-permute-start.3
  15.5 1.9 %maps_again.1 = (bf16[3,384,256]{2,1,0:T(8,128)(2,1)S(1)}, bf16[3,256,384]{2,1,0:T(8,128)(2,1)S(1)}) custom-call(s32[9,64]{1,0:T(8,128)S(1)} %bitcast.15, s32[9,64]{1,0:T(8,128)S(1)} %bitcast.17, f32[9,3,64]{2,1,0:T(4,128)S(1)} %bitcast.13), custom_call_target="tpu_custom_call" | custom-call | tf_op jit(solution)/shard_map/maps_again/pallas_call | solution.py:508
  17.4 2.1 %collective-permute-done.4 = bf16[2,96,512]{2,1,0:T(8,128)(2,1)S(1)} collective-permute-done((bf16[2,96,512]{2,1,0:T(8,128)(2,1)S(1)}, bf16[2,96,512]{2,1,0:T(8,128)(2,1)S(1)}, u32[]{:S(2)}, u32[]{:S(2)}) %collective-permute-start.4) | collective-permute-done | bytes 196640 | tf_op jit(solution)/shard_map/ppermute | solution.py:552
  19.6 1.1 %collective-permute-done.5.near_half = bf16[688,512]{1,0:T(8,128)(2,1)S(1)} collective-permute-done((bf16[688,512]{1,0:T(8,128)(2,1)S(1)}, bf16[688,512]{1,0:T(8,128)(2,1)S(1)}, u32[]{:S(2)}, u32[]{:S(2)}) %collective-permute-start.5) | collective-permute-done | bytes 704544 | tf_op jit(solution)/shard_map/ppermute | solution.py:527
  20.6 0.0 collective-permute-start.6
  20.6 0.5 %collective-permute-start.7 = (bf16[688,512]{1,0:T(8,128)(2,1)S(1)}, bf16[688,512]{1,0:T(8,128)(2,1)S(1)}, u32[]{:S(2)}, u32[]{:S(2)}) collective-permute-start(bf16[688,512]{1,0:T(8,128)(2,1)S(1)} %collective-permute-done.5.near_half), channel_id=1, source_target_pairs={{0,8},{8,0},{16,24},{24,16},{1,9},{9,1},{17,25},{25,17},{2,10},{10... | collective-permute-start | bytes 2113544 | tf_op jit(solution)/shard_map/ppermute | solution.py:568
  21.1 0.0 copy-done
  21.2 1.8 %collective-permute-start.8 = (bf16[160,512]{1,0:T(8,128)(2,1)S(1)}, bf16[160,512]{1,0:T(8,128)(2,1)S(1)}, u32[]{:S(2)}, u32[]{:S(2)}) collective-permute-start(bf16[160,512]{1,0:T(8,128)(2,1)S(1)} %pad_maximum_fusion.4), channel_id=1, source_target_pairs={{0,1},{1,0},{2,3},{3,2},{4,5},{5,4},{6,7},{7,6},{8,9},{9,8},{10,11... | collective-permute-start | bytes 491528 | tf_op jit(solution)/shard_map/ppermute | solution.py:526
  23.0 0.0 collective-permute-done.3.b1
  23.0 0.0 collective-permute-done.6.b3
  23.0 3.8 %early.1 = (bf16[1024,1536]{1,0:T(8,128)(2,1)S(1)}, bf16[512,384]{1,0:T(8,128)(2,1)S(1)}, bf16[2,4,96,512]{3,2,1,0:T(8,128)(2,1)S(1)}, bf16[2,64,512]{2,1,0:T(8,128)(2,1)S(1)}) custom-call(bf16[2,224,512]{2,1,0:T(8,128)(2,1)S(1)} %pad_maximum_fusion.b0, bf16[2,224,512]{2,1,0:T(8,128)(2,1)S(1)} %collective-permute-done.3.b1, ...), custom_call_target="tpu_custom_call" | custom-call | flops 3000000000 | bytes 3000000 | tf_op jit(solution)/shard_map/early/pallas_call | solution.py:508
  26.8 0.0 collective-permute-done.7.far_half
  26.8 0.1 partial.1
  26.9 0.4 %collective-permute-done.8.ends = bf16[160,512]{1,0:T(8,128)(2,1)S(1)} collective-permute-done((bf16[160,512]{1,0:T(8,128)(2,1)S(1)}, bf16[160,512]{1,0:T(8,128)(2,1)S(1)}, u32[]{:S(2)}, u32[]{:S(2)}) %collective-permute-start.8) | collective-permute-done | bytes 163872 | tf_op jit(solution)/shard_map/ppermute | solution.py:526
  27.3 4.2 %chain.1 = (bf16[1536,512]{1,0:T(8,128)(2,1)S(1)}, bf16[2,64,512]{2,1,0:T(8,128)(2,1)S(1)}, bf16[2,64,512]{2,1,0:T(8,128)(2,1)S(1)}, bf16[768,512]{1,0:T(8,128)(...) custom-call(bf16[2,224,512]{2,1,0:T(8,128)(2,1)S(1)} %pad_maximum_fu, ...), custom_call_target="tpu_custom_call", output_to_operand_aliasing={{0}: (5, {})} | custom-call | flops 6000000000 | bytes 6000000 | tf_op jit(solution)/shard_map/chain/pallas_call | solution.py:508
  31.5 3.8 %collective-permute-start.9 = (bf16[384,128]{1,0:T(8,128)(2,1)S(1)}, bf16[384,128]{1,0:T(8,128)(2,1)S(1)}, u32[]{:S(2)}, u32[]{:S(2)}) collective-permute-start(bf16[384,128]{1,0:T(8,128)(2,1)S(1)} %get-tuple-element.76), channel_id=1, source_target_pairs={{0,4},{2,6},{4,0},{6,2},{1,5},{3,7},{5,1},{7,3},{8,12},{10,14},{12... | collective-permute-start | bytes 294920 | tf_op jit(solution)/shard_map/ppermute | solution.py:620
  35.3 0.7 %collective-permute-start.10 = (bf16[384,128]{1,0:T(8,128)(2,1)S(1)}, bf16[384,128]{1,0:T(8,128)(2,1)S(1)}, u32[]{:S(2)}, u32[]{:S(2)}) collective-permute-start(bf16[384,128]{1,0:T(8,128)(2,1)S(1)} %get-tuple-element.77), channel_id=1, source_target_pairs={{0,2},{2,0},{4,6},{6,4},{1,3},{3,1},{5,7},{7,5},{8,10},{10,8},{12,... | collective-permute-start | bytes 294920 | tf_op jit(solution)/shard_map/ppermute | solution.py:620
  36.0 0.8 %collective-permute-start.11 = (bf16[384,128]{1,0:T(8,128)(2,1)S(1)}, bf16[384,128]{1,0:T(8,128)(2,1)S(1)}, u32[]{:S(2)}, u32[]{:S(2)}) collective-permute-start(bf16[384,128]{1,0:T(8,128)(2,1)S(1)} %get-tuple-element.78), channel_id=1, source_target_pairs={{0,6},{2,4},{4,2},{6,0},{1,7},{3,5},{5,3},{7,1},{8,14},{10,12},{12... | collective-permute-start | bytes 294920 | tf_op jit(solution)/shard_map/ppermute | solution.py:620
  36.8 2.5 %finish.1 = (bf16[2,16,4,512]{3,2,1,0:T(4,128)(2,1)}, bf16[2,16,4,512]{3,2,1,0:T(4,128)(2,1)}) custom-call(bf16[1536,512]{1,0:T(8,128)(2,1)S(1)} %bitcast.11, bf16[3,256,384]{2,1,0:T(8,128)(2,1)S(1)} %get-tuple-element.54.backward, bf16[768,512]{1,0:T(8,128)(2,1)S(1)} %get-tuple-element.70.gates, bf16[2,64,512]{2,1,0:T(8,128)(2,1)S(1)} %get-tuple-element.71.next_ref, ...), custom_call_target="tpu_custom_call" | custom-call | flops 2000000000 | bytes 2000000 | tf_op jit(solution)/shard_map/finish/pallas_call | solution.py:508
  39.3 2.0 %collective-permute-done.9.p1 = bf16[384,128]{1,0:T(8,128)(2,1)S(1)} collective-permute-done((bf16[384,128]{1,0:T(8,128)(2,1)S(1)}, bf16[384,128]{1,0:T(8,128)(2,1)S(1)}, u32[]{:S(2)}, u32[]{:S(2)}) %collective-permute-start.9) | collective-permute-done | bytes 98336 | tf_op jit(solution)/shard_map/ppermute | solution.py:620
  41.2 0.4 collective-permute-done.10.p2
  41.6 0.8 %collective-permute-done.11.p3 = bf16[384,128]{1,0:T(8,128)(2,1)S(1)} collective-permute-done((bf16[384,128]{1,0:T(8,128)(2,1)S(1)}, bf16[384,128]{1,0:T(8,128)(2,1)S(1)}, u32[]{:S(2)}, u32[]{:S(2)}) %collective-permute-start.11) | collective-permute-done | bytes 98336 | tf_op jit(solution)/shard_map/ppermute | solution.py:620
  42.5 0.7 %add_up.1 = f32[384,128]{1,0:T(8,128)} custom-call(f32[384,128]{1,0:T(8,128)S(1)} %get-tuple-element.75.mine, bf16[384,128]{1,0:T(8,128)(2,1)S(1)} %collective-permute-done.9.p1, bf16[384,128]{1,0:T(8,128)(2,1)S(1)} %collective-permute-done.10.p2, bf16[384,128]{1,0:T(8,128)(2,1)S(1)} %collective-permute-done.11.p3), custom_call_target="tpu_custom_call" | custom-call | flops 100000000 | bytes 100000 | tf_op jit(solution)/shard_map/add_up/pallas_call | solution.py:508
  (7 shorter events, 0.1 us)
Async XLA Ops:
  0.6 9.3 %copy-start.3 = (s32[64,9]{0,1:T(8,128)S(1)}, s32[64,9]{0,1:T(8,128)}, u32[]{:S(2)}) copy-start(s32[64,9]{0,1:T(8,128)} %param.11) | copy-start | bytes 6916
  0.6 9.3 %copy-start.2 = (s32[64,9]{0,1:T(8,128)S(1)}, s32[64,9]{0,1:T(8,128)}, u32[]{:S(2)}) copy-start(s32[64,9]{0,1:T(8,128)} %param.10) | copy-start | bytes 6916
  0.7 9.3 %copy-start.1 = (f32[64,9,3]{0,2,1:T(4,128)S(1)}, f32[64,9,3]{0,2,1:T(4,128)}, u32[]{:S(2)}) copy-start(f32[64,9,3]{0,2,1:T(4,128)} %param.9) | copy-start | bytes 20740
  1.8 18.8 %collective-permute-start.5 = (bf16[688,512]{1,0:T(8,128)(2,1)S(1)}, bf16[688,512]{1,0:T(8,128)(2,1)S(1)}, u32[]{:S(2)}, u32[]{:S(2)}) collective-permute-start(bf16[688,512]{1,0:T(8,128)(2,1)S(1)} %constant_dynamic-slice_fusion), channel_id=1, source_target_pairs={{0,1},{1,0},{2,3},{3,2},{4,5},{5,4},{6,7},{7,6},{8,9},{9,8},{10,11... | collective-permute-start | bytes 2113544 | tf_op jit(solution)/shard_map/ppermute | solution.py:527
  6.0 7.8 %collective-permute-start.2 = (bf16[2,128,512]{2,1,0:T(8,128)(2,1)S(1)}, bf16[2,128,512]{2,1,0:T(8,128)(2,1)S(1)}, u32[]{:S(2)}, u32[]{:S(2)}) collective-permute-start(bf16[2,128,512]{2,1,0:T(8,128)(2,1)S(1)} %prep.1.both), channel_id=1, source_target_pairs={{0,16},{8,24},{16,0},{24,8},{1,17},{9,25},{17,1},{25,9},{2,18},{10... | collective-permute-start | bytes 786440 | tf_op jit(solution)/shard_map/ppermute | solution.py:533
  7.6 13.5 %copy-start = (bf16[1,3,512,512]{3,2,1,0:T(8,128)(2,1)S(1)}, bf16[1,3,512,512]{3,2,1,0:T(8,128)(2,1)}, u32[]{:S(2)}) copy-start(bf16[1,3,512,512]{3,2,1,0:T(8,128)(2,1)} %param.8) | copy-start | bytes 4718596
  7.6 4.8 %collective-permute-start = (bf16[2,48,512]{2,1,0:T(8,128)(2,1)S(1)}, bf16[2,48,512]{2,1,0:T(8,128)(2,1)S(1)}, u32[]{:S(2)}, u32[]{:S(2)}) collective-permute-start(bf16[2,48,512]{2,1,0:T(8,128)(2,1)S(1)} %get-tuple-element.43), channel_id=1, source_target_pairs={{0,2},{2,0},{4,6},{6,4},{1,3},{3,1},{5,7},{7,5},{8,10},{10,8},{12,... | collective-permute-start | bytes 294920 | tf_op jit(solution)/shard_map/ppermute | solution.py:536
  9.3 3.1 %collective-permute-start.1 = (bf16[2,48,512]{2,1,0:T(8,128)(2,1)S(1)}, bf16[2,48,512]{2,1,0:T(8,128)(2,1)S(1)}, u32[]{:S(2)}, u32[]{:S(2)}) collective-permute-start(bf16[2,48,512]{2,1,0:T(8,128)(2,1)S(1)} %get-tuple-element.44), channel_id=1, source_target_pairs={{2,4},{4,2},{3,5},{5,3},{10,12},{12,10},{11,13},{13,11},{18,20},{2... | collective-permute-start | bytes 294920 | tf_op jit(solution)/shard_map/ppermute | solution.py:537
  13.9 5.7 %collective-permute-start.4 = (bf16[2,96,512]{2,1,0:T(8,128)(2,1)S(1)}, bf16[2,96,512]{2,1,0:T(8,128)(2,1)S(1)}, u32[]{:S(2)}, u32[]{:S(2)}) collective-permute-start(bf16[2,96,512]{2,1,0:T(8,128)(2,1)S(1)} %pad_maximum_fusion.3), channel_id=1, source_target_pairs={{0,16},{8,24},{16,0},{24,8},{1,17},{9,25},{17,1},{25,9},{2,18},{10... | collective-permute-start | bytes 589832 | tf_op jit(solution)/shard_map/ppermute | solution.py:552
  15.4 7.6 %collective-permute-start.3 = (bf16[2,224,512]{2,1,0:T(8,128)(2,1)S(1)}, bf16[2,224,512]{2,1,0:T(8,128)(2,1)S(1)}, u32[]{:S(2)}, u32[]{:S(2)}) collective-permute-start(bf16[2,224,512]{2,1,0:T(8,128)(2,1)S(1)} %pad_maximum_fusion.b0), channel_id=1, source_target_pairs={{0,8},{8,0},{16,24},{24,16},{1,9},{9,1},{17,25},{25,17},{2,10},{10... | collective-permute-start | bytes 1376264 | tf_op jit(solution)/shard_map/ppermute | solution.py:554
  20.6 2.4 %collective-permute-start.6 = (bf16[2,224,512]{2,1,0:T(8,128)(2,1)S(1)}, bf16[2,224,512]{2,1,0:T(8,128)(2,1)S(1)}, u32[]{:S(2)}, u32[]{:S(2)}) collective-permute-start(bf16[2,224,512]{2,1,0:T(8,128)(2,1)S(1)} %pad_maximum_fusion.1.b2), channel_id=1, source_target_pairs={{0,8},{8,0},{16,24},{24,16},{1,9},{9,1},{17,25},{25,17},{2,10},{10... | collective-permute-start | bytes 1376264 | tf_op jit(solution)/shard_map/ppermute | solution.py:567
  20.6 6.2 %collective-permute-start.7 = (bf16[688,512]{1,0:T(8,128)(2,1)S(1)}, bf16[688,512]{1,0:T(8,128)(2,1)S(1)}, u32[]{:S(2)}, u32[]{:S(2)}) collective-permute-start(bf16[688,512]{1,0:T(8,128)(2,1)S(1)} %collective-permute-done.5.near_half), channel_id=1, source_target_pairs={{0,8},{8,0},{16,24},{24,16},{1,9},{9,1},{17,25},{25,17},{2,10},{10... | collective-permute-start | bytes 2113544 | tf_op jit(solution)/shard_map/ppermute | solution.py:568
  21.2 6.2 %collective-permute-start.8 = (bf16[160,512]{1,0:T(8,128)(2,1)S(1)}, bf16[160,512]{1,0:T(8,128)(2,1)S(1)}, u32[]{:S(2)}, u32[]{:S(2)}) collective-permute-start(bf16[160,512]{1,0:T(8,128)(2,1)S(1)} %pad_maximum_fusion.4), channel_id=1, source_target_pairs={{0,1},{1,0},{2,3},{3,2},{4,5},{5,4},{6,7},{7,6},{8,9},{9,8},{10,11... | collective-permute-start | bytes 491528 | tf_op jit(solution)/shard_map/ppermute | solution.py:526
  31.5 9.7 %collective-permute-start.9 = (bf16[384,128]{1,0:T(8,128)(2,1)S(1)}, bf16[384,128]{1,0:T(8,128)(2,1)S(1)}, u32[]{:S(2)}, u32[]{:S(2)}) collective-permute-start(bf16[384,128]{1,0:T(8,128)(2,1)S(1)} %get-tuple-element.76), channel_id=1, source_target_pairs={{0,4},{2,6},{4,0},{6,2},{1,5},{3,7},{5,1},{7,3},{8,12},{10,14},{12... | collective-permute-start | bytes 294920 | tf_op jit(solution)/shard_map/ppermute | solution.py:620
  35.3 6.4 %collective-permute-start.10 = (bf16[384,128]{1,0:T(8,128)(2,1)S(1)}, bf16[384,128]{1,0:T(8,128)(2,1)S(1)}, u32[]{:S(2)}, u32[]{:S(2)}) collective-permute-start(bf16[384,128]{1,0:T(8,128)(2,1)S(1)} %get-tuple-element.77), channel_id=1, source_target_pairs={{0,2},{2,0},{4,6},{6,4},{1,3},{3,1},{5,7},{7,5},{8,10},{10,8},{12,... | collective-permute-start | bytes 294920 | tf_op jit(solution)/shard_map/ppermute | solution.py:620
  36.0 6.5 %collective-permute-start.11 = (bf16[384,128]{1,0:T(8,128)(2,1)S(1)}, bf16[384,128]{1,0:T(8,128)(2,1)S(1)}, u32[]{:S(2)}, u32[]{:S(2)}) collective-permute-start(bf16[384,128]{1,0:T(8,128)(2,1)S(1)} %get-tuple-element.78), channel_id=1, source_target_pairs={{0,6},{2,4},{4,2},{6,0},{1,7},{3,5},{5,3},{7,1},{8,14},{10,12},{12... | collective-permute-start | bytes 294920 | tf_op jit(solution)/shard_map/ppermute | solution.py:620

commit v16 on v15

--- a/solution.py
+++ b/solution.py
@@ -519,7 +519,7 @@
 
     prep, edges, maps, early, partial, chain, finish = make_steps(lat_rows, lon_cols, blocks, members, channels, lat_devices)
     kernel = weights.reshape(width, channels)
-    rest = width // 2 * 5 // 48
+    rest = width // 2 // 12
     rows = width // 2 - rest
     half = lax.dynamic_slice_in_dim(kernel, lax.axis_index("lon") % 2 * (width // 2), rows, 0)
     ends = jnp.concatenate([kernel[rows : rows + rest], kernel[width - rest :]], axis=0)

time: 43.4 us -> 43.2 us (level)
  starting transfers between devices: 16.1 us -> 15.4 us
  waiting for transfers between devices: 8.24 us -> 8.68 us
    ppermute x3, starting transfers between devices: 5.3 us -> 4.63 us  [whole_ring(): lax.ppermute(parts[bit - 1], 'lat', swap('lat', bit))]
    ppermute x3, waiting for transfers between devices: 3.19 us -> 3.72 us  [whole_ring(): lax.ppermute(parts[bit - 1], 'lat', swap('lat', bit))]
  transfers between devices with their start and end apart: 12 -> 12, of which waited for: 7 -> 4; matrix products, arithmetic and copies ran while one was open for 3% -> 3% of each run, Pallas kernels for 25% -> 25%
where the time goes in v16:
time: 43.2 us; the launch traced here: 43 us
  Pallas kernels  15.7 us (36%)
  starting transfers between devices  15.4 us (36%)
  waiting for transfers between devices  8.68 us (20%)
  other arithmetic  1.23 us (3%)
  local copies, waits for them, and re-layouts  1.19 us (3%)
  between operations  0.83 us (2%)
    pallas_call x9, Pallas kernels, call(): pl.pallas_call(body, out_shape=outs, in_specs=[vmem] * len(ins), out_spec...  15.7 us
    ppermute x3, starting transfers between devices, whole_ring(): lax.ppermute(parts[bit - 1], 'lat', swap('lat', bit))  4.63 us
    ppermute x3, waiting for transfers between devices, whole_ring(): lax.ppermute(parts[bit - 1], 'lat', swap('lat', bit))  3.72 us
    ppermute x1, starting transfers between devices, whole_ring(): near_half = lax.ppermute(half, 'segment', swap('segment', 1))  3 us
    ppermute x1, waiting for transfers between devices, whole_ring(): sides_y = lax.ppermute(sides, 'lon', swap('lon', 2))  2.12 us
    ppermute x1, starting transfers between devices, whole_ring(): near_ends = lax.ppermute(ends, 'segment', swap('segment', 1))  1.81 us
    ppermute x1, starting transfers between devices, whole_ring(): from_near = lax.ppermute(toward, 'lat', near_pairs)  1.64 us
    ppermute x1, starting transfers between devices, whole_ring(): both_y = lax.ppermute(both, 'lon', swap('lon', 2))  1.58 us
  transfers between devices with their start and end apart: 12, of which 4 were waited for; matrix products, arithmetic and copies ran while one was open for 3% of the time, Pallas kernels for 25%

profile of v16, /device:TPU:0, one launch (start us, length us, event | category | flops | bytes accessed | tf_op | source)
XLA Modules:
  0.0 43.0 jit_solution(10313579799888783707)
XLA Ops:
  0.6 0.0 copy-start.3
  0.6 0.0 copy-start.2
  0.7 0.0 copy-start.1
  0.7 1.2 %constant_dynamic-slice_fusion = bf16[704,512]{1,0:T(8,128)(2,1)S(1)} fusion(bf16[1536,512]{1,0:T(8,128)(2,1)} %bitcast.7, s32[]{:T(128)S(6)} %select_n.11), kind=kLoop, calls=%fused_computation.5 | loop fusion | bytes 1441796 | tf_op jit(solution)/shard_map/dynamic_slice | solution.py:524
  1.8 3.0 %collective-permute-start.5 = (bf16[704,512]{1,0:T(8,128)(2,1)S(1)}, bf16[704,512]{1,0:T(8,128)(2,1)S(1)}, u32[]{:S(2)}, u32[]{:S(2)}) collective-permute-start(bf16[704,512]{1,0:T(8,128)(2,1)S(1)} %constant_dynamic-slice_fusion), channel_id=1, source_target_pairs={{0,1},{1,0},{2,3},{3,2},{4,5},{5,4},{6,7},{7,6},{8,9},{9,8},{10,11... | collective-permute-start | bytes 2162696 | tf_op jit(solution)/shard_map/ppermute | solution.py:527
  4.8 1.1 %pad_maximum_fusion.2.loaded = bf16[4,16,4,512]{3,2,1,0:T(4,128)(2,1)S(1)} fusion(bf16[2,16,4,512]{3,2,1,0:T(4,128)(2,1)} %param.7, bf16[2,16,4,512]{3,2,1,0:T(4,128)(2,1)} %param.6), kind=kLoop, calls=%fused_computation.2 | loop fusion | flops 131072 | bytes 524288 | tf_op jit(solution)/shard_map/concatenate | solution.py:529
  6.0 1.6 %collective-permute-start.2 = (bf16[2,128,512]{2,1,0:T(8,128)(2,1)S(1)}, bf16[2,128,512]{2,1,0:T(8,128)(2,1)S(1)}, u32[]{:S(2)}, u32[]{:S(2)}) collective-permute-start(bf16[2,128,512]{2,1,0:T(8,128)(2,1)S(1)} %prep.1.both), channel_id=1, source_target_pairs={{0,16},{8,24},{16,0},{24,8},{1,17},{9,25},{17,1},{25,9},{2,18},{10... | collective-permute-start | bytes 786440 | tf_op jit(solution)/shard_map/ppermute | solution.py:533
  7.6 0.0 copy-start
  7.6 1.6 %collective-permute-start = (bf16[2,48,512]{2,1,0:T(8,128)(2,1)S(1)}, bf16[2,48,512]{2,1,0:T(8,128)(2,1)S(1)}, u32[]{:S(2)}, u32[]{:S(2)}) collective-permute-start(bf16[2,48,512]{2,1,0:T(8,128)(2,1)S(1)} %get-tuple-element.43), channel_id=1, source_target_pairs={{0,2},{2,0},{4,6},{6,4},{1,3},{3,1},{5,7},{7,5},{8,10},{10,8},{12,... | collective-permute-start | bytes 294920 | tf_op jit(solution)/shard_map/ppermute | solution.py:536
  9.3 0.7 %collective-permute-start.1 = (bf16[2,48,512]{2,1,0:T(8,128)(2,1)S(1)}, bf16[2,48,512]{2,1,0:T(8,128)(2,1)S(1)}, u32[]{:S(2)}, u32[]{:S(2)}) collective-permute-start(bf16[2,48,512]{2,1,0:T(8,128)(2,1)S(1)} %get-tuple-element.44), channel_id=1, source_target_pairs={{2,4},{4,2},{3,5},{5,3},{10,12},{12,10},{11,13},{13,11},{18,20},{2... | collective-permute-start | bytes 294920 | tf_op jit(solution)/shard_map/ppermute | solution.py:537
  9.9 0.0 copy-done.3
  10.0 0.0 copy-done.2
  10.0 0.0 copy-done.1
  10.0 2.4 %maps_first.1.forward = bf16[4,384,256]{2,1,0:T(8,128)(2,1)S(1)} custom-call(s32[9,64]{1,0:T(8,128)S(1)} %bitcast.14, s32[9,64]{1,0:T(8,128)S(1)} %bitcast.16, f32[9,3,64]{2,1,0:T(4,128)S(1)} %bitcast.12), custom_call_target="tpu_custom_call" | custom-call | tf_op jit(solution)/shard_map/maps_first/pallas_call | solution.py:508
  12.4 0.0 collective-permute-done
  12.4 0.0 collective-permute-done.1
  12.4 1.4 %collective-permute-done.2 = bf16[2,128,512]{2,1,0:T(8,128)(2,1)S(1)} collective-permute-done((bf16[2,128,512]{2,1,0:T(8,128)(2,1)S(1)}, bf16[2,128,512]{2,1,0:T(8,128)(2,1)S(1)}, u32[]{:S(2)}, u32[]{:S(2)}) %collective-permute-start.2) | collective-permute-done | bytes 262176 | tf_op jit(solution)/shard_map/ppermute | solution.py:533
  13.9 1.5 %collective-permute-start.4 = (bf16[2,96,512]{2,1,0:T(8,128)(2,1)S(1)}, bf16[2,96,512]{2,1,0:T(8,128)(2,1)S(1)}, u32[]{:S(2)}, u32[]{:S(2)}) collective-permute-start(bf16[2,96,512]{2,1,0:T(8,128)(2,1)S(1)} %pad_maximum_fusion.3), channel_id=1, source_target_pairs={{0,16},{8,24},{16,0},{24,8},{1,17},{9,25},{17,1},{25,9},{2,18},{10... | collective-permute-start | bytes 589832 | tf_op jit(solution)/shard_map/ppermute | solution.py:552
  15.4 0.1 collective-permute-start.3
  15.5 1.9 %maps_again.1 = (bf16[3,384,256]{2,1,0:T(8,128)(2,1)S(1)}, bf16[3,256,384]{2,1,0:T(8,128)(2,1)S(1)}) custom-call(s32[9,64]{1,0:T(8,128)S(1)} %bitcast.15, s32[9,64]{1,0:T(8,128)S(1)} %bitcast.17, f32[9,3,64]{2,1,0:T(4,128)S(1)} %bitcast.13), custom_call_target="tpu_custom_call" | custom-call | tf_op jit(solution)/shard_map/maps_again/pallas_call | solution.py:508
  17.4 2.1 %collective-permute-done.4 = bf16[2,96,512]{2,1,0:T(8,128)(2,1)S(1)} collective-permute-done((bf16[2,96,512]{2,1,0:T(8,128)(2,1)S(1)}, bf16[2,96,512]{2,1,0:T(8,128)(2,1)S(1)}, u32[]{:S(2)}, u32[]{:S(2)}) %collective-permute-start.4) | collective-permute-done | bytes 196640 | tf_op jit(solution)/shard_map/ppermute | solution.py:552
  19.6 1.4 %collective-permute-done.5.near_half = bf16[704,512]{1,0:T(8,128)(2,1)S(1)} collective-permute-done((bf16[704,512]{1,0:T(8,128)(2,1)S(1)}, bf16[704,512]{1,0:T(8,128)(2,1)S(1)}, u32[]{:S(2)}, u32[]{:S(2)}) %collective-permute-start.5) | collective-permute-done | bytes 720928 | tf_op jit(solution)/shard_map/ppermute | solution.py:527
  21.0 0.0 collective-permute-start.6
  21.0 0.5 %collective-permute-start.7 = (bf16[704,512]{1,0:T(8,128)(2,1)S(1)}, bf16[704,512]{1,0:T(8,128)(2,1)S(1)}, u32[]{:S(2)}, u32[]{:S(2)}) collective-permute-start(bf16[704,512]{1,0:T(8,128)(2,1)S(1)} %collective-permute-done.5.near_half), channel_id=1, source_target_pairs={{0,8},{8,0},{16,24},{24,16},{1,9},{9,1},{17,25},{25,17},{2,10},{10... | collective-permute-start | bytes 2162696 | tf_op jit(solution)/shard_map/ppermute | solution.py:568
  21.5 0.0 copy-done
  21.5 1.8 %collective-permute-start.8 = (bf16[128,512]{1,0:T(8,128)(2,1)S(1)}, bf16[128,512]{1,0:T(8,128)(2,1)S(1)}, u32[]{:S(2)}, u32[]{:S(2)}) collective-permute-start(bf16[128,512]{1,0:T(8,128)(2,1)S(1)} %pad_maximum_fusion.4), channel_id=1, source_target_pairs={{0,1},{1,0},{2,3},{3,2},{4,5},{5,4},{6,7},{7,6},{8,9},{9,8},{10,11... | collective-permute-start | bytes 393224 | tf_op jit(solution)/shard_map/ppermute | solution.py:526
  23.3 0.0 collective-permute-done.3.b1
  23.3 0.0 collective-permute-done.6.b3
  23.3 3.8 %early.1 = (bf16[1024,1536]{1,0:T(8,128)(2,1)S(1)}, bf16[512,384]{1,0:T(8,128)(2,1)S(1)}, bf16[2,4,96,512]{3,2,1,0:T(8,128)(2,1)S(1)}, bf16[2,64,512]{2,1,0:T(8,128)(2,1)S(1)}) custom-call(bf16[2,224,512]{2,1,0:T(8,128)(2,1)S(1)} %pad_maximum_fusion.b0, bf16[2,224,512]{2,1,0:T(8,128)(2,1)S(1)} %collective-permute-done.3.b1, ...), custom_call_target="tpu_custom_call" | custom-call | flops 3000000000 | bytes 3000000 | tf_op jit(solution)/shard_map/early/pallas_call | solution.py:508
  27.2 0.0 collective-permute-done.7.far_half
  27.2 0.1 partial.1
  27.3 0.0 collective-permute-done.8.ends
  27.3 4.2 %chain.1 = (bf16[1536,512]{1,0:T(8,128)(2,1)S(1)}, bf16[2,64,512]{2,1,0:T(8,128)(2,1)S(1)}, bf16[2,64,512]{2,1,0:T(8,128)(2,1)S(1)}, bf16[768,512]{1,0:T(8,128)(...) custom-call(bf16[2,224,512]{2,1,0:T(8,128)(2,1)S(1)} %pad_maximum_fu, ...), custom_call_target="tpu_custom_call", output_to_operand_aliasing={{0}: (5, {})} | custom-call | flops 6000000000 | bytes 6000000 | tf_op jit(solution)/shard_map/chain/pallas_call | solution.py:508
  31.5 3.1 %collective-permute-start.9 = (bf16[384,128]{1,0:T(8,128)(2,1)S(1)}, bf16[384,128]{1,0:T(8,128)(2,1)S(1)}, u32[]{:S(2)}, u32[]{:S(2)}) collective-permute-start(bf16[384,128]{1,0:T(8,128)(2,1)S(1)} %get-tuple-element.76), channel_id=1, source_target_pairs={{0,4},{2,6},{4,0},{6,2},{1,5},{3,7},{5,1},{7,3},{8,12},{10,14},{12... | collective-permute-start | bytes 294920 | tf_op jit(solution)/shard_map/ppermute | solution.py:620
  34.6 1.1 %collective-permute-start.10 = (bf16[384,128]{1,0:T(8,128)(2,1)S(1)}, bf16[384,128]{1,0:T(8,128)(2,1)S(1)}, u32[]{:S(2)}, u32[]{:S(2)}) collective-permute-start(bf16[384,128]{1,0:T(8,128)(2,1)S(1)} %get-tuple-element.77), channel_id=1, source_target_pairs={{0,2},{2,0},{4,6},{6,4},{1,3},{3,1},{5,7},{7,5},{8,10},{10,8},{12,... | collective-permute-start | bytes 294920 | tf_op jit(solution)/shard_map/ppermute | solution.py:620
  35.7 0.4 collective-permute-start.11
  36.1 2.5 %finish.1 = (bf16[2,16,4,512]{3,2,1,0:T(4,128)(2,1)}, bf16[2,16,4,512]{3,2,1,0:T(4,128)(2,1)}) custom-call(bf16[1536,512]{1,0:T(8,128)(2,1)S(1)} %bitcast.11, bf16[3,256,384]{2,1,0:T(8,128)(2,1)S(1)} %get-tuple-element.54.backward, bf16[768,512]{1,0:T(8,128)(2,1)S(1)} %get-tuple-element.70.gates, bf16[2,64,512]{2,1,0:T(8,128)(2,1)S(1)} %get-tuple-element.71.next_ref, ...), custom_call_target="tpu_custom_call" | custom-call | flops 2000000000 | bytes 2000000 | tf_op jit(solution)/shard_map/finish/pallas_call | solution.py:508
  38.6 3.7 %collective-permute-done.9.p1 = bf16[384,128]{1,0:T(8,128)(2,1)S(1)} collective-permute-done((bf16[384,128]{1,0:T(8,128)(2,1)S(1)}, bf16[384,128]{1,0:T(8,128)(2,1)S(1)}, u32[]{:S(2)}, u32[]{:S(2)}) %collective-permute-start.9) | collective-permute-done | bytes 98336 | tf_op jit(solution)/shard_map/ppermute | solution.py:620
  42.3 0.0 collective-permute-done.10.p2
  42.3 0.0 collective-permute-done.11.p3
  42.3 0.7 %add_up.1 = f32[384,128]{1,0:T(8,128)} custom-call(f32[384,128]{1,0:T(8,128)S(1)} %get-tuple-element.75.mine, bf16[384,128]{1,0:T(8,128)(2,1)S(1)} %collective-permute-done.9.p1, bf16[384,128]{1,0:T(8,128)(2,1)S(1)} %collective-permute-done.10.p2, bf16[384,128]{1,0:T(8,128)(2,1)S(1)} %collective-permute-done.11.p3), custom_call_target="tpu_custom_call" | custom-call | flops 100000000 | bytes 100000 | tf_op jit(solution)/shard_map/add_up/pallas_call | solution.py:508
  (7 shorter events, 0.1 us)
Async XLA Ops:
  0.6 9.3 %copy-start.3 = (s32[64,9]{0,1:T(8,128)S(1)}, s32[64,9]{0,1:T(8,128)}, u32[]{:S(2)}) copy-start(s32[64,9]{0,1:T(8,128)} %param.11) | copy-start | bytes 6916
  0.6 9.3 %copy-start.2 = (s32[64,9]{0,1:T(8,128)S(1)}, s32[64,9]{0,1:T(8,128)}, u32[]{:S(2)}) copy-start(s32[64,9]{0,1:T(8,128)} %param.10) | copy-start | bytes 6916
  0.7 9.3 %copy-start.1 = (f32[64,9,3]{0,2,1:T(4,128)S(1)}, f32[64,9,3]{0,2,1:T(4,128)}, u32[]{:S(2)}) copy-start(f32[64,9,3]{0,2,1:T(4,128)} %param.9) | copy-start | bytes 20740
  1.8 19.1 %collective-permute-start.5 = (bf16[704,512]{1,0:T(8,128)(2,1)S(1)}, bf16[704,512]{1,0:T(8,128)(2,1)S(1)}, u32[]{:S(2)}, u32[]{:S(2)}) collective-permute-start(bf16[704,512]{1,0:T(8,128)(2,1)S(1)} %constant_dynamic-slice_fusion), channel_id=1, source_target_pairs={{0,1},{1,0},{2,3},{3,2},{4,5},{5,4},{6,7},{7,6},{8,9},{9,8},{10,11... | collective-permute-start | bytes 2162696 | tf_op jit(solution)/shard_map/ppermute | solution.py:527
  6.0 7.8 %collective-permute-start.2 = (bf16[2,128,512]{2,1,0:T(8,128)(2,1)S(1)}, bf16[2,128,512]{2,1,0:T(8,128)(2,1)S(1)}, u32[]{:S(2)}, u32[]{:S(2)}) collective-permute-start(bf16[2,128,512]{2,1,0:T(8,128)(2,1)S(1)} %prep.1.both), channel_id=1, source_target_pairs={{0,16},{8,24},{16,0},{24,8},{1,17},{9,25},{17,1},{25,9},{2,18},{10... | collective-permute-start | bytes 786440 | tf_op jit(solution)/shard_map/ppermute | solution.py:533
  7.6 13.9 %copy-start = (bf16[1,3,512,512]{3,2,1,0:T(8,128)(2,1)S(1)}, bf16[1,3,512,512]{3,2,1,0:T(8,128)(2,1)}, u32[]{:S(2)}) copy-start(bf16[1,3,512,512]{3,2,1,0:T(8,128)(2,1)} %param.8) | copy-start | bytes 4718596
  7.6 4.8 %collective-permute-start = (bf16[2,48,512]{2,1,0:T(8,128)(2,1)S(1)}, bf16[2,48,512]{2,1,0:T(8,128)(2,1)S(1)}, u32[]{:S(2)}, u32[]{:S(2)}) collective-permute-start(bf16[2,48,512]{2,1,0:T(8,128)(2,1)S(1)} %get-tuple-element.43), channel_id=1, source_target_pairs={{0,2},{2,0},{4,6},{6,4},{1,3},{3,1},{5,7},{7,5},{8,10},{10,8},{12,... | collective-permute-start | bytes 294920 | tf_op jit(solution)/shard_map/ppermute | solution.py:536
  9.3 3.1 %collective-permute-start.1 = (bf16[2,48,512]{2,1,0:T(8,128)(2,1)S(1)}, bf16[2,48,512]{2,1,0:T(8,128)(2,1)S(1)}, u32[]{:S(2)}, u32[]{:S(2)}) collective-permute-start(bf16[2,48,512]{2,1,0:T(8,128)(2,1)S(1)} %get-tuple-element.44), channel_id=1, source_target_pairs={{2,4},{4,2},{3,5},{5,3},{10,12},{12,10},{11,13},{13,11},{18,20},{2... | collective-permute-start | bytes 294920 | tf_op jit(solution)/shard_map/ppermute | solution.py:537
  13.9 5.7 %collective-permute-start.4 = (bf16[2,96,512]{2,1,0:T(8,128)(2,1)S(1)}, bf16[2,96,512]{2,1,0:T(8,128)(2,1)S(1)}, u32[]{:S(2)}, u32[]{:S(2)}) collective-permute-start(bf16[2,96,512]{2,1,0:T(8,128)(2,1)S(1)} %pad_maximum_fusion.3), channel_id=1, source_target_pairs={{0,16},{8,24},{16,0},{24,8},{1,17},{9,25},{17,1},{25,9},{2,18},{10... | collective-permute-start | bytes 589832 | tf_op jit(solution)/shard_map/ppermute | solution.py:552
  15.4 7.9 %collective-permute-start.3 = (bf16[2,224,512]{2,1,0:T(8,128)(2,1)S(1)}, bf16[2,224,512]{2,1,0:T(8,128)(2,1)S(1)}, u32[]{:S(2)}, u32[]{:S(2)}) collective-permute-start(bf16[2,224,512]{2,1,0:T(8,128)(2,1)S(1)} %pad_maximum_fusion.b0), channel_id=1, source_target_pairs={{0,8},{8,0},{16,24},{24,16},{1,9},{9,1},{17,25},{25,17},{2,10},{10... | collective-permute-start | bytes 1376264 | tf_op jit(solution)/shard_map/ppermute | solution.py:554
  21.0 2.4 %collective-permute-start.6 = (bf16[2,224,512]{2,1,0:T(8,128)(2,1)S(1)}, bf16[2,224,512]{2,1,0:T(8,128)(2,1)S(1)}, u32[]{:S(2)}, u32[]{:S(2)}) collective-permute-start(bf16[2,224,512]{2,1,0:T(8,128)(2,1)S(1)} %pad_maximum_fusion.1.b2), channel_id=1, source_target_pairs={{0,8},{8,0},{16,24},{24,16},{1,9},{9,1},{17,25},{25,17},{2,10},{10... | collective-permute-start | bytes 1376264 | tf_op jit(solution)/shard_map/ppermute | solution.py:567
  21.0 6.2 %collective-permute-start.7 = (bf16[704,512]{1,0:T(8,128)(2,1)S(1)}, bf16[704,512]{1,0:T(8,128)(2,1)S(1)}, u32[]{:S(2)}, u32[]{:S(2)}) collective-permute-start(bf16[704,512]{1,0:T(8,128)(2,1)S(1)} %collective-permute-done.5.near_half), channel_id=1, source_target_pairs={{0,8},{8,0},{16,24},{24,16},{1,9},{9,1},{17,25},{25,17},{2,10},{10... | collective-permute-start | bytes 2162696 | tf_op jit(solution)/shard_map/ppermute | solution.py:568
  21.5 5.8 %collective-permute-start.8 = (bf16[128,512]{1,0:T(8,128)(2,1)S(1)}, bf16[128,512]{1,0:T(8,128)(2,1)S(1)}, u32[]{:S(2)}, u32[]{:S(2)}) collective-permute-start(bf16[128,512]{1,0:T(8,128)(2,1)S(1)} %pad_maximum_fusion.4), channel_id=1, source_target_pairs={{0,1},{1,0},{2,3},{3,2},{4,5},{5,4},{6,7},{7,6},{8,9},{9,8},{10,11... | collective-permute-start | bytes 393224 | tf_op jit(solution)/shard_map/ppermute | solution.py:526
  31.5 10.8 %collective-permute-start.9 = (bf16[384,128]{1,0:T(8,128)(2,1)S(1)}, bf16[384,128]{1,0:T(8,128)(2,1)S(1)}, u32[]{:S(2)}, u32[]{:S(2)}) collective-permute-start(bf16[384,128]{1,0:T(8,128)(2,1)S(1)} %get-tuple-element.76), channel_id=1, source_target_pairs={{0,4},{2,6},{4,0},{6,2},{1,5},{3,7},{5,1},{7,3},{8,12},{10,14},{12... | collective-permute-start | bytes 294920 | tf_op jit(solution)/shard_map/ppermute | solution.py:620
  34.6 7.7 %collective-permute-start.10 = (bf16[384,128]{1,0:T(8,128)(2,1)S(1)}, bf16[384,128]{1,0:T(8,128)(2,1)S(1)}, u32[]{:S(2)}, u32[]{:S(2)}) collective-permute-start(bf16[384,128]{1,0:T(8,128)(2,1)S(1)} %get-tuple-element.77), channel_id=1, source_target_pairs={{0,2},{2,0},{4,6},{6,4},{1,3},{3,1},{5,7},{7,5},{8,10},{10,8},{12,... | collective-permute-start | bytes 294920 | tf_op jit(solution)/shard_map/ppermute | solution.py:620
  35.7 6.6 %collective-permute-start.11 = (bf16[384,128]{1,0:T(8,128)(2,1)S(1)}, bf16[384,128]{1,0:T(8,128)(2,1)S(1)}, u32[]{:S(2)}, u32[]{:S(2)}) collective-permute-start(bf16[384,128]{1,0:T(8,128)(2,1)S(1)} %get-tuple-element.78), channel_id=1, source_target_pairs={{0,6},{2,4},{4,2},{6,0},{1,7},{3,5},{5,3},{7,1},{8,14},{10,12},{12... | collective-permute-start | bytes 294920 | tf_op jit(solution)/shard_map/ppermute | solution.py:620
